TPU v7x, 512 devices: a whole 4x4x16 slice. The times are simulated.
512 devices in a mesh: expert: 16 (over z), replica: 32 (over y, x, core).
Axes of the slice: x: 4, y: 4, z: 16, core: 2. Of those that a mesh axis runs over, the one named last changes fastest.
Arguments:
- grads: bfloat16 [32, 2048, 2560], P('replica', 'expert'), may hold values from -6 to 6
- routes: int32 [32, 2048, 6], P('replica', 'expert'), may hold values from 0 to 15, all different within a row; in each aligned block of 128 rows (0 to 127, 128 to 255, ..., all dimensions but the last counted through in order) at most 56 rows name the same one
- gates: bfloat16 [32, 2048, 6], P('replica', 'expert'), may hold values from 0.049804688 to 0.5
- hidden: bfloat16 [32, 14336, 768], P('replica', 'expert'), may hold values from -0.375 to 0.375
- down_weight: bfloat16 [768, 16, 2560], P('replica', 'expert'), may hold values from -0.21875 to 0.21875
Outputs:
- d_hidden: bfloat16 [32, 14336, 768], P('replica', 'expert')
- down_grad: float32 [768, 16, 2560], P('replica', 'expert')
Inputs may be any that keep to these rules, and one draw needn't show every extreme that they name: `routes`: among the 128 tokens of one device no expert is named more than 56 times, and in every draw some expert is named exactly 56 times by the tokens of some device; a token names 6 different experts.
All inputs are finite; a program needn't handle non-finite values.
Results may differ from a plain program's by a relative error of at most 0.019.
Values may be sent and summed in bfloat16 or wider, within the bound.
No kernel may reach another device: no remote copies, remote signals or barrier semaphores. Data moves between devices by JAX's collectives and lax.ppermute only.
A program may use at most 128 MiB of HBM per device.

v0:
```python
import jax
import jax.numpy as jnp
from jax import lax
from jax.sharding import PartitionSpec as P


def body(grads, routes, gates, hidden, down_weight):
    groups = lax.axis_size("expert")
    width = grads.shape[2]
    tok_count = routes.shape[1]
    choices_per = routes.shape[2]
    exp_dev = down_weight.shape[1]
    experts = exp_dev * groups
    rows_dev = hidden.shape[1]
    hidden_width = hidden.shape[2]
    capacity = rows_dev // experts
    flat_routes = routes.reshape(tok_count * choices_per)
    onehot = (flat_routes[:, None] == jnp.arange(experts, dtype=jnp.int32)[None, :]).astype(
        jnp.int32
    )
    slot_rank = jnp.sum((jnp.cumsum(onehot, axis=0) - 1) * onehot, axis=1)
    target = flat_routes * capacity + slot_rank
    repeated = jnp.repeat(grads[0], choices_per, axis=0)
    weights_full = lax.all_gather(down_weight, "replica", axis=0, tiled=True)
    saved = hidden.reshape(groups, exp_dev, capacity, hidden_width)
    scaled_rows = (
        repeated.astype(jnp.float32)
        * gates.reshape(tok_count * choices_per)[:, None].astype(jnp.float32)
    ).astype(jnp.bfloat16)
    outgoing = jnp.zeros((experts * capacity, width), jnp.bfloat16).at[target].set(scaled_rows)
    outgoing = outgoing.reshape(groups, exp_dev, capacity, width)
    received = lax.all_to_all(outgoing, "expert", split_axis=0, concat_axis=0, tiled=True)
    d_part = jnp.einsum(
        "sjcd,fjd->sjcf", received, weights_full, preferred_element_type=jnp.float32
    )
    d_rows = d_part.astype(jnp.bfloat16)
    d_hidden = d_rows.reshape(1, rows_dev, hidden_width)
    weight_term = jnp.einsum("sjcf,sjcd->fjd", saved, received, preferred_element_type=jnp.float32)
    down_grad = lax.psum_scatter(
        weight_term.astype(jnp.bfloat16), "replica", scatter_dimension=0, tiled=True
    ).astype(jnp.float32)
    return (d_hidden, down_grad)


def solution(mesh):
    placed = (
        P("replica", "expert", None),
        P("replica", "expert", None),
        P("replica", "expert", None),
        P("replica", "expert", None),
        P("replica", "expert", None),
    )
    return jax.shard_map(
        body,
        mesh=mesh,
        in_specs=placed,
        out_specs=(P("replica", "expert", None), P("replica", "expert", None)),
        check_vma=False,
    )
```

profile of v0, /device:TPU:1, one launch (start us, length us, event | category | flops | bytes accessed | tf_op | source)
XLA Modules:
  0.0 442.5 jit_solution(6218299733479400681)
XLA Ops:
  7.2 0.0 copy-start
  7.2 0.9 copy.15
  8.1 0.1 eq.29
  8.2 0.1 eq.25
  8.4 0.7 broadcast_multiply_fusion
  9.1 1.7 reduce-window.6
  10.8 0.3 slice_reduce_fusion
  11.0 0.1 copy.14
  11.2 0.1 mul.29
  11.3 1.2 bitcast_convert_fusion.1
  12.5 5.3 %broadcast_in_dim.9 = f32[128,6,2560]{2,1,0:T(8,128)} broadcast(f32[128,2560]{1,0:T(8,128)S(1)} %bitcast_convert_fusion.1), dimensions={0,2} | broadcast | bytes 9175040 | tf_op jit(solution)/shard_map/broadcast_in_dim | solution.py:23
  17.8 0.0 copy-start.1
  17.8 9.5 %convert_element_type.56 = f32[768,2560]{1,0:T(8,128)} reshape(f32[128,6,2560]{2,1,0:T(8,128)} %broadcast_in_dim.9) | data formatting | bytes 15728640 | tf_op jit(solution)/shard_map/convert_element_type | solution.py:27
  27.3 0.0 copy-done.1
  27.3 0.1 copy.18
  27.5 0.1 reshape.94
  27.6 0.1 fusion.16
  27.7 16.0 %scatter_custom_fusion = bf16[896,2560]{1,0:T(8,128)(2,1)} fusion(s32[768]{0:T(1024)S(1)} %fusion.18, f32[768,2560]{1,0:T(8,128)} %convert_element_type.56, f32[768]{0:T(1024)S(1)} %reshape.94, bf16[]{:T(256)} %constant.5.clone.1), kind=kCustom, calls=%fused_computation.7 | custom fusion | flops 3932160 | bytes 12455938 | tf_op jit(solution)/shard_map/scatter | solution.py:30
  43.7 15.8 %all-to-all-start = ((bf16[16,1,56,2560]{3,2,1,0:T(8,128)(2,1)}), bf16[16,1,56,2560]{3,2,1,0:T(8,128)(2,1)}, u32[]{:S(2)}, u32[]{:S(2)}) async-start(bf16[16,1,56,2560]{3,2,1,0:T(8,128)(2,1)} %bitcast.54), calls=%async_computation | async-start | bytes 9175040 | tf_op jit(solution)/shard_map/all_to_all | solution.py:32
  59.5 0.0 all-gather.2.cloned.1.call-start
  59.6 0.7 all-gather.2.cloned.1.call-update
  60.3 0.2 all-reduce.3.cloned.1.call-start
  60.5 197.7 %all-to-all-done = bf16[16,1,56,2560]{3,2,1,0:T(8,128)(2,1)} async-done(((bf16[16,1,56,2560]{3,2,1,0:T(8,128)(2,1)}), bf16[16,1,56,2560]{3,2,1,0:T(8,128)(2,1)}, u32[]{:S(2)}, u32[]{:S(2)}) %all-to-all-start) | async-done | bytes 4587552 | tf_op jit(solution)/shard_map/all_to_all | solution.py:32
  258.2 0.0 copy-done
  258.2 8.3 %fusion.3 = bf16[768,1,2560]{0,2,1:T(8,128)(2,1)} fusion(bf16[16,56,768]{2,1,0:T(8,128)(2,1)S(1)} %bitcast.53, bf16[16,1,56,2560]{3,2,1,0:T(8,128)(2,1)} %all-to-all-done), kind=kOutput, calls=%fused_computation.6 | convolution fusion | flops 3525181440 | bytes 9895936 | tf_op jit(solution)/shard_map/sjcf,sjcd->fjd/dot_general | solution.py:38
  266.5 16.5 %copy.19 = bf16[768,1,2560]{2,1,0:T(2,128)(2,1)} copy(bf16[768,1,2560]{0,2,1:T(8,128)(2,1)} %fusion.3) | data formatting | bytes 7864320 | tf_op jit(solution)/shard_map/convert_element_type | solution.py:40
  282.9 0.0 all-reduce.3.cloned.1.call-update
  283.0 1.3 dynamic-slice
  284.9 0.0 all-gather.2.cloned.1.call-done
  284.9 8.4 %fusion.10 = bf16[16,56,768]{2,1,0:T(8,128)(2,1)} fusion(bf16[768,1,2560]{2,0,1:T(8,128)(2,1)} %all-gather.2.cloned.1.call-done, bf16[16,1,56,2560]{3,2,1,0:T(8,128)(2,1)} %all-to-all-done), kind=kOutput, calls=%fused_computation.11 | convolution fusion | flops 3523903488 | bytes 9895936 | tf_op jit(solution)/shard_map/sjcd,fjd->sjcf/dot_general | solution.py:33
  293.3 140.5 %all-reduce.3.cloned.1.call-done = bf16[768,1,2560]{2,1,0:T(2,128)(2,1)} async-done(((bf16[768,1,2560]{2,1,0:T(2,128)(2,1)}), bf16[768,1,2560]{2,1,0:T(2,128)(2,1)}) %all-reduce.3.cloned.1.call-update) | async-done | bytes 3932176
  433.7 1.9 dynamic-slice_convert_fusion
  (3 shorter events, 0.0 us)
Async XLA Ops:
  7.2 251.0 %copy-start = (bf16[1,896,768]{2,1,0:T(8,128)(2,1)S(1)}, bf16[1,896,768]{2,1,0:T(8,128)(2,1)}, u32[]{:S(2)}) copy-start(bf16[1,896,768]{2,1,0:T(8,128)(2,1)} %param.8) | copy-start | bytes 4128772
  17.8 9.5 %copy-start.1 = (bf16[1,128,6]{1,2,0:T(8,128)(2,1)S(1)}, bf16[1,128,6]{1,2,0:T(8,128)(2,1)}, u32[]{:S(2)}) copy-start(bf16[1,128,6]{1,2,0:T(8,128)(2,1)} %param.7) | copy-start | bytes 4612
  43.7 214.4 %all-to-all-start = ((bf16[16,1,56,2560]{3,2,1,0:T(8,128)(2,1)}), bf16[16,1,56,2560]{3,2,1,0:T(8,128)(2,1)}, u32[]{:S(2)}, u32[]{:S(2)}) async-start(bf16[16,1,56,2560]{3,2,1,0:T(8,128)(2,1)} %bitcast.54), calls=%async_computation | async-start | bytes 9175040 | tf_op jit(solution)/shard_map/all_to_all | solution.py:32
  59.5 225.4 %all-gather.2.cloned.1.call-start = ((), (), s32[]{:S(2)}) async-start(), calls=%async_computation.1 | async-start | bytes 4055040 | tf_op jit(solution)/shard_map/all_gather | solution.py:24
  60.3 373.5 %all-reduce.3.cloned.1.call-start = ((), (), s32[]{:S(2)}) async-start(), calls=%async_computation.2 | async-start | bytes 15728640
Sparse Core Ops, SparseCore 0:
  63.5 63.0 all-gather.1
  283.1 150.6 all-reduce.2
where the time goes:
time: 443 us; the launch traced here: 442 us
  waiting for transfers between devices  339 us (77%)
  local copies, waits for them, and re-layouts  34.5 us (8%)
  other arithmetic  21.7 us (5%)
  matrix products  16.7 us (4%)
  starting transfers between devices  16 us (4%)
  between operations  14.8 us (3%)
    all_to_all x1, waiting for transfers between devices, body(): lax.all_to_all(outgoing, 'expert', split_axis=0, concat_axis=0, tiled=True)  198 us
    unnamed x3, waiting for transfers between devices  141 us
    convert_element_type x1, local copies, waits for them, and re-layouts, body(): weight_term.astype(jnp.bfloat16)  16.5 us
    scatter x1, other arithmetic, body(): jnp.zeros((experts * capacity, width), jnp.bfloat16).at[target]  16 us
    all_to_all x1, starting transfers between devices, body(): lax.all_to_all(outgoing, 'expert', split_axis=0, concat_axis=0, tiled=True)  15.8 us
    convert_element_type x1, local copies, waits for them, and re-layouts, body(): repeated.astype(jnp.float32)  9.5 us
  transfers between devices with their start and end apart: 3, of which 2 were waited for; matrix products, arithmetic and copies ran while one was open for 8% of the time, Pallas kernels for 0%

commit v1 on v0

v1 whole, which is shorter than its diff:
```python
import jax
import jax.numpy as jnp
from jax import lax
from jax.experimental import pallas as pl
from jax.experimental.pallas import tpu as pltpu
from jax.sharding import PartitionSpec as P

BF = jnp.bfloat16
F32 = jnp.float32
LANES = 128
INFO_ROWS = 8


def _info_kernel(routes_ref, gates_ref, info_ref):
    tokens, top = routes_ref.shape
    routes = routes_ref[...]
    gates = gates_ref[...].astype(F32)
    lane = lax.broadcasted_iota(jnp.int32, (tokens, LANES), 1)
    gate = jnp.zeros((tokens, LANES), F32)
    named = jnp.zeros((tokens, LANES), F32)
    for k in range(top):
        hit = routes[:, k : k + 1] == lane
        gate = jnp.where(hit, gates[:, k : k + 1], gate)
        named = jnp.where(hit, 1.0, named)
    row = lax.broadcasted_iota(jnp.int32, (tokens, tokens), 0)
    col = lax.broadcasted_iota(jnp.int32, (tokens, tokens), 1)
    earlier = jnp.where(col < row, 1.0, 0.0).astype(BF)
    rank = jnp.dot(earlier, named.astype(BF), preferred_element_type=F32)
    slot = jnp.where(named > 0.5, rank, -1.0)
    slot_t = slot.T
    gate_t = gate.T
    n = INFO_ROWS
    info_ref[...] = jnp.zeros_like(info_ref)
    info_ref[:, 0:tokens] = slot_t[0:n].astype(BF)
    info_ref[:, tokens : 2 * tokens] = gate_t[0:n].astype(BF)
    info_ref[:, 2 * tokens : 3 * tokens] = slot_t[n : 2 * n].astype(BF)
    info_ref[:, 3 * tokens : 4 * tokens] = gate_t[n : 2 * n].astype(BF)


def _info(routes, gates, width):
    return pl.pallas_call(
        _info_kernel,
        out_shape=jax.ShapeDtypeStruct((INFO_ROWS, width), BF),
        cost_estimate=pl.CostEstimate(flops=1 << 22, bytes_accessed=1 << 16, transcendentals=0),
        name="route_info",
    )(routes, gates)


def _select_kernel(count, tokens, meta_ref, *refs):
    firsts, seconds, out_ref = refs[:count], refs[count : 2 * count], refs[-1]
    capacity = out_ref.shape[1]
    half = firsts[0].shape[1]
    me = meta_ref[0]
    step = pl.program_id(0)
    for i in range(count):

        @pl.when(step == i)
        def _():
            info = seconds[i][tokens : tokens + INFO_ROWS, 0 : 4 * tokens].astype(F32)
            info = jnp.where(me >= INFO_ROWS, info[:, 2 * tokens :], info[:, : 2 * tokens])
            row = lax.broadcasted_iota(jnp.int32, info.shape, 0)
            mine = jnp.sum(jnp.where(row == lax.rem(me, INFO_ROWS), info, 0.0), axis=0, keepdims=True)
            slot = lax.broadcasted_iota(jnp.int32, (capacity, tokens), 0).astype(F32)
            pick = jnp.where(mine[:, :tokens] == slot, mine[:, tokens:], 0.0).astype(BF)
            out_ref[0, :, :half] = jnp.dot(
                pick, firsts[i][0:tokens, :], preferred_element_type=F32
            ).astype(BF)
            out_ref[0, :, half:] = jnp.dot(
                pick, seconds[i][0:tokens, :], preferred_element_type=F32
            ).astype(BF)


def _select(meta, firsts, seconds, rows, shape, name):
    count = len(firsts)
    tokens = firsts[0].shape[0]
    whole = [pl.BlockSpec(a.shape, lambda i, m: (0, 0)) for a in firsts + seconds]
    operands = list(firsts) + list(seconds)
    aliases = {}
    if rows is not None:
        whole.append(pl.BlockSpec(memory_space=pl.ANY))
        operands.append(rows)
        aliases = {1 + 2 * count: 0}

    def kernel(meta_ref, *refs):
        _select_kernel(count, tokens, meta_ref, *refs)

    return pl.pallas_call(
        kernel,
        grid_spec=pltpu.PrefetchScalarGridSpec(
            num_scalar_prefetch=1,
            grid=(count,),
            in_specs=whole,
            out_specs=pl.BlockSpec((1,) + shape[1:], lambda i, m: (m[1 + i], 0, 0)),
        ),
        out_shape=jax.ShapeDtypeStruct(shape, BF),
        input_output_aliases=aliases,
        compiler_params=pltpu.CompilerParams(vmem_limit_bytes=40 << 20),
        cost_estimate=pl.CostEstimate(
            flops=2 * count * shape[1] * tokens * shape[2],
            bytes_accessed=2 * count * (tokens + shape[1]) * shape[2],
            transcendentals=0,
        ),
        name=name,
    )(meta, *operands)


def _term_kernel(saved_ref, rows_ref, out_ref):
    out_ref[...] = jnp.dot(saved_ref[...], rows_ref[...], preferred_element_type=F32).astype(BF)


def _term(saved_t, rows, name):
    units, depth = saved_t.shape
    width = rows.shape[1]
    block = 512 if width % 512 == 0 else LANES
    return pl.pallas_call(
        _term_kernel,
        grid=(width // block,),
        in_specs=[
            pl.BlockSpec((units, depth), lambda j: (0, 0)),
            pl.BlockSpec((depth, block), lambda j: (0, j)),
        ],
        out_specs=pl.BlockSpec((units, block), lambda j: (0, j)),
        out_shape=jax.ShapeDtypeStruct((units, width), BF),
        compiler_params=pltpu.CompilerParams(vmem_limit_bytes=40 << 20),
        cost_estimate=pl.CostEstimate(
            flops=2 * units * depth * width,
            bytes_accessed=2 * (units * depth + depth * width + units * width),
            transcendentals=0,
        ),
        name=name,
    )(saved_t, rows)


def body(grads, routes, gates, hidden, down_weight):
    groups = lax.axis_size("expert")
    replicas = lax.axis_size("replica")
    chips = replicas // 2
    width = grads.shape[2]
    units_dev = down_weight.shape[0]
    rows_dev = hidden.shape[1]
    units = hidden.shape[2]
    capacity = rows_dev // groups
    half = width // 2
    me = lax.axis_index("expert")
    core = lax.rem(lax.axis_index("replica"), 2)

    weights = lax.all_gather(down_weight, "replica", axis=0, tiled=True)

    own_first = grads[0, :, :half]
    own_second = jnp.concatenate(
        [grads[0, :, half:], _info(routes[0], gates[0], half)], axis=0
    )
    up = [(i, (i + 1) % groups) for i in range(groups)]
    down = [(i, (i - 1) % groups) for i in range(groups)]
    far = groups // 2
    got_first, got_second = {0: own_first}, {0: own_second}
    a_up = a_down = own_first
    b_up = b_down = own_second
    for hop in range(1, far + 1):
        a_up = lax.ppermute(a_up, "expert", up)
        if hop < far:
            a_down = lax.ppermute(a_down, "expert", down)
            b_up = lax.ppermute(b_up, "expert", up)
        b_down = lax.ppermute(b_down, "expert", down)
        got_first[-hop], got_second[hop] = a_up, b_down
        if hop < far:
            got_first[hop], got_second[-hop] = a_down, b_up
    got_second[-far] = got_second.pop(far)

    saved_t = hidden[0].T.reshape(chips, 2, units_dev, rows_dev).transpose(1, 0, 2, 3)
    saved_t = saved_t.reshape(2, units // 2, rows_dev)
    saved_mine = lax.dynamic_index_in_dim(saved_t, core, 0, keepdims=False)
    saved_other = lax.dynamic_index_in_dim(saved_t, 1 - core, 0, keepdims=False)

    rows = None
    shape = (groups, capacity, width)
    batches = [
        [0, -1, 1, -2, 2],
        [-3, 3, -4, 4],
        [-5, 5, -6, 6],
        [-7, 7, -8],
    ]
    for number, batch in enumerate(batches):
        source = [lax.rem(me + off + groups, groups) for off in batch]
        meta = jnp.stack([me] + source).astype(jnp.int32)
        rows = _select(
            meta,
            [got_first[off] for off in batch],
            [got_second[off] for off in batch],
            rows,
            shape,
            f"select_{number}",
        )
    rows = rows.reshape(rows_dev, width)

    other = _term(saved_other, rows, "term_other")
    arrived = lax.ppermute(other, "replica", [(i, i ^ 1) for i in range(replicas)])
    mine = _term(saved_mine, rows, "term_mine")
    pair = (mine.astype(F32) + arrived.astype(F32)).astype(BF)
    parts = lax.all_to_all(
        pair.reshape(chips, units_dev, width),
        "replica",
        split_axis=0,
        concat_axis=0,
        tiled=True,
        axis_index_groups=[[2 * q + c for q in range(chips)] for c in range(2)],
    )
    down_grad = jnp.sum(parts.astype(F32), axis=0)[:, None, :]

    d_rows = lax.dot_general(
        rows, weights[:, 0, :], (((1,), (1,)), ((), ())), preferred_element_type=F32
    )
    d_hidden = d_rows.astype(BF)[None]
    return (d_hidden, down_grad)


def solution(mesh):
    placed = (P("replica", "expert", None),) * 5
    return jax.shard_map(
        body,
        mesh=mesh,
        in_specs=placed,
        out_specs=(P("replica", "expert", None), P("replica", "expert", None)),
        check_vma=False,
    )
```

time: 443 us -> 214 us (0.48)
  waiting for transfers between devices: 339 us -> 4.73 us
  starting transfers between devices: 16 us -> 110 us
  blocking collectives: 0 us -> 33 us
  other arithmetic: 21.7 us -> 1.58 us
  Pallas kernels: 0 us -> 17.5 us
  local copies, waits for them, and re-layouts: 34.5 us -> 22 us
  matrix products: 16.7 us -> 8.34 us
    all_to_all x1 -> x0, waiting for transfers between devices: 198 us -> none  [body(): lax.all_to_all(outgoing, 'expert', split_axis=0, concat_axis=0, tiled=True)]
    unnamed x3 -> x1, waiting for transfers between devices: 141 us -> 0.02 us
    ppermute x0 -> x31, starting transfers between devices: none -> 110 us  [the longest x8 44.7 us: body(): b_down = lax.ppermute(b_down, 'expert', down)]
    all_to_all x0 -> x1, blocking collectives: none -> 33 us  [body(): lax.all_to_all(pair.reshape(chips, units_dev, width), 'replica', split_ax...]
    convert_element_type x4 -> x0, local copies, waits for them, and re-layouts: 26.2 us -> none  [the longest x1 16.5 us: body(): weight_term.astype(jnp.bfloat16)]
    pallas_call x0 -> x7, Pallas kernels: none -> 17.5 us  [the longest x4 9.08 us: _select(): pl.pallas_call(kernel, grid_spec=pltpu.PrefetchScalarGridSpec(num_scalar_...]
    scatter x1 -> x0, other arithmetic: 16 us -> none  [body(): jnp.zeros((experts * capacity, width), jnp.bfloat16).at[target]]
    all_to_all x1 -> x0, starting transfers between devices: 15.8 us -> none  [body(): lax.all_to_all(outgoing, 'expert', split_axis=0, concat_axis=0, tiled=True)]
  transfers between devices with their start and end apart: 3 -> 32, of which waited for: 2 -> 5; matrix products, arithmetic and copies ran while one was open for 8% -> 4% of each run, Pallas kernels for 0% -> 7%
where the time goes in v1:
time: 214 us; the launch traced here: 212 us
  starting transfers between devices  110 us (51%)
  blocking collectives  33 us (15%)
  local copies, waits for them, and re-layouts  22 us (10%)
  Pallas kernels  17.5 us (8%)
  between operations  14.8 us (7%)
  matrix products  8.34 us (4%)
  waiting for transfers between devices  4.73 us (2%)
    ppermute x8, starting transfers between devices, body(): b_down = lax.ppermute(b_down, 'expert', down)  44.7 us
    all_to_all x1, blocking collectives, body(): lax.all_to_all(pair.reshape(chips, units_dev, width), 'replica', split_ax...  33 us
    ppermute x7, starting transfers between devices, body(): a_down = lax.ppermute(a_down, 'expert', down)  23.4 us
    ppermute x8, starting transfers between devices, body(): a_up = lax.ppermute(a_up, 'expert', up)  18.6 us
    unnamed x61, local copies, waits for them, and re-layouts  15.7 us
    ppermute x7, starting transfers between devices, body(): b_up = lax.ppermute(b_up, 'expert', up)  13.4 us
    ppermute x1, starting transfers between devices, body(): lax.ppermute(other, 'replica', [(i, i ^ 1) for i in range(replicas)])  10.3 us
    pallas_call x4, Pallas kernels, _select(): pl.pallas_call(kernel, grid_spec=pltpu.PrefetchScalarGridSpec(num_scalar_...  9.08 us
  transfers between devices with their start and end apart: 32, of which 5 were waited for; matrix products, arithmetic and copies ran while one was open for 4% of the time, Pallas kernels for 7%

profile of v1, /device:TPU:1, one launch (start us, length us, event | category | flops | bytes accessed | tf_op | source)
XLA Modules:
  0.0 212.3 jit_solution(6541901998932886357)
XLA Ops:
  13.8 12.0 %collective-permute-start.22 = (bf16[136,1280]{1,0:T(8,128)(2,1)S(1)}, bf16[136,1280]{1,0:T(8,128)(2,1)S(1)}, u32[]{:S(2)}, u32[]{:S(2)}) collective-permute-start(bf16[136,1280]{1,0:T(8,128)(2,1)S(1)} %pad_maximum_fusion.refs_5_), channel_id=1, source_target_pairs={{0,480},{32,0},{64,32},{96,64},{128,96},{160,128},{192,160},{224,1... | collective-permute-start | bytes 1044488 | tf_op jit(solution)/shard_map/ppermute | solution.py:164
  25.7 1.9 collective-permute-start
  27.7 1.9 collective-permute-start.15
  29.6 2.9 %collective-permute-done.22.refs_7_ = bf16[136,1280]{1,0:T(8,128)(2,1)S(1)} collective-permute-done((bf16[136,1280]{1,0:T(8,128)(2,1)S(1)}, bf16[136,1280]{1,0:T(8,128)(2,1)S(1)}, u32[]{:S(2)}, u32[]{:S(2)}) %collective-permute-start.22) | collective-permute-done | bytes 348192 | tf_op jit(solution)/shard_map/ppermute | solution.py:164
  32.5 5.3 %collective-permute-start.23 = (bf16[136,1280]{1,0:T(8,128)(2,1)S(1)}, bf16[136,1280]{1,0:T(8,128)(2,1)S(1)}, u32[]{:S(2)}, u32[]{:S(2)}) collective-permute-start(bf16[136,1280]{1,0:T(8,128)(2,1)S(1)} %collective-permute-done.22.refs_7_), channel_id=1, source_target_pairs={{0,480},{32,0},{64,32},{96,64},{128,96},{160,128},{192,160},{224,1... | collective-permute-start | bytes 1044488 | tf_op jit(solution)/shard_map/ppermute | solution.py:164
  37.8 1.9 collective-permute-start.7
  39.8 3.4 %collective-permute-start.1 = (bf16[128,1280]{1,0:T(8,128)(2,1)S(1)}, bf16[128,1280]{1,0:T(8,128)(2,1)S(1)}, u32[]{:S(2)}, u32[]{:S(2)}) collective-permute-start(bf16[128,1280]{1,0:T(8,128)(2,1)S(1)} %collective-permute-done.refs_1_), channel_id=1, source_target_pairs={{0,32},{32,64},{64,96},{96,128},{128,160},{160,192},{192,224},{224... | collective-permute-start | bytes 983048 | tf_op jit(solution)/shard_map/ppermute | solution.py:160
  46.5 4.6 %collective-permute-start.24 = (bf16[136,1280]{1,0:T(8,128)(2,1)S(1)}, bf16[136,1280]{1,0:T(8,128)(2,1)S(1)}, u32[]{:S(2)}, u32[]{:S(2)}) collective-permute-start(bf16[136,1280]{1,0:T(8,128)(2,1)S(1)} %collective-permute-done.23.refs_9_), channel_id=1, source_target_pairs={{0,480},{32,0},{64,32},{96,64},{128,96},{160,128},{192,160},{224,1... | collective-permute-start | bytes 1044488 | tf_op jit(solution)/shard_map/ppermute | solution.py:164
  51.1 5.0 %collective-permute-start.8 = (bf16[128,1280]{1,0:T(8,128)(2,1)S(1)}, bf16[128,1280]{1,0:T(8,128)(2,1)S(1)}, u32[]{:S(2)}, u32[]{:S(2)}) collective-permute-start(bf16[128,1280]{1,0:T(8,128)(2,1)S(1)} %collective-permute-done.7.refs_2_), channel_id=1, source_target_pairs={{0,480},{32,0},{64,32},{96,64},{128,96},{160,128},{192,160},{224,1... | collective-permute-start | bytes 983048 | tf_op jit(solution)/shard_map/ppermute | solution.py:162
  61.3 4.6 %collective-permute-start.25 = (bf16[136,1280]{1,0:T(8,128)(2,1)S(1)}, bf16[136,1280]{1,0:T(8,128)(2,1)S(1)}, u32[]{:S(2)}, u32[]{:S(2)}) collective-permute-start(bf16[136,1280]{1,0:T(8,128)(2,1)S(1)} %collective-permute-done.24.refs_5_), channel_id=1, source_target_pairs={{0,480},{32,0},{64,32},{96,64},{128,96},{160,128},{192,160},{224,1... | collective-permute-start | bytes 1044488 | tf_op jit(solution)/shard_map/ppermute | solution.py:164
  65.9 4.9 %collective-permute-start.9 = (bf16[128,1280]{1,0:T(8,128)(2,1)S(1)}, bf16[128,1280]{1,0:T(8,128)(2,1)S(1)}, u32[]{:S(2)}, u32[]{:S(2)}) collective-permute-start(bf16[128,1280]{1,0:T(8,128)(2,1)S(1)} %collective-permute-done.8.refs_4_), channel_id=1, source_target_pairs={{0,480},{32,0},{64,32},{96,64},{128,96},{160,128},{192,160},{224,1... | collective-permute-start | bytes 983048 | tf_op jit(solution)/shard_map/ppermute | solution.py:162
  76.2 4.6 %collective-permute-start.26 = (bf16[136,1280]{1,0:T(8,128)(2,1)S(1)}, bf16[136,1280]{1,0:T(8,128)(2,1)S(1)}, u32[]{:S(2)}, u32[]{:S(2)}) collective-permute-start(bf16[136,1280]{1,0:T(8,128)(2,1)S(1)} %collective-permute-done.25.refs_7_), channel_id=1, source_target_pairs={{0,480},{32,0},{64,32},{96,64},{128,96},{160,128},{192,160},{224,1... | collective-permute-start | bytes 1044488 | tf_op jit(solution)/shard_map/ppermute | solution.py:164
  80.7 3.4 %collective-permute-start.10 = (bf16[128,1280]{1,0:T(8,128)(2,1)S(1)}, bf16[128,1280]{1,0:T(8,128)(2,1)S(1)}, u32[]{:S(2)}, u32[]{:S(2)}) collective-permute-start(bf16[128,1280]{1,0:T(8,128)(2,1)S(1)} %collective-permute-done.9.refs_1_), channel_id=1, source_target_pairs={{0,480},{32,0},{64,32},{96,64},{128,96},{160,128},{192,160},{224,1... | collective-permute-start | bytes 983048 | tf_op jit(solution)/shard_map/ppermute | solution.py:162
  89.7 4.6 %collective-permute-start.27 = (bf16[136,1280]{1,0:T(8,128)(2,1)S(1)}, bf16[136,1280]{1,0:T(8,128)(2,1)S(1)}, u32[]{:S(2)}, u32[]{:S(2)}) collective-permute-start(bf16[136,1280]{1,0:T(8,128)(2,1)S(1)} %collective-permute-done.26.refs_5_), channel_id=1, source_target_pairs={{0,480},{32,0},{64,32},{96,64},{128,96},{160,128},{192,160},{224,1... | collective-permute-start | bytes 1044488 | tf_op jit(solution)/shard_map/ppermute | solution.py:164
  95.0 3.1 %collective-permute-start.11 = (bf16[128,1280]{1,0:T(8,128)(2,1)S(1)}, bf16[128,1280]{1,0:T(8,128)(2,1)S(1)}, u32[]{:S(2)}, u32[]{:S(2)}) collective-permute-start(bf16[128,1280]{1,0:T(8,128)(2,1)S(1)} %collective-permute-done.10.refs_3_), channel_id=1, source_target_pairs={{0,480},{32,0},{64,32},{96,64},{128,96},{160,128},{192,160},{224,1... | collective-permute-start | bytes 983048 | tf_op jit(solution)/shard_map/ppermute | solution.py:162
  98.9 2.2 %collective-permute-start.5 = (bf16[128,1280]{1,0:T(8,128)(2,1)S(1)}, bf16[128,1280]{1,0:T(8,128)(2,1)S(1)}, u32[]{:S(2)}, u32[]{:S(2)}) collective-permute-start(bf16[128,1280]{1,0:T(8,128)(2,1)S(1)} %collective-permute-done.4.refs_0_), channel_id=1, source_target_pairs={{0,32},{32,64},{64,96},{96,128},{128,160},{160,192},{192,224},{224... | collective-permute-start | bytes 983048 | tf_op jit(solution)/shard_map/ppermute | solution.py:160
  105.0 4.6 %collective-permute-start.28 = (bf16[136,1280]{1,0:T(8,128)(2,1)S(1)}, bf16[136,1280]{1,0:T(8,128)(2,1)}, u32[]{:S(2)}, u32[]{:S(2)}) collective-permute-start(bf16[136,1280]{1,0:T(8,128)(2,1)S(1)} %collective-permute-done.27.refs_7_), channel_id=1, source_target_pairs={{0,480},{32,0},{64,32},{96,64},{128,96},{160,128},{192,160},{224,1... | collective-permute-start | bytes 1044488 | tf_op jit(solution)/shard_map/ppermute | solution.py:164
  110.3 2.6 %collective-permute-start.12 = (bf16[128,1280]{1,0:T(8,128)(2,1)S(1)}, bf16[128,1280]{1,0:T(8,128)(2,1)}, u32[]{:S(2)}, u32[]{:S(2)}) collective-permute-start(bf16[128,1280]{1,0:T(8,128)(2,1)S(1)} %collective-permute-done.11.refs_1_), channel_id=1, source_target_pairs={{0,480},{32,0},{64,32},{96,64},{128,96},{160,128},{192,160},{224,1... | collective-permute-start | bytes 983048 | tf_op jit(solution)/shard_map/ppermute | solution.py:162
  113.6 2.7 %collective-permute-start.6 = (bf16[128,1280]{1,0:T(8,128)(2,1)S(1)}, bf16[128,1280]{1,0:T(8,128)(2,1)}, u32[]{:S(2)}, u32[]{:S(2)}) collective-permute-start(bf16[128,1280]{1,0:T(8,128)(2,1)S(1)} %collective-permute-done.5.refs_2_), channel_id=1, source_target_pairs={{0,32},{32,64},{64,96},{96,128},{128,160},{160,192},{192,224},{224... | collective-permute-start | bytes 983048 | tf_op jit(solution)/shard_map/ppermute | solution.py:160
  117.1 1.9 collective-permute-start.21
  119.0 4.6 %collective-permute-start.29 = (bf16[136,1280]{1,0:T(8,128)(2,1)}, bf16[136,1280]{1,0:T(8,128)(2,1)}, u32[]{:S(2)}, u32[]{:S(2)}) collective-permute-start(bf16[136,1280]{1,0:T(8,128)(2,1)} %collective-permute-done.28.refs_4_), channel_id=1, source_target_pairs={{0,480},{32,0},{64,32},{96,64},{128,96},{160,128},{192,160},{224,1... | collective-permute-start | bytes 1044488 | tf_op jit(solution)/shard_map/ppermute | solution.py:164
  123.6 2.6 %collective-permute-start.13 = (bf16[128,1280]{1,0:T(8,128)(2,1)}, bf16[128,1280]{1,0:T(8,128)(2,1)}, u32[]{:S(2)}, u32[]{:S(2)}) collective-permute-start(bf16[128,1280]{1,0:T(8,128)(2,1)} %collective-permute-done.12.refs_3_), channel_id=1, source_target_pairs={{0,480},{32,0},{64,32},{96,64},{128,96},{160,128},{192,160},{224,1... | collective-permute-start | bytes 983048 | tf_op jit(solution)/shard_map/ppermute | solution.py:162
  126.2 2.7 %collective-permute-start.14 = (bf16[128,1280]{1,0:T(8,128)(2,1)}, bf16[128,1280]{1,0:T(8,128)(2,1)}, u32[]{:S(2)}, u32[]{:S(2)}) collective-permute-start(bf16[128,1280]{1,0:T(8,128)(2,1)} %collective-permute-done.6.refs_0_), channel_id=1, source_target_pairs={{0,32},{32,64},{64,96},{96,128},{128,160},{160,192},{192,224},{224... | collective-permute-start | bytes 983048 | tf_op jit(solution)/shard_map/ppermute | solution.py:160
  128.9 2.5 %copy.18 = bf16[1,896,768]{1,2,0:T(8,128)(2,1)} copy(bf16[1,896,768]{2,1,0:T(8,128)(2,1)} %param.8) | data formatting | bytes 2752512 | tf_op args[3]
  131.4 2.6 %copy.19 = bf16[2,16,24,896]{3,2,1,0:T(8,128)(2,1)} copy(bf16[2,16,24,896]{3,2,0,1:T(8,128)(2,1)} %bitcast.52) | data formatting | bytes 2752512 | tf_op jit(solution)/shard_map/transpose | solution.py:170
  139.6 2.7 %select_2.1.refs_6_ = bf16[16,56,2560]{2,1,0:T(8,128)(2,1)S(1)} custom-call(s32[5]{0:T(128)S(1)} %stack.75.meta_ref, bf16[128,1280]{1,0:T(8,128)(2,1)S(1)} %copy-done.24, bf16[128,1280]{1,0:T(8,128)(2,1)S(1)} %copy-done.26, bf16[128,1280]{1,0:T(8,128)(2,1)S(1)} %copy-done.28, ...), custom_call_target="tpu_custom_call", output_to_operand_aliasing={{}: (9, {})} | custom-call | flops 146800640 | bytes 3768320 | tf_op jit(solution)/shard_map/select_2/pallas_call | solution.py:87
  142.4 2.9 %select_3.1 = bf16[16,56,2560]{2,1,0:T(8,128)(2,1)S(1)} custom-call(s32[4]{0:T(128)S(1)} %pad_add_fusion.meta_ref, bf16[128,1280]{1,0:T(8,128)(2,1)} %collective-permute-done.6.refs_0_, bf16[128,1280]{1,0:T(8,128)(2,1)} %collective-permute-done.13.refs_1_, bf16[128,1280]{1,0:T(8,128)(2,1)} %collective-permute-done.14.refs_2_, ...), custom_call_target="tpu_custom_call", output_to_operand_aliasing={{}: (7, {})} | custom-call | flops 110100480 | bytes 2826240 | tf_op jit(solution)/shard_map/select_3/pallas_call | solution.py:87
  145.3 3.3 %term_other.1 = bf16[384,2560]{1,0:T(8,128)(2,1)S(1)} custom-call(bf16[384,896]{1,0:T(8,128)(2,1)S(1)} %get-tuple-element.3.saved_ref, bf16[896,2560]{1,0:T(8,128)(2,1)S(1)} %bitcast.47), custom_call_target="tpu_custom_call" | custom-call | flops 1761607680 | bytes 7241728 | tf_op jit(solution)/shard_map/term_other/pallas_call | solution.py:115
  148.6 10.3 %collective-permute-start.30 = (bf16[384,2560]{1,0:T(8,128)(2,1)S(1)}, bf16[384,2560]{1,0:T(8,128)(2,1)S(1)}, u32[]{:S(2)}, u32[]{:S(2)}) collective-permute-start(bf16[384,2560]{1,0:T(8,128)(2,1)S(1)} %term_other.1), channel_id=1, source_target_pairs={{0,1},{1,0},{2,3},{3,2},{4,5},{5,4},{6,7},{7,6},{8,9},{9,8},{10,11... | collective-permute-start | bytes 5898248 | tf_op jit(solution)/shard_map/ppermute | solution.py:197
  158.9 3.3 %term_mine.1 = bf16[384,2560]{1,0:T(8,128)(2,1)S(1)} custom-call(bf16[384,896]{1,0:T(8,128)(2,1)S(1)} %get-tuple-element.2.saved_ref, bf16[896,2560]{1,0:T(8,128)(2,1)S(1)} %bitcast.48), custom_call_target="tpu_custom_call" | custom-call | flops 1761607680 | bytes 7241728 | tf_op jit(solution)/shard_map/term_mine/pallas_call | solution.py:115
  163.0 33.0 %all_to_all.5 = bf16[16,24,2560]{2,1,0:T(8,128)(2,1)S(1)} all-to-all(bf16[16,24,2560]{2,1,0:T(8,128)(2,1)S(1)} %bitcast.50), channel_id=1, replica_groups={{0,2,4,6,8,10,12,14,16,18,20,22,24,26,28,30},{1,3,5,7,9,11,13,15,17,19,..., dimensions={0} | all-to-all | bytes 3932160 | tf_op jit(solution)/shard_map/all_to_all | solution.py:200
  197.1 8.3 %fusion.5 = bf16[1,896,768]{2,1,0:T(8,128)(2,1)} fusion(bf16[896,2560]{1,0:T(8,128)(2,1)} %bitcast.49, bf16[768,1,2560]{2,0,1:T(8,128)(2,1)} %all-gather.2.cloned.1.call-done), kind=kOutput, calls=%fused_computation.5 | convolution fusion | flops 3523903488 | bytes 9895936 | tf_op jit(solution)/shard_map/dot_general | solution.py:210
  (114 shorter events, 40.9 us)
Async XLA Ops:
  7.2 189.9 %all-gather.2.cloned.1.call-start = ((), (), s32[]{:S(2)}) async-start(), calls=%async_computation.1 | async-start | bytes 4055040 | tf_op jit(solution)/shard_map/all_gather | solution.py:147
  13.8 18.8 %collective-permute-start.22 = (bf16[136,1280]{1,0:T(8,128)(2,1)S(1)}, bf16[136,1280]{1,0:T(8,128)(2,1)S(1)}, u32[]{:S(2)}, u32[]{:S(2)}) collective-permute-start(bf16[136,1280]{1,0:T(8,128)(2,1)S(1)} %pad_maximum_fusion.refs_5_), channel_id=1, source_target_pairs={{0,480},{32,0},{64,32},{96,64},{128,96},{160,128},{192,160},{224,1... | collective-permute-start | bytes 1044488 | tf_op jit(solution)/shard_map/ppermute | solution.py:164
  25.7 14.0 %collective-permute-start = (bf16[128,1280]{1,0:T(8,128)(2,1)S(1)}, bf16[128,1280]{1,0:T(8,128)(2,1)S(1)}, u32[]{:S(2)}, u32[]{:S(2)}) collective-permute-start(bf16[128,1280]{1,0:T(8,128)(2,1)S(1)} %get-tuple-element.5.refs_0_), channel_id=1, source_target_pairs={{0,32},{32,64},{64,96},{96,128},{128,160},{160,192},{192,224},{224... | collective-permute-start | bytes 983048 | tf_op jit(solution)/shard_map/ppermute | solution.py:160
  27.7 16.9 %collective-permute-start.15 = (bf16[136,1280]{1,0:T(8,128)(2,1)S(1)}, bf16[136,1280]{1,0:T(8,128)(2,1)S(1)}, u32[]{:S(2)}, u32[]{:S(2)}) collective-permute-start(bf16[136,1280]{1,0:T(8,128)(2,1)S(1)} %pad_maximum_fusion.refs_5_), channel_id=1, source_target_pairs={{0,32},{32,64},{64,96},{96,128},{128,160},{160,192},{192,224},{224... | collective-permute-start | bytes 1044488 | tf_op jit(solution)/shard_map/ppermute | solution.py:163
  32.5 14.0 %collective-permute-start.23 = (bf16[136,1280]{1,0:T(8,128)(2,1)S(1)}, bf16[136,1280]{1,0:T(8,128)(2,1)S(1)}, u32[]{:S(2)}, u32[]{:S(2)}) collective-permute-start(bf16[136,1280]{1,0:T(8,128)(2,1)S(1)} %collective-permute-done.22.refs_7_), channel_id=1, source_target_pairs={{0,480},{32,0},{64,32},{96,64},{128,96},{160,128},{192,160},{224,1... | collective-permute-start | bytes 1044488 | tf_op jit(solution)/shard_map/ppermute | solution.py:164
  37.8 13.2 %collective-permute-start.7 = (bf16[128,1280]{1,0:T(8,128)(2,1)S(1)}, bf16[128,1280]{1,0:T(8,128)(2,1)S(1)}, u32[]{:S(2)}, u32[]{:S(2)}) collective-permute-start(bf16[128,1280]{1,0:T(8,128)(2,1)S(1)} %get-tuple-element.5.refs_0_), channel_id=1, source_target_pairs={{0,480},{32,0},{64,32},{96,64},{128,96},{160,128},{192,160},{224,1... | collective-permute-start | bytes 983048 | tf_op jit(solution)/shard_map/ppermute | solution.py:162
  39.8 17.0 %collective-permute-start.1 = (bf16[128,1280]{1,0:T(8,128)(2,1)S(1)}, bf16[128,1280]{1,0:T(8,128)(2,1)S(1)}, u32[]{:S(2)}, u32[]{:S(2)}) collective-permute-start(bf16[128,1280]{1,0:T(8,128)(2,1)S(1)} %collective-permute-done.refs_1_), channel_id=1, source_target_pairs={{0,32},{32,64},{64,96},{96,128},{128,160},{160,192},{192,224},{224... | collective-permute-start | bytes 983048 | tf_op jit(solution)/shard_map/ppermute | solution.py:160
  44.5 14.9 %collective-permute-start.16 = (bf16[136,1280]{1,0:T(8,128)(2,1)S(1)}, bf16[136,1280]{1,0:T(8,128)(2,1)S(1)}, u32[]{:S(2)}, u32[]{:S(2)}) collective-permute-start(bf16[136,1280]{1,0:T(8,128)(2,1)S(1)} %collective-permute-done.15.refs_6_), channel_id=1, source_target_pairs={{0,32},{32,64},{64,96},{96,128},{128,160},{160,192},{192,224},{224... | collective-permute-start | bytes 1044488 | tf_op jit(solution)/shard_map/ppermute | solution.py:163
  46.5 14.9 %collective-permute-start.24 = (bf16[136,1280]{1,0:T(8,128)(2,1)S(1)}, bf16[136,1280]{1,0:T(8,128)(2,1)S(1)}, u32[]{:S(2)}, u32[]{:S(2)}) collective-permute-start(bf16[136,1280]{1,0:T(8,128)(2,1)S(1)} %collective-permute-done.23.refs_9_), channel_id=1, source_target_pairs={{0,480},{32,0},{64,32},{96,64},{128,96},{160,128},{192,160},{224,1... | collective-permute-start | bytes 1044488 | tf_op jit(solution)/shard_map/ppermute | solution.py:164
  51.1 14.9 %collective-permute-start.8 = (bf16[128,1280]{1,0:T(8,128)(2,1)S(1)}, bf16[128,1280]{1,0:T(8,128)(2,1)S(1)}, u32[]{:S(2)}, u32[]{:S(2)}) collective-permute-start(bf16[128,1280]{1,0:T(8,128)(2,1)S(1)} %collective-permute-done.7.refs_2_), channel_id=1, source_target_pairs={{0,480},{32,0},{64,32},{96,64},{128,96},{160,128},{192,160},{224,1... | collective-permute-start | bytes 983048 | tf_op jit(solution)/shard_map/ppermute | solution.py:162
  56.8 14.8 %collective-permute-start.2 = (bf16[128,1280]{1,0:T(8,128)(2,1)S(1)}, bf16[128,1280]{1,0:T(8,128)(2,1)S(1)}, u32[]{:S(2)}, u32[]{:S(2)}) collective-permute-start(bf16[128,1280]{1,0:T(8,128)(2,1)S(1)} %collective-permute-done.1.refs_3_), channel_id=1, source_target_pairs={{0,32},{32,64},{64,96},{96,128},{128,160},{160,192},{192,224},{224... | collective-permute-start | bytes 983048 | tf_op jit(solution)/shard_map/ppermute | solution.py:160
  59.4 14.8 %collective-permute-start.17 = (bf16[136,1280]{1,0:T(8,128)(2,1)S(1)}, bf16[136,1280]{1,0:T(8,128)(2,1)S(1)}, u32[]{:S(2)}, u32[]{:S(2)}) collective-permute-start(bf16[136,1280]{1,0:T(8,128)(2,1)S(1)} %collective-permute-done.16.refs_8_), channel_id=1, source_target_pairs={{0,32},{32,64},{64,96},{96,128},{128,160},{160,192},{192,224},{224... | collective-permute-start | bytes 1044488 | tf_op jit(solution)/shard_map/ppermute | solution.py:163
  61.3 14.8 %collective-permute-start.25 = (bf16[136,1280]{1,0:T(8,128)(2,1)S(1)}, bf16[136,1280]{1,0:T(8,128)(2,1)S(1)}, u32[]{:S(2)}, u32[]{:S(2)}) collective-permute-start(bf16[136,1280]{1,0:T(8,128)(2,1)S(1)} %collective-permute-done.24.refs_5_), channel_id=1, source_target_pairs={{0,480},{32,0},{64,32},{96,64},{128,96},{160,128},{192,160},{224,1... | collective-permute-start | bytes 1044488 | tf_op jit(solution)/shard_map/ppermute | solution.py:164
  65.9 14.8 %collective-permute-start.9 = (bf16[128,1280]{1,0:T(8,128)(2,1)S(1)}, bf16[128,1280]{1,0:T(8,128)(2,1)S(1)}, u32[]{:S(2)}, u32[]{:S(2)}) collective-permute-start(bf16[128,1280]{1,0:T(8,128)(2,1)S(1)} %collective-permute-done.8.refs_4_), channel_id=1, source_target_pairs={{0,480},{32,0},{64,32},{96,64},{128,96},{160,128},{192,160},{224,1... | collective-permute-start | bytes 983048 | tf_op jit(solution)/shard_map/ppermute | solution.py:162
  71.5 13.3 %collective-permute-start.3 = (bf16[128,1280]{1,0:T(8,128)(2,1)S(1)}, bf16[128,1280]{1,0:T(8,128)(2,1)S(1)}, u32[]{:S(2)}, u32[]{:S(2)}) collective-permute-start(bf16[128,1280]{1,0:T(8,128)(2,1)S(1)} %collective-permute-done.2.refs_0_), channel_id=1, source_target_pairs={{0,32},{32,64},{64,96},{96,128},{128,160},{160,192},{192,224},{224... | collective-permute-start | bytes 983048 | tf_op jit(solution)/shard_map/ppermute | solution.py:160
  74.2 13.5 %collective-permute-start.18 = (bf16[136,1280]{1,0:T(8,128)(2,1)S(1)}, bf16[136,1280]{1,0:T(8,128)(2,1)S(1)}, u32[]{:S(2)}, u32[]{:S(2)}) collective-permute-start(bf16[136,1280]{1,0:T(8,128)(2,1)S(1)} %collective-permute-done.17.refs_4_), channel_id=1, source_target_pairs={{0,32},{32,64},{64,96},{96,128},{128,160},{160,192},{192,224},{224... | collective-permute-start | bytes 1044488 | tf_op jit(solution)/shard_map/ppermute | solution.py:163
  76.2 13.5 %collective-permute-start.26 = (bf16[136,1280]{1,0:T(8,128)(2,1)S(1)}, bf16[136,1280]{1,0:T(8,128)(2,1)S(1)}, u32[]{:S(2)}, u32[]{:S(2)}) collective-permute-start(bf16[136,1280]{1,0:T(8,128)(2,1)S(1)} %collective-permute-done.25.refs_7_), channel_id=1, source_target_pairs={{0,480},{32,0},{64,32},{96,64},{128,96},{160,128},{192,160},{224,1... | collective-permute-start | bytes 1044488 | tf_op jit(solution)/shard_map/ppermute | solution.py:164
  80.7 14.3 %collective-permute-start.10 = (bf16[128,1280]{1,0:T(8,128)(2,1)S(1)}, bf16[128,1280]{1,0:T(8,128)(2,1)S(1)}, u32[]{:S(2)}, u32[]{:S(2)}) collective-permute-start(bf16[128,1280]{1,0:T(8,128)(2,1)S(1)} %collective-permute-done.9.refs_1_), channel_id=1, source_target_pairs={{0,480},{32,0},{64,32},{96,64},{128,96},{160,128},{192,160},{224,1... | collective-permute-start | bytes 983048 | tf_op jit(solution)/shard_map/ppermute | solution.py:162
  84.8 14.0 %collective-permute-start.4 = (bf16[128,1280]{1,0:T(8,128)(2,1)S(1)}, bf16[128,1280]{1,0:T(8,128)(2,1)S(1)}, u32[]{:S(2)}, u32[]{:S(2)}) collective-permute-start(bf16[128,1280]{1,0:T(8,128)(2,1)S(1)} %collective-permute-done.3.refs_2_), channel_id=1, source_target_pairs={{0,32},{32,64},{64,96},{96,128},{128,160},{160,192},{192,224},{224... | collective-permute-start | bytes 983048 | tf_op jit(solution)/shard_map/ppermute | solution.py:160
  87.8 14.5 %collective-permute-start.19 = (bf16[136,1280]{1,0:T(8,128)(2,1)S(1)}, bf16[136,1280]{1,0:T(8,128)(2,1)S(1)}, u32[]{:S(2)}, u32[]{:S(2)}) collective-permute-start(bf16[136,1280]{1,0:T(8,128)(2,1)S(1)} %collective-permute-done.18.refs_6_), channel_id=1, source_target_pairs={{0,32},{32,64},{64,96},{96,128},{128,160},{160,192},{192,224},{224... | collective-permute-start | bytes 1044488 | tf_op jit(solution)/shard_map/ppermute | solution.py:163
  89.7 15.3 %collective-permute-start.27 = (bf16[136,1280]{1,0:T(8,128)(2,1)S(1)}, bf16[136,1280]{1,0:T(8,128)(2,1)S(1)}, u32[]{:S(2)}, u32[]{:S(2)}) collective-permute-start(bf16[136,1280]{1,0:T(8,128)(2,1)S(1)} %collective-permute-done.26.refs_5_), channel_id=1, source_target_pairs={{0,480},{32,0},{64,32},{96,64},{128,96},{160,128},{192,160},{224,1... | collective-permute-start | bytes 1044488 | tf_op jit(solution)/shard_map/ppermute | solution.py:164
  95.0 15.3 %collective-permute-start.11 = (bf16[128,1280]{1,0:T(8,128)(2,1)S(1)}, bf16[128,1280]{1,0:T(8,128)(2,1)S(1)}, u32[]{:S(2)}, u32[]{:S(2)}) collective-permute-start(bf16[128,1280]{1,0:T(8,128)(2,1)S(1)} %collective-permute-done.10.refs_3_), channel_id=1, source_target_pairs={{0,480},{32,0},{64,32},{96,64},{128,96},{160,128},{192,160},{224,1... | collective-permute-start | bytes 983048 | tf_op jit(solution)/shard_map/ppermute | solution.py:162
  98.9 14.8 %collective-permute-start.5 = (bf16[128,1280]{1,0:T(8,128)(2,1)S(1)}, bf16[128,1280]{1,0:T(8,128)(2,1)S(1)}, u32[]{:S(2)}, u32[]{:S(2)}) collective-permute-start(bf16[128,1280]{1,0:T(8,128)(2,1)S(1)} %collective-permute-done.4.refs_0_), channel_id=1, source_target_pairs={{0,32},{32,64},{64,96},{96,128},{128,160},{160,192},{192,224},{224... | collective-permute-start | bytes 983048 | tf_op jit(solution)/shard_map/ppermute | solution.py:160
  102.3 14.8 %collective-permute-start.20 = (bf16[136,1280]{1,0:T(8,128)(2,1)S(1)}, bf16[136,1280]{1,0:T(8,128)(2,1)}, u32[]{:S(2)}, u32[]{:S(2)}) collective-permute-start(bf16[136,1280]{1,0:T(8,128)(2,1)S(1)} %collective-permute-done.19.refs_4_), channel_id=1, source_target_pairs={{0,32},{32,64},{64,96},{96,128},{128,160},{160,192},{192,224},{224... | collective-permute-start | bytes 1044488 | tf_op jit(solution)/shard_map/ppermute | solution.py:163
  105.0 14.0 %collective-permute-start.28 = (bf16[136,1280]{1,0:T(8,128)(2,1)S(1)}, bf16[136,1280]{1,0:T(8,128)(2,1)}, u32[]{:S(2)}, u32[]{:S(2)}) collective-permute-start(bf16[136,1280]{1,0:T(8,128)(2,1)S(1)} %collective-permute-done.27.refs_7_), channel_id=1, source_target_pairs={{0,480},{32,0},{64,32},{96,64},{128,96},{160,128},{192,160},{224,1... | collective-permute-start | bytes 1044488 | tf_op jit(solution)/shard_map/ppermute | solution.py:164
  110.3 13.3 %collective-permute-start.12 = (bf16[128,1280]{1,0:T(8,128)(2,1)S(1)}, bf16[128,1280]{1,0:T(8,128)(2,1)}, u32[]{:S(2)}, u32[]{:S(2)}) collective-permute-start(bf16[128,1280]{1,0:T(8,128)(2,1)S(1)} %collective-permute-done.11.refs_1_), channel_id=1, source_target_pairs={{0,480},{32,0},{64,32},{96,64},{128,96},{160,128},{192,160},{224,1... | collective-permute-start | bytes 983048 | tf_op jit(solution)/shard_map/ppermute | solution.py:162
  113.6 12.6 %collective-permute-start.6 = (bf16[128,1280]{1,0:T(8,128)(2,1)S(1)}, bf16[128,1280]{1,0:T(8,128)(2,1)}, u32[]{:S(2)}, u32[]{:S(2)}) collective-permute-start(bf16[128,1280]{1,0:T(8,128)(2,1)S(1)} %collective-permute-done.5.refs_2_), channel_id=1, source_target_pairs={{0,32},{32,64},{64,96},{96,128},{128,160},{160,192},{192,224},{224... | collective-permute-start | bytes 983048 | tf_op jit(solution)/shard_map/ppermute | solution.py:160
  117.1 25.3 %collective-permute-start.21 = (bf16[136,1280]{1,0:T(8,128)(2,1)}, bf16[136,1280]{1,0:T(8,128)(2,1)}, u32[]{:S(2)}, u32[]{:S(2)}) collective-permute-start(bf16[136,1280]{1,0:T(8,128)(2,1)} %collective-permute-done.20.refs_6_), channel_id=1, source_target_pairs={{0,32},{32,64},{64,96},{96,128},{128,160},{160,192},{192,224},{224... | collective-permute-start | bytes 1044488 | tf_op jit(solution)/shard_map/ppermute | solution.py:163
  119.0 23.4 %collective-permute-start.29 = (bf16[136,1280]{1,0:T(8,128)(2,1)}, bf16[136,1280]{1,0:T(8,128)(2,1)}, u32[]{:S(2)}, u32[]{:S(2)}) collective-permute-start(bf16[136,1280]{1,0:T(8,128)(2,1)} %collective-permute-done.28.refs_4_), channel_id=1, source_target_pairs={{0,480},{32,0},{64,32},{96,64},{128,96},{160,128},{192,160},{224,1... | collective-permute-start | bytes 1044488 | tf_op jit(solution)/shard_map/ppermute | solution.py:164
  123.6 18.8 %collective-permute-start.13 = (bf16[128,1280]{1,0:T(8,128)(2,1)}, bf16[128,1280]{1,0:T(8,128)(2,1)}, u32[]{:S(2)}, u32[]{:S(2)}) collective-permute-start(bf16[128,1280]{1,0:T(8,128)(2,1)} %collective-permute-done.12.refs_3_), channel_id=1, source_target_pairs={{0,480},{32,0},{64,32},{96,64},{128,96},{160,128},{192,160},{224,1... | collective-permute-start | bytes 983048 | tf_op jit(solution)/shard_map/ppermute | solution.py:162
  126.2 16.2 %collective-permute-start.14 = (bf16[128,1280]{1,0:T(8,128)(2,1)}, bf16[128,1280]{1,0:T(8,128)(2,1)}, u32[]{:S(2)}, u32[]{:S(2)}) collective-permute-start(bf16[128,1280]{1,0:T(8,128)(2,1)} %collective-permute-done.6.refs_0_), channel_id=1, source_target_pairs={{0,32},{32,64},{64,96},{96,128},{128,160},{160,192},{192,224},{224... | collective-permute-start | bytes 983048 | tf_op jit(solution)/shard_map/ppermute | solution.py:160
  148.6 13.9 %collective-permute-start.30 = (bf16[384,2560]{1,0:T(8,128)(2,1)S(1)}, bf16[384,2560]{1,0:T(8,128)(2,1)S(1)}, u32[]{:S(2)}, u32[]{:S(2)}) collective-permute-start(bf16[384,2560]{1,0:T(8,128)(2,1)S(1)} %term_other.1), channel_id=1, source_target_pairs={{0,1},{1,0},{2,3},{3,2},{4,5},{5,4},{6,7},{7,6},{8,9},{9,8},{10,11... | collective-permute-start | bytes 5898248 | tf_op jit(solution)/shard_map/ppermute | solution.py:197
  (29 other events, 48.3 us)
Sparse Core Ops, SparseCore 0:
  27.8 58.7 all-gather.1

commit v2 on v1

--- a/solution.py
+++ b/solution.py
@@ -1,5 +1,6 @@
 import jax
 import jax.numpy as jnp
+import numpy as np
 from jax import lax
 from jax.experimental import pallas as pl
 from jax.experimental.pallas import tpu as pltpu
@@ -12,45 +13,77 @@
 
 
 def _info_kernel(routes_ref, gates_ref, info_ref):
-    tokens, top = routes_ref.shape
+    top, tokens = routes_ref.shape
+    experts = 2 * INFO_ROWS
     routes = routes_ref[...]
     gates = gates_ref[...].astype(F32)
-    lane = lax.broadcasted_iota(jnp.int32, (tokens, LANES), 1)
-    gate = jnp.zeros((tokens, LANES), F32)
-    named = jnp.zeros((tokens, LANES), F32)
+    expert = lax.broadcasted_iota(jnp.int32, (experts, tokens), 0)
+    gate = jnp.zeros((experts, tokens), F32)
+    named = jnp.zeros((experts, tokens), F32)
     for k in range(top):
-        hit = routes[:, k : k + 1] == lane
-        gate = jnp.where(hit, gates[:, k : k + 1], gate)
+        hit = routes[k : k + 1, :] == expert
+        gate = jnp.where(hit, gates[k : k + 1, :], gate)
         named = jnp.where(hit, 1.0, named)
     row = lax.broadcasted_iota(jnp.int32, (tokens, tokens), 0)
     col = lax.broadcasted_iota(jnp.int32, (tokens, tokens), 1)
-    earlier = jnp.where(col < row, 1.0, 0.0).astype(BF)
-    rank = jnp.dot(earlier, named.astype(BF), preferred_element_type=F32)
+    earlier = jnp.where(row < col, 1.0, 0.0).astype(BF)
+    rank = jnp.dot(named.astype(BF), earlier, preferred_element_type=F32)
     slot = jnp.where(named > 0.5, rank, -1.0)
-    slot_t = slot.T
-    gate_t = gate.T
     n = INFO_ROWS
     info_ref[...] = jnp.zeros_like(info_ref)
-    info_ref[:, 0:tokens] = slot_t[0:n].astype(BF)
-    info_ref[:, tokens : 2 * tokens] = gate_t[0:n].astype(BF)
-    info_ref[:, 2 * tokens : 3 * tokens] = slot_t[n : 2 * n].astype(BF)
-    info_ref[:, 3 * tokens : 4 * tokens] = gate_t[n : 2 * n].astype(BF)
-
-
-def _info(routes, gates, width):
+    info_ref[:, 0:tokens] = slot[0:n].astype(BF)
+    info_ref[:, tokens : 2 * tokens] = gate[0:n].astype(BF)
+    info_ref[:, 2 * tokens : 3 * tokens] = slot[n : 2 * n].astype(BF)
+    info_ref[:, 3 * tokens : 4 * tokens] = gate[n : 2 * n].astype(BF)
+
+
+def _info(routes_t, gates_t, width):
     return pl.pallas_call(
         _info_kernel,
         out_shape=jax.ShapeDtypeStruct((INFO_ROWS, width), BF),
-        cost_estimate=pl.CostEstimate(flops=1 << 22, bytes_accessed=1 << 16, transcendentals=0),
+        cost_estimate=pl.CostEstimate(flops=1 << 20, bytes_accessed=1 << 16, transcendentals=0),
         name="route_info",
-    )(routes, gates)
-
-
-def _select_kernel(count, tokens, meta_ref, *refs):
+    )(routes_t, gates_t)
+
+
+def _split_kernel(units_dev, core_ref, hidden_ref, mine_ref, other_ref):
+    block, units = hidden_ref.shape
+    turned = hidden_ref[...].astype(F32).T.reshape(units // (2 * units_dev), 2, units_dev, block)
+    even = turned[:, 0].reshape(units // 2, block)
+    odd = turned[:, 1].reshape(units // 2, block)
+    first = core_ref[0] == 0
+    mine_ref[...] = jnp.where(first, even, odd).astype(BF)
+    other_ref[...] = jnp.where(first, odd, even).astype(BF)
+
+
+def _split(hidden, core, units_dev):
+    rows, units = hidden.shape
+    block = LANES
+
+    def kernel(*refs):
+        _split_kernel(units_dev, *refs)
+
+    return pl.pallas_call(
+        kernel,
+        grid_spec=pltpu.PrefetchScalarGridSpec(
+            num_scalar_prefetch=1,
+            grid=(rows // block,),
+            in_specs=[pl.BlockSpec((block, units), lambda i, m: (i, 0))],
+            out_specs=[pl.BlockSpec((units // 2, block), lambda i, m: (0, i))] * 2,
+        ),
+        out_shape=[jax.ShapeDtypeStruct((units // 2, rows), BF)] * 2,
+        cost_estimate=pl.CostEstimate(
+            flops=rows * units, bytes_accessed=4 * rows * units, transcendentals=0
+        ),
+        name="split_hidden",
+    )(core, hidden)
+
+
+def _select_kernel(count, tokens, me_ref, _, *refs):
     firsts, seconds, out_ref = refs[:count], refs[count : 2 * count], refs[-1]
     capacity = out_ref.shape[1]
     half = firsts[0].shape[1]
-    me = meta_ref[0]
+    me = me_ref[0]
     step = pl.program_id(0)
     for i in range(count):
 
@@ -70,27 +103,31 @@
             ).astype(BF)
 
 
-def _select(meta, firsts, seconds, rows, shape, name):
+def _select(me, offsets, firsts, seconds, rows, shape, name):
     count = len(firsts)
+    groups = shape[0]
+    steps = np.array([(off + groups) % groups for off in offsets], np.int32)
     tokens = firsts[0].shape[0]
-    whole = [pl.BlockSpec(a.shape, lambda i, m: (0, 0)) for a in firsts + seconds]
+    whole = [pl.BlockSpec(a.shape, lambda i, m, o: (0, 0)) for a in firsts + seconds]
     operands = list(firsts) + list(seconds)
     aliases = {}
     if rows is not None:
         whole.append(pl.BlockSpec(memory_space=pl.ANY))
         operands.append(rows)
-        aliases = {1 + 2 * count: 0}
-
-    def kernel(meta_ref, *refs):
-        _select_kernel(count, tokens, meta_ref, *refs)
+        aliases = {2 + 2 * count: 0}
+
+    def kernel(*refs):
+        _select_kernel(count, tokens, *refs)
 
     return pl.pallas_call(
         kernel,
         grid_spec=pltpu.PrefetchScalarGridSpec(
-            num_scalar_prefetch=1,
+            num_scalar_prefetch=2,
             grid=(count,),
             in_specs=whole,
-            out_specs=pl.BlockSpec((1,) + shape[1:], lambda i, m: (m[1 + i], 0, 0)),
+            out_specs=pl.BlockSpec(
+                (1,) + shape[1:], lambda i, m, o: (lax.rem(m[0] + o[i], groups), 0, 0)
+            ),
         ),
         out_shape=jax.ShapeDtypeStruct(shape, BF),
         input_output_aliases=aliases,
@@ -101,7 +138,7 @@
             transcendentals=0,
         ),
         name=name,
-    )(meta, *operands)
+    )(me, steps, *operands)
 
 
 def _term_kernel(saved_ref, rows_ref, out_ref):
@@ -141,15 +178,17 @@
     units = hidden.shape[2]
     capacity = rows_dev // groups
     half = width // 2
-    me = lax.axis_index("expert")
+    me = lax.axis_index("expert").astype(jnp.int32).reshape(1)
     core = lax.rem(lax.axis_index("replica"), 2)
 
     weights = lax.all_gather(down_weight, "replica", axis=0, tiled=True)
 
     own_first = grads[0, :, :half]
-    own_second = jnp.concatenate(
-        [grads[0, :, half:], _info(routes[0], gates[0], half)], axis=0
-    )
+    info = _info(routes[0].T, gates[0].T, half)
+    own_second = jnp.concatenate([grads[0, :, half:], info], axis=0)
+    hidden, own_second = lax.optimization_barrier((hidden, own_second))
+    saved_mine, saved_other = _split(hidden[0], core.reshape(1), units_dev)
+
     up = [(i, (i + 1) % groups) for i in range(groups)]
     down = [(i, (i - 1) % groups) for i in range(groups)]
     far = groups // 2
@@ -157,6 +196,14 @@
     a_up = a_down = own_first
     b_up = b_down = own_second
     for hop in range(1, far + 1):
+        if hop == 2:
+            a_up, saved_mine, saved_other = lax.optimization_barrier(
+                (a_up, saved_mine, saved_other)
+            )
+        if hop == far:
+            me, a_up, a_down, b_up, b_down = lax.optimization_barrier(
+                (me, a_up, a_down, b_up, b_down)
+            )
         a_up = lax.ppermute(a_up, "expert", up)
         if hop < far:
             a_down = lax.ppermute(a_down, "expert", down)
@@ -167,24 +214,18 @@
             got_first[hop], got_second[-hop] = a_down, b_up
     got_second[-far] = got_second.pop(far)
 
-    saved_t = hidden[0].T.reshape(chips, 2, units_dev, rows_dev).transpose(1, 0, 2, 3)
-    saved_t = saved_t.reshape(2, units // 2, rows_dev)
-    saved_mine = lax.dynamic_index_in_dim(saved_t, core, 0, keepdims=False)
-    saved_other = lax.dynamic_index_in_dim(saved_t, 1 - core, 0, keepdims=False)
-
     rows = None
     shape = (groups, capacity, width)
     batches = [
         [0, -1, 1, -2, 2],
         [-3, 3, -4, 4],
-        [-5, 5, -6, 6],
-        [-7, 7, -8],
+        [-5, 5, -6, 6, -7, 7],
+        [-8],
     ]
     for number, batch in enumerate(batches):
-        source = [lax.rem(me + off + groups, groups) for off in batch]
-        meta = jnp.stack([me] + source).astype(jnp.int32)
         rows = _select(
-            meta,
+            me,
+            batch,
             [got_first[off] for off in batch],
             [got_second[off] for off in batch],
             rows,
@@ -197,6 +238,7 @@
     arrived = lax.ppermute(other, "replica", [(i, i ^ 1) for i in range(replicas)])
     mine = _term(saved_mine, rows, "term_mine")
     pair = (mine.astype(F32) + arrived.astype(F32)).astype(BF)
+    pair, rows, weights = lax.optimization_barrier((pair, rows, weights))
     parts = lax.all_to_all(
         pair.reshape(chips, units_dev, width),
         "replica",
@@ -205,12 +247,12 @@
         tiled=True,
         axis_index_groups=[[2 * q + c for q in range(chips)] for c in range(2)],
     )
-    down_grad = jnp.sum(parts.astype(F32), axis=0)[:, None, :]
-
     d_rows = lax.dot_general(
         rows, weights[:, 0, :], (((1,), (1,)), ((), ())), preferred_element_type=F32
     )
     d_hidden = d_rows.astype(BF)[None]
+    parts, d_hidden = lax.optimization_barrier((parts, d_hidden))
+    down_grad = jnp.sum(parts.astype(F32), axis=0)[:, None, :]
     return (d_hidden, down_grad)
 
 

time: 214 us -> 216 us (level)
  blocking collectives: 33 us -> 0 us
  waiting for transfers between devices: 4.73 us -> 30.1 us
  starting transfers between devices: 110 us -> 120 us
  local copies, waits for them, and re-layouts: 22 us -> 17.4 us
  Pallas kernels: 17.5 us -> 21.2 us
    all_to_all x1 -> x0, blocking collectives: 33 us -> none  [body(): lax.all_to_all(pair.reshape(chips, units_dev, width), 'replica', split_ax...]
    all_to_all x0 -> x1, waiting for transfers between devices: none -> 21.5 us  [body(): lax.all_to_all(pair.reshape(chips, units_dev, width), 'replica', split_ax...]
    ppermute x7, starting transfers between devices: 23.4 us -> 32 us  [body(): a_down = lax.ppermute(a_down, 'expert', down)]
    all_to_all x0 -> x1, starting transfers between devices: none -> 6.76 us  [body(): lax.all_to_all(pair.reshape(chips, units_dev, width), 'replica', split_ax...]
    ppermute x8, waiting for transfers between devices: 0.02 us -> 5.59 us  [body(): a_up = lax.ppermute(a_up, 'expert', up)]
    pallas_call x0 -> x1, Pallas kernels: none -> 5.35 us  [_split(): pl.pallas_call(kernel, grid_spec=pltpu.PrefetchScalarGridSpec(num_scalar_...]
    ppermute x8, starting transfers between devices: 18.6 us -> 15.3 us  [body(): a_up = lax.ppermute(a_up, 'expert', up)]
    ppermute x8, waiting for transfers between devices: 2.93 us -> 0.02 us  [body(): b_down = lax.ppermute(b_down, 'expert', down)]
  transfers between devices with their start and end apart: 32 -> 33, of which waited for: 5 -> 4; matrix products, arithmetic and copies ran while one was open for 4% -> 6% of each run, Pallas kernels for 7% -> 10%
where the time goes in v2:
time: 216 us; the launch traced here: 215 us
  starting transfers between devices  120 us (56%)
  waiting for transfers between devices  30.1 us (14%)
  Pallas kernels  21.2 us (10%)
  local copies, waits for them, and re-layouts  17.4 us (8%)
  between operations  14.8 us (7%)
  matrix products  8.34 us (4%)
  other arithmetic  2.77 us (1%)
    ppermute x8, starting transfers between devices, body(): b_down = lax.ppermute(b_down, 'expert', down)  42.4 us
    ppermute x7, starting transfers between devices, body(): a_down = lax.ppermute(a_down, 'expert', down)  32 us
    all_to_all x1, waiting for transfers between devices, body(): lax.all_to_all(pair.reshape(chips, units_dev, width), 'replica', split_ax...  21.5 us
    ppermute x7, starting transfers between devices, body(): b_up = lax.ppermute(b_up, 'expert', up)  15.8 us
    unnamed x61, local copies, waits for them, and re-layouts  15.4 us
    ppermute x8, starting transfers between devices, body(): a_up = lax.ppermute(a_up, 'expert', up)  15.3 us
    dot_general x1, matrix products, body(): lax.dot_general(rows, weights[:, 0, :], (((1,), (1,)), ((), ())), preferr...  8.34 us
    pallas_call x4, Pallas kernels, _select(): pl.pallas_call(kernel, grid_spec=pltpu.PrefetchScalarGridSpec(num_scalar_...  7.79 us
  transfers between devices with their start and end apart: 33, of which 4 were waited for; matrix products, arithmetic and copies ran while one was open for 6% of the time, Pallas kernels for 10%

profile of v2, /device:TPU:1, one launch (start us, length us, event | category | flops | bytes accessed | tf_op | source)
XLA Modules:
  0.0 214.6 jit_solution(2822189108945891706)
XLA Ops:
  12.5 4.4 %collective-permute-start.14 = (bf16[136,1280]{1,0:T(8,128)(2,1)S(1)}, bf16[136,1280]{1,0:T(8,128)(2,1)S(1)}, u32[]{:S(2)}, u32[]{:S(2)}) collective-permute-start(bf16[136,1280]{1,0:T(8,128)(2,1)S(1)} %pad_maximum_fusion.refs_7_), channel_id=1, source_target_pairs={{0,32},{32,64},{64,96},{96,128},{128,160},{160,192},{192,224},{224... | collective-permute-start | bytes 1044488 | tf_op jit(solution)/shard_map/ppermute | solution.py:210
  16.9 9.5 %collective-permute-start.21 = (bf16[136,1280]{1,0:T(8,128)(2,1)S(1)}, bf16[136,1280]{1,0:T(8,128)(2,1)S(1)}, u32[]{:S(2)}, u32[]{:S(2)}) collective-permute-start(bf16[136,1280]{1,0:T(8,128)(2,1)S(1)} %pad_maximum_fusion.refs_7_), channel_id=1, source_target_pairs={{0,480},{32,0},{64,32},{96,64},{128,96},{160,128},{192,160},{224,1... | collective-permute-start | bytes 1044488 | tf_op jit(solution)/shard_map/ppermute | solution.py:211
  26.4 1.9 collective-permute-start
  28.3 4.6 %collective-permute-start.7 = (bf16[128,1280]{1,0:T(8,128)(2,1)S(1)}, bf16[128,1280]{1,0:T(8,128)(2,1)S(1)}, u32[]{:S(2)}, u32[]{:S(2)}) collective-permute-start(bf16[128,1280]{1,0:T(8,128)(2,1)S(1)} %get-tuple-element.33.refs_2_), channel_id=1, source_target_pairs={{0,480},{32,0},{64,32},{96,64},{128,96},{160,128},{192,160},{224,1... | collective-permute-start | bytes 983048 | tf_op jit(solution)/shard_map/ppermute | solution.py:209
  32.9 1.9 collective-permute-start.15
  34.8 4.6 %collective-permute-start.22 = (bf16[136,1280]{1,0:T(8,128)(2,1)S(1)}, bf16[136,1280]{1,0:T(8,128)(2,1)S(1)}, u32[]{:S(2)}, u32[]{:S(2)}) collective-permute-start(bf16[136,1280]{1,0:T(8,128)(2,1)S(1)} %collective-permute-done.21.refs_9_), channel_id=1, source_target_pairs={{0,480},{32,0},{64,32},{96,64},{128,96},{160,128},{192,160},{224,1... | collective-permute-start | bytes 1044488 | tf_op jit(solution)/shard_map/ppermute | solution.py:211
  39.4 5.4 %split_hidden.1 = (bf16[384,896]{1,0:T(8,128)(2,1)}, bf16[384,896]{1,0:T(8,128)(2,1)}) custom-call(s32[1]{0:T(128)} %bitcast.1.refs_0_, bf16[896,768]{1,0:T(8,128)(2,1)} %bitcast.30), custom_call_target="tpu_custom_call" | custom-call | flops 688128 | bytes 2752512 | tf_op jit(solution)/shard_map/split_hidden/pallas_call | solution.py:66
  47.4 4.6 %collective-permute-start.8 = (bf16[128,1280]{1,0:T(8,128)(2,1)S(1)}, bf16[128,1280]{1,0:T(8,128)(2,1)S(1)}, u32[]{:S(2)}, u32[]{:S(2)}) collective-permute-start(bf16[128,1280]{1,0:T(8,128)(2,1)S(1)} %collective-permute-done.7.refs_4_), channel_id=1, source_target_pairs={{0,480},{32,0},{64,32},{96,64},{128,96},{160,128},{192,160},{224,1... | collective-permute-start | bytes 983048 | tf_op jit(solution)/shard_map/ppermute | solution.py:209
  54.6 4.6 %collective-permute-start.23 = (bf16[136,1280]{1,0:T(8,128)(2,1)S(1)}, bf16[136,1280]{1,0:T(8,128)(2,1)S(1)}, u32[]{:S(2)}, u32[]{:S(2)}) collective-permute-start(bf16[136,1280]{1,0:T(8,128)(2,1)S(1)} %collective-permute-done.22.refs_11_), channel_id=1, source_target_pairs={{0,480},{32,0},{64,32},{96,64},{128,96},{160,128},{192,160},{224,1... | collective-permute-start | bytes 1044488 | tf_op jit(solution)/shard_map/ppermute | solution.py:211
  59.2 1.9 collective-permute-start.2
  61.9 4.6 %collective-permute-start.9 = (bf16[128,1280]{1,0:T(8,128)(2,1)S(1)}, bf16[128,1280]{1,0:T(8,128)(2,1)S(1)}, u32[]{:S(2)}, u32[]{:S(2)}) collective-permute-start(bf16[128,1280]{1,0:T(8,128)(2,1)S(1)} %collective-permute-done.8.refs_6_), channel_id=1, source_target_pairs={{0,480},{32,0},{64,32},{96,64},{128,96},{160,128},{192,160},{224,1... | collective-permute-start | bytes 983048 | tf_op jit(solution)/shard_map/ppermute | solution.py:209
  69.1 4.6 %collective-permute-start.24 = (bf16[136,1280]{1,0:T(8,128)(2,1)S(1)}, bf16[136,1280]{1,0:T(8,128)(2,1)S(1)}, u32[]{:S(2)}, u32[]{:S(2)}) collective-permute-start(bf16[136,1280]{1,0:T(8,128)(2,1)S(1)} %collective-permute-done.23.refs_7_), channel_id=1, source_target_pairs={{0,480},{32,0},{64,32},{96,64},{128,96},{160,128},{192,160},{224,1... | collective-permute-start | bytes 1044488 | tf_op jit(solution)/shard_map/ppermute | solution.py:211
  73.7 1.9 collective-permute-start.3
  76.4 4.6 %collective-permute-start.10 = (bf16[128,1280]{1,0:T(8,128)(2,1)S(1)}, bf16[128,1280]{1,0:T(8,128)(2,1)S(1)}, u32[]{:S(2)}, u32[]{:S(2)}) collective-permute-start(bf16[128,1280]{1,0:T(8,128)(2,1)S(1)} %collective-permute-done.9.refs_3_), channel_id=1, source_target_pairs={{0,480},{32,0},{64,32},{96,64},{128,96},{160,128},{192,160},{224,1... | collective-permute-start | bytes 983048 | tf_op jit(solution)/shard_map/ppermute | solution.py:209
  83.7 4.6 %collective-permute-start.25 = (bf16[136,1280]{1,0:T(8,128)(2,1)S(1)}, bf16[136,1280]{1,0:T(8,128)(2,1)S(1)}, u32[]{:S(2)}, u32[]{:S(2)}) collective-permute-start(bf16[136,1280]{1,0:T(8,128)(2,1)S(1)} %collective-permute-done.24.refs_9_), channel_id=1, source_target_pairs={{0,480},{32,0},{64,32},{96,64},{128,96},{160,128},{192,160},{224,1... | collective-permute-start | bytes 1044488 | tf_op jit(solution)/shard_map/ppermute | solution.py:211
  88.3 1.9 collective-permute-start.4
  91.0 4.6 %collective-permute-start.11 = (bf16[128,1280]{1,0:T(8,128)(2,1)S(1)}, bf16[128,1280]{1,0:T(8,128)(2,1)S(1)}, u32[]{:S(2)}, u32[]{:S(2)}) collective-permute-start(bf16[128,1280]{1,0:T(8,128)(2,1)S(1)} %collective-permute-done.10.refs_5_), channel_id=1, source_target_pairs={{0,480},{32,0},{64,32},{96,64},{128,96},{160,128},{192,160},{224,1... | collective-permute-start | bytes 983048 | tf_op jit(solution)/shard_map/ppermute | solution.py:209
  99.0 4.6 %collective-permute-start.26 = (bf16[136,1280]{1,0:T(8,128)(2,1)S(1)}, bf16[136,1280]{1,0:T(8,128)(2,1)}, u32[]{:S(2)}, u32[]{:S(2)}) collective-permute-start(bf16[136,1280]{1,0:T(8,128)(2,1)S(1)} %collective-permute-done.25.refs_9_), channel_id=1, source_target_pairs={{0,480},{32,0},{64,32},{96,64},{128,96},{160,128},{192,160},{224,1... | collective-permute-start | bytes 1044488 | tf_op jit(solution)/shard_map/ppermute | solution.py:211
  106.9 4.6 %collective-permute-start.12 = (bf16[128,1280]{1,0:T(8,128)(2,1)S(1)}, bf16[128,1280]{1,0:T(8,128)(2,1)}, u32[]{:S(2)}, u32[]{:S(2)}) collective-permute-start(bf16[128,1280]{1,0:T(8,128)(2,1)S(1)} %collective-permute-done.11.refs_3_), channel_id=1, source_target_pairs={{0,480},{32,0},{64,32},{96,64},{128,96},{160,128},{192,160},{224,1... | collective-permute-start | bytes 983048 | tf_op jit(solution)/shard_map/ppermute | solution.py:209
  114.1 4.6 %collective-permute-start.27 = (bf16[136,1280]{1,0:T(8,128)(2,1)}, bf16[136,1280]{1,0:T(8,128)(2,1)}, u32[]{:S(2)}, u32[]{:S(2)}) collective-permute-start(bf16[136,1280]{1,0:T(8,128)(2,1)} %collective-permute-done.26.refs_11_), channel_id=1, source_target_pairs={{0,480},{32,0},{64,32},{96,64},{128,96},{160,128},{192,160},{224,1... | collective-permute-start | bytes 1044488 | tf_op jit(solution)/shard_map/ppermute | solution.py:211
  118.7 1.9 collective-permute-start.6
  120.7 4.6 %collective-permute-start.13 = (bf16[128,1280]{1,0:T(8,128)(2,1)}, bf16[128,1280]{1,0:T(8,128)(2,1)}, u32[]{:S(2)}, u32[]{:S(2)}) collective-permute-start(bf16[128,1280]{1,0:T(8,128)(2,1)} %collective-permute-done.12.refs_5_), channel_id=1, source_target_pairs={{0,480},{32,0},{64,32},{96,64},{128,96},{160,128},{192,160},{224,1... | collective-permute-start | bytes 983048 | tf_op jit(solution)/shard_map/ppermute | solution.py:209
  125.3 5.6 %collective-permute-done.6.refs_6_ = bf16[128,1280]{1,0:T(8,128)(2,1)} collective-permute-done((bf16[128,1280]{1,0:T(8,128)(2,1)}, bf16[128,1280]{1,0:T(8,128)(2,1)}, u32[]{:S(2)}, u32[]{:S(2)}) %collective-permute-start.6) | collective-permute-done | bytes 327712 | tf_op jit(solution)/shard_map/ppermute | solution.py:207
  130.8 2.0 collective-permute-done.13.refs_7_
  132.9 5.5 %collective-permute-start.29 = (bf16[136,1280]{1,0:T(8,128)(2,1)}, bf16[136,1280]{1,0:T(8,128)(2,1)S(1)}, u32[]{:S(2)}, u32[]{:S(2)}) collective-permute-start(bf16[136,1280]{1,0:T(8,128)(2,1)} %collective-permute-done.27.refs_13_), channel_id=1, source_target_pairs={{0,480},{32,0},{64,32},{96,64},{128,96},{160,128},{192,160},{224,1... | collective-permute-start | bytes 1044488 | tf_op jit(solution)/shard_map/ppermute | solution.py:211
  148.5 4.0 %select_2.1.refs_4_ = bf16[16,56,2560]{2,1,0:T(8,128)(2,1)S(1)} custom-call(s32[1]{0:T(128)} %bitcast.7.refs_0_, s32[6]{0:T(128)S(1)} %copy-done.27, bf16[128,1280]{1,0:T(8,128)(2,1)S(1)} %copy-done.16, bf16[128,1280]{1,0:T(8,128)(2,1)S(1)} %copy-done.18, bf16[128,1280]{1,0:T(8,128)(2,1)} %collective-permute-done.5.refs_4_, ...), custom_call_target="tpu_custom_call", output_to_operand_aliasing={{}: (14, {})} | custom-call | flops 220200960 | bytes 5652480 | tf_op jit(solution)/shard_map/select_2/pallas_call | solution.py:122
  153.6 3.3 %term_other.1 = bf16[384,2560]{1,0:T(8,128)(2,1)S(1)} custom-call(bf16[384,896]{1,0:T(8,128)(2,1)S(1)} %copy-done.2, bf16[896,2560]{1,0:T(8,128)(2,1)S(1)} %bitcast.27), custom_call_target="tpu_custom_call" | custom-call | flops 1761607680 | bytes 7241728 | tf_op jit(solution)/shard_map/term_other/pallas_call | solution.py:152
  156.9 7.7 %collective-permute-start.30 = (bf16[384,2560]{1,0:T(8,128)(2,1)S(1)}, bf16[384,2560]{1,0:T(8,128)(2,1)S(1)}, u32[]{:S(2)}, u32[]{:S(2)}) collective-permute-start(bf16[384,2560]{1,0:T(8,128)(2,1)S(1)} %term_other.1), channel_id=1, source_target_pairs={{0,1},{1,0},{2,3},{3,2},{4,5},{5,4},{6,7},{7,6},{8,9},{9,8},{10,11... | collective-permute-start | bytes 5898248 | tf_op jit(solution)/shard_map/ppermute | solution.py:238
  164.7 3.3 %term_mine.1 = bf16[384,2560]{1,0:T(8,128)(2,1)S(1)} custom-call(bf16[384,896]{1,0:T(8,128)(2,1)S(1)} %copy-done.1, bf16[896,2560]{1,0:T(8,128)(2,1)S(1)} %bitcast.28), custom_call_target="tpu_custom_call" | custom-call | flops 1761607680 | bytes 7241728 | tf_op jit(solution)/shard_map/term_mine/pallas_call | solution.py:152
  170.0 6.8 %all-to-all-start = ((bf16[16,24,2560]{2,1,0:T(8,128)(2,1)}), bf16[16,24,2560]{2,1,0:T(8,128)(2,1)S(1)}, u32[]{:S(2)}, u32[]{:S(2)}) async-start(bf16[16,24,2560]{2,1,0:T(8,128)(2,1)} %bitcast.9), calls=%async_computation | async-start | bytes 3932160 | tf_op jit(solution)/shard_map/all_to_all | solution.py:242
  176.8 8.3 %fusion.5 = bf16[1,896,768]{2,1,0:T(8,128)(2,1)} fusion(bf16[896,2560]{1,0:T(8,128)(2,1)} %bitcast.29, bf16[768,1,2560]{2,0,1:T(8,128)(2,1)} %all-gather.2.cloned.1.call-done), kind=kOutput, calls=%fused_computation.5 | convolution fusion | flops 3523903488 | bytes 9895936 | tf_op jit(solution)/shard_map/dot_general | solution.py:250
  185.1 21.5 %all-to-all-done = bf16[16,24,2560]{2,1,0:T(8,128)(2,1)S(1)} async-done(((bf16[16,24,2560]{2,1,0:T(8,128)(2,1)}), bf16[16,24,2560]{2,1,0:T(8,128)(2,1)S(1)}, u32[]{:S(2)}, u32[]{:S(2)}) %all-to-all-start) | async-done | bytes 1966112 | tf_op jit(solution)/shard_map/all_to_all | solution.py:242
  (110 shorter events, 41.7 us)
Async XLA Ops:
  7.2 162.9 %all-gather.2.cloned.1.call-start = ((), (), s32[]{:S(2)}) async-start(), calls=%async_computation.1 | async-start | bytes 4055040 | tf_op jit(solution)/shard_map/all_gather | solution.py:184
  12.5 20.4 %collective-permute-start.14 = (bf16[136,1280]{1,0:T(8,128)(2,1)S(1)}, bf16[136,1280]{1,0:T(8,128)(2,1)S(1)}, u32[]{:S(2)}, u32[]{:S(2)}) collective-permute-start(bf16[136,1280]{1,0:T(8,128)(2,1)S(1)} %pad_maximum_fusion.refs_7_), channel_id=1, source_target_pairs={{0,32},{32,64},{64,96},{96,128},{128,160},{160,192},{192,224},{224... | collective-permute-start | bytes 1044488 | tf_op jit(solution)/shard_map/ppermute | solution.py:210
  16.9 18.0 %collective-permute-start.21 = (bf16[136,1280]{1,0:T(8,128)(2,1)S(1)}, bf16[136,1280]{1,0:T(8,128)(2,1)S(1)}, u32[]{:S(2)}, u32[]{:S(2)}) collective-permute-start(bf16[136,1280]{1,0:T(8,128)(2,1)S(1)} %pad_maximum_fusion.refs_7_), channel_id=1, source_target_pairs={{0,480},{32,0},{64,32},{96,64},{128,96},{160,128},{192,160},{224,1... | collective-permute-start | bytes 1044488 | tf_op jit(solution)/shard_map/ppermute | solution.py:211
  26.4 18.4 %collective-permute-start = (bf16[128,1280]{1,0:T(8,128)(2,1)S(1)}, bf16[128,1280]{1,0:T(8,128)(2,1)S(1)}, u32[]{:S(2)}, u32[]{:S(2)}) collective-permute-start(bf16[128,1280]{1,0:T(8,128)(2,1)S(1)} %get-tuple-element.33.refs_2_), channel_id=1, source_target_pairs={{0,32},{32,64},{64,96},{96,128},{128,160},{160,192},{192,224},{224... | collective-permute-start | bytes 983048 | tf_op jit(solution)/shard_map/ppermute | solution.py:207
  28.3 19.1 %collective-permute-start.7 = (bf16[128,1280]{1,0:T(8,128)(2,1)S(1)}, bf16[128,1280]{1,0:T(8,128)(2,1)S(1)}, u32[]{:S(2)}, u32[]{:S(2)}) collective-permute-start(bf16[128,1280]{1,0:T(8,128)(2,1)S(1)} %get-tuple-element.33.refs_2_), channel_id=1, source_target_pairs={{0,480},{32,0},{64,32},{96,64},{128,96},{160,128},{192,160},{224,1... | collective-permute-start | bytes 983048 | tf_op jit(solution)/shard_map/ppermute | solution.py:209
  32.9 19.8 %collective-permute-start.15 = (bf16[136,1280]{1,0:T(8,128)(2,1)S(1)}, bf16[136,1280]{1,0:T(8,128)(2,1)S(1)}, u32[]{:S(2)}, u32[]{:S(2)}) collective-permute-start(bf16[136,1280]{1,0:T(8,128)(2,1)S(1)} %collective-permute-done.14.refs_8_), channel_id=1, source_target_pairs={{0,32},{32,64},{64,96},{96,128},{128,160},{160,192},{192,224},{224... | collective-permute-start | bytes 1044488 | tf_op jit(solution)/shard_map/ppermute | solution.py:210
  34.8 19.8 %collective-permute-start.22 = (bf16[136,1280]{1,0:T(8,128)(2,1)S(1)}, bf16[136,1280]{1,0:T(8,128)(2,1)S(1)}, u32[]{:S(2)}, u32[]{:S(2)}) collective-permute-start(bf16[136,1280]{1,0:T(8,128)(2,1)S(1)} %collective-permute-done.21.refs_9_), channel_id=1, source_target_pairs={{0,480},{32,0},{64,32},{96,64},{128,96},{160,128},{192,160},{224,1... | collective-permute-start | bytes 1044488 | tf_op jit(solution)/shard_map/ppermute | solution.py:211
  44.8 14.5 %collective-permute-start.1 = (bf16[128,1280]{1,0:T(8,128)(2,1)S(1)}, bf16[128,1280]{1,0:T(8,128)(2,1)S(1)}, u32[]{:S(2)}, u32[]{:S(2)}) collective-permute-start(bf16[128,1280]{1,0:T(8,128)(2,1)S(1)} %collective-permute-done.refs_3_), channel_id=1, source_target_pairs={{0,32},{32,64},{64,96},{96,128},{128,160},{160,192},{192,224},{224... | collective-permute-start | bytes 983048 | tf_op jit(solution)/shard_map/ppermute | solution.py:207
  47.4 14.5 %collective-permute-start.8 = (bf16[128,1280]{1,0:T(8,128)(2,1)S(1)}, bf16[128,1280]{1,0:T(8,128)(2,1)S(1)}, u32[]{:S(2)}, u32[]{:S(2)}) collective-permute-start(bf16[128,1280]{1,0:T(8,128)(2,1)S(1)} %collective-permute-done.7.refs_4_), channel_id=1, source_target_pairs={{0,480},{32,0},{64,32},{96,64},{128,96},{160,128},{192,160},{224,1... | collective-permute-start | bytes 983048 | tf_op jit(solution)/shard_map/ppermute | solution.py:209
  52.7 14.5 %collective-permute-start.16 = (bf16[136,1280]{1,0:T(8,128)(2,1)S(1)}, bf16[136,1280]{1,0:T(8,128)(2,1)S(1)}, u32[]{:S(2)}, u32[]{:S(2)}) collective-permute-start(bf16[136,1280]{1,0:T(8,128)(2,1)S(1)} %collective-permute-done.15.refs_10_), channel_id=1, source_target_pairs={{0,32},{32,64},{64,96},{96,128},{128,160},{160,192},{192,224},{224... | collective-permute-start | bytes 1044488 | tf_op jit(solution)/shard_map/ppermute | solution.py:210
  54.6 14.5 %collective-permute-start.23 = (bf16[136,1280]{1,0:T(8,128)(2,1)S(1)}, bf16[136,1280]{1,0:T(8,128)(2,1)S(1)}, u32[]{:S(2)}, u32[]{:S(2)}) collective-permute-start(bf16[136,1280]{1,0:T(8,128)(2,1)S(1)} %collective-permute-done.22.refs_11_), channel_id=1, source_target_pairs={{0,480},{32,0},{64,32},{96,64},{128,96},{160,128},{192,160},{224,1... | collective-permute-start | bytes 1044488 | tf_op jit(solution)/shard_map/ppermute | solution.py:211
  59.2 14.5 %collective-permute-start.2 = (bf16[128,1280]{1,0:T(8,128)(2,1)S(1)}, bf16[128,1280]{1,0:T(8,128)(2,1)S(1)}, u32[]{:S(2)}, u32[]{:S(2)}) collective-permute-start(bf16[128,1280]{1,0:T(8,128)(2,1)S(1)} %collective-permute-done.1.refs_5_), channel_id=1, source_target_pairs={{0,32},{32,64},{64,96},{96,128},{128,160},{160,192},{192,224},{224... | collective-permute-start | bytes 983048 | tf_op jit(solution)/shard_map/ppermute | solution.py:207
  61.9 14.5 %collective-permute-start.9 = (bf16[128,1280]{1,0:T(8,128)(2,1)S(1)}, bf16[128,1280]{1,0:T(8,128)(2,1)S(1)}, u32[]{:S(2)}, u32[]{:S(2)}) collective-permute-start(bf16[128,1280]{1,0:T(8,128)(2,1)S(1)} %collective-permute-done.8.refs_6_), channel_id=1, source_target_pairs={{0,480},{32,0},{64,32},{96,64},{128,96},{160,128},{192,160},{224,1... | collective-permute-start | bytes 983048 | tf_op jit(solution)/shard_map/ppermute | solution.py:209
  67.2 14.6 %collective-permute-start.17 = (bf16[136,1280]{1,0:T(8,128)(2,1)S(1)}, bf16[136,1280]{1,0:T(8,128)(2,1)S(1)}, u32[]{:S(2)}, u32[]{:S(2)}) collective-permute-start(bf16[136,1280]{1,0:T(8,128)(2,1)S(1)} %collective-permute-done.16.refs_6_), channel_id=1, source_target_pairs={{0,32},{32,64},{64,96},{96,128},{128,160},{160,192},{192,224},{224... | collective-permute-start | bytes 1044488 | tf_op jit(solution)/shard_map/ppermute | solution.py:210
  69.1 14.5 %collective-permute-start.24 = (bf16[136,1280]{1,0:T(8,128)(2,1)S(1)}, bf16[136,1280]{1,0:T(8,128)(2,1)S(1)}, u32[]{:S(2)}, u32[]{:S(2)}) collective-permute-start(bf16[136,1280]{1,0:T(8,128)(2,1)S(1)} %collective-permute-done.23.refs_7_), channel_id=1, source_target_pairs={{0,480},{32,0},{64,32},{96,64},{128,96},{160,128},{192,160},{224,1... | collective-permute-start | bytes 1044488 | tf_op jit(solution)/shard_map/ppermute | solution.py:211
  73.7 14.5 %collective-permute-start.3 = (bf16[128,1280]{1,0:T(8,128)(2,1)S(1)}, bf16[128,1280]{1,0:T(8,128)(2,1)S(1)}, u32[]{:S(2)}, u32[]{:S(2)}) collective-permute-start(bf16[128,1280]{1,0:T(8,128)(2,1)S(1)} %collective-permute-done.2.refs_2_), channel_id=1, source_target_pairs={{0,32},{32,64},{64,96},{96,128},{128,160},{160,192},{192,224},{224... | collective-permute-start | bytes 983048 | tf_op jit(solution)/shard_map/ppermute | solution.py:207
  76.4 14.5 %collective-permute-start.10 = (bf16[128,1280]{1,0:T(8,128)(2,1)S(1)}, bf16[128,1280]{1,0:T(8,128)(2,1)S(1)}, u32[]{:S(2)}, u32[]{:S(2)}) collective-permute-start(bf16[128,1280]{1,0:T(8,128)(2,1)S(1)} %collective-permute-done.9.refs_3_), channel_id=1, source_target_pairs={{0,480},{32,0},{64,32},{96,64},{128,96},{160,128},{192,160},{224,1... | collective-permute-start | bytes 983048 | tf_op jit(solution)/shard_map/ppermute | solution.py:209
  81.8 14.5 %collective-permute-start.18 = (bf16[136,1280]{1,0:T(8,128)(2,1)S(1)}, bf16[136,1280]{1,0:T(8,128)(2,1)S(1)}, u32[]{:S(2)}, u32[]{:S(2)}) collective-permute-start(bf16[136,1280]{1,0:T(8,128)(2,1)S(1)} %collective-permute-done.17.refs_8_), channel_id=1, source_target_pairs={{0,32},{32,64},{64,96},{96,128},{128,160},{160,192},{192,224},{224... | collective-permute-start | bytes 1044488 | tf_op jit(solution)/shard_map/ppermute | solution.py:210
  83.7 15.3 %collective-permute-start.25 = (bf16[136,1280]{1,0:T(8,128)(2,1)S(1)}, bf16[136,1280]{1,0:T(8,128)(2,1)S(1)}, u32[]{:S(2)}, u32[]{:S(2)}) collective-permute-start(bf16[136,1280]{1,0:T(8,128)(2,1)S(1)} %collective-permute-done.24.refs_9_), channel_id=1, source_target_pairs={{0,480},{32,0},{64,32},{96,64},{128,96},{160,128},{192,160},{224,1... | collective-permute-start | bytes 1044488 | tf_op jit(solution)/shard_map/ppermute | solution.py:211
  88.3 16.0 %collective-permute-start.4 = (bf16[128,1280]{1,0:T(8,128)(2,1)S(1)}, bf16[128,1280]{1,0:T(8,128)(2,1)S(1)}, u32[]{:S(2)}, u32[]{:S(2)}) collective-permute-start(bf16[128,1280]{1,0:T(8,128)(2,1)S(1)} %collective-permute-done.3.refs_4_), channel_id=1, source_target_pairs={{0,32},{32,64},{64,96},{96,128},{128,160},{160,192},{192,224},{224... | collective-permute-start | bytes 983048 | tf_op jit(solution)/shard_map/ppermute | solution.py:207
  91.0 16.0 %collective-permute-start.11 = (bf16[128,1280]{1,0:T(8,128)(2,1)S(1)}, bf16[128,1280]{1,0:T(8,128)(2,1)S(1)}, u32[]{:S(2)}, u32[]{:S(2)}) collective-permute-start(bf16[128,1280]{1,0:T(8,128)(2,1)S(1)} %collective-permute-done.10.refs_5_), channel_id=1, source_target_pairs={{0,480},{32,0},{64,32},{96,64},{128,96},{160,128},{192,160},{224,1... | collective-permute-start | bytes 983048 | tf_op jit(solution)/shard_map/ppermute | solution.py:209
  96.3 15.9 %collective-permute-start.19 = (bf16[136,1280]{1,0:T(8,128)(2,1)S(1)}, bf16[136,1280]{1,0:T(8,128)(2,1)}, u32[]{:S(2)}, u32[]{:S(2)}) collective-permute-start(bf16[136,1280]{1,0:T(8,128)(2,1)S(1)} %collective-permute-done.18.refs_8_), channel_id=1, source_target_pairs={{0,32},{32,64},{64,96},{96,128},{128,160},{160,192},{192,224},{224... | collective-permute-start | bytes 1044488 | tf_op jit(solution)/shard_map/ppermute | solution.py:210
  99.0 15.2 %collective-permute-start.26 = (bf16[136,1280]{1,0:T(8,128)(2,1)S(1)}, bf16[136,1280]{1,0:T(8,128)(2,1)}, u32[]{:S(2)}, u32[]{:S(2)}) collective-permute-start(bf16[136,1280]{1,0:T(8,128)(2,1)S(1)} %collective-permute-done.25.refs_9_), channel_id=1, source_target_pairs={{0,480},{32,0},{64,32},{96,64},{128,96},{160,128},{192,160},{224,1... | collective-permute-start | bytes 1044488 | tf_op jit(solution)/shard_map/ppermute | solution.py:211
  104.3 14.4 %collective-permute-start.5 = (bf16[128,1280]{1,0:T(8,128)(2,1)S(1)}, bf16[128,1280]{1,0:T(8,128)(2,1)}, u32[]{:S(2)}, u32[]{:S(2)}) collective-permute-start(bf16[128,1280]{1,0:T(8,128)(2,1)S(1)} %collective-permute-done.4.refs_2_), channel_id=1, source_target_pairs={{0,32},{32,64},{64,96},{96,128},{128,160},{160,192},{192,224},{224... | collective-permute-start | bytes 983048 | tf_op jit(solution)/shard_map/ppermute | solution.py:207
  106.9 13.7 %collective-permute-start.12 = (bf16[128,1280]{1,0:T(8,128)(2,1)S(1)}, bf16[128,1280]{1,0:T(8,128)(2,1)}, u32[]{:S(2)}, u32[]{:S(2)}) collective-permute-start(bf16[128,1280]{1,0:T(8,128)(2,1)S(1)} %collective-permute-done.11.refs_3_), channel_id=1, source_target_pairs={{0,480},{32,0},{64,32},{96,64},{128,96},{160,128},{192,160},{224,1... | collective-permute-start | bytes 983048 | tf_op jit(solution)/shard_map/ppermute | solution.py:209
  112.2 20.6 %collective-permute-start.20 = (bf16[136,1280]{1,0:T(8,128)(2,1)}, bf16[136,1280]{1,0:T(8,128)(2,1)}, u32[]{:S(2)}, u32[]{:S(2)}) collective-permute-start(bf16[136,1280]{1,0:T(8,128)(2,1)} %collective-permute-done.19.refs_10_), channel_id=1, source_target_pairs={{0,32},{32,64},{64,96},{96,128},{128,160},{160,192},{192,224},{224... | collective-permute-start | bytes 1044488 | tf_op jit(solution)/shard_map/ppermute | solution.py:210
  114.1 18.7 %collective-permute-start.27 = (bf16[136,1280]{1,0:T(8,128)(2,1)}, bf16[136,1280]{1,0:T(8,128)(2,1)}, u32[]{:S(2)}, u32[]{:S(2)}) collective-permute-start(bf16[136,1280]{1,0:T(8,128)(2,1)} %collective-permute-done.26.refs_11_), channel_id=1, source_target_pairs={{0,480},{32,0},{64,32},{96,64},{128,96},{160,128},{192,160},{224,1... | collective-permute-start | bytes 1044488 | tf_op jit(solution)/shard_map/ppermute | solution.py:211
  118.7 12.1 %collective-permute-start.6 = (bf16[128,1280]{1,0:T(8,128)(2,1)}, bf16[128,1280]{1,0:T(8,128)(2,1)}, u32[]{:S(2)}, u32[]{:S(2)}) collective-permute-start(bf16[128,1280]{1,0:T(8,128)(2,1)} %collective-permute-done.5.refs_4_), channel_id=1, source_target_pairs={{0,32},{32,64},{64,96},{96,128},{128,160},{160,192},{192,224},{224... | collective-permute-start | bytes 983048 | tf_op jit(solution)/shard_map/ppermute | solution.py:207
  120.7 12.2 %collective-permute-start.13 = (bf16[128,1280]{1,0:T(8,128)(2,1)}, bf16[128,1280]{1,0:T(8,128)(2,1)}, u32[]{:S(2)}, u32[]{:S(2)}) collective-permute-start(bf16[128,1280]{1,0:T(8,128)(2,1)} %collective-permute-done.12.refs_5_), channel_id=1, source_target_pairs={{0,480},{32,0},{64,32},{96,64},{128,96},{160,128},{192,160},{224,1... | collective-permute-start | bytes 983048 | tf_op jit(solution)/shard_map/ppermute | solution.py:209
  132.9 19.7 %collective-permute-start.29 = (bf16[136,1280]{1,0:T(8,128)(2,1)}, bf16[136,1280]{1,0:T(8,128)(2,1)S(1)}, u32[]{:S(2)}, u32[]{:S(2)}) collective-permute-start(bf16[136,1280]{1,0:T(8,128)(2,1)} %collective-permute-done.27.refs_13_), channel_id=1, source_target_pairs={{0,480},{32,0},{64,32},{96,64},{128,96},{160,128},{192,160},{224,1... | collective-permute-start | bytes 1044488 | tf_op jit(solution)/shard_map/ppermute | solution.py:211
  138.3 14.2 %collective-permute-start.28 = (bf16[128,1280]{1,0:T(8,128)(2,1)}, bf16[128,1280]{1,0:T(8,128)(2,1)S(1)}, u32[]{:S(2)}, u32[]{:S(2)}) collective-permute-start(bf16[128,1280]{1,0:T(8,128)(2,1)} %collective-permute-done.6.refs_6_), channel_id=1, source_target_pairs={{0,32},{32,64},{64,96},{96,128},{128,160},{160,192},{192,224},{224... | collective-permute-start | bytes 983048 | tf_op jit(solution)/shard_map/ppermute | solution.py:207
  170.0 36.7 %all-to-all-start = ((bf16[16,24,2560]{2,1,0:T(8,128)(2,1)}), bf16[16,24,2560]{2,1,0:T(8,128)(2,1)S(1)}, u32[]{:S(2)}, u32[]{:S(2)}) async-start(bf16[16,24,2560]{2,1,0:T(8,128)(2,1)} %bitcast.9), calls=%async_computation | async-start | bytes 3932160 | tf_op jit(solution)/shard_map/all_to_all | solution.py:242
  (31 other events, 130.8 us)
Sparse Core Ops, SparseCore 0:
  11.1 66.7 all-gather.1

commit v3 on v2

v3 whole, which is shorter than its diff:
```python
import jax
import jax.numpy as jnp
from jax import lax
from jax.experimental import pallas as pl
from jax.experimental.pallas import tpu as pltpu
from jax.sharding import PartitionSpec as P

BF = jnp.bfloat16
F32 = jnp.float32
LANES = 128
INFO_ROWS = 8
VMEM = 16 << 20


def _pack_kernel(grads_ref, routes_ref, gates_ref, first_ref, second_ref):
    top, _, tokens = routes_ref.shape
    half = first_ref.shape[1]
    experts = 2 * INFO_ROWS
    first_ref[...] = grads_ref[:, 0:half]
    second_ref[0:tokens, :] = grads_ref[:, half:]
    gates = gates_ref[...].astype(F32)
    expert = lax.broadcasted_iota(jnp.int32, (experts, tokens), 0)
    gate = jnp.zeros((experts, tokens), F32)
    named = jnp.zeros((experts, tokens), F32)
    for k in range(top):
        hit = routes_ref[k] == expert
        gate = jnp.where(hit, gates[k : k + 1, :], gate)
        named = jnp.where(hit, 1.0, named)
    row = lax.broadcasted_iota(jnp.int32, (tokens, tokens), 0)
    col = lax.broadcasted_iota(jnp.int32, (tokens, tokens), 1)
    earlier = jnp.where(row < col, 1.0, 0.0).astype(BF)
    rank = jnp.dot(named.astype(BF), earlier, preferred_element_type=F32)
    slot = jnp.where(named > 0.5, rank, -1.0)
    n = INFO_ROWS
    parts = [slot[0:n], gate[0:n], slot[n : 2 * n], gate[n : 2 * n]]
    parts.append(jnp.zeros((n, half - 4 * tokens), F32))
    second_ref[tokens : tokens + n, :] = jnp.concatenate(parts, axis=1).astype(BF)


def _pack(grads, routes_t, gates_t):
    tokens, width = grads.shape
    half = width // 2
    return pl.pallas_call(
        _pack_kernel,
        out_shape=[
            jax.ShapeDtypeStruct((tokens, half), BF),
            jax.ShapeDtypeStruct((tokens + INFO_ROWS, half), BF),
        ],
        compiler_params=pltpu.CompilerParams(vmem_limit_bytes=VMEM),
        cost_estimate=pl.CostEstimate(
            flops=1 << 20, bytes_accessed=4 * tokens * width, transcendentals=0
        ),
        name="pack_tokens",
    )(grads, routes_t, gates_t)


def _split_kernel(units_dev, core_ref, hidden_ref, mine_ref, other_ref):
    units = hidden_ref.shape[1]
    half = units // 2
    row = lax.broadcasted_iota(jnp.int32, (half, units), 0)
    col = lax.broadcasted_iota(jnp.int32, (half, units), 1)
    even = row + units_dev * (row // units_dev)
    for flip, out_ref in ((0, mine_ref), (1, other_ref)):
        core = lax.rem(core_ref[0] + flip, 2)
        pick = jnp.where(col == even + core * units_dev, 1.0, 0.0).astype(BF)
        out_ref[...] = lax.dot_general(
            pick, hidden_ref[...], (((1,), (1,)), ((), ())), preferred_element_type=F32
        ).astype(BF)


def _split(hidden, core, units_dev):
    rows, units = hidden.shape

    def kernel(*refs):
        _split_kernel(units_dev, *refs)

    return pl.pallas_call(
        kernel,
        grid_spec=pltpu.PrefetchScalarGridSpec(
            num_scalar_prefetch=1,
            grid=(1,),
            in_specs=[pl.BlockSpec((rows, units), lambda i, m: (0, 0))],
            out_specs=[pl.BlockSpec((units // 2, rows), lambda i, m: (0, 0))] * 2,
        ),
        out_shape=[jax.ShapeDtypeStruct((units // 2, rows), BF)] * 2,
        compiler_params=pltpu.CompilerParams(vmem_limit_bytes=VMEM),
        cost_estimate=pl.CostEstimate(
            flops=2 * rows * units * units, bytes_accessed=4 * rows * units, transcendentals=0
        ),
        name="split_hidden",
    )(core, hidden)


def _select_kernel(count, tokens, me_ref, *refs):
    firsts, seconds, out_ref = refs[:count], refs[count : 2 * count], refs[-1]
    capacity = out_ref.shape[1]
    half = firsts[0].shape[1]
    me = me_ref[0]
    step = pl.program_id(0)
    for i in range(count):

        @pl.when(step == i)
        def _():
            info = seconds[i][tokens : tokens + INFO_ROWS, 0 : 4 * tokens].astype(F32)
            info = jnp.where(me >= INFO_ROWS, info[:, 2 * tokens :], info[:, : 2 * tokens])
            row = lax.broadcasted_iota(jnp.int32, info.shape, 0)
            mine = jnp.sum(jnp.where(row == lax.rem(me, INFO_ROWS), info, 0.0), axis=0, keepdims=True)
            slot = lax.broadcasted_iota(jnp.int32, (capacity, tokens), 0).astype(F32)
            pick = jnp.where(mine[:, :tokens] == slot, mine[:, tokens:], 0.0).astype(BF)
            out_ref[0, :, :half] = jnp.dot(
                pick, firsts[i][0:tokens, :], preferred_element_type=F32
            ).astype(BF)
            out_ref[0, :, half:] = jnp.dot(
                pick, seconds[i][0:tokens, :], preferred_element_type=F32
            ).astype(BF)


def _select(me, offsets, firsts, seconds, rows, shape, name):
    count = len(firsts)
    groups = shape[0]
    steps = [(off + groups) % groups for off in offsets]

    def place(i, m):
        step = steps[0]
        for k in range(1, count):
            step = jnp.where(i == k, steps[k], step)
        return (lax.rem(m[0] + step, groups), 0, 0)

    tokens = firsts[0].shape[0]
    whole = [pl.BlockSpec(a.shape, lambda i, m: (0, 0)) for a in firsts + seconds]
    operands = list(firsts) + list(seconds)
    aliases = {}
    if rows is not None:
        whole.append(pl.BlockSpec(memory_space=pltpu.HBM))
        operands.append(rows)
        aliases = {1 + 2 * count: 0}

    def kernel(*refs):
        _select_kernel(count, tokens, *refs)

    return pl.pallas_call(
        kernel,
        grid_spec=pltpu.PrefetchScalarGridSpec(
            num_scalar_prefetch=1,
            grid=(count,),
            in_specs=whole,
            out_specs=pl.BlockSpec((1,) + shape[1:], place),
        ),
        out_shape=pltpu.HBM(shape, BF),
        input_output_aliases=aliases,
        compiler_params=pltpu.CompilerParams(vmem_limit_bytes=VMEM),
        cost_estimate=pl.CostEstimate(
            flops=2 * count * shape[1] * tokens * shape[2],
            bytes_accessed=2 * count * (tokens + shape[1]) * shape[2],
            transcendentals=0,
        ),
        name=name,
    )(me, *operands)


def _term_kernel(saved_ref, rows_ref, out_ref):
    out_ref[...] = jnp.dot(saved_ref[...], rows_ref[...], preferred_element_type=F32).astype(BF)


def _term(saved_t, rows, name):
    units, depth = saved_t.shape
    width = rows.shape[1]
    block = 512 if width % 512 == 0 else LANES
    return pl.pallas_call(
        _term_kernel,
        grid=(width // block,),
        in_specs=[
            pl.BlockSpec((units, depth), lambda j: (0, 0)),
            pl.BlockSpec((depth, block), lambda j: (0, j)),
        ],
        out_specs=pl.BlockSpec((units, block), lambda j: (0, j)),
        out_shape=jax.ShapeDtypeStruct((units, width), BF),
        compiler_params=pltpu.CompilerParams(vmem_limit_bytes=VMEM),
        cost_estimate=pl.CostEstimate(
            flops=2 * units * depth * width,
            bytes_accessed=2 * (units * depth + depth * width + units * width),
            transcendentals=0,
        ),
        name=name,
    )(saved_t, rows)


def body(grads, routes, gates, hidden, down_weight):
    groups = lax.axis_size("expert")
    replicas = lax.axis_size("replica")
    chips = replicas // 2
    width = grads.shape[2]
    units_dev = down_weight.shape[0]
    rows_dev = hidden.shape[1]
    units = hidden.shape[2]
    capacity = rows_dev // groups
    half = width // 2
    me = lax.axis_index("expert").astype(jnp.int32).reshape(1)
    core = lax.rem(lax.axis_index("replica"), 2)

    weights = lax.all_gather(down_weight, "replica", axis=0, tiled=True)

    own_first, own_second = _pack(grads[0], routes.transpose(2, 0, 1), gates[0].T)

    up = [(i, (i + 1) % groups) for i in range(groups)]
    down = [(i, (i - 1) % groups) for i in range(groups)]
    far = groups // 2
    got_first, got_second = {0: own_first}, {0: own_second}
    a_up = a_down = own_first
    b_up = b_down = own_second
    rows = None
    shape = (groups, capacity, width)

    def pick(rows, batch, name):
        firsts = [got_first[off] for off in batch]
        seconds = [got_second[off] for off in batch]
        return _select(me, batch, firsts, seconds, rows, shape, name)

    for hop in range(1, far + 1):
        if 3 <= hop < far:
            a_up, rows = lax.optimization_barrier((a_up, rows))
        if hop == far:
            me, hidden, a_up = lax.optimization_barrier((me, hidden, a_up))
        a_up = lax.ppermute(a_up, "expert", up)
        if hop < far:
            a_down = lax.ppermute(a_down, "expert", down)
            b_up = lax.ppermute(b_up, "expert", up)
        b_down = lax.ppermute(b_down, "expert", down)
        got_first[-hop], got_second[hop] = a_up, b_down
        if hop < far:
            got_first[hop], got_second[-hop] = a_down, b_up
        if hop == 2:
            rows = pick(rows, [0, -1, 1], "select_1")
        elif 3 <= hop < far - 1:
            rows = pick(rows, [1 - hop, hop - 1], f"select_{hop - 1}")
    got_second[-far] = got_second.pop(far)

    rows = pick(rows, [2 - far, far - 2, 1 - far, far - 1], "select_near_last")
    saved_mine, saved_other = _split(hidden[0], core.reshape(1), units_dev)
    rows = pick(rows, [-far], "select_last")
    rows = rows.reshape(rows_dev, width)

    other = _term(saved_other, rows, "term_other")
    arrived = lax.ppermute(other, "replica", [(i, i ^ 1) for i in range(replicas)])
    mine = _term(saved_mine, rows, "term_mine")
    pair = (mine.astype(F32) + arrived.astype(F32)).astype(BF)
    pair, rows, weights = lax.optimization_barrier((pair, rows, weights))
    parts = lax.all_to_all(
        pair.reshape(chips, units_dev, width),
        "replica",
        split_axis=0,
        concat_axis=0,
        tiled=True,
        axis_index_groups=[[2 * q + c for q in range(chips)] for c in range(2)],
    )
    d_rows = lax.dot_general(
        rows, weights[:, 0, :], (((1,), (1,)), ((), ())), preferred_element_type=F32
    )
    d_hidden = d_rows.astype(BF)[None]
    parts, d_hidden = lax.optimization_barrier((parts, d_hidden))
    down_grad = jnp.sum(parts.astype(F32), axis=0)[:, None, :]
    return (d_hidden, down_grad)


def solution(mesh):
    placed = (P("replica", "expert", None),) * 5
    return jax.shard_map(
        body,
        mesh=mesh,
        in_specs=placed,
        out_specs=(P("replica", "expert", None), P("replica", "expert", None)),
        check_vma=False,
    )
```

time: 216 us -> 202 us (0.935)
  local copies, waits for them, and re-layouts: 17.4 us -> 6.94 us
  starting transfers between devices: 120 us -> 114 us
  waiting for transfers between devices: 30.1 us -> 35.7 us
    ppermute x7, starting transfers between devices: 32 us -> 18.7 us  [body(): a_down = lax.ppermute(a_down, 'expert', down)]
    unnamed x61 -> x10, local copies, waits for them, and re-layouts: 15.4 us -> 6.08 us
    ppermute x8, starting transfers between devices: 15.3 us -> 21.8 us  [body(): a_up = lax.ppermute(a_up, 'expert', up)]
    ppermute x7, waiting for transfers between devices: 0.02 us -> 5.64 us  [body(): b_up = lax.ppermute(b_up, 'expert', up)]
    ppermute x8, waiting for transfers between devices: 5.59 us -> 0.44 us  [body(): a_up = lax.ppermute(a_up, 'expert', up)]
    pallas_call x1, Pallas kernels: 5.35 us -> 1.42 us  [_split(): pl.pallas_call(kernel, grid_spec=pltpu.PrefetchScalarGridSpec(num_scalar_...]
    pallas_call x4 -> x7, Pallas kernels: 7.79 us -> 11.2 us  [_select(): pl.pallas_call(kernel, grid_spec=pltpu.PrefetchScalarGridSpec(num_scalar_...]
    ppermute x8, waiting for transfers between devices: 0.02 us -> 2.96 us  [body(): b_down = lax.ppermute(b_down, 'expert', down)]
  transfers between devices with their start and end apart: 33 -> 33, of which waited for: 4 -> 10; matrix products, arithmetic and copies ran while one was open for 6% -> 5% of each run, Pallas kernels for 10% -> 10%
where the time goes in v3:
time: 202 us; the launch traced here: 201 us
  starting transfers between devices  114 us (56%)
  waiting for transfers between devices  35.7 us (18%)
  Pallas kernels  19.4 us (10%)
  between operations  14.5 us (7%)
  matrix products  8.33 us (4%)
  local copies, waits for them, and re-layouts  6.94 us (3%)
  other arithmetic  2.04 us (1%)
    ppermute x8, starting transfers between devices, body(): b_down = lax.ppermute(b_down, 'expert', down)  44.7 us
    ppermute x8, starting transfers between devices, body(): a_up = lax.ppermute(a_up, 'expert', up)  21.8 us
    all_to_all x1, waiting for transfers between devices, body(): lax.all_to_all(pair.reshape(chips, units_dev, width), 'replica', split_ax...  21.6 us
    ppermute x7, starting transfers between devices, body(): a_down = lax.ppermute(a_down, 'expert', down)  18.7 us
    ppermute x7, starting transfers between devices, body(): b_up = lax.ppermute(b_up, 'expert', up)  13.4 us
    pallas_call x7, Pallas kernels, _select(): pl.pallas_call(kernel, grid_spec=pltpu.PrefetchScalarGridSpec(num_scalar_...  11.2 us
    ppermute x1, starting transfers between devices, body(): lax.ppermute(other, 'replica', [(i, i ^ 1) for i in range(replicas)])  8.65 us
    dot_general x1, matrix products, body(): lax.dot_general(rows, weights[:, 0, :], (((1,), (1,)), ((), ())), preferr...  8.33 us
  transfers between devices with their start and end apart: 33, of which 10 were waited for; matrix products, arithmetic and copies ran while one was open for 5% of the time, Pallas kernels for 10%

profile of v3, /device:TPU:1, one launch (start us, length us, event | category | flops | bytes accessed | tf_op | source)
XLA Modules:
  0.0 200.8 jit_solution(8638330286328785949)
XLA Ops:
  10.5 11.9 %collective-permute-start.4 = (bf16[136,1280]{1,0:T(8,128)(2,1)S(1)}, bf16[136,1280]{1,0:T(8,128)(2,1)S(1)}, u32[]{:S(2)}, u32[]{:S(2)}) collective-permute-start(bf16[136,1280]{1,0:T(8,128)(2,1)S(1)} %get-tuple-element.25.refs_4_), channel_id=1, source_target_pairs={{0,480},{32,0},{64,32},{96,64},{128,96},{160,128},{192,160},{224,1... | collective-permute-start | bytes 1044488 | tf_op jit(solution)/shard_map/ppermute | solution.py:228
  22.4 1.9 collective-permute-start
  24.4 1.9 collective-permute-start.3
  26.3 2.9 %collective-permute-done.4.refs_6_ = bf16[136,1280]{1,0:T(8,128)(2,1)S(1)} collective-permute-done((bf16[136,1280]{1,0:T(8,128)(2,1)S(1)}, bf16[136,1280]{1,0:T(8,128)(2,1)S(1)}, u32[]{:S(2)}, u32[]{:S(2)}) %collective-permute-start.4) | collective-permute-done | bytes 348192 | tf_op jit(solution)/shard_map/ppermute | solution.py:228
  29.2 5.3 %collective-permute-start.8 = (bf16[136,1280]{1,0:T(8,128)(2,1)S(1)}, bf16[136,1280]{1,0:T(8,128)(2,1)S(1)}, u32[]{:S(2)}, u32[]{:S(2)}) collective-permute-start(bf16[136,1280]{1,0:T(8,128)(2,1)S(1)} %collective-permute-done.4.refs_6_), channel_id=1, source_target_pairs={{0,480},{32,0},{64,32},{96,64},{128,96},{160,128},{192,160},{224,1... | collective-permute-start | bytes 1044488 | tf_op jit(solution)/shard_map/ppermute | solution.py:228
  34.6 1.9 collective-permute-start.2
  36.5 3.4 %collective-permute-start.1 = (bf16[128,1280]{1,0:T(8,128)(2,1)}, bf16[128,1280]{1,0:T(8,128)(2,1)S(1)}, u32[]{:S(2)}, u32[]{:S(2)}) collective-permute-start(bf16[128,1280]{1,0:T(8,128)(2,1)} %collective-permute-done.refs_2_), channel_id=1, source_target_pairs={{0,32},{32,64},{64,96},{96,128},{128,160},{160,192},{192,224},{224... | collective-permute-start | bytes 983048 | tf_op jit(solution)/shard_map/ppermute | solution.py:224
  43.2 4.6 %collective-permute-start.12 = (bf16[136,1280]{1,0:T(8,128)(2,1)S(1)}, bf16[136,1280]{1,0:T(8,128)(2,1)S(1)}, u32[]{:S(2)}, u32[]{:S(2)}) collective-permute-start(bf16[136,1280]{1,0:T(8,128)(2,1)S(1)} %collective-permute-done.8.refs_4_), channel_id=1, source_target_pairs={{0,480},{32,0},{64,32},{96,64},{128,96},{160,128},{192,160},{224,1... | collective-permute-start | bytes 1044488 | tf_op jit(solution)/shard_map/ppermute | solution.py:228
  47.8 5.0 %collective-permute-start.6 = (bf16[128,1280]{1,0:T(8,128)(2,1)S(1)}, bf16[128,1280]{1,0:T(8,128)(2,1)S(1)}, u32[]{:S(2)}, u32[]{:S(2)}) collective-permute-start(bf16[128,1280]{1,0:T(8,128)(2,1)S(1)} %collective-permute-done.2.refs_3_), channel_id=1, source_target_pairs={{0,480},{32,0},{64,32},{96,64},{128,96},{160,128},{192,160},{224,1... | collective-permute-start | bytes 983048 | tf_op jit(solution)/shard_map/ppermute | solution.py:226
  52.8 2.9 %select_1.1.refs_5_ = bf16[16,56,2560]{2,1,0:T(8,128)(2,1)} custom-call(s32[1]{0:T(128)} %bitcast.1.refs_0_, bf16[128,1280]{1,0:T(8,128)(2,1)S(1)} %get-tuple-element.24.refs_1_, bf16[128,1280]{1,0:T(8,128)(2,1)} %collective-permute-done.refs_2_, bf16[128,1280]{1,0:T(8,128)(2,1)S(1)} %collective-permute-done.2.refs_3_, ...), custom_call_target="tpu_custom_call" | custom-call | flops 110100480 | bytes 2826240 | tf_op jit(solution)/shard_map/select_1/pallas_call | solution.py:141
  57.6 1.9 collective-permute-start.11
  59.6 4.6 %collective-permute-start.16 = (bf16[136,1280]{1,0:T(8,128)(2,1)S(1)}, bf16[136,1280]{1,0:T(8,128)(2,1)S(1)}, u32[]{:S(2)}, u32[]{:S(2)}) collective-permute-start(bf16[136,1280]{1,0:T(8,128)(2,1)S(1)} %collective-permute-done.12.refs_4_), channel_id=1, source_target_pairs={{0,480},{32,0},{64,32},{96,64},{128,96},{160,128},{192,160},{224,1... | collective-permute-start | bytes 1044488 | tf_op jit(solution)/shard_map/ppermute | solution.py:228
  64.2 3.4 %collective-permute-start.10 = (bf16[128,1280]{1,0:T(8,128)(2,1)S(1)}, bf16[128,1280]{1,0:T(8,128)(2,1)S(1)}, u32[]{:S(2)}, u32[]{:S(2)}) collective-permute-start(bf16[128,1280]{1,0:T(8,128)(2,1)S(1)} %collective-permute-done.6.refs_2_), channel_id=1, source_target_pairs={{0,480},{32,0},{64,32},{96,64},{128,96},{160,128},{192,160},{224,1... | collective-permute-start | bytes 983048 | tf_op jit(solution)/shard_map/ppermute | solution.py:226
  73.4 4.6 %collective-permute-start.20 = (bf16[136,1280]{1,0:T(8,128)(2,1)S(1)}, bf16[136,1280]{1,0:T(8,128)(2,1)S(1)}, u32[]{:S(2)}, u32[]{:S(2)}) collective-permute-start(bf16[136,1280]{1,0:T(8,128)(2,1)S(1)} %collective-permute-done.16.refs_4_), channel_id=1, source_target_pairs={{0,480},{32,0},{64,32},{96,64},{128,96},{160,128},{192,160},{224,1... | collective-permute-start | bytes 1044488 | tf_op jit(solution)/shard_map/ppermute | solution.py:228
  78.0 2.6 %collective-permute-start.14 = (bf16[128,1280]{1,0:T(8,128)(2,1)S(1)}, bf16[128,1280]{1,0:T(8,128)(2,1)S(1)}, u32[]{:S(2)}, u32[]{:S(2)}) collective-permute-start(bf16[128,1280]{1,0:T(8,128)(2,1)S(1)} %collective-permute-done.10.refs_2_), channel_id=1, source_target_pairs={{0,480},{32,0},{64,32},{96,64},{128,96},{160,128},{192,160},{224,1... | collective-permute-start | bytes 983048 | tf_op jit(solution)/shard_map/ppermute | solution.py:226
  81.9 2.6 %collective-permute-start.13 = (bf16[128,1280]{1,0:T(8,128)(2,1)S(1)}, bf16[128,1280]{1,0:T(8,128)(2,1)S(1)}, u32[]{:S(2)}, u32[]{:S(2)}) collective-permute-start(bf16[128,1280]{1,0:T(8,128)(2,1)S(1)} %collective-permute-done.9.refs_1_), channel_id=1, source_target_pairs={{0,32},{32,64},{64,96},{96,128},{128,160},{160,192},{192,224},{224... | collective-permute-start | bytes 983048 | tf_op jit(solution)/shard_map/ppermute | solution.py:224
  88.2 4.6 %collective-permute-start.23 = (bf16[136,1280]{1,0:T(8,128)(2,1)S(1)}, bf16[136,1280]{1,0:T(8,128)(2,1)S(1)}, u32[]{:S(2)}, u32[]{:S(2)}) collective-permute-start(bf16[136,1280]{1,0:T(8,128)(2,1)S(1)} %collective-permute-done.20.refs_4_), channel_id=1, source_target_pairs={{0,480},{32,0},{64,32},{96,64},{128,96},{160,128},{192,160},{224,1... | collective-permute-start | bytes 1044488 | tf_op jit(solution)/shard_map/ppermute | solution.py:228
  92.8 1.9 collective-permute-start.18
  96.0 3.4 %collective-permute-start.17 = (bf16[128,1280]{1,0:T(8,128)(2,1)S(1)}, bf16[128,1280]{1,0:T(8,128)(2,1)S(1)}, u32[]{:S(2)}, u32[]{:S(2)}) collective-permute-start(bf16[128,1280]{1,0:T(8,128)(2,1)S(1)} %collective-permute-done.13.refs_1_), channel_id=1, source_target_pairs={{0,32},{32,64},{64,96},{96,128},{128,160},{160,192},{192,224},{224... | collective-permute-start | bytes 983048 | tf_op jit(solution)/shard_map/ppermute | solution.py:224
  102.9 4.6 %collective-permute-start.24 = (bf16[136,1280]{1,0:T(8,128)(2,1)S(1)}, bf16[136,1280]{1,0:T(8,128)(2,1)S(1)}, u32[]{:S(2)}, u32[]{:S(2)}) collective-permute-start(bf16[136,1280]{1,0:T(8,128)(2,1)S(1)} %collective-permute-done.23.refs_6_), channel_id=1, source_target_pairs={{0,480},{32,0},{64,32},{96,64},{128,96},{160,128},{192,160},{224,1... | collective-permute-start | bytes 1044488 | tf_op jit(solution)/shard_map/ppermute | solution.py:228
  110.7 3.3 %collective-permute-start.21 = (bf16[128,1280]{1,0:T(8,128)(2,1)S(1)}, bf16[128,1280]{1,0:T(8,128)(2,1)S(1)}, u32[]{:S(2)}, u32[]{:S(2)}) collective-permute-start(bf16[128,1280]{1,0:T(8,128)(2,1)S(1)} %collective-permute-done.17.refs_1_), channel_id=1, source_target_pairs={{0,32},{32,64},{64,96},{96,128},{128,160},{160,192},{192,224},{224... | collective-permute-start | bytes 983048 | tf_op jit(solution)/shard_map/ppermute | solution.py:224
  116.2 4.6 %collective-permute-start.25 = (bf16[136,1280]{1,0:T(8,128)(2,1)S(1)}, bf16[136,1280]{1,0:T(8,128)(2,1)S(1)}, u32[]{:S(2)}, u32[]{:S(2)}) collective-permute-start(bf16[136,1280]{1,0:T(8,128)(2,1)S(1)} %collective-permute-done.24.refs_8_), channel_id=1, source_target_pairs={{0,480},{32,0},{64,32},{96,64},{128,96},{160,128},{192,160},{224,1... | collective-permute-start | bytes 1044488 | tf_op jit(solution)/shard_map/ppermute | solution.py:228
  122.7 3.4 %collective-permute-start.22 = (bf16[128,1280]{1,0:T(8,128)(2,1)S(1)}, bf16[128,1280]{1,0:T(8,128)(2,1)S(1)}, u32[]{:S(2)}, u32[]{:S(2)}) collective-permute-start(bf16[128,1280]{1,0:T(8,128)(2,1)S(1)} %collective-permute-done.21.refs_3_), channel_id=1, source_target_pairs={{0,32},{32,64},{64,96},{96,128},{128,160},{160,192},{192,224},{224... | collective-permute-start | bytes 983048 | tf_op jit(solution)/shard_map/ppermute | solution.py:224
  128.9 4.1 %collective-permute-done.27.refs_4_ = bf16[128,1280]{1,0:T(8,128)(2,1)S(1)} collective-permute-done((bf16[128,1280]{1,0:T(8,128)(2,1)S(1)}, bf16[128,1280]{1,0:T(8,128)(2,1)S(1)}, u32[]{:S(2)}, u32[]{:S(2)}) %collective-permute-start.27) | collective-permute-done | bytes 327712 | tf_op jit(solution)/shard_map/ppermute | solution.py:226
  133.0 2.2 %select_near_last.1.refs_3_ = bf16[16,56,2560]{2,1,0:T(8,128)(2,1)} custom-call(s32[1]{0:T(128)} %bitcast.1.refs_0_, bf16[128,1280]{1,0:T(8,128)(2,1)S(1)} %collective-permute-done.17.refs_1_, bf16[128,1280]{1,0:T(8,128)(2,1)S(1)} %collective-permute-done.26.refs_2_, ...), custom_call_target="tpu_custom_call", output_to_operand_aliasing={{}: (9, {})} | custom-call | flops 146800640 | bytes 3768320 | tf_op jit(solution)/shard_map/select_near_last/pallas_call | solution.py:141
  136.6 2.3 %copy-done = bf16[16,56,2560]{2,1,0:T(8,128)(2,1)S(1)} copy-done((bf16[16,56,2560]{2,1,0:T(8,128)(2,1)S(1)}, bf16[16,56,2560]{2,1,0:T(8,128)(2,1)}, u32[]{:S(2)}) %copy-start) | copy-done | bytes 4587544
  138.9 3.3 %term_other.1 = bf16[384,2560]{1,0:T(8,128)(2,1)S(1)} custom-call(bf16[384,896]{1,0:T(8,128)(2,1)S(1)} %get-tuple-element.40.saved_ref, bf16[896,2560]{1,0:T(8,128)(2,1)S(1)} %bitcast.21), custom_call_target="tpu_custom_call" | custom-call | flops 1761607680 | bytes 7241728 | tf_op jit(solution)/shard_map/term_other/pallas_call | solution.py:169
  142.2 8.6 %collective-permute-start.30 = (bf16[384,2560]{1,0:T(8,128)(2,1)S(1)}, bf16[384,2560]{1,0:T(8,128)(2,1)S(1)}, u32[]{:S(2)}, u32[]{:S(2)}) collective-permute-start(bf16[384,2560]{1,0:T(8,128)(2,1)S(1)} %term_other.1), channel_id=1, source_target_pairs={{0,1},{1,0},{2,3},{3,2},{4,5},{5,4},{6,7},{7,6},{8,9},{9,8},{10,11... | collective-permute-start | bytes 5898248 | tf_op jit(solution)/shard_map/ppermute | solution.py:244
  150.8 3.3 %term_mine.1 = bf16[384,2560]{1,0:T(8,128)(2,1)S(1)} custom-call(bf16[384,896]{1,0:T(8,128)(2,1)S(1)} %get-tuple-element.36.saved_ref, bf16[896,2560]{1,0:T(8,128)(2,1)S(1)} %bitcast.22), custom_call_target="tpu_custom_call" | custom-call | flops 1761607680 | bytes 7241728 | tf_op jit(solution)/shard_map/term_mine/pallas_call | solution.py:169
  156.2 6.8 %all-to-all-start = ((bf16[16,24,2560]{2,1,0:T(8,128)(2,1)}), bf16[16,24,2560]{2,1,0:T(8,128)(2,1)S(1)}, u32[]{:S(2)}, u32[]{:S(2)}) async-start(bf16[16,24,2560]{2,1,0:T(8,128)(2,1)} %bitcast.8), calls=%async_computation | async-start | bytes 3932160 | tf_op jit(solution)/shard_map/all_to_all | solution.py:248
  163.0 8.3 %fusion.5 = bf16[1,896,768]{2,1,0:T(8,128)(2,1)} fusion(bf16[896,2560]{1,0:T(8,128)(2,1)} %bitcast.20, bf16[768,1,2560]{2,0,1:T(8,128)(2,1)} %all-gather.2.cloned.1.call-done), kind=kOutput, calls=%fused_computation.5 | convolution fusion | flops 3523903488 | bytes 9895936 | tf_op jit(solution)/shard_map/dot_general | solution.py:256
  171.3 21.6 %all-to-all-done = bf16[16,24,2560]{2,1,0:T(8,128)(2,1)S(1)} async-done(((bf16[16,24,2560]{2,1,0:T(8,128)(2,1)}), bf16[16,24,2560]{2,1,0:T(8,128)(2,1)S(1)}, u32[]{:S(2)}, u32[]{:S(2)}) %all-to-all-start) | async-done | bytes 1966112 | tf_op jit(solution)/shard_map/all_to_all | solution.py:248
  (60 shorter events, 38.7 us)
Async XLA Ops:
  7.2 149.0 %all-gather.2.cloned.1.call-start = ((), (), s32[]{:S(2)}) async-start(), calls=%async_computation.1 | async-start | bytes 4055040 | tf_op jit(solution)/shard_map/all_gather | solution.py:201
  10.5 18.7 %collective-permute-start.4 = (bf16[136,1280]{1,0:T(8,128)(2,1)S(1)}, bf16[136,1280]{1,0:T(8,128)(2,1)S(1)}, u32[]{:S(2)}, u32[]{:S(2)}) collective-permute-start(bf16[136,1280]{1,0:T(8,128)(2,1)S(1)} %get-tuple-element.25.refs_4_), channel_id=1, source_target_pairs={{0,480},{32,0},{64,32},{96,64},{128,96},{160,128},{192,160},{224,1... | collective-permute-start | bytes 1044488 | tf_op jit(solution)/shard_map/ppermute | solution.py:228
  22.4 14.0 %collective-permute-start = (bf16[128,1280]{1,0:T(8,128)(2,1)S(1)}, bf16[128,1280]{1,0:T(8,128)(2,1)}, u32[]{:S(2)}, u32[]{:S(2)}) collective-permute-start(bf16[128,1280]{1,0:T(8,128)(2,1)S(1)} %get-tuple-element.24.refs_1_), channel_id=1, source_target_pairs={{0,32},{32,64},{64,96},{96,128},{128,160},{160,192},{192,224},{224... | collective-permute-start | bytes 983048 | tf_op jit(solution)/shard_map/ppermute | solution.py:224
  24.4 16.9 %collective-permute-start.3 = (bf16[136,1280]{1,0:T(8,128)(2,1)S(1)}, bf16[136,1280]{1,0:T(8,128)(2,1)S(1)}, u32[]{:S(2)}, u32[]{:S(2)}) collective-permute-start(bf16[136,1280]{1,0:T(8,128)(2,1)S(1)} %get-tuple-element.25.refs_4_), channel_id=1, source_target_pairs={{0,32},{32,64},{64,96},{96,128},{128,160},{160,192},{192,224},{224... | collective-permute-start | bytes 1044488 | tf_op jit(solution)/shard_map/ppermute | solution.py:227
  29.2 14.0 %collective-permute-start.8 = (bf16[136,1280]{1,0:T(8,128)(2,1)S(1)}, bf16[136,1280]{1,0:T(8,128)(2,1)S(1)}, u32[]{:S(2)}, u32[]{:S(2)}) collective-permute-start(bf16[136,1280]{1,0:T(8,128)(2,1)S(1)} %collective-permute-done.4.refs_6_), channel_id=1, source_target_pairs={{0,480},{32,0},{64,32},{96,64},{128,96},{160,128},{192,160},{224,1... | collective-permute-start | bytes 1044488 | tf_op jit(solution)/shard_map/ppermute | solution.py:228
  34.6 13.2 %collective-permute-start.2 = (bf16[128,1280]{1,0:T(8,128)(2,1)S(1)}, bf16[128,1280]{1,0:T(8,128)(2,1)S(1)}, u32[]{:S(2)}, u32[]{:S(2)}) collective-permute-start(bf16[128,1280]{1,0:T(8,128)(2,1)S(1)} %get-tuple-element.24.refs_1_), channel_id=1, source_target_pairs={{0,480},{32,0},{64,32},{96,64},{128,96},{160,128},{192,160},{224,1... | collective-permute-start | bytes 983048 | tf_op jit(solution)/shard_map/ppermute | solution.py:226
  36.5 19.2 %collective-permute-start.1 = (bf16[128,1280]{1,0:T(8,128)(2,1)}, bf16[128,1280]{1,0:T(8,128)(2,1)S(1)}, u32[]{:S(2)}, u32[]{:S(2)}) collective-permute-start(bf16[128,1280]{1,0:T(8,128)(2,1)} %collective-permute-done.refs_2_), channel_id=1, source_target_pairs={{0,32},{32,64},{64,96},{96,128},{128,160},{160,192},{192,224},{224... | collective-permute-start | bytes 983048 | tf_op jit(solution)/shard_map/ppermute | solution.py:224
  41.3 16.3 %collective-permute-start.7 = (bf16[136,1280]{1,0:T(8,128)(2,1)S(1)}, bf16[136,1280]{1,0:T(8,128)(2,1)S(1)}, u32[]{:S(2)}, u32[]{:S(2)}) collective-permute-start(bf16[136,1280]{1,0:T(8,128)(2,1)S(1)} %collective-permute-done.3.refs_5_), channel_id=1, source_target_pairs={{0,32},{32,64},{64,96},{96,128},{128,160},{160,192},{192,224},{224... | collective-permute-start | bytes 1044488 | tf_op jit(solution)/shard_map/ppermute | solution.py:227
  43.2 16.4 %collective-permute-start.12 = (bf16[136,1280]{1,0:T(8,128)(2,1)S(1)}, bf16[136,1280]{1,0:T(8,128)(2,1)S(1)}, u32[]{:S(2)}, u32[]{:S(2)}) collective-permute-start(bf16[136,1280]{1,0:T(8,128)(2,1)S(1)} %collective-permute-done.8.refs_4_), channel_id=1, source_target_pairs={{0,480},{32,0},{64,32},{96,64},{128,96},{160,128},{192,160},{224,1... | collective-permute-start | bytes 1044488 | tf_op jit(solution)/shard_map/ppermute | solution.py:228
  47.8 16.4 %collective-permute-start.6 = (bf16[128,1280]{1,0:T(8,128)(2,1)S(1)}, bf16[128,1280]{1,0:T(8,128)(2,1)S(1)}, u32[]{:S(2)}, u32[]{:S(2)}) collective-permute-start(bf16[128,1280]{1,0:T(8,128)(2,1)S(1)} %collective-permute-done.2.refs_3_), channel_id=1, source_target_pairs={{0,480},{32,0},{64,32},{96,64},{128,96},{160,128},{192,160},{224,1... | collective-permute-start | bytes 983048 | tf_op jit(solution)/shard_map/ppermute | solution.py:226
  55.7 13.1 %collective-permute-start.5 = (bf16[128,1280]{1,0:T(8,128)(2,1)S(1)}, bf16[128,1280]{1,0:T(8,128)(2,1)S(1)}, u32[]{:S(2)}, u32[]{:S(2)}) collective-permute-start(bf16[128,1280]{1,0:T(8,128)(2,1)S(1)} %collective-permute-done.1.refs_1_), channel_id=1, source_target_pairs={{0,32},{32,64},{64,96},{96,128},{128,160},{160,192},{192,224},{224... | collective-permute-start | bytes 983048 | tf_op jit(solution)/shard_map/ppermute | solution.py:224
  57.6 13.9 %collective-permute-start.11 = (bf16[136,1280]{1,0:T(8,128)(2,1)S(1)}, bf16[136,1280]{1,0:T(8,128)(2,1)S(1)}, u32[]{:S(2)}, u32[]{:S(2)}) collective-permute-start(bf16[136,1280]{1,0:T(8,128)(2,1)S(1)} %collective-permute-done.7.refs_3_), channel_id=1, source_target_pairs={{0,32},{32,64},{64,96},{96,128},{128,160},{160,192},{192,224},{224... | collective-permute-start | bytes 1044488 | tf_op jit(solution)/shard_map/ppermute | solution.py:227
  59.6 13.9 %collective-permute-start.16 = (bf16[136,1280]{1,0:T(8,128)(2,1)S(1)}, bf16[136,1280]{1,0:T(8,128)(2,1)S(1)}, u32[]{:S(2)}, u32[]{:S(2)}) collective-permute-start(bf16[136,1280]{1,0:T(8,128)(2,1)S(1)} %collective-permute-done.12.refs_4_), channel_id=1, source_target_pairs={{0,480},{32,0},{64,32},{96,64},{128,96},{160,128},{192,160},{224,1... | collective-permute-start | bytes 1044488 | tf_op jit(solution)/shard_map/ppermute | solution.py:228
  64.2 13.9 %collective-permute-start.10 = (bf16[128,1280]{1,0:T(8,128)(2,1)S(1)}, bf16[128,1280]{1,0:T(8,128)(2,1)S(1)}, u32[]{:S(2)}, u32[]{:S(2)}) collective-permute-start(bf16[128,1280]{1,0:T(8,128)(2,1)S(1)} %collective-permute-done.6.refs_2_), channel_id=1, source_target_pairs={{0,480},{32,0},{64,32},{96,64},{128,96},{160,128},{192,160},{224,1... | collective-permute-start | bytes 983048 | tf_op jit(solution)/shard_map/ppermute | solution.py:226
  68.8 13.1 %collective-permute-start.9 = (bf16[128,1280]{1,0:T(8,128)(2,1)S(1)}, bf16[128,1280]{1,0:T(8,128)(2,1)S(1)}, u32[]{:S(2)}, u32[]{:S(2)}) collective-permute-start(bf16[128,1280]{1,0:T(8,128)(2,1)S(1)} %collective-permute-done.5.refs_1_), channel_id=1, source_target_pairs={{0,32},{32,64},{64,96},{96,128},{128,160},{160,192},{192,224},{224... | collective-permute-start | bytes 983048 | tf_op jit(solution)/shard_map/ppermute | solution.py:224
  71.5 14.7 %collective-permute-start.15 = (bf16[136,1280]{1,0:T(8,128)(2,1)S(1)}, bf16[136,1280]{1,0:T(8,128)(2,1)S(1)}, u32[]{:S(2)}, u32[]{:S(2)}) collective-permute-start(bf16[136,1280]{1,0:T(8,128)(2,1)S(1)} %collective-permute-done.11.refs_3_), channel_id=1, source_target_pairs={{0,32},{32,64},{64,96},{96,128},{128,160},{160,192},{192,224},{224... | collective-permute-start | bytes 1044488 | tf_op jit(solution)/shard_map/ppermute | solution.py:227
  73.4 14.7 %collective-permute-start.20 = (bf16[136,1280]{1,0:T(8,128)(2,1)S(1)}, bf16[136,1280]{1,0:T(8,128)(2,1)S(1)}, u32[]{:S(2)}, u32[]{:S(2)}) collective-permute-start(bf16[136,1280]{1,0:T(8,128)(2,1)S(1)} %collective-permute-done.16.refs_4_), channel_id=1, source_target_pairs={{0,480},{32,0},{64,32},{96,64},{128,96},{160,128},{192,160},{224,1... | collective-permute-start | bytes 1044488 | tf_op jit(solution)/shard_map/ppermute | solution.py:228
  78.0 14.7 %collective-permute-start.14 = (bf16[128,1280]{1,0:T(8,128)(2,1)S(1)}, bf16[128,1280]{1,0:T(8,128)(2,1)S(1)}, u32[]{:S(2)}, u32[]{:S(2)}) collective-permute-start(bf16[128,1280]{1,0:T(8,128)(2,1)S(1)} %collective-permute-done.10.refs_2_), channel_id=1, source_target_pairs={{0,480},{32,0},{64,32},{96,64},{128,96},{160,128},{192,160},{224,1... | collective-permute-start | bytes 983048 | tf_op jit(solution)/shard_map/ppermute | solution.py:226
  81.9 14.0 %collective-permute-start.13 = (bf16[128,1280]{1,0:T(8,128)(2,1)S(1)}, bf16[128,1280]{1,0:T(8,128)(2,1)S(1)}, u32[]{:S(2)}, u32[]{:S(2)}) collective-permute-start(bf16[128,1280]{1,0:T(8,128)(2,1)S(1)} %collective-permute-done.9.refs_1_), channel_id=1, source_target_pairs={{0,32},{32,64},{64,96},{96,128},{128,160},{160,192},{192,224},{224... | collective-permute-start | bytes 983048 | tf_op jit(solution)/shard_map/ppermute | solution.py:224
  86.2 14.7 %collective-permute-start.19 = (bf16[136,1280]{1,0:T(8,128)(2,1)S(1)}, bf16[136,1280]{1,0:T(8,128)(2,1)S(1)}, u32[]{:S(2)}, u32[]{:S(2)}) collective-permute-start(bf16[136,1280]{1,0:T(8,128)(2,1)S(1)} %collective-permute-done.15.refs_3_), channel_id=1, source_target_pairs={{0,32},{32,64},{64,96},{96,128},{128,160},{160,192},{192,224},{224... | collective-permute-start | bytes 1044488 | tf_op jit(solution)/shard_map/ppermute | solution.py:227
  88.2 14.7 %collective-permute-start.23 = (bf16[136,1280]{1,0:T(8,128)(2,1)S(1)}, bf16[136,1280]{1,0:T(8,128)(2,1)S(1)}, u32[]{:S(2)}, u32[]{:S(2)}) collective-permute-start(bf16[136,1280]{1,0:T(8,128)(2,1)S(1)} %collective-permute-done.20.refs_4_), channel_id=1, source_target_pairs={{0,480},{32,0},{64,32},{96,64},{128,96},{160,128},{192,160},{224,1... | collective-permute-start | bytes 1044488 | tf_op jit(solution)/shard_map/ppermute | solution.py:228
  92.8 14.7 %collective-permute-start.18 = (bf16[128,1280]{1,0:T(8,128)(2,1)S(1)}, bf16[128,1280]{1,0:T(8,128)(2,1)S(1)}, u32[]{:S(2)}, u32[]{:S(2)}) collective-permute-start(bf16[128,1280]{1,0:T(8,128)(2,1)S(1)} %collective-permute-done.14.refs_2_), channel_id=1, source_target_pairs={{0,480},{32,0},{64,32},{96,64},{128,96},{160,128},{192,160},{224,1... | collective-permute-start | bytes 983048 | tf_op jit(solution)/shard_map/ppermute | solution.py:226
  96.0 14.8 %collective-permute-start.17 = (bf16[128,1280]{1,0:T(8,128)(2,1)S(1)}, bf16[128,1280]{1,0:T(8,128)(2,1)S(1)}, u32[]{:S(2)}, u32[]{:S(2)}) collective-permute-start(bf16[128,1280]{1,0:T(8,128)(2,1)S(1)} %collective-permute-done.13.refs_1_), channel_id=1, source_target_pairs={{0,32},{32,64},{64,96},{96,128},{128,160},{160,192},{192,224},{224... | collective-permute-start | bytes 983048 | tf_op jit(solution)/shard_map/ppermute | solution.py:224
  101.0 13.3 %collective-permute-start.28 = (bf16[136,1280]{1,0:T(8,128)(2,1)S(1)}, bf16[136,1280]{1,0:T(8,128)(2,1)S(1)}, u32[]{:S(2)}, u32[]{:S(2)}) collective-permute-start(bf16[136,1280]{1,0:T(8,128)(2,1)S(1)} %collective-permute-done.19.refs_3_), channel_id=1, source_target_pairs={{0,32},{32,64},{64,96},{96,128},{128,160},{160,192},{192,224},{224... | collective-permute-start | bytes 1044488 | tf_op jit(solution)/shard_map/ppermute | solution.py:227
  102.9 13.3 %collective-permute-start.24 = (bf16[136,1280]{1,0:T(8,128)(2,1)S(1)}, bf16[136,1280]{1,0:T(8,128)(2,1)S(1)}, u32[]{:S(2)}, u32[]{:S(2)}) collective-permute-start(bf16[136,1280]{1,0:T(8,128)(2,1)S(1)} %collective-permute-done.23.refs_6_), channel_id=1, source_target_pairs={{0,480},{32,0},{64,32},{96,64},{128,96},{160,128},{192,160},{224,1... | collective-permute-start | bytes 1044488 | tf_op jit(solution)/shard_map/ppermute | solution.py:228
  107.5 13.3 %collective-permute-start.26 = (bf16[128,1280]{1,0:T(8,128)(2,1)S(1)}, bf16[128,1280]{1,0:T(8,128)(2,1)S(1)}, u32[]{:S(2)}, u32[]{:S(2)}) collective-permute-start(bf16[128,1280]{1,0:T(8,128)(2,1)S(1)} %collective-permute-done.18.refs_2_), channel_id=1, source_target_pairs={{0,480},{32,0},{64,32},{96,64},{128,96},{160,128},{192,160},{224,1... | collective-permute-start | bytes 983048 | tf_op jit(solution)/shard_map/ppermute | solution.py:226
  114.3 18.7 %collective-permute-start.29 = (bf16[136,1280]{1,0:T(8,128)(2,1)S(1)}, bf16[136,1280]{1,0:T(8,128)(2,1)S(1)}, u32[]{:S(2)}, u32[]{:S(2)}) collective-permute-start(bf16[136,1280]{1,0:T(8,128)(2,1)S(1)} %collective-permute-done.28.refs_5_), channel_id=1, source_target_pairs={{0,32},{32,64},{64,96},{96,128},{128,160},{160,192},{192,224},{224... | collective-permute-start | bytes 1044488 | tf_op jit(solution)/shard_map/ppermute | solution.py:227
  116.2 19.4 %collective-permute-start.25 = (bf16[136,1280]{1,0:T(8,128)(2,1)S(1)}, bf16[136,1280]{1,0:T(8,128)(2,1)S(1)}, u32[]{:S(2)}, u32[]{:S(2)}) collective-permute-start(bf16[136,1280]{1,0:T(8,128)(2,1)S(1)} %collective-permute-done.24.refs_8_), channel_id=1, source_target_pairs={{0,480},{32,0},{64,32},{96,64},{128,96},{160,128},{192,160},{224,1... | collective-permute-start | bytes 1044488 | tf_op jit(solution)/shard_map/ppermute | solution.py:228
  120.8 12.2 %collective-permute-start.27 = (bf16[128,1280]{1,0:T(8,128)(2,1)S(1)}, bf16[128,1280]{1,0:T(8,128)(2,1)S(1)}, u32[]{:S(2)}, u32[]{:S(2)}) collective-permute-start(bf16[128,1280]{1,0:T(8,128)(2,1)S(1)} %collective-permute-done.26.refs_2_), channel_id=1, source_target_pairs={{0,480},{32,0},{64,32},{96,64},{128,96},{160,128},{192,160},{224,1... | collective-permute-start | bytes 983048 | tf_op jit(solution)/shard_map/ppermute | solution.py:226
  122.7 12.9 %collective-permute-start.22 = (bf16[128,1280]{1,0:T(8,128)(2,1)S(1)}, bf16[128,1280]{1,0:T(8,128)(2,1)S(1)}, u32[]{:S(2)}, u32[]{:S(2)}) collective-permute-start(bf16[128,1280]{1,0:T(8,128)(2,1)S(1)} %collective-permute-done.21.refs_3_), channel_id=1, source_target_pairs={{0,32},{32,64},{64,96},{96,128},{128,160},{160,192},{192,224},{224... | collective-permute-start | bytes 983048 | tf_op jit(solution)/shard_map/ppermute | solution.py:224
  142.2 12.2 %collective-permute-start.30 = (bf16[384,2560]{1,0:T(8,128)(2,1)S(1)}, bf16[384,2560]{1,0:T(8,128)(2,1)S(1)}, u32[]{:S(2)}, u32[]{:S(2)}) collective-permute-start(bf16[384,2560]{1,0:T(8,128)(2,1)S(1)} %term_other.1), channel_id=1, source_target_pairs={{0,1},{1,0},{2,3},{3,2},{4,5},{5,4},{6,7},{7,6},{8,9},{9,8},{10,11... | collective-permute-start | bytes 5898248 | tf_op jit(solution)/shard_map/ppermute | solution.py:244
  156.2 36.6 %all-to-all-start = ((bf16[16,24,2560]{2,1,0:T(8,128)(2,1)}), bf16[16,24,2560]{2,1,0:T(8,128)(2,1)S(1)}, u32[]{:S(2)}, u32[]{:S(2)}) async-start(bf16[16,24,2560]{2,1,0:T(8,128)(2,1)} %bitcast.8), calls=%async_computation | async-start | bytes 3932160 | tf_op jit(solution)/shard_map/all_to_all | solution.py:248
  (6 other events, 18.1 us)
Sparse Core Ops, SparseCore 0:
  11.1 66.7 all-gather.1

commit v4 on v3

--- a/solution.py
+++ b/solution.py
@@ -76,12 +76,11 @@
 
     return pl.pallas_call(
         kernel,
-        grid_spec=pltpu.PrefetchScalarGridSpec(
-            num_scalar_prefetch=1,
-            grid=(1,),
-            in_specs=[pl.BlockSpec((rows, units), lambda i, m: (0, 0))],
-            out_specs=[pl.BlockSpec((units // 2, rows), lambda i, m: (0, 0))] * 2,
-        ),
+        in_specs=[
+            pl.BlockSpec(memory_space=pltpu.SMEM),
+            pl.BlockSpec(memory_space=pltpu.VMEM),
+        ],
+        out_specs=[pl.BlockSpec(memory_space=pltpu.VMEM)] * 2,
         out_shape=[jax.ShapeDtypeStruct((units // 2, rows), BF)] * 2,
         compiler_params=pltpu.CompilerParams(vmem_limit_bytes=VMEM),
         cost_estimate=pl.CostEstimate(
@@ -91,71 +90,107 @@
     )(core, hidden)
 
 
-def _select_kernel(count, tokens, me_ref, *refs):
-    firsts, seconds, out_ref = refs[:count], refs[count : 2 * count], refs[-1]
-    capacity = out_ref.shape[1]
-    half = firsts[0].shape[1]
-    me = me_ref[0]
-    step = pl.program_id(0)
-    for i in range(count):
-
-        @pl.when(step == i)
-        def _():
-            info = seconds[i][tokens : tokens + INFO_ROWS, 0 : 4 * tokens].astype(F32)
-            info = jnp.where(me >= INFO_ROWS, info[:, 2 * tokens :], info[:, : 2 * tokens])
-            row = lax.broadcasted_iota(jnp.int32, info.shape, 0)
-            mine = jnp.sum(jnp.where(row == lax.rem(me, INFO_ROWS), info, 0.0), axis=0, keepdims=True)
-            slot = lax.broadcasted_iota(jnp.int32, (capacity, tokens), 0).astype(F32)
-            pick = jnp.where(mine[:, :tokens] == slot, mine[:, tokens:], 0.0).astype(BF)
-            out_ref[0, :, :half] = jnp.dot(
-                pick, firsts[i][0:tokens, :], preferred_element_type=F32
+def _picker(expert, second_ref, capacity):
+    tokens = second_ref.shape[0] - INFO_ROWS
+    info = second_ref[tokens : tokens + INFO_ROWS, 0 : 4 * tokens].astype(F32)
+    info = jnp.where(expert >= INFO_ROWS, info[:, 2 * tokens :], info[:, : 2 * tokens])
+    row = lax.broadcasted_iota(jnp.int32, info.shape, 0)
+    mine = jnp.sum(jnp.where(row == lax.rem(expert, INFO_ROWS), info, 0.0), axis=0, keepdims=True)
+    slot = lax.broadcasted_iota(jnp.int32, (capacity, tokens), 0).astype(F32)
+    return jnp.where(mine[:, :tokens] == slot, mine[:, tokens:], 0.0).astype(BF)
+
+
+def _select(me, offsets, firsts, seconds, rows, shape, name):
+    count = len(offsets)
+    groups, capacity, width = shape
+    half = width // 2
+    tokens = firsts[0].shape[0]
+
+    def kernel(me_ref, *refs):
+        out_ref = refs[-1]
+        for i, off in enumerate(offsets):
+            first_ref, second_ref = refs[i], refs[count + i]
+            pick = _picker(me_ref[0], second_ref, capacity)
+            place = lax.rem(me_ref[0] + (off + groups) % groups, groups)
+            out_ref[place, :, :half] = jnp.dot(
+                pick, first_ref[...], preferred_element_type=F32
             ).astype(BF)
-            out_ref[0, :, half:] = jnp.dot(
-                pick, seconds[i][0:tokens, :], preferred_element_type=F32
+            out_ref[place, :, half:] = jnp.dot(
+                pick, second_ref[0:tokens, :], preferred_element_type=F32
             ).astype(BF)
 
-
-def _select(me, offsets, firsts, seconds, rows, shape, name):
-    count = len(firsts)
-    groups = shape[0]
-    steps = [(off + groups) % groups for off in offsets]
-
-    def place(i, m):
-        step = steps[0]
-        for k in range(1, count):
-            step = jnp.where(i == k, steps[k], step)
-        return (lax.rem(m[0] + step, groups), 0, 0)
-
-    tokens = firsts[0].shape[0]
-    whole = [pl.BlockSpec(a.shape, lambda i, m: (0, 0)) for a in firsts + seconds]
-    operands = list(firsts) + list(seconds)
-    aliases = {}
-    if rows is not None:
-        whole.append(pl.BlockSpec(memory_space=pltpu.HBM))
-        operands.append(rows)
-        aliases = {1 + 2 * count: 0}
-
-    def kernel(*refs):
-        _select_kernel(count, tokens, *refs)
-
+    operands = list(firsts) + list(seconds) + ([] if rows is None else [rows])
     return pl.pallas_call(
         kernel,
-        grid_spec=pltpu.PrefetchScalarGridSpec(
-            num_scalar_prefetch=1,
-            grid=(count,),
-            in_specs=whole,
-            out_specs=pl.BlockSpec((1,) + shape[1:], place),
-        ),
-        out_shape=pltpu.HBM(shape, BF),
-        input_output_aliases=aliases,
-        compiler_params=pltpu.CompilerParams(vmem_limit_bytes=VMEM),
-        cost_estimate=pl.CostEstimate(
-            flops=2 * count * shape[1] * tokens * shape[2],
-            bytes_accessed=2 * count * (tokens + shape[1]) * shape[2],
+        in_specs=[pl.BlockSpec(memory_space=pltpu.SMEM)]
+        + [pl.BlockSpec(memory_space=pltpu.VMEM)] * len(operands),
+        out_specs=pl.BlockSpec(memory_space=pltpu.VMEM),
+        out_shape=jax.ShapeDtypeStruct(shape, BF),
+        input_output_aliases={} if rows is None else {len(operands): 0},
+        compiler_params=pltpu.CompilerParams(vmem_limit_bytes=VMEM),
+        cost_estimate=pl.CostEstimate(
+            flops=2 * count * capacity * tokens * width,
+            bytes_accessed=2 * count * (tokens + capacity) * width,
             transcendentals=0,
         ),
         name=name,
     )(me, *operands)
+
+
+def _forward(me, step, block, info_block, rows, name):
+    tokens = info_block.shape[0] - INFO_ROWS
+    groups, capacity, _ = rows.shape
+    width = block.shape[1]
+
+    def kernel(me_ref, block_ref, info_ref, _, out_ref, __):
+        expert = lax.rem(me_ref[0] + (step + groups) % groups, groups)
+        pick = _picker(expert, info_ref, capacity)
+        out_ref[...] = jnp.dot(
+            pick, block_ref[0:tokens, :], preferred_element_type=F32
+        ).astype(BF)
+
+    return pl.pallas_call(
+        kernel,
+        in_specs=[pl.BlockSpec(memory_space=pltpu.SMEM)]
+        + [pl.BlockSpec(memory_space=pltpu.VMEM)] * 3,
+        out_specs=[pl.BlockSpec(memory_space=pltpu.VMEM)] * 2,
+        out_shape=[
+            jax.ShapeDtypeStruct((capacity, width), BF),
+            jax.ShapeDtypeStruct(rows.shape, BF),
+        ],
+        input_output_aliases={3: 1},
+        compiler_params=pltpu.CompilerParams(vmem_limit_bytes=VMEM),
+        cost_estimate=pl.CostEstimate(
+            flops=2 * capacity * tokens * width,
+            bytes_accessed=2 * (tokens + capacity) * width,
+            transcendentals=0,
+        ),
+        name=name,
+    )(me, block, info_block, rows)
+
+
+def _place(me, off, first, second, rows):
+    groups, capacity, width = rows.shape
+    half = width // 2
+
+    def kernel(me_ref, first_ref, second_ref, _, out_ref):
+        place = lax.rem(me_ref[0] + (off + groups) % groups, groups)
+        out_ref[place, :, :half] = first_ref[...]
+        out_ref[place, :, half:] = second_ref[...]
+
+    return pl.pallas_call(
+        kernel,
+        in_specs=[pl.BlockSpec(memory_space=pltpu.SMEM)]
+        + [pl.BlockSpec(memory_space=pltpu.VMEM)] * 3,
+        out_specs=pl.BlockSpec(memory_space=pltpu.VMEM),
+        out_shape=jax.ShapeDtypeStruct(rows.shape, BF),
+        input_output_aliases={3: 0},
+        compiler_params=pltpu.CompilerParams(vmem_limit_bytes=VMEM),
+        cost_estimate=pl.CostEstimate(
+            flops=0, bytes_accessed=4 * capacity * width, transcendentals=0
+        ),
+        name="place_last",
+    )(me, first, second, rows)
 
 
 def _term_kernel(saved_ref, rows_ref, out_ref):
@@ -216,28 +251,31 @@
         seconds = [got_second[off] for off in batch]
         return _select(me, batch, firsts, seconds, rows, shape, name)
 
-    for hop in range(1, far + 1):
-        if 3 <= hop < far:
+    saved_mine, saved_other = _split(hidden[0], core.reshape(1), units_dev)
+    for hop in range(1, far):
+        if hop == 2:
+            b_up, saved_mine, saved_other = lax.optimization_barrier(
+                (b_up, saved_mine, saved_other)
+            )
+        if hop >= 3:
             a_up, rows = lax.optimization_barrier((a_up, rows))
-        if hop == far:
-            me, hidden, a_up = lax.optimization_barrier((me, hidden, a_up))
         a_up = lax.ppermute(a_up, "expert", up)
-        if hop < far:
-            a_down = lax.ppermute(a_down, "expert", down)
-            b_up = lax.ppermute(b_up, "expert", up)
+        a_down = lax.ppermute(a_down, "expert", down)
+        b_up = lax.ppermute(b_up, "expert", up)
         b_down = lax.ppermute(b_down, "expert", down)
         got_first[-hop], got_second[hop] = a_up, b_down
-        if hop < far:
-            got_first[hop], got_second[-hop] = a_down, b_up
+        got_first[hop], got_second[-hop] = a_down, b_up
         if hop == 2:
             rows = pick(rows, [0, -1, 1], "select_1")
-        elif 3 <= hop < far - 1:
+        elif hop >= 3:
             rows = pick(rows, [1 - hop, hop - 1], f"select_{hop - 1}")
-    got_second[-far] = got_second.pop(far)
-
-    rows = pick(rows, [2 - far, far - 2, 1 - far, far - 1], "select_near_last")
-    saved_mine, saved_other = _split(hidden[0], core.reshape(1), units_dev)
-    rows = pick(rows, [-far], "select_last")
+
+    last_first, rows = _forward(me, 1, a_up, b_up, rows, "forward_up")
+    last_first = lax.ppermute(last_first, "expert", up)
+    last_second, rows = _forward(me, -1, b_down, b_down, rows, "forward_down")
+    last_second = lax.ppermute(last_second, "expert", down)
+    rows = pick(rows, [1 - far, far - 1], f"select_{far - 1}")
+    rows = _place(me, far, last_first, last_second, rows)
     rows = rows.reshape(rows_dev, width)
 
     other = _term(saved_other, rows, "term_other")

time: 202 us -> 197 us (0.975)
  Pallas kernels: 19.4 us -> 13.2 us
  starting transfers between devices: 114 us -> 119 us
  waiting for transfers between devices: 35.7 us -> 32.7 us
    ppermute x7, starting transfers between devices: 18.7 us -> 32 us  [body(): a_down = lax.ppermute(a_down, 'expert', down)]
    ppermute x8 -> x7, starting transfers between devices: 21.8 us -> 13.4 us  [body(): a_up = lax.ppermute(a_up, 'expert', up)]
    ppermute x8 -> x7, starting transfers between devices: 44.7 us -> 36.9 us  [body(): b_down = lax.ppermute(b_down, 'expert', down)]
    ppermute x8 -> x7, waiting for transfers between devices: 0.44 us -> 6.86 us  [body(): a_up = lax.ppermute(a_up, 'expert', up)]
    pallas_call x8 -> x11, Pallas kernels: 12.7 us -> 6.46 us  [the longest x7 4.64 us: _select(): pl.pallas_call(kernel, in_specs=[pl.BlockSpec(memory_space=pltpu.SMEM)] +...]
    ppermute x7, waiting for transfers between devices: 5.64 us -> 0.02 us  [body(): b_up = lax.ppermute(b_up, 'expert', up)]
    ppermute x0 -> x2, starting transfers between devices: none -> 5.28 us  [the longest x1 3.36 us: body(): last_first = lax.ppermute(last_first, 'expert', up)]
    ppermute x7, waiting for transfers between devices: 4.13 us -> 0.02 us  [body(): a_down = lax.ppermute(a_down, 'expert', down)]
  transfers between devices with their start and end apart: 33 -> 33, of which waited for: 10 -> 5; matrix products, arithmetic and copies ran while one was open for 5% -> 5% of each run, Pallas kernels for 10% -> 7%
where the time goes in v4:
time: 197 us; the launch traced here: 196 us
  starting transfers between devices  119 us (60%)
  waiting for transfers between devices  32.7 us (17%)
  between operations  14.6 us (7%)
  Pallas kernels  13.2 us (7%)
  matrix products  8.34 us (4%)
  local copies, waits for them, and re-layouts  5.62 us (3%)
  other arithmetic  2.02 us (1%)
    ppermute x7, starting transfers between devices, body(): b_down = lax.ppermute(b_down, 'expert', down)  36.9 us
    ppermute x7, starting transfers between devices, body(): a_down = lax.ppermute(a_down, 'expert', down)  32 us
    all_to_all x1, waiting for transfers between devices, body(): lax.all_to_all(pair.reshape(chips, units_dev, width), 'replica', split_ax...  21.5 us
    ppermute x7, starting transfers between devices, body(): b_up = lax.ppermute(b_up, 'expert', up)  15.9 us
    ppermute x7, starting transfers between devices, body(): a_up = lax.ppermute(a_up, 'expert', up)  13.4 us
    ppermute x1, starting transfers between devices, body(): lax.ppermute(other, 'replica', [(i, i ^ 1) for i in range(replicas)])  8.57 us
    dot_general x1, matrix products, body(): lax.dot_general(rows, weights[:, 0, :], (((1,), (1,)), ((), ())), preferr...  8.34 us
    ppermute x7, waiting for transfers between devices, body(): a_up = lax.ppermute(a_up, 'expert', up)  6.86 us
  transfers between devices with their start and end apart: 33, of which 5 were waited for; matrix products, arithmetic and copies ran while one was open for 5% of the time, Pallas kernels for 7%

profile of v4, /device:TPU:1, one launch (start us, length us, event | category | flops | bytes accessed | tf_op | source)
XLA Modules:
  0.0 195.5 jit_solution(2299558423008011327)
XLA Ops:
  10.5 4.4 %collective-permute-start = (bf16[136,1280]{1,0:T(8,128)(2,1)S(1)}, bf16[136,1280]{1,0:T(8,128)(2,1)S(1)}, u32[]{:S(2)}, u32[]{:S(2)}) collective-permute-start(bf16[136,1280]{1,0:T(8,128)(2,1)S(1)} %get-tuple-element.28.refs_3_), channel_id=1, source_target_pairs={{0,32},{32,64},{64,96},{96,128},{128,160},{160,192},{192,224},{224... | collective-permute-start | bytes 1044488 | tf_op jit(solution)/shard_map/ppermute | solution.py:264
  14.9 9.5 %collective-permute-start.4 = (bf16[136,1280]{1,0:T(8,128)(2,1)S(1)}, bf16[136,1280]{1,0:T(8,128)(2,1)S(1)}, u32[]{:S(2)}, u32[]{:S(2)}) collective-permute-start(bf16[136,1280]{1,0:T(8,128)(2,1)S(1)} %get-tuple-element.28.refs_3_), channel_id=1, source_target_pairs={{0,480},{32,0},{64,32},{96,64},{128,96},{160,128},{192,160},{224,1... | collective-permute-start | bytes 1044488 | tf_op jit(solution)/shard_map/ppermute | solution.py:265
  24.4 1.9 collective-permute-start.1
  26.3 4.6 %collective-permute-start.3 = (bf16[128,1280]{1,0:T(8,128)(2,1)S(1)}, bf16[128,1280]{1,0:T(8,128)(2,1)}, u32[]{:S(2)}, u32[]{:S(2)}) collective-permute-start(bf16[128,1280]{1,0:T(8,128)(2,1)S(1)} %get-tuple-element.32.refs_0_), channel_id=1, source_target_pairs={{0,480},{32,0},{64,32},{96,64},{128,96},{160,128},{192,160},{224,1... | collective-permute-start | bytes 983048 | tf_op jit(solution)/shard_map/ppermute | solution.py:263
  33.7 1.9 collective-permute-start.7
  35.6 4.6 %collective-permute-start.8 = (bf16[136,1280]{1,0:T(8,128)(2,1)S(1)}, bf16[136,1280]{1,0:T(8,128)(2,1)}, u32[]{:S(2)}, u32[]{:S(2)}) collective-permute-start(bf16[136,1280]{1,0:T(8,128)(2,1)S(1)} %collective-permute-done.4.refs_5_), channel_id=1, source_target_pairs={{0,480},{32,0},{64,32},{96,64},{128,96},{160,128},{192,160},{224,1... | collective-permute-start | bytes 1044488 | tf_op jit(solution)/shard_map/ppermute | solution.py:265
  40.2 1.9 collective-permute-start.2
  42.1 4.6 %collective-permute-start.6 = (bf16[128,1280]{1,0:T(8,128)(2,1)}, bf16[128,1280]{1,0:T(8,128)(2,1)}, u32[]{:S(2)}, u32[]{:S(2)}) collective-permute-start(bf16[128,1280]{1,0:T(8,128)(2,1)} %collective-permute-done.3.refs_2_), channel_id=1, source_target_pairs={{0,480},{32,0},{64,32},{96,64},{128,96},{160,128},{192,160},{224,1... | collective-permute-start | bytes 983048 | tf_op jit(solution)/shard_map/ppermute | solution.py:263
  46.7 1.9 collective-permute-start.11
  48.7 4.6 %collective-permute-start.12 = (bf16[136,1280]{1,0:T(8,128)(2,1)}, bf16[136,1280]{1,0:T(8,128)(2,1)S(1)}, u32[]{:S(2)}, u32[]{:S(2)}) collective-permute-start(bf16[136,1280]{1,0:T(8,128)(2,1)} %collective-permute-done.8.refs_3_), channel_id=1, source_target_pairs={{0,480},{32,0},{64,32},{96,64},{128,96},{160,128},{192,160},{224,1... | collective-permute-start | bytes 1044488 | tf_op jit(solution)/shard_map/ppermute | solution.py:265
  57.7 4.6 %collective-permute-start.10 = (bf16[128,1280]{1,0:T(8,128)(2,1)}, bf16[128,1280]{1,0:T(8,128)(2,1)S(1)}, u32[]{:S(2)}, u32[]{:S(2)}) collective-permute-start(bf16[128,1280]{1,0:T(8,128)(2,1)} %collective-permute-done.6.refs_1_), channel_id=1, source_target_pairs={{0,480},{32,0},{64,32},{96,64},{128,96},{160,128},{192,160},{224,1... | collective-permute-start | bytes 983048 | tf_op jit(solution)/shard_map/ppermute | solution.py:263
  64.2 4.6 %collective-permute-start.16 = (bf16[136,1280]{1,0:T(8,128)(2,1)S(1)}, bf16[136,1280]{1,0:T(8,128)(2,1)S(1)}, u32[]{:S(2)}, u32[]{:S(2)}) collective-permute-start(bf16[136,1280]{1,0:T(8,128)(2,1)S(1)} %collective-permute-done.12.refs_3_), channel_id=1, source_target_pairs={{0,480},{32,0},{64,32},{96,64},{128,96},{160,128},{192,160},{224,1... | collective-permute-start | bytes 1044488 | tf_op jit(solution)/shard_map/ppermute | solution.py:265
  70.3 1.9 collective-permute-start.9
  72.3 4.6 %collective-permute-start.14 = (bf16[128,1280]{1,0:T(8,128)(2,1)S(1)}, bf16[128,1280]{1,0:T(8,128)(2,1)S(1)}, u32[]{:S(2)}, u32[]{:S(2)}) collective-permute-start(bf16[128,1280]{1,0:T(8,128)(2,1)S(1)} %collective-permute-done.10.refs_1_), channel_id=1, source_target_pairs={{0,480},{32,0},{64,32},{96,64},{128,96},{160,128},{192,160},{224,1... | collective-permute-start | bytes 983048 | tf_op jit(solution)/shard_map/ppermute | solution.py:263
  76.9 1.9 collective-permute-start.19
  78.8 4.6 %collective-permute-start.20 = (bf16[136,1280]{1,0:T(8,128)(2,1)S(1)}, bf16[136,1280]{1,0:T(8,128)(2,1)S(1)}, u32[]{:S(2)}, u32[]{:S(2)}) collective-permute-start(bf16[136,1280]{1,0:T(8,128)(2,1)S(1)} %collective-permute-done.16.refs_3_), channel_id=1, source_target_pairs={{0,480},{32,0},{64,32},{96,64},{128,96},{160,128},{192,160},{224,1... | collective-permute-start | bytes 1044488 | tf_op jit(solution)/shard_map/ppermute | solution.py:265
  85.7 4.6 %collective-permute-start.18 = (bf16[128,1280]{1,0:T(8,128)(2,1)S(1)}, bf16[128,1280]{1,0:T(8,128)(2,1)S(1)}, u32[]{:S(2)}, u32[]{:S(2)}) collective-permute-start(bf16[128,1280]{1,0:T(8,128)(2,1)S(1)} %collective-permute-done.14.refs_1_), channel_id=1, source_target_pairs={{0,480},{32,0},{64,32},{96,64},{128,96},{160,128},{192,160},{224,1... | collective-permute-start | bytes 983048 | tf_op jit(solution)/shard_map/ppermute | solution.py:263
  92.2 4.6 %collective-permute-start.25 = (bf16[136,1280]{1,0:T(8,128)(2,1)S(1)}, bf16[136,1280]{1,0:T(8,128)(2,1)S(1)}, u32[]{:S(2)}, u32[]{:S(2)}) collective-permute-start(bf16[136,1280]{1,0:T(8,128)(2,1)S(1)} %collective-permute-done.20.refs_3_), channel_id=1, source_target_pairs={{0,480},{32,0},{64,32},{96,64},{128,96},{160,128},{192,160},{224,1... | collective-permute-start | bytes 1044488 | tf_op jit(solution)/shard_map/ppermute | solution.py:265
  99.1 4.6 %collective-permute-start.24 = (bf16[128,1280]{1,0:T(8,128)(2,1)S(1)}, bf16[128,1280]{1,0:T(8,128)(2,1)S(1)}, u32[]{:S(2)}, u32[]{:S(2)}) collective-permute-start(bf16[128,1280]{1,0:T(8,128)(2,1)S(1)} %collective-permute-done.18.refs_1_), channel_id=1, source_target_pairs={{0,480},{32,0},{64,32},{96,64},{128,96},{160,128},{192,160},{224,1... | collective-permute-start | bytes 983048 | tf_op jit(solution)/shard_map/ppermute | solution.py:263
  105.6 4.6 %collective-permute-start.27 = (bf16[136,1280]{1,0:T(8,128)(2,1)S(1)}, bf16[136,1280]{1,0:T(8,128)(2,1)S(1)}, u32[]{:S(2)}, u32[]{:S(2)}) collective-permute-start(bf16[136,1280]{1,0:T(8,128)(2,1)S(1)} %collective-permute-done.25.refs_3_), channel_id=1, source_target_pairs={{0,480},{32,0},{64,32},{96,64},{128,96},{160,128},{192,160},{224,1... | collective-permute-start | bytes 1044488 | tf_op jit(solution)/shard_map/ppermute | solution.py:265
  110.5 1.9 collective-permute-start.21
  112.5 4.6 %collective-permute-start.29 = (bf16[128,1280]{1,0:T(8,128)(2,1)S(1)}, bf16[128,1280]{1,0:T(8,128)(2,1)S(1)}, u32[]{:S(2)}, u32[]{:S(2)}) collective-permute-start(bf16[128,1280]{1,0:T(8,128)(2,1)S(1)} %collective-permute-done.24.refs_1_), channel_id=1, source_target_pairs={{0,480},{32,0},{64,32},{96,64},{128,96},{160,128},{192,160},{224,1... | collective-permute-start | bytes 983048 | tf_op jit(solution)/shard_map/ppermute | solution.py:263
  117.4 6.8 %collective-permute-done.21.block_ref.refs_0_ = bf16[128,1280]{1,0:T(8,128)(2,1)S(1)} collective-permute-done((bf16[128,1280]{1,0:T(8,128)(2,1)S(1)}, bf16[128,1280]{1,0:T(8,128)(2,1)S(1)}, u32[]{:S(2)}, u32[]{:S(2)}) %collective-permute-start.21) | collective-permute-done | bytes 327712 | tf_op jit(solution)/shard_map/ppermute | solution.py:262
  124.6 1.9 collective-permute-start.28
  126.5 3.4 %collective-permute-start.26 = (bf16[56,1280]{1,0:T(8,128)(2,1)S(1)}, bf16[56,1280]{1,0:T(8,128)(2,1)S(1)}, u32[]{:S(2)}, u32[]{:S(2)}) collective-permute-start(bf16[56,1280]{1,0:T(8,128)(2,1)S(1)} %get-tuple-element.44), channel_id=1, source_target_pairs={{0,32},{32,64},{64,96},{96,128},{128,160},{160,192},{192,224},{224... | collective-permute-start | bytes 430088 | tf_op jit(solution)/shard_map/ppermute | solution.py:274
  130.5 3.1 %collective-permute-done.26.first_ref = bf16[56,1280]{1,0:T(8,128)(2,1)S(1)} collective-permute-done((bf16[56,1280]{1,0:T(8,128)(2,1)S(1)}, bf16[56,1280]{1,0:T(8,128)(2,1)S(1)}, u32[]{:S(2)}, u32[]{:S(2)}) %collective-permute-start.26) | collective-permute-done | bytes 143392 | tf_op jit(solution)/shard_map/ppermute | solution.py:274
  133.6 3.3 %term_other.1 = bf16[384,2560]{1,0:T(8,128)(2,1)S(1)} custom-call(bf16[384,896]{1,0:T(8,128)(2,1)S(1)} %get-tuple-element.48.saved_ref, bf16[896,2560]{1,0:T(8,128)(2,1)S(1)} %bitcast.20), custom_call_target="tpu_custom_call" | custom-call | flops 1761607680 | bytes 7241728 | tf_op jit(solution)/shard_map/term_other/pallas_call | solution.py:204
  136.9 8.6 %collective-permute-start.30 = (bf16[384,2560]{1,0:T(8,128)(2,1)S(1)}, bf16[384,2560]{1,0:T(8,128)(2,1)S(1)}, u32[]{:S(2)}, u32[]{:S(2)}) collective-permute-start(bf16[384,2560]{1,0:T(8,128)(2,1)S(1)} %term_other.1), channel_id=1, source_target_pairs={{0,1},{1,0},{2,3},{3,2},{4,5},{5,4},{6,7},{7,6},{8,9},{9,8},{10,11... | collective-permute-start | bytes 5898248 | tf_op jit(solution)/shard_map/ppermute | solution.py:282
  145.5 3.3 %term_mine.1 = bf16[384,2560]{1,0:T(8,128)(2,1)S(1)} custom-call(bf16[384,896]{1,0:T(8,128)(2,1)S(1)} %get-tuple-element.31.saved_ref, bf16[896,2560]{1,0:T(8,128)(2,1)S(1)} %bitcast.21), custom_call_target="tpu_custom_call" | custom-call | flops 1761607680 | bytes 7241728 | tf_op jit(solution)/shard_map/term_mine/pallas_call | solution.py:204
  150.9 6.8 %all-to-all-start = ((bf16[16,24,2560]{2,1,0:T(8,128)(2,1)}), bf16[16,24,2560]{2,1,0:T(8,128)(2,1)S(1)}, u32[]{:S(2)}, u32[]{:S(2)}) async-start(bf16[16,24,2560]{2,1,0:T(8,128)(2,1)} %bitcast.8), calls=%async_computation | async-start | bytes 3932160 | tf_op jit(solution)/shard_map/all_to_all | solution.py:286
  157.7 8.3 %fusion.5 = bf16[1,896,768]{2,1,0:T(8,128)(2,1)} fusion(bf16[896,2560]{1,0:T(8,128)(2,1)} %bitcast.22, bf16[768,1,2560]{2,0,1:T(8,128)(2,1)} %all-gather.2.cloned.1.call-done), kind=kOutput, calls=%fused_computation.5 | convolution fusion | flops 3523903488 | bytes 9895936 | tf_op jit(solution)/shard_map/dot_general | solution.py:294
  166.0 21.5 %all-to-all-done = bf16[16,24,2560]{2,1,0:T(8,128)(2,1)S(1)} async-done(((bf16[16,24,2560]{2,1,0:T(8,128)(2,1)}), bf16[16,24,2560]{2,1,0:T(8,128)(2,1)S(1)}, u32[]{:S(2)}, u32[]{:S(2)}) %all-to-all-start) | async-done | bytes 1966112 | tf_op jit(solution)/shard_map/all_to_all | solution.py:286
  (67 shorter events, 27.0 us)
Async XLA Ops:
  7.2 143.7 %all-gather.2.cloned.1.call-start = ((), (), s32[]{:S(2)}) async-start(), calls=%async_computation.1 | async-start | bytes 4055040 | tf_op jit(solution)/shard_map/all_gather | solution.py:236
  10.5 23.2 %collective-permute-start = (bf16[136,1280]{1,0:T(8,128)(2,1)S(1)}, bf16[136,1280]{1,0:T(8,128)(2,1)S(1)}, u32[]{:S(2)}, u32[]{:S(2)}) collective-permute-start(bf16[136,1280]{1,0:T(8,128)(2,1)S(1)} %get-tuple-element.28.refs_3_), channel_id=1, source_target_pairs={{0,32},{32,64},{64,96},{96,128},{128,160},{160,192},{192,224},{224... | collective-permute-start | bytes 1044488 | tf_op jit(solution)/shard_map/ppermute | solution.py:264
  14.9 20.7 %collective-permute-start.4 = (bf16[136,1280]{1,0:T(8,128)(2,1)S(1)}, bf16[136,1280]{1,0:T(8,128)(2,1)S(1)}, u32[]{:S(2)}, u32[]{:S(2)}) collective-permute-start(bf16[136,1280]{1,0:T(8,128)(2,1)S(1)} %get-tuple-element.28.refs_3_), channel_id=1, source_target_pairs={{0,480},{32,0},{64,32},{96,64},{128,96},{160,128},{192,160},{224,1... | collective-permute-start | bytes 1044488 | tf_op jit(solution)/shard_map/ppermute | solution.py:265
  24.4 15.8 %collective-permute-start.1 = (bf16[128,1280]{1,0:T(8,128)(2,1)S(1)}, bf16[128,1280]{1,0:T(8,128)(2,1)}, u32[]{:S(2)}, u32[]{:S(2)}) collective-permute-start(bf16[128,1280]{1,0:T(8,128)(2,1)S(1)} %get-tuple-element.32.refs_0_), channel_id=1, source_target_pairs={{0,32},{32,64},{64,96},{96,128},{128,160},{160,192},{192,224},{224... | collective-permute-start | bytes 983048 | tf_op jit(solution)/shard_map/ppermute | solution.py:262
  26.3 15.8 %collective-permute-start.3 = (bf16[128,1280]{1,0:T(8,128)(2,1)S(1)}, bf16[128,1280]{1,0:T(8,128)(2,1)}, u32[]{:S(2)}, u32[]{:S(2)}) collective-permute-start(bf16[128,1280]{1,0:T(8,128)(2,1)S(1)} %get-tuple-element.32.refs_0_), channel_id=1, source_target_pairs={{0,480},{32,0},{64,32},{96,64},{128,96},{160,128},{192,160},{224,1... | collective-permute-start | bytes 983048 | tf_op jit(solution)/shard_map/ppermute | solution.py:263
  33.7 13.1 %collective-permute-start.7 = (bf16[136,1280]{1,0:T(8,128)(2,1)S(1)}, bf16[136,1280]{1,0:T(8,128)(2,1)S(1)}, u32[]{:S(2)}, u32[]{:S(2)}) collective-permute-start(bf16[136,1280]{1,0:T(8,128)(2,1)S(1)} %collective-permute-done.refs_4_), channel_id=1, source_target_pairs={{0,32},{32,64},{64,96},{96,128},{128,160},{160,192},{192,224},{224... | collective-permute-start | bytes 1044488 | tf_op jit(solution)/shard_map/ppermute | solution.py:264
  35.6 13.1 %collective-permute-start.8 = (bf16[136,1280]{1,0:T(8,128)(2,1)S(1)}, bf16[136,1280]{1,0:T(8,128)(2,1)}, u32[]{:S(2)}, u32[]{:S(2)}) collective-permute-start(bf16[136,1280]{1,0:T(8,128)(2,1)S(1)} %collective-permute-done.4.refs_5_), channel_id=1, source_target_pairs={{0,480},{32,0},{64,32},{96,64},{128,96},{160,128},{192,160},{224,1... | collective-permute-start | bytes 1044488 | tf_op jit(solution)/shard_map/ppermute | solution.py:265
  40.2 15.5 %collective-permute-start.2 = (bf16[128,1280]{1,0:T(8,128)(2,1)}, bf16[128,1280]{1,0:T(8,128)(2,1)}, u32[]{:S(2)}, u32[]{:S(2)}) collective-permute-start(bf16[128,1280]{1,0:T(8,128)(2,1)} %collective-permute-done.1.refs_1_), channel_id=1, source_target_pairs={{0,32},{32,64},{64,96},{96,128},{128,160},{160,192},{192,224},{224... | collective-permute-start | bytes 983048 | tf_op jit(solution)/shard_map/ppermute | solution.py:262
  42.1 15.5 %collective-permute-start.6 = (bf16[128,1280]{1,0:T(8,128)(2,1)}, bf16[128,1280]{1,0:T(8,128)(2,1)}, u32[]{:S(2)}, u32[]{:S(2)}) collective-permute-start(bf16[128,1280]{1,0:T(8,128)(2,1)} %collective-permute-done.3.refs_2_), channel_id=1, source_target_pairs={{0,480},{32,0},{64,32},{96,64},{128,96},{160,128},{192,160},{224,1... | collective-permute-start | bytes 983048 | tf_op jit(solution)/shard_map/ppermute | solution.py:263
  46.7 15.5 %collective-permute-start.11 = (bf16[136,1280]{1,0:T(8,128)(2,1)S(1)}, bf16[136,1280]{1,0:T(8,128)(2,1)S(1)}, u32[]{:S(2)}, u32[]{:S(2)}) collective-permute-start(bf16[136,1280]{1,0:T(8,128)(2,1)S(1)} %collective-permute-done.7.refs_2_), channel_id=1, source_target_pairs={{0,32},{32,64},{64,96},{96,128},{128,160},{160,192},{192,224},{224... | collective-permute-start | bytes 1044488 | tf_op jit(solution)/shard_map/ppermute | solution.py:264
  48.7 15.5 %collective-permute-start.12 = (bf16[136,1280]{1,0:T(8,128)(2,1)}, bf16[136,1280]{1,0:T(8,128)(2,1)S(1)}, u32[]{:S(2)}, u32[]{:S(2)}) collective-permute-start(bf16[136,1280]{1,0:T(8,128)(2,1)} %collective-permute-done.8.refs_3_), channel_id=1, source_target_pairs={{0,480},{32,0},{64,32},{96,64},{128,96},{160,128},{192,160},{224,1... | collective-permute-start | bytes 1044488 | tf_op jit(solution)/shard_map/ppermute | solution.py:265
  55.7 14.6 %collective-permute-start.5 = (bf16[128,1280]{1,0:T(8,128)(2,1)}, bf16[128,1280]{1,0:T(8,128)(2,1)S(1)}, u32[]{:S(2)}, u32[]{:S(2)}) collective-permute-start(bf16[128,1280]{1,0:T(8,128)(2,1)} %collective-permute-done.2.refs_0_), channel_id=1, source_target_pairs={{0,32},{32,64},{64,96},{96,128},{128,160},{160,192},{192,224},{224... | collective-permute-start | bytes 983048 | tf_op jit(solution)/shard_map/ppermute | solution.py:262
  57.7 14.6 %collective-permute-start.10 = (bf16[128,1280]{1,0:T(8,128)(2,1)}, bf16[128,1280]{1,0:T(8,128)(2,1)S(1)}, u32[]{:S(2)}, u32[]{:S(2)}) collective-permute-start(bf16[128,1280]{1,0:T(8,128)(2,1)} %collective-permute-done.6.refs_1_), channel_id=1, source_target_pairs={{0,480},{32,0},{64,32},{96,64},{128,96},{160,128},{192,160},{224,1... | collective-permute-start | bytes 983048 | tf_op jit(solution)/shard_map/ppermute | solution.py:263
  62.3 14.6 %collective-permute-start.15 = (bf16[136,1280]{1,0:T(8,128)(2,1)S(1)}, bf16[136,1280]{1,0:T(8,128)(2,1)S(1)}, u32[]{:S(2)}, u32[]{:S(2)}) collective-permute-start(bf16[136,1280]{1,0:T(8,128)(2,1)S(1)} %collective-permute-done.11.refs_2_), channel_id=1, source_target_pairs={{0,32},{32,64},{64,96},{96,128},{128,160},{160,192},{192,224},{224... | collective-permute-start | bytes 1044488 | tf_op jit(solution)/shard_map/ppermute | solution.py:264
  64.2 14.6 %collective-permute-start.16 = (bf16[136,1280]{1,0:T(8,128)(2,1)S(1)}, bf16[136,1280]{1,0:T(8,128)(2,1)S(1)}, u32[]{:S(2)}, u32[]{:S(2)}) collective-permute-start(bf16[136,1280]{1,0:T(8,128)(2,1)S(1)} %collective-permute-done.12.refs_3_), channel_id=1, source_target_pairs={{0,480},{32,0},{64,32},{96,64},{128,96},{160,128},{192,160},{224,1... | collective-permute-start | bytes 1044488 | tf_op jit(solution)/shard_map/ppermute | solution.py:265
  70.3 13.4 %collective-permute-start.9 = (bf16[128,1280]{1,0:T(8,128)(2,1)S(1)}, bf16[128,1280]{1,0:T(8,128)(2,1)S(1)}, u32[]{:S(2)}, u32[]{:S(2)}) collective-permute-start(bf16[128,1280]{1,0:T(8,128)(2,1)S(1)} %collective-permute-done.5.refs_0_), channel_id=1, source_target_pairs={{0,32},{32,64},{64,96},{96,128},{128,160},{160,192},{192,224},{224... | collective-permute-start | bytes 983048 | tf_op jit(solution)/shard_map/ppermute | solution.py:262
  72.3 13.4 %collective-permute-start.14 = (bf16[128,1280]{1,0:T(8,128)(2,1)S(1)}, bf16[128,1280]{1,0:T(8,128)(2,1)S(1)}, u32[]{:S(2)}, u32[]{:S(2)}) collective-permute-start(bf16[128,1280]{1,0:T(8,128)(2,1)S(1)} %collective-permute-done.10.refs_1_), channel_id=1, source_target_pairs={{0,480},{32,0},{64,32},{96,64},{128,96},{160,128},{192,160},{224,1... | collective-permute-start | bytes 983048 | tf_op jit(solution)/shard_map/ppermute | solution.py:263
  76.9 13.4 %collective-permute-start.19 = (bf16[136,1280]{1,0:T(8,128)(2,1)S(1)}, bf16[136,1280]{1,0:T(8,128)(2,1)S(1)}, u32[]{:S(2)}, u32[]{:S(2)}) collective-permute-start(bf16[136,1280]{1,0:T(8,128)(2,1)S(1)} %collective-permute-done.15.refs_2_), channel_id=1, source_target_pairs={{0,32},{32,64},{64,96},{96,128},{128,160},{160,192},{192,224},{224... | collective-permute-start | bytes 1044488 | tf_op jit(solution)/shard_map/ppermute | solution.py:264
  78.8 13.4 %collective-permute-start.20 = (bf16[136,1280]{1,0:T(8,128)(2,1)S(1)}, bf16[136,1280]{1,0:T(8,128)(2,1)S(1)}, u32[]{:S(2)}, u32[]{:S(2)}) collective-permute-start(bf16[136,1280]{1,0:T(8,128)(2,1)S(1)} %collective-permute-done.16.refs_3_), channel_id=1, source_target_pairs={{0,480},{32,0},{64,32},{96,64},{128,96},{160,128},{192,160},{224,1... | collective-permute-start | bytes 1044488 | tf_op jit(solution)/shard_map/ppermute | solution.py:265
  83.7 13.4 %collective-permute-start.13 = (bf16[128,1280]{1,0:T(8,128)(2,1)S(1)}, bf16[128,1280]{1,0:T(8,128)(2,1)S(1)}, u32[]{:S(2)}, u32[]{:S(2)}) collective-permute-start(bf16[128,1280]{1,0:T(8,128)(2,1)S(1)} %collective-permute-done.9.refs_0_), channel_id=1, source_target_pairs={{0,32},{32,64},{64,96},{96,128},{128,160},{160,192},{192,224},{224... | collective-permute-start | bytes 983048 | tf_op jit(solution)/shard_map/ppermute | solution.py:262
  85.7 13.4 %collective-permute-start.18 = (bf16[128,1280]{1,0:T(8,128)(2,1)S(1)}, bf16[128,1280]{1,0:T(8,128)(2,1)S(1)}, u32[]{:S(2)}, u32[]{:S(2)}) collective-permute-start(bf16[128,1280]{1,0:T(8,128)(2,1)S(1)} %collective-permute-done.14.refs_1_), channel_id=1, source_target_pairs={{0,480},{32,0},{64,32},{96,64},{128,96},{160,128},{192,160},{224,1... | collective-permute-start | bytes 983048 | tf_op jit(solution)/shard_map/ppermute | solution.py:263
  90.3 13.4 %collective-permute-start.22 = (bf16[136,1280]{1,0:T(8,128)(2,1)S(1)}, bf16[136,1280]{1,0:T(8,128)(2,1)S(1)}, u32[]{:S(2)}, u32[]{:S(2)}) collective-permute-start(bf16[136,1280]{1,0:T(8,128)(2,1)S(1)} %collective-permute-done.19.refs_2_), channel_id=1, source_target_pairs={{0,32},{32,64},{64,96},{96,128},{128,160},{160,192},{192,224},{224... | collective-permute-start | bytes 1044488 | tf_op jit(solution)/shard_map/ppermute | solution.py:264
  92.2 13.4 %collective-permute-start.25 = (bf16[136,1280]{1,0:T(8,128)(2,1)S(1)}, bf16[136,1280]{1,0:T(8,128)(2,1)S(1)}, u32[]{:S(2)}, u32[]{:S(2)}) collective-permute-start(bf16[136,1280]{1,0:T(8,128)(2,1)S(1)} %collective-permute-done.20.refs_3_), channel_id=1, source_target_pairs={{0,480},{32,0},{64,32},{96,64},{128,96},{160,128},{192,160},{224,1... | collective-permute-start | bytes 1044488 | tf_op jit(solution)/shard_map/ppermute | solution.py:265
  97.1 13.4 %collective-permute-start.17 = (bf16[128,1280]{1,0:T(8,128)(2,1)S(1)}, bf16[128,1280]{1,0:T(8,128)(2,1)S(1)}, u32[]{:S(2)}, u32[]{:S(2)}) collective-permute-start(bf16[128,1280]{1,0:T(8,128)(2,1)S(1)} %collective-permute-done.13.refs_0_), channel_id=1, source_target_pairs={{0,32},{32,64},{64,96},{96,128},{128,160},{160,192},{192,224},{224... | collective-permute-start | bytes 983048 | tf_op jit(solution)/shard_map/ppermute | solution.py:262
  99.1 13.4 %collective-permute-start.24 = (bf16[128,1280]{1,0:T(8,128)(2,1)S(1)}, bf16[128,1280]{1,0:T(8,128)(2,1)S(1)}, u32[]{:S(2)}, u32[]{:S(2)}) collective-permute-start(bf16[128,1280]{1,0:T(8,128)(2,1)S(1)} %collective-permute-done.18.refs_1_), channel_id=1, source_target_pairs={{0,480},{32,0},{64,32},{96,64},{128,96},{160,128},{192,160},{224,1... | collective-permute-start | bytes 983048 | tf_op jit(solution)/shard_map/ppermute | solution.py:263
  103.6 20.6 %collective-permute-start.23 = (bf16[136,1280]{1,0:T(8,128)(2,1)S(1)}, bf16[136,1280]{1,0:T(8,128)(2,1)S(1)}, u32[]{:S(2)}, u32[]{:S(2)}) collective-permute-start(bf16[136,1280]{1,0:T(8,128)(2,1)S(1)} %collective-permute-done.22.refs_2_), channel_id=1, source_target_pairs={{0,32},{32,64},{64,96},{96,128},{128,160},{160,192},{192,224},{224... | collective-permute-start | bytes 1044488 | tf_op jit(solution)/shard_map/ppermute | solution.py:264
  105.6 18.8 %collective-permute-start.27 = (bf16[136,1280]{1,0:T(8,128)(2,1)S(1)}, bf16[136,1280]{1,0:T(8,128)(2,1)S(1)}, u32[]{:S(2)}, u32[]{:S(2)}) collective-permute-start(bf16[136,1280]{1,0:T(8,128)(2,1)S(1)} %collective-permute-done.25.refs_3_), channel_id=1, source_target_pairs={{0,480},{32,0},{64,32},{96,64},{128,96},{160,128},{192,160},{224,1... | collective-permute-start | bytes 1044488 | tf_op jit(solution)/shard_map/ppermute | solution.py:265
  110.5 13.7 %collective-permute-start.21 = (bf16[128,1280]{1,0:T(8,128)(2,1)S(1)}, bf16[128,1280]{1,0:T(8,128)(2,1)S(1)}, u32[]{:S(2)}, u32[]{:S(2)}) collective-permute-start(bf16[128,1280]{1,0:T(8,128)(2,1)S(1)} %collective-permute-done.17.refs_0_), channel_id=1, source_target_pairs={{0,32},{32,64},{64,96},{96,128},{128,160},{160,192},{192,224},{224... | collective-permute-start | bytes 983048 | tf_op jit(solution)/shard_map/ppermute | solution.py:262
  112.5 17.5 %collective-permute-start.29 = (bf16[128,1280]{1,0:T(8,128)(2,1)S(1)}, bf16[128,1280]{1,0:T(8,128)(2,1)S(1)}, u32[]{:S(2)}, u32[]{:S(2)}) collective-permute-start(bf16[128,1280]{1,0:T(8,128)(2,1)S(1)} %collective-permute-done.24.refs_1_), channel_id=1, source_target_pairs={{0,480},{32,0},{64,32},{96,64},{128,96},{160,128},{192,160},{224,1... | collective-permute-start | bytes 983048 | tf_op jit(solution)/shard_map/ppermute | solution.py:263
  126.5 7.1 %collective-permute-start.26 = (bf16[56,1280]{1,0:T(8,128)(2,1)S(1)}, bf16[56,1280]{1,0:T(8,128)(2,1)S(1)}, u32[]{:S(2)}, u32[]{:S(2)}) collective-permute-start(bf16[56,1280]{1,0:T(8,128)(2,1)S(1)} %get-tuple-element.44), channel_id=1, source_target_pairs={{0,32},{32,64},{64,96},{96,128},{128,160},{160,192},{192,224},{224... | collective-permute-start | bytes 430088 | tf_op jit(solution)/shard_map/ppermute | solution.py:274
  136.9 12.2 %collective-permute-start.30 = (bf16[384,2560]{1,0:T(8,128)(2,1)S(1)}, bf16[384,2560]{1,0:T(8,128)(2,1)S(1)}, u32[]{:S(2)}, u32[]{:S(2)}) collective-permute-start(bf16[384,2560]{1,0:T(8,128)(2,1)S(1)} %term_other.1), channel_id=1, source_target_pairs={{0,1},{1,0},{2,3},{3,2},{4,5},{5,4},{6,7},{7,6},{8,9},{9,8},{10,11... | collective-permute-start | bytes 5898248 | tf_op jit(solution)/shard_map/ppermute | solution.py:282
  150.9 36.7 %all-to-all-start = ((bf16[16,24,2560]{2,1,0:T(8,128)(2,1)}), bf16[16,24,2560]{2,1,0:T(8,128)(2,1)S(1)}, u32[]{:S(2)}, u32[]{:S(2)}) async-start(bf16[16,24,2560]{2,1,0:T(8,128)(2,1)} %bitcast.8), calls=%async_computation | async-start | bytes 3932160 | tf_op jit(solution)/shard_map/all_to_all | solution.py:286
  (8 other events, 62.1 us)
Sparse Core Ops, SparseCore 0:
  11.1 66.7 all-gather.1

commit v5 on v4

--- a/solution.py
+++ b/solution.py
@@ -100,7 +100,7 @@
     return jnp.where(mine[:, :tokens] == slot, mine[:, tokens:], 0.0).astype(BF)
 
 
-def _select(me, offsets, firsts, seconds, rows, shape, name):
+def _select(me, offsets, firsts, seconds, rows, shape, name, after=()):
     count = len(offsets)
     groups, capacity, width = shape
     half = width // 2
@@ -123,7 +123,8 @@
     return pl.pallas_call(
         kernel,
         in_specs=[pl.BlockSpec(memory_space=pltpu.SMEM)]
-        + [pl.BlockSpec(memory_space=pltpu.VMEM)] * len(operands),
+        + [pl.BlockSpec(memory_space=pltpu.VMEM)] * len(operands)
+        + [pl.BlockSpec(memory_space=pltpu.HBM)] * len(after),
         out_specs=pl.BlockSpec(memory_space=pltpu.VMEM),
         out_shape=jax.ShapeDtypeStruct(shape, BF),
         input_output_aliases={} if rows is None else {len(operands): 0},
@@ -134,7 +135,7 @@
             transcendentals=0,
         ),
         name=name,
-    )(me, *operands)
+    )(me, *operands, *after)
 
 
 def _forward(me, step, block, info_block, rows, name):
@@ -191,6 +192,24 @@
         ),
         name="place_last",
     )(me, first, second, rows)
+
+
+def _copies(array, copies):
+    def kernel(array_ref, out_ref):
+        for i in range(copies):
+            out_ref[i] = array_ref[...]
+
+    return pl.pallas_call(
+        kernel,
+        in_specs=[pl.BlockSpec(memory_space=pltpu.VMEM)],
+        out_specs=pl.BlockSpec(memory_space=pltpu.VMEM),
+        out_shape=jax.ShapeDtypeStruct((copies,) + array.shape, BF),
+        compiler_params=pltpu.CompilerParams(vmem_limit_bytes=VMEM),
+        cost_estimate=pl.CostEstimate(
+            flops=0, bytes_accessed=2 * (copies + 1) * array.size, transcendentals=0
+        ),
+        name="unit_copies",
+    )(array)
 
 
 def _term_kernel(saved_ref, rows_ref, out_ref):
@@ -233,7 +252,17 @@
     me = lax.axis_index("expert").astype(jnp.int32).reshape(1)
     core = lax.rem(lax.axis_index("replica"), 2)
 
-    weights = lax.all_gather(down_weight, "replica", axis=0, tiled=True)
+    chip_groups = [[2 * q + c for q in range(chips)] for c in range(2)]
+
+    def over_chips(array):
+        return lax.all_to_all(
+            array, "replica", split_axis=0, concat_axis=0, tiled=True, axis_index_groups=chip_groups
+        )
+
+    def other_core(array):
+        return lax.ppermute(array, "replica", [(i, i ^ 1) for i in range(replicas)])
+
+    weights_mine = over_chips(_copies(down_weight[:, 0, :], chips))
 
     own_first, own_second = _pack(grads[0], routes.transpose(2, 0, 1), gates[0].T)
 
@@ -246,10 +275,10 @@
     rows = None
     shape = (groups, capacity, width)
 
-    def pick(rows, batch, name):
+    def pick(rows, batch, name, after=()):
         firsts = [got_first[off] for off in batch]
         seconds = [got_second[off] for off in batch]
-        return _select(me, batch, firsts, seconds, rows, shape, name)
+        return _select(me, batch, firsts, seconds, rows, shape, name, after)
 
     saved_mine, saved_other = _split(hidden[0], core.reshape(1), units_dev)
     for hop in range(1, far):
@@ -266,7 +295,7 @@
         got_first[-hop], got_second[hop] = a_up, b_down
         got_first[hop], got_second[-hop] = a_down, b_up
         if hop == 2:
-            rows = pick(rows, [0, -1, 1], "select_1")
+            rows = pick(rows, [0, -1, 1], "select_1", (weights_mine,))
         elif hop >= 3:
             rows = pick(rows, [1 - hop, hop - 1], f"select_{hop - 1}")
 
@@ -279,24 +308,22 @@
     rows = rows.reshape(rows_dev, width)
 
     other = _term(saved_other, rows, "term_other")
-    arrived = lax.ppermute(other, "replica", [(i, i ^ 1) for i in range(replicas)])
+    arrived = other_core(other)
     mine = _term(saved_mine, rows, "term_mine")
     pair = (mine.astype(F32) + arrived.astype(F32)).astype(BF)
-    pair, rows, weights = lax.optimization_barrier((pair, rows, weights))
-    parts = lax.all_to_all(
-        pair.reshape(chips, units_dev, width),
-        "replica",
-        split_axis=0,
-        concat_axis=0,
-        tiled=True,
-        axis_index_groups=[[2 * q + c for q in range(chips)] for c in range(2)],
-    )
-    d_rows = lax.dot_general(
-        rows, weights[:, 0, :], (((1,), (1,)), ((), ())), preferred_element_type=F32
-    )
+    pair, rows, weights_mine = lax.optimization_barrier((pair, rows, weights_mine))
+    sums = over_chips(pair.reshape(chips, units_dev, width))
+
+    weights_other = other_core(weights_mine)
+    both = jnp.where(
+        core == 0,
+        jnp.stack([weights_mine, weights_other], axis=1),
+        jnp.stack([weights_other, weights_mine], axis=1),
+    ).reshape(units, width)
+    d_rows = lax.dot_general(rows, both, (((1,), (1,)), ((), ())), preferred_element_type=F32)
     d_hidden = d_rows.astype(BF)[None]
-    parts, d_hidden = lax.optimization_barrier((parts, d_hidden))
-    down_grad = jnp.sum(parts.astype(F32), axis=0)[:, None, :]
+    sums, d_hidden = lax.optimization_barrier((sums, d_hidden))
+    down_grad = jnp.sum(sums.astype(F32), axis=0)[:, None, :]
     return (d_hidden, down_grad)
 
 

time: 197 us -> 196 us (level)
  between operations: 14.6 us -> 1.34 us
  starting transfers between devices: 119 us -> 128 us
  other arithmetic: 2.02 us -> 6.22 us
  matrix products: 8.34 us -> 4.79 us
  Pallas kernels: 13.2 us -> 15.7 us
    all_to_all x1 -> x2, starting transfers between devices: 6.8 us -> 14.4 us  [over_chips(): lax.all_to_all(array, 'replica', split_axis=0, concat_axis=0, tiled=True,...]
    dot_general x1, matrix products: 8.34 us -> 4.79 us  [body(): lax.dot_general(rows, both, (((1,), (1,)), ((), ())), preferred_element_t...]
    select_n x0 -> x1, other arithmetic: none -> 2.58 us  [body(): jnp.where(core == 0, jnp.stack([weights_mine, weights_other], axis=1), jn...]
    ppermute x1 -> x2, starting transfers between devices: 8.57 us -> 10.8 us  [other_core(): return lax.ppermute(array, 'replica', [(i, i ^ 1) for i in range(replicas)])]
    all_to_all x1 -> x2, waiting for transfers between devices: 21.5 us -> 22.5 us  [over_chips(): lax.all_to_all(array, 'replica', split_axis=0, concat_axis=0, tiled=True,...]
    unnamed x14 -> x18, local copies, waits for them, and re-layouts: 4.76 us -> 4.32 us
  transfers between devices with their start and end apart: 33 -> 34, of which waited for: 5 -> 6; matrix products, arithmetic and copies ran while one was open for 5% -> 4% of each run, Pallas kernels for 7% -> 6%
where the time goes in v5:
time: 196 us; the launch traced here: 195 us
  starting transfers between devices  128 us (65%)
  waiting for transfers between devices  33.4 us (17%)
  Pallas kernels  15.7 us (8%)
  other arithmetic  6.22 us (3%)
  local copies, waits for them, and re-layouts  5.66 us (3%)
  matrix products  4.79 us (2%)
    ppermute x7, starting transfers between devices, body(): b_down = lax.ppermute(b_down, 'expert', down)  36.9 us
    ppermute x7, starting transfers between devices, body(): a_down = lax.ppermute(a_down, 'expert', down)  32 us
    all_to_all x2, waiting for transfers between devices, over_chips(): lax.all_to_all(array, 'replica', split_axis=0, concat_axis=0, tiled=True,...  22.5 us
    ppermute x7, starting transfers between devices, body(): b_up = lax.ppermute(b_up, 'expert', up)  15.1 us
    all_to_all x2, starting transfers between devices, over_chips(): lax.all_to_all(array, 'replica', split_axis=0, concat_axis=0, tiled=True,...  14.4 us
    ppermute x7, starting transfers between devices, body(): a_up = lax.ppermute(a_up, 'expert', up)  13.4 us
    ppermute x2, starting transfers between devices, other_core(): return lax.ppermute(array, 'replica', [(i, i ^ 1) for i in range(replicas)])  10.8 us
    ppermute x7, waiting for transfers between devices, body(): a_up = lax.ppermute(a_up, 'expert', up)  7.04 us
  transfers between devices with their start and end apart: 34, of which 6 were waited for; matrix products, arithmetic and copies ran while one was open for 4% of the time, Pallas kernels for 6%

profile of v5, /device:TPU:1, one launch (start us, length us, event | category | flops | bytes accessed | tf_op | source)
XLA Modules:
  0.0 194.9 jit_solution(17277256671386585822)
XLA Ops:
  3.1 7.6 %all-to-all-start = ((bf16[16,24,2560]{2,1,0:T(8,128)(2,1)}), bf16[16,24,2560]{2,1,0:T(8,128)(2,1)S(1)}, u32[]{:S(2)}, u32[]{:S(2)}) async-start(bf16[16,24,2560]{2,1,0:T(8,128)(2,1)} %copy-done.1), calls=%async_computation | async-start | bytes 3932160 | tf_op jit(solution)/shard_map/all_to_all | solution.py:258
  11.6 3.5 %collective-permute-start = (bf16[136,1280]{1,0:T(8,128)(2,1)}, bf16[136,1280]{1,0:T(8,128)(2,1)}, u32[]{:S(2)}, u32[]{:S(2)}) collective-permute-start(bf16[136,1280]{1,0:T(8,128)(2,1)} %get-tuple-element.28.refs_3_), channel_id=1, source_target_pairs={{0,32},{32,64},{64,96},{96,128},{128,160},{160,192},{192,224},{224... | collective-permute-start | bytes 1044488 | tf_op jit(solution)/shard_map/ppermute | solution.py:293
  15.1 9.5 %collective-permute-start.4 = (bf16[136,1280]{1,0:T(8,128)(2,1)}, bf16[136,1280]{1,0:T(8,128)(2,1)}, u32[]{:S(2)}, u32[]{:S(2)}) collective-permute-start(bf16[136,1280]{1,0:T(8,128)(2,1)} %get-tuple-element.28.refs_3_), channel_id=1, source_target_pairs={{0,480},{32,0},{64,32},{96,64},{128,96},{160,128},{192,160},{224,1... | collective-permute-start | bytes 1044488 | tf_op jit(solution)/shard_map/ppermute | solution.py:294
  24.6 1.9 collective-permute-start.1
  26.5 4.6 %collective-permute-start.3 = (bf16[128,1280]{1,0:T(8,128)(2,1)}, bf16[128,1280]{1,0:T(8,128)(2,1)}, u32[]{:S(2)}, u32[]{:S(2)}) collective-permute-start(bf16[128,1280]{1,0:T(8,128)(2,1)} %get-tuple-element.32.refs_0_), channel_id=1, source_target_pairs={{0,480},{32,0},{64,32},{96,64},{128,96},{160,128},{192,160},{224,1... | collective-permute-start | bytes 983048 | tf_op jit(solution)/shard_map/ppermute | solution.py:292
  33.9 1.9 collective-permute-start.7
  35.8 4.6 %collective-permute-start.8 = (bf16[136,1280]{1,0:T(8,128)(2,1)}, bf16[136,1280]{1,0:T(8,128)(2,1)}, u32[]{:S(2)}, u32[]{:S(2)}) collective-permute-start(bf16[136,1280]{1,0:T(8,128)(2,1)} %collective-permute-done.4.refs_5_), channel_id=1, source_target_pairs={{0,480},{32,0},{64,32},{96,64},{128,96},{160,128},{192,160},{224,1... | collective-permute-start | bytes 1044488 | tf_op jit(solution)/shard_map/ppermute | solution.py:294
  40.4 1.9 collective-permute-start.2
  42.4 4.6 %collective-permute-start.6 = (bf16[128,1280]{1,0:T(8,128)(2,1)}, bf16[128,1280]{1,0:T(8,128)(2,1)}, u32[]{:S(2)}, u32[]{:S(2)}) collective-permute-start(bf16[128,1280]{1,0:T(8,128)(2,1)} %collective-permute-done.3.refs_2_), channel_id=1, source_target_pairs={{0,480},{32,0},{64,32},{96,64},{128,96},{160,128},{192,160},{224,1... | collective-permute-start | bytes 983048 | tf_op jit(solution)/shard_map/ppermute | solution.py:292
  47.0 1.9 collective-permute-start.11
  48.9 4.6 %collective-permute-start.12 = (bf16[136,1280]{1,0:T(8,128)(2,1)}, bf16[136,1280]{1,0:T(8,128)(2,1)}, u32[]{:S(2)}, u32[]{:S(2)}) collective-permute-start(bf16[136,1280]{1,0:T(8,128)(2,1)} %collective-permute-done.8.refs_3_), channel_id=1, source_target_pairs={{0,480},{32,0},{64,32},{96,64},{128,96},{160,128},{192,160},{224,1... | collective-permute-start | bytes 1044488 | tf_op jit(solution)/shard_map/ppermute | solution.py:294
  57.4 4.6 %collective-permute-start.10 = (bf16[128,1280]{1,0:T(8,128)(2,1)}, bf16[128,1280]{1,0:T(8,128)(2,1)S(1)}, u32[]{:S(2)}, u32[]{:S(2)}) collective-permute-start(bf16[128,1280]{1,0:T(8,128)(2,1)} %collective-permute-done.6.refs_1_), channel_id=1, source_target_pairs={{0,480},{32,0},{64,32},{96,64},{128,96},{160,128},{192,160},{224,1... | collective-permute-start | bytes 983048 | tf_op jit(solution)/shard_map/ppermute | solution.py:292
  63.9 4.6 %collective-permute-start.16 = (bf16[136,1280]{1,0:T(8,128)(2,1)}, bf16[136,1280]{1,0:T(8,128)(2,1)S(1)}, u32[]{:S(2)}, u32[]{:S(2)}) collective-permute-start(bf16[136,1280]{1,0:T(8,128)(2,1)} %collective-permute-done.12.refs_3_), channel_id=1, source_target_pairs={{0,480},{32,0},{64,32},{96,64},{128,96},{160,128},{192,160},{224,1... | collective-permute-start | bytes 1044488 | tf_op jit(solution)/shard_map/ppermute | solution.py:294
  72.0 4.6 %collective-permute-start.14 = (bf16[128,1280]{1,0:T(8,128)(2,1)S(1)}, bf16[128,1280]{1,0:T(8,128)(2,1)S(1)}, u32[]{:S(2)}, u32[]{:S(2)}) collective-permute-start(bf16[128,1280]{1,0:T(8,128)(2,1)S(1)} %collective-permute-done.10.refs_1_), channel_id=1, source_target_pairs={{0,480},{32,0},{64,32},{96,64},{128,96},{160,128},{192,160},{224,1... | collective-permute-start | bytes 983048 | tf_op jit(solution)/shard_map/ppermute | solution.py:292
  78.6 4.6 %collective-permute-start.20 = (bf16[136,1280]{1,0:T(8,128)(2,1)S(1)}, bf16[136,1280]{1,0:T(8,128)(2,1)S(1)}, u32[]{:S(2)}, u32[]{:S(2)}) collective-permute-start(bf16[136,1280]{1,0:T(8,128)(2,1)S(1)} %collective-permute-done.16.refs_3_), channel_id=1, source_target_pairs={{0,480},{32,0},{64,32},{96,64},{128,96},{160,128},{192,160},{224,1... | collective-permute-start | bytes 1044488 | tf_op jit(solution)/shard_map/ppermute | solution.py:294
  86.5 4.6 %collective-permute-start.18 = (bf16[128,1280]{1,0:T(8,128)(2,1)S(1)}, bf16[128,1280]{1,0:T(8,128)(2,1)S(1)}, u32[]{:S(2)}, u32[]{:S(2)}) collective-permute-start(bf16[128,1280]{1,0:T(8,128)(2,1)S(1)} %collective-permute-done.14.refs_1_), channel_id=1, source_target_pairs={{0,480},{32,0},{64,32},{96,64},{128,96},{160,128},{192,160},{224,1... | collective-permute-start | bytes 983048 | tf_op jit(solution)/shard_map/ppermute | solution.py:292
  93.0 4.6 %collective-permute-start.25 = (bf16[136,1280]{1,0:T(8,128)(2,1)S(1)}, bf16[136,1280]{1,0:T(8,128)(2,1)S(1)}, u32[]{:S(2)}, u32[]{:S(2)}) collective-permute-start(bf16[136,1280]{1,0:T(8,128)(2,1)S(1)} %collective-permute-done.20.refs_3_), channel_id=1, source_target_pairs={{0,480},{32,0},{64,32},{96,64},{128,96},{160,128},{192,160},{224,1... | collective-permute-start | bytes 1044488 | tf_op jit(solution)/shard_map/ppermute | solution.py:294
  98.0 1.9 collective-permute-start.17
  99.9 4.6 %collective-permute-start.24 = (bf16[128,1280]{1,0:T(8,128)(2,1)S(1)}, bf16[128,1280]{1,0:T(8,128)(2,1)S(1)}, u32[]{:S(2)}, u32[]{:S(2)}) collective-permute-start(bf16[128,1280]{1,0:T(8,128)(2,1)S(1)} %collective-permute-done.18.refs_1_), channel_id=1, source_target_pairs={{0,480},{32,0},{64,32},{96,64},{128,96},{160,128},{192,160},{224,1... | collective-permute-start | bytes 983048 | tf_op jit(solution)/shard_map/ppermute | solution.py:292
  106.4 4.6 %collective-permute-start.27 = (bf16[136,1280]{1,0:T(8,128)(2,1)S(1)}, bf16[136,1280]{1,0:T(8,128)(2,1)S(1)}, u32[]{:S(2)}, u32[]{:S(2)}) collective-permute-start(bf16[136,1280]{1,0:T(8,128)(2,1)S(1)} %collective-permute-done.25.refs_3_), channel_id=1, source_target_pairs={{0,480},{32,0},{64,32},{96,64},{128,96},{160,128},{192,160},{224,1... | collective-permute-start | bytes 1044488 | tf_op jit(solution)/shard_map/ppermute | solution.py:294
  113.3 4.6 %collective-permute-start.29 = (bf16[128,1280]{1,0:T(8,128)(2,1)S(1)}, bf16[128,1280]{1,0:T(8,128)(2,1)S(1)}, u32[]{:S(2)}, u32[]{:S(2)}) collective-permute-start(bf16[128,1280]{1,0:T(8,128)(2,1)S(1)} %collective-permute-done.24.refs_1_), channel_id=1, source_target_pairs={{0,480},{32,0},{64,32},{96,64},{128,96},{160,128},{192,160},{224,1... | collective-permute-start | bytes 983048 | tf_op jit(solution)/shard_map/ppermute | solution.py:292
  118.4 7.0 %collective-permute-done.21.block_ref.refs_0_ = bf16[128,1280]{1,0:T(8,128)(2,1)S(1)} collective-permute-done((bf16[128,1280]{1,0:T(8,128)(2,1)S(1)}, bf16[128,1280]{1,0:T(8,128)(2,1)S(1)}, u32[]{:S(2)}, u32[]{:S(2)}) %collective-permute-start.21) | collective-permute-done | bytes 327712 | tf_op jit(solution)/shard_map/ppermute | solution.py:291
  127.7 3.4 %collective-permute-start.26 = (bf16[56,1280]{1,0:T(8,128)(2,1)S(1)}, bf16[56,1280]{1,0:T(8,128)(2,1)S(1)}, u32[]{:S(2)}, u32[]{:S(2)}) collective-permute-start(bf16[56,1280]{1,0:T(8,128)(2,1)S(1)} %get-tuple-element.44), channel_id=1, source_target_pairs={{0,32},{32,64},{64,96},{96,128},{128,160},{160,192},{192,224},{224... | collective-permute-start | bytes 430088 | tf_op jit(solution)/shard_map/ppermute | solution.py:303
  131.6 3.1 %collective-permute-done.26.first_ref = bf16[56,1280]{1,0:T(8,128)(2,1)S(1)} collective-permute-done((bf16[56,1280]{1,0:T(8,128)(2,1)S(1)}, bf16[56,1280]{1,0:T(8,128)(2,1)S(1)}, u32[]{:S(2)}, u32[]{:S(2)}) %collective-permute-start.26) | collective-permute-done | bytes 143392 | tf_op jit(solution)/shard_map/ppermute | solution.py:303
  134.8 3.3 %term_other.1 = bf16[384,2560]{1,0:T(8,128)(2,1)S(1)} custom-call(bf16[384,896]{1,0:T(8,128)(2,1)S(1)} %get-tuple-element.48.saved_ref, bf16[896,2560]{1,0:T(8,128)(2,1)S(1)} %bitcast.18), custom_call_target="tpu_custom_call" | custom-call | flops 1761607680 | bytes 7241728 | tf_op jit(solution)/shard_map/term_other/pallas_call | solution.py:223
  138.1 8.5 %collective-permute-start.30 = (bf16[384,2560]{1,0:T(8,128)(2,1)S(1)}, bf16[384,2560]{1,0:T(8,128)(2,1)S(1)}, u32[]{:S(2)}, u32[]{:S(2)}) collective-permute-start(bf16[384,2560]{1,0:T(8,128)(2,1)S(1)} %term_other.1), channel_id=1, source_target_pairs={{0,1},{1,0},{2,3},{3,2},{4,5},{5,4},{6,7},{7,6},{8,9},{9,8},{10,11... | collective-permute-start | bytes 5898248 | tf_op jit(solution)/shard_map/ppermute | solution.py:263
  146.7 3.3 %term_mine.1 = bf16[384,2560]{1,0:T(8,128)(2,1)S(1)} custom-call(bf16[384,896]{1,0:T(8,128)(2,1)S(1)} %get-tuple-element.31.saved_ref, bf16[896,2560]{1,0:T(8,128)(2,1)S(1)} %bitcast.19), custom_call_target="tpu_custom_call" | custom-call | flops 1761607680 | bytes 7241728 | tf_op jit(solution)/shard_map/term_mine/pallas_call | solution.py:223
  152.1 2.3 %collective-permute-start.31 = (bf16[16,24,2560]{2,1,0:T(8,128)(2,1)S(1)}, bf16[16,24,2560]{2,1,0:T(8,128)(2,1)}, u32[]{:S(2)}, u32[]{:S(2)}) collective-permute-start(bf16[16,24,2560]{2,1,0:T(8,128)(2,1)S(1)} %all-to-all-done.refs_6_), channel_id=1, source_target_pairs={{0,1},{1,0},{2,3},{3,2},{4,5},{5,4},{6,7},{7,6},{8,9},{9,8},{10,11... | collective-permute-start | bytes 5898248 | tf_op jit(solution)/shard_map/ppermute | solution.py:263
  154.3 6.8 %all-to-all-start.1 = ((bf16[16,24,2560]{2,1,0:T(8,128)(2,1)}), bf16[16,24,2560]{2,1,0:T(8,128)(2,1)}, u32[]{:S(2)}, u32[]{:S(2)}) async-start(bf16[16,24,2560]{2,1,0:T(8,128)(2,1)} %bitcast.29), calls=%async_computation.1 | async-start | bytes 3932160 | tf_op jit(solution)/shard_map/all_to_all | solution.py:258
  161.2 2.6 %maximum_select_fusion = bf16[16,2,24,2560]{3,2,0,1:T(8,128)(2,1)S(1)} fusion(bf16[16,1,24,2560]{3,2,0,1:T(8,128)(2,1)} %bitcast.11, bf16[16,1,24,2560]{3,2,0,1:T(8,128)(2,1)S(1)} %bitcast.23, pred[]{:T(512)S(6)} %eq.3), kind=kLoop, calls=%fused_computation | loop fusion | flops 5898240 | bytes 7864321 | tf_op jit(solution)/shard_map/jit(_where)/select_n | solution.py:318
  164.9 4.8 %fusion = bf16[1,896,768]{2,1,0:T(8,128)(2,1)} fusion(bf16[896,2560]{1,0:T(8,128)(2,1)S(1)} %bitcast.22, bf16[768,2560]{1,0:T(8,128)(2,1)S(1)} %bitcast.30), kind=kOutput, calls=%fused_computation.4 | convolution fusion | flops 3523903488 | bytes 9895936 | tf_op jit(solution)/shard_map/dot_general | solution.py:323
  169.7 22.5 %all-to-all-done.1 = bf16[16,24,2560]{2,1,0:T(8,128)(2,1)} async-done(((bf16[16,24,2560]{2,1,0:T(8,128)(2,1)}), bf16[16,24,2560]{2,1,0:T(8,128)(2,1)}, u32[]{:S(2)}, u32[]{:S(2)}) %all-to-all-start.1) | async-done | bytes 1966112 | tf_op jit(solution)/shard_map/all_to_all | solution.py:258
  (76 shorter events, 36.3 us)
Async XLA Ops:
  3.1 50.4 %all-to-all-start = ((bf16[16,24,2560]{2,1,0:T(8,128)(2,1)}), bf16[16,24,2560]{2,1,0:T(8,128)(2,1)S(1)}, u32[]{:S(2)}, u32[]{:S(2)}) async-start(bf16[16,24,2560]{2,1,0:T(8,128)(2,1)} %copy-done.1), calls=%async_computation | async-start | bytes 3932160 | tf_op jit(solution)/shard_map/all_to_all | solution.py:258
  11.6 22.3 %collective-permute-start = (bf16[136,1280]{1,0:T(8,128)(2,1)}, bf16[136,1280]{1,0:T(8,128)(2,1)}, u32[]{:S(2)}, u32[]{:S(2)}) collective-permute-start(bf16[136,1280]{1,0:T(8,128)(2,1)} %get-tuple-element.28.refs_3_), channel_id=1, source_target_pairs={{0,32},{32,64},{64,96},{96,128},{128,160},{160,192},{192,224},{224... | collective-permute-start | bytes 1044488 | tf_op jit(solution)/shard_map/ppermute | solution.py:293
  15.1 20.7 %collective-permute-start.4 = (bf16[136,1280]{1,0:T(8,128)(2,1)}, bf16[136,1280]{1,0:T(8,128)(2,1)}, u32[]{:S(2)}, u32[]{:S(2)}) collective-permute-start(bf16[136,1280]{1,0:T(8,128)(2,1)} %get-tuple-element.28.refs_3_), channel_id=1, source_target_pairs={{0,480},{32,0},{64,32},{96,64},{128,96},{160,128},{192,160},{224,1... | collective-permute-start | bytes 1044488 | tf_op jit(solution)/shard_map/ppermute | solution.py:294
  24.6 15.8 %collective-permute-start.1 = (bf16[128,1280]{1,0:T(8,128)(2,1)}, bf16[128,1280]{1,0:T(8,128)(2,1)}, u32[]{:S(2)}, u32[]{:S(2)}) collective-permute-start(bf16[128,1280]{1,0:T(8,128)(2,1)} %get-tuple-element.32.refs_0_), channel_id=1, source_target_pairs={{0,32},{32,64},{64,96},{96,128},{128,160},{160,192},{192,224},{224... | collective-permute-start | bytes 983048 | tf_op jit(solution)/shard_map/ppermute | solution.py:291
  26.5 15.8 %collective-permute-start.3 = (bf16[128,1280]{1,0:T(8,128)(2,1)}, bf16[128,1280]{1,0:T(8,128)(2,1)}, u32[]{:S(2)}, u32[]{:S(2)}) collective-permute-start(bf16[128,1280]{1,0:T(8,128)(2,1)} %get-tuple-element.32.refs_0_), channel_id=1, source_target_pairs={{0,480},{32,0},{64,32},{96,64},{128,96},{160,128},{192,160},{224,1... | collective-permute-start | bytes 983048 | tf_op jit(solution)/shard_map/ppermute | solution.py:292
  33.9 13.1 %collective-permute-start.7 = (bf16[136,1280]{1,0:T(8,128)(2,1)}, bf16[136,1280]{1,0:T(8,128)(2,1)}, u32[]{:S(2)}, u32[]{:S(2)}) collective-permute-start(bf16[136,1280]{1,0:T(8,128)(2,1)} %collective-permute-done.refs_4_), channel_id=1, source_target_pairs={{0,32},{32,64},{64,96},{96,128},{128,160},{160,192},{192,224},{224... | collective-permute-start | bytes 1044488 | tf_op jit(solution)/shard_map/ppermute | solution.py:293
  35.8 13.1 %collective-permute-start.8 = (bf16[136,1280]{1,0:T(8,128)(2,1)}, bf16[136,1280]{1,0:T(8,128)(2,1)}, u32[]{:S(2)}, u32[]{:S(2)}) collective-permute-start(bf16[136,1280]{1,0:T(8,128)(2,1)} %collective-permute-done.4.refs_5_), channel_id=1, source_target_pairs={{0,480},{32,0},{64,32},{96,64},{128,96},{160,128},{192,160},{224,1... | collective-permute-start | bytes 1044488 | tf_op jit(solution)/shard_map/ppermute | solution.py:294
  40.4 15.0 %collective-permute-start.2 = (bf16[128,1280]{1,0:T(8,128)(2,1)}, bf16[128,1280]{1,0:T(8,128)(2,1)}, u32[]{:S(2)}, u32[]{:S(2)}) collective-permute-start(bf16[128,1280]{1,0:T(8,128)(2,1)} %collective-permute-done.1.refs_1_), channel_id=1, source_target_pairs={{0,32},{32,64},{64,96},{96,128},{128,160},{160,192},{192,224},{224... | collective-permute-start | bytes 983048 | tf_op jit(solution)/shard_map/ppermute | solution.py:291
  42.4 15.0 %collective-permute-start.6 = (bf16[128,1280]{1,0:T(8,128)(2,1)}, bf16[128,1280]{1,0:T(8,128)(2,1)}, u32[]{:S(2)}, u32[]{:S(2)}) collective-permute-start(bf16[128,1280]{1,0:T(8,128)(2,1)} %collective-permute-done.3.refs_2_), channel_id=1, source_target_pairs={{0,480},{32,0},{64,32},{96,64},{128,96},{160,128},{192,160},{224,1... | collective-permute-start | bytes 983048 | tf_op jit(solution)/shard_map/ppermute | solution.py:292
  47.0 15.0 %collective-permute-start.11 = (bf16[136,1280]{1,0:T(8,128)(2,1)}, bf16[136,1280]{1,0:T(8,128)(2,1)}, u32[]{:S(2)}, u32[]{:S(2)}) collective-permute-start(bf16[136,1280]{1,0:T(8,128)(2,1)} %collective-permute-done.7.refs_2_), channel_id=1, source_target_pairs={{0,32},{32,64},{64,96},{96,128},{128,160},{160,192},{192,224},{224... | collective-permute-start | bytes 1044488 | tf_op jit(solution)/shard_map/ppermute | solution.py:293
  48.9 15.0 %collective-permute-start.12 = (bf16[136,1280]{1,0:T(8,128)(2,1)}, bf16[136,1280]{1,0:T(8,128)(2,1)}, u32[]{:S(2)}, u32[]{:S(2)}) collective-permute-start(bf16[136,1280]{1,0:T(8,128)(2,1)} %collective-permute-done.8.refs_3_), channel_id=1, source_target_pairs={{0,480},{32,0},{64,32},{96,64},{128,96},{160,128},{192,160},{224,1... | collective-permute-start | bytes 1044488 | tf_op jit(solution)/shard_map/ppermute | solution.py:294
  55.4 14.7 %collective-permute-start.5 = (bf16[128,1280]{1,0:T(8,128)(2,1)}, bf16[128,1280]{1,0:T(8,128)(2,1)S(1)}, u32[]{:S(2)}, u32[]{:S(2)}) collective-permute-start(bf16[128,1280]{1,0:T(8,128)(2,1)} %collective-permute-done.2.refs_0_), channel_id=1, source_target_pairs={{0,32},{32,64},{64,96},{96,128},{128,160},{160,192},{192,224},{224... | collective-permute-start | bytes 983048 | tf_op jit(solution)/shard_map/ppermute | solution.py:291
  57.4 14.7 %collective-permute-start.10 = (bf16[128,1280]{1,0:T(8,128)(2,1)}, bf16[128,1280]{1,0:T(8,128)(2,1)S(1)}, u32[]{:S(2)}, u32[]{:S(2)}) collective-permute-start(bf16[128,1280]{1,0:T(8,128)(2,1)} %collective-permute-done.6.refs_1_), channel_id=1, source_target_pairs={{0,480},{32,0},{64,32},{96,64},{128,96},{160,128},{192,160},{224,1... | collective-permute-start | bytes 983048 | tf_op jit(solution)/shard_map/ppermute | solution.py:292
  61.9 14.7 %collective-permute-start.15 = (bf16[136,1280]{1,0:T(8,128)(2,1)}, bf16[136,1280]{1,0:T(8,128)(2,1)S(1)}, u32[]{:S(2)}, u32[]{:S(2)}) collective-permute-start(bf16[136,1280]{1,0:T(8,128)(2,1)} %collective-permute-done.11.refs_2_), channel_id=1, source_target_pairs={{0,32},{32,64},{64,96},{96,128},{128,160},{160,192},{192,224},{224... | collective-permute-start | bytes 1044488 | tf_op jit(solution)/shard_map/ppermute | solution.py:293
  63.9 14.7 %collective-permute-start.16 = (bf16[136,1280]{1,0:T(8,128)(2,1)}, bf16[136,1280]{1,0:T(8,128)(2,1)S(1)}, u32[]{:S(2)}, u32[]{:S(2)}) collective-permute-start(bf16[136,1280]{1,0:T(8,128)(2,1)} %collective-permute-done.12.refs_3_), channel_id=1, source_target_pairs={{0,480},{32,0},{64,32},{96,64},{128,96},{160,128},{192,160},{224,1... | collective-permute-start | bytes 1044488 | tf_op jit(solution)/shard_map/ppermute | solution.py:294
  70.1 14.5 %collective-permute-start.9 = (bf16[128,1280]{1,0:T(8,128)(2,1)S(1)}, bf16[128,1280]{1,0:T(8,128)(2,1)S(1)}, u32[]{:S(2)}, u32[]{:S(2)}) collective-permute-start(bf16[128,1280]{1,0:T(8,128)(2,1)S(1)} %collective-permute-done.5.refs_0_), channel_id=1, source_target_pairs={{0,32},{32,64},{64,96},{96,128},{128,160},{160,192},{192,224},{224... | collective-permute-start | bytes 983048 | tf_op jit(solution)/shard_map/ppermute | solution.py:291
  72.0 14.5 %collective-permute-start.14 = (bf16[128,1280]{1,0:T(8,128)(2,1)S(1)}, bf16[128,1280]{1,0:T(8,128)(2,1)S(1)}, u32[]{:S(2)}, u32[]{:S(2)}) collective-permute-start(bf16[128,1280]{1,0:T(8,128)(2,1)S(1)} %collective-permute-done.10.refs_1_), channel_id=1, source_target_pairs={{0,480},{32,0},{64,32},{96,64},{128,96},{160,128},{192,160},{224,1... | collective-permute-start | bytes 983048 | tf_op jit(solution)/shard_map/ppermute | solution.py:292
  76.6 14.5 %collective-permute-start.19 = (bf16[136,1280]{1,0:T(8,128)(2,1)S(1)}, bf16[136,1280]{1,0:T(8,128)(2,1)S(1)}, u32[]{:S(2)}, u32[]{:S(2)}) collective-permute-start(bf16[136,1280]{1,0:T(8,128)(2,1)S(1)} %collective-permute-done.15.refs_2_), channel_id=1, source_target_pairs={{0,32},{32,64},{64,96},{96,128},{128,160},{160,192},{192,224},{224... | collective-permute-start | bytes 1044488 | tf_op jit(solution)/shard_map/ppermute | solution.py:293
  78.6 14.5 %collective-permute-start.20 = (bf16[136,1280]{1,0:T(8,128)(2,1)S(1)}, bf16[136,1280]{1,0:T(8,128)(2,1)S(1)}, u32[]{:S(2)}, u32[]{:S(2)}) collective-permute-start(bf16[136,1280]{1,0:T(8,128)(2,1)S(1)} %collective-permute-done.16.refs_3_), channel_id=1, source_target_pairs={{0,480},{32,0},{64,32},{96,64},{128,96},{160,128},{192,160},{224,1... | collective-permute-start | bytes 1044488 | tf_op jit(solution)/shard_map/ppermute | solution.py:294
  84.6 13.4 %collective-permute-start.13 = (bf16[128,1280]{1,0:T(8,128)(2,1)S(1)}, bf16[128,1280]{1,0:T(8,128)(2,1)S(1)}, u32[]{:S(2)}, u32[]{:S(2)}) collective-permute-start(bf16[128,1280]{1,0:T(8,128)(2,1)S(1)} %collective-permute-done.9.refs_0_), channel_id=1, source_target_pairs={{0,32},{32,64},{64,96},{96,128},{128,160},{160,192},{192,224},{224... | collective-permute-start | bytes 983048 | tf_op jit(solution)/shard_map/ppermute | solution.py:291
  86.5 13.4 %collective-permute-start.18 = (bf16[128,1280]{1,0:T(8,128)(2,1)S(1)}, bf16[128,1280]{1,0:T(8,128)(2,1)S(1)}, u32[]{:S(2)}, u32[]{:S(2)}) collective-permute-start(bf16[128,1280]{1,0:T(8,128)(2,1)S(1)} %collective-permute-done.14.refs_1_), channel_id=1, source_target_pairs={{0,480},{32,0},{64,32},{96,64},{128,96},{160,128},{192,160},{224,1... | collective-permute-start | bytes 983048 | tf_op jit(solution)/shard_map/ppermute | solution.py:292
  91.1 13.4 %collective-permute-start.22 = (bf16[136,1280]{1,0:T(8,128)(2,1)S(1)}, bf16[136,1280]{1,0:T(8,128)(2,1)S(1)}, u32[]{:S(2)}, u32[]{:S(2)}) collective-permute-start(bf16[136,1280]{1,0:T(8,128)(2,1)S(1)} %collective-permute-done.19.refs_2_), channel_id=1, source_target_pairs={{0,32},{32,64},{64,96},{96,128},{128,160},{160,192},{192,224},{224... | collective-permute-start | bytes 1044488 | tf_op jit(solution)/shard_map/ppermute | solution.py:293
  93.0 13.4 %collective-permute-start.25 = (bf16[136,1280]{1,0:T(8,128)(2,1)S(1)}, bf16[136,1280]{1,0:T(8,128)(2,1)S(1)}, u32[]{:S(2)}, u32[]{:S(2)}) collective-permute-start(bf16[136,1280]{1,0:T(8,128)(2,1)S(1)} %collective-permute-done.20.refs_3_), channel_id=1, source_target_pairs={{0,480},{32,0},{64,32},{96,64},{128,96},{160,128},{192,160},{224,1... | collective-permute-start | bytes 1044488 | tf_op jit(solution)/shard_map/ppermute | solution.py:294
  98.0 13.4 %collective-permute-start.17 = (bf16[128,1280]{1,0:T(8,128)(2,1)S(1)}, bf16[128,1280]{1,0:T(8,128)(2,1)S(1)}, u32[]{:S(2)}, u32[]{:S(2)}) collective-permute-start(bf16[128,1280]{1,0:T(8,128)(2,1)S(1)} %collective-permute-done.13.refs_0_), channel_id=1, source_target_pairs={{0,32},{32,64},{64,96},{96,128},{128,160},{160,192},{192,224},{224... | collective-permute-start | bytes 983048 | tf_op jit(solution)/shard_map/ppermute | solution.py:291
  99.9 13.4 %collective-permute-start.24 = (bf16[128,1280]{1,0:T(8,128)(2,1)S(1)}, bf16[128,1280]{1,0:T(8,128)(2,1)S(1)}, u32[]{:S(2)}, u32[]{:S(2)}) collective-permute-start(bf16[128,1280]{1,0:T(8,128)(2,1)S(1)} %collective-permute-done.18.refs_1_), channel_id=1, source_target_pairs={{0,480},{32,0},{64,32},{96,64},{128,96},{160,128},{192,160},{224,1... | collective-permute-start | bytes 983048 | tf_op jit(solution)/shard_map/ppermute | solution.py:292
  104.5 13.9 %collective-permute-start.23 = (bf16[136,1280]{1,0:T(8,128)(2,1)S(1)}, bf16[136,1280]{1,0:T(8,128)(2,1)S(1)}, u32[]{:S(2)}, u32[]{:S(2)}) collective-permute-start(bf16[136,1280]{1,0:T(8,128)(2,1)S(1)} %collective-permute-done.22.refs_2_), channel_id=1, source_target_pairs={{0,32},{32,64},{64,96},{96,128},{128,160},{160,192},{192,224},{224... | collective-permute-start | bytes 1044488 | tf_op jit(solution)/shard_map/ppermute | solution.py:293
  106.4 19.1 %collective-permute-start.27 = (bf16[136,1280]{1,0:T(8,128)(2,1)S(1)}, bf16[136,1280]{1,0:T(8,128)(2,1)S(1)}, u32[]{:S(2)}, u32[]{:S(2)}) collective-permute-start(bf16[136,1280]{1,0:T(8,128)(2,1)S(1)} %collective-permute-done.25.refs_3_), channel_id=1, source_target_pairs={{0,480},{32,0},{64,32},{96,64},{128,96},{160,128},{192,160},{224,1... | collective-permute-start | bytes 1044488 | tf_op jit(solution)/shard_map/ppermute | solution.py:294
  111.4 14.0 %collective-permute-start.21 = (bf16[128,1280]{1,0:T(8,128)(2,1)S(1)}, bf16[128,1280]{1,0:T(8,128)(2,1)S(1)}, u32[]{:S(2)}, u32[]{:S(2)}) collective-permute-start(bf16[128,1280]{1,0:T(8,128)(2,1)S(1)} %collective-permute-done.17.refs_0_), channel_id=1, source_target_pairs={{0,32},{32,64},{64,96},{96,128},{128,160},{160,192},{192,224},{224... | collective-permute-start | bytes 983048 | tf_op jit(solution)/shard_map/ppermute | solution.py:291
  113.3 17.8 %collective-permute-start.29 = (bf16[128,1280]{1,0:T(8,128)(2,1)S(1)}, bf16[128,1280]{1,0:T(8,128)(2,1)S(1)}, u32[]{:S(2)}, u32[]{:S(2)}) collective-permute-start(bf16[128,1280]{1,0:T(8,128)(2,1)S(1)} %collective-permute-done.24.refs_1_), channel_id=1, source_target_pairs={{0,480},{32,0},{64,32},{96,64},{128,96},{160,128},{192,160},{224,1... | collective-permute-start | bytes 983048 | tf_op jit(solution)/shard_map/ppermute | solution.py:292
  138.1 12.1 %collective-permute-start.30 = (bf16[384,2560]{1,0:T(8,128)(2,1)S(1)}, bf16[384,2560]{1,0:T(8,128)(2,1)S(1)}, u32[]{:S(2)}, u32[]{:S(2)}) collective-permute-start(bf16[384,2560]{1,0:T(8,128)(2,1)S(1)} %term_other.1), channel_id=1, source_target_pairs={{0,1},{1,0},{2,3},{3,2},{4,5},{5,4},{6,7},{7,6},{8,9},{9,8},{10,11... | collective-permute-start | bytes 5898248 | tf_op jit(solution)/shard_map/ppermute | solution.py:263
  152.1 9.1 %collective-permute-start.31 = (bf16[16,24,2560]{2,1,0:T(8,128)(2,1)S(1)}, bf16[16,24,2560]{2,1,0:T(8,128)(2,1)}, u32[]{:S(2)}, u32[]{:S(2)}) collective-permute-start(bf16[16,24,2560]{2,1,0:T(8,128)(2,1)S(1)} %all-to-all-done.refs_6_), channel_id=1, source_target_pairs={{0,1},{1,0},{2,3},{3,2},{4,5},{5,4},{6,7},{7,6},{8,9},{9,8},{10,11... | collective-permute-start | bytes 5898248 | tf_op jit(solution)/shard_map/ppermute | solution.py:263
  154.3 37.9 %all-to-all-start.1 = ((bf16[16,24,2560]{2,1,0:T(8,128)(2,1)}), bf16[16,24,2560]{2,1,0:T(8,128)(2,1)}, u32[]{:S(2)}, u32[]{:S(2)}) async-start(bf16[16,24,2560]{2,1,0:T(8,128)(2,1)} %bitcast.29), calls=%async_computation.1 | async-start | bytes 3932160 | tf_op jit(solution)/shard_map/all_to_all | solution.py:258
  (11 other events, 64.4 us)

commit v6 on v5

--- a/solution.py
+++ b/solution.py
@@ -54,7 +54,7 @@
     )(grads, routes_t, gates_t)
 
 
-def _split_kernel(units_dev, core_ref, hidden_ref, mine_ref, other_ref):
+def _split_kernel(units_dev, core_ref, hidden_ref, _, mine_ref, other_ref):
     units = hidden_ref.shape[1]
     half = units // 2
     row = lax.broadcasted_iota(jnp.int32, (half, units), 0)
@@ -68,7 +68,7 @@
         ).astype(BF)
 
 
-def _split(hidden, core, units_dev):
+def _split(hidden, core, units_dev, after):
     rows, units = hidden.shape
 
     def kernel(*refs):
@@ -79,6 +79,7 @@
         in_specs=[
             pl.BlockSpec(memory_space=pltpu.SMEM),
             pl.BlockSpec(memory_space=pltpu.VMEM),
+            pl.BlockSpec(memory_space=pl.ANY),
         ],
         out_specs=[pl.BlockSpec(memory_space=pltpu.VMEM)] * 2,
         out_shape=[jax.ShapeDtypeStruct((units // 2, rows), BF)] * 2,
@@ -87,7 +88,7 @@
             flops=2 * rows * units * units, bytes_accessed=4 * rows * units, transcendentals=0
         ),
         name="split_hidden",
-    )(core, hidden)
+    )(core, hidden, after)
 
 
 def _picker(expert, second_ref, capacity):
@@ -138,60 +139,65 @@
     )(me, *operands, *after)
 
 
-def _forward(me, step, block, info_block, rows, name):
-    tokens = info_block.shape[0] - INFO_ROWS
+def _forward(me, sends, first, second, rows, name, after=()):
+    tokens = second.shape[0] - INFO_ROWS
+    half = first.shape[1]
     groups, capacity, _ = rows.shape
-    width = block.shape[1]
-
-    def kernel(me_ref, block_ref, info_ref, _, out_ref, __):
-        expert = lax.rem(me_ref[0] + (step + groups) % groups, groups)
-        pick = _picker(expert, info_ref, capacity)
-        out_ref[...] = jnp.dot(
-            pick, block_ref[0:tokens, :], preferred_element_type=F32
-        ).astype(BF)
+    widths = [half * len(chunks) for _, chunks in sends]
+
+    def kernel(me_ref, first_ref, second_ref, _, *refs):
+        for (step, chunks), out_ref in zip(sends, refs[len(after) :]):
+            expert = lax.rem(me_ref[0] + (step + groups) % groups, groups)
+            pick = _picker(expert, second_ref, capacity)
+            for n, chunk in enumerate(chunks):
+                block_ref = (first_ref, second_ref)[chunk]
+                out_ref[:, n * half : (n + 1) * half] = jnp.dot(
+                    pick, block_ref[0:tokens, :], preferred_element_type=F32
+                ).astype(BF)
 
     return pl.pallas_call(
         kernel,
         in_specs=[pl.BlockSpec(memory_space=pltpu.SMEM)]
-        + [pl.BlockSpec(memory_space=pltpu.VMEM)] * 3,
-        out_specs=[pl.BlockSpec(memory_space=pltpu.VMEM)] * 2,
-        out_shape=[
-            jax.ShapeDtypeStruct((capacity, width), BF),
-            jax.ShapeDtypeStruct(rows.shape, BF),
-        ],
-        input_output_aliases={3: 1},
-        compiler_params=pltpu.CompilerParams(vmem_limit_bytes=VMEM),
-        cost_estimate=pl.CostEstimate(
-            flops=2 * capacity * tokens * width,
-            bytes_accessed=2 * (tokens + capacity) * width,
+        + [pl.BlockSpec(memory_space=pltpu.VMEM)] * 3
+        + [pl.BlockSpec(memory_space=pl.ANY)] * len(after),
+        out_specs=[pl.BlockSpec(memory_space=pltpu.VMEM)] * (len(sends) + 1),
+        out_shape=[jax.ShapeDtypeStruct((capacity, w), BF) for w in widths]
+        + [jax.ShapeDtypeStruct(rows.shape, BF)],
+        input_output_aliases={3: len(sends)},
+        compiler_params=pltpu.CompilerParams(vmem_limit_bytes=VMEM),
+        cost_estimate=pl.CostEstimate(
+            flops=2 * capacity * tokens * sum(widths),
+            bytes_accessed=2 * (tokens + capacity) * sum(widths),
             transcendentals=0,
         ),
         name=name,
-    )(me, block, info_block, rows)
-
-
-def _place(me, off, first, second, rows):
-    groups, capacity, width = rows.shape
-    half = width // 2
-
-    def kernel(me_ref, first_ref, second_ref, _, out_ref):
-        place = lax.rem(me_ref[0] + (off + groups) % groups, groups)
-        out_ref[place, :, :half] = first_ref[...]
-        out_ref[place, :, half:] = second_ref[...]
-
+    )(me, first, second, rows, *after)
+
+
+def _place(me, parts, rows, name):
+    groups, capacity, _ = rows.shape
+    count = len(parts)
+
+    def kernel(me_ref, *refs):
+        out_ref = refs[-1]
+        for (off, column, part), part_ref in zip(parts, refs):
+            place = lax.rem(me_ref[0] + (off + groups) % groups, groups)
+            out_ref[place, :, column : column + part.shape[1]] = part_ref[...]
+
+    arrays = [part for _, _, part in parts]
     return pl.pallas_call(
         kernel,
         in_specs=[pl.BlockSpec(memory_space=pltpu.SMEM)]
-        + [pl.BlockSpec(memory_space=pltpu.VMEM)] * 3,
+        + [pl.BlockSpec(memory_space=pltpu.VMEM)] * (count + 1),
         out_specs=pl.BlockSpec(memory_space=pltpu.VMEM),
         out_shape=jax.ShapeDtypeStruct(rows.shape, BF),
-        input_output_aliases={3: 0},
-        compiler_params=pltpu.CompilerParams(vmem_limit_bytes=VMEM),
-        cost_estimate=pl.CostEstimate(
-            flops=0, bytes_accessed=4 * capacity * width, transcendentals=0
-        ),
-        name="place_last",
-    )(me, first, second, rows)
+        input_output_aliases={count + 1: 0},
+        compiler_params=pltpu.CompilerParams(vmem_limit_bytes=VMEM),
+        cost_estimate=pl.CostEstimate(
+            flops=0, bytes_accessed=4 * sum(a.size for a in arrays), transcendentals=0
+        ),
+        name=name,
+    )(me, *arrays, rows)
 
 
 def _copies(array, copies):
@@ -210,6 +216,46 @@
         ),
         name="unit_copies",
     )(array)
+
+
+def _once(array, after):
+    def kernel(*_):
+        pass
+
+    return pl.pallas_call(
+        kernel,
+        in_specs=[pl.BlockSpec(memory_space=pltpu.HBM), pl.BlockSpec(memory_space=pl.ANY)],
+        out_specs=pl.BlockSpec(memory_space=pltpu.HBM),
+        out_shape=pltpu.HBM(array.shape, BF),
+        input_output_aliases={0: 0},
+        cost_estimate=pl.CostEstimate(flops=0, bytes_accessed=0, transcendentals=0),
+        name="once",
+    )(array, after)
+
+
+def _sum_kernel(parts_ref, out_ref):
+    total = parts_ref[0].astype(F32)
+    for i in range(1, parts_ref.shape[0]):
+        total += parts_ref[i].astype(F32)
+    for i in range(total.shape[0]):
+        out_ref[i, :, :] = total[i : i + 1, :]
+
+
+def _sum(parts):
+    chips, units, width = parts.shape
+    block = 512 if width % 512 == 0 else LANES
+    return pl.pallas_call(
+        _sum_kernel,
+        grid=(width // block,),
+        in_specs=[pl.BlockSpec((chips, units, block), lambda j: (0, 0, j))],
+        out_specs=pl.BlockSpec((units, 1, block), lambda j: (0, 0, j)),
+        out_shape=jax.ShapeDtypeStruct((units, 1, width), F32),
+        compiler_params=pltpu.CompilerParams(vmem_limit_bytes=VMEM),
+        cost_estimate=pl.CostEstimate(
+            flops=parts.size, bytes_accessed=2 * parts.size, transcendentals=0
+        ),
+        name="sum_parts",
+    )(parts)
 
 
 def _term_kernel(saved_ref, rows_ref, out_ref):
@@ -266,9 +312,12 @@
 
     own_first, own_second = _pack(grads[0], routes.transpose(2, 0, 1), gates[0].T)
 
-    up = [(i, (i + 1) % groups) for i in range(groups)]
-    down = [(i, (i - 1) % groups) for i in range(groups)]
     far = groups // 2
+    relay = far - 3
+
+    def shift(array, places):
+        return lax.ppermute(array, "expert", [(i, (i + places) % groups) for i in range(groups)])
+
     got_first, got_second = {0: own_first}, {0: own_second}
     a_up = a_down = own_first
     b_up = b_down = own_second
@@ -280,38 +329,44 @@
         seconds = [got_second[off] for off in batch]
         return _select(me, batch, firsts, seconds, rows, shape, name, after)
 
-    saved_mine, saved_other = _split(hidden[0], core.reshape(1), units_dev)
-    for hop in range(1, far):
+    saved_mine, saved_other = _split(hidden[0], core.reshape(1), units_dev, own_first)
+    for hop in range(1, relay + 1):
         if hop == 2:
             b_up, saved_mine, saved_other = lax.optimization_barrier(
                 (b_up, saved_mine, saved_other)
             )
         if hop >= 3:
             a_up, rows = lax.optimization_barrier((a_up, rows))
-        a_up = lax.ppermute(a_up, "expert", up)
-        a_down = lax.ppermute(a_down, "expert", down)
-        b_up = lax.ppermute(b_up, "expert", up)
-        b_down = lax.ppermute(b_down, "expert", down)
-        got_first[-hop], got_second[hop] = a_up, b_down
-        got_first[hop], got_second[-hop] = a_down, b_up
+        a_up, a_down = shift(a_up, 1), shift(a_down, -1)
+        b_up, b_down = shift(b_up, 1), shift(b_down, -1)
+        got_first[-hop], got_first[hop] = a_up, a_down
+        got_second[-hop], got_second[hop] = b_up, b_down
         if hop == 2:
             rows = pick(rows, [0, -1, 1], "select_1", (weights_mine,))
         elif hop >= 3:
             rows = pick(rows, [1 - hop, hop - 1], f"select_{hop - 1}")
 
-    last_first, rows = _forward(me, 1, a_up, b_up, rows, "forward_up")
-    last_first = lax.ppermute(last_first, "expert", up)
-    last_second, rows = _forward(me, -1, b_down, b_down, rows, "forward_down")
-    last_second = lax.ppermute(last_second, "expert", down)
-    rows = pick(rows, [1 - far, far - 1], f"select_{far - 1}")
-    rows = _place(me, far, last_first, last_second, rows)
+    far_down, rows = _forward(me, [(-3, (1,))], b_down, b_down, rows, "forward_far")
+    far_down = shift(far_down, -3)
+    up_2, up_3, up_1, rows = _forward(
+        me, [(2, (0, 1)), (3, (0,)), (1, (0, 1))], a_up, b_up, rows, "forward_up"
+    )
+    down_2, down_1, rows = _forward(
+        me, [(-2, (0, 1)), (-1, (0, 1))], a_down, b_down, rows, "forward_down"
+    )
+    rows = pick(rows, [-relay, relay], f"select_{relay}")
+    up_2, down_2, far_up = shift(up_2, 2), shift(down_2, -2), shift(up_3, 3)
+    up_1, down_1 = shift(up_1, 1), shift(down_1, -1)
+    parts = [(-relay - 2, 0, up_2), (relay + 2, 0, down_2), (far, 0, far_up), (far, half, far_down)]
+    rows = _place(me, parts, rows, "place_far")
+    rows = _place(me, [(-relay - 1, 0, up_1), (relay + 1, 0, down_1)], rows, "place_near")
     rows = rows.reshape(rows_dev, width)
 
     other = _term(saved_other, rows, "term_other")
     arrived = other_core(other)
     mine = _term(saved_mine, rows, "term_mine")
     pair = (mine.astype(F32) + arrived.astype(F32)).astype(BF)
-    pair, rows, weights_mine = lax.optimization_barrier((pair, rows, weights_mine))
+    pair, rows = lax.optimization_barrier((pair, rows))
     sums = over_chips(pair.reshape(chips, units_dev, width))
 
     weights_other = other_core(weights_mine)
@@ -323,7 +378,7 @@
     d_rows = lax.dot_general(rows, both, (((1,), (1,)), ((), ())), preferred_element_type=F32)
     d_hidden = d_rows.astype(BF)[None]
     sums, d_hidden = lax.optimization_barrier((sums, d_hidden))
-    down_grad = jnp.sum(sums.astype(F32), axis=0)[:, None, :]
+    down_grad = _sum(sums)
     return (d_hidden, down_grad)
 
 

time: 196 us -> 192 us (0.980)
  starting transfers between devices: 128 us -> 114 us
  waiting for transfers between devices: 33.4 us -> 40.6 us
  Pallas kernels: 15.7 us -> 19.5 us
    ppermute x30 -> x26, starting transfers between devices: 103 us -> 85.9 us  [shift(): lax.ppermute(array, 'expert', [(i, (i + places) % groups) for i in range(...]
    ppermute x30 -> x26, waiting for transfers between devices: 10.6 us -> 19.7 us  [shift(): lax.ppermute(array, 'expert', [(i, (i + places) % groups) for i in range(...]
    pallas_call x0 -> x1, Pallas kernels: none -> 3.91 us  [_sum(): pl.pallas_call(_sum_kernel, grid=(width // block,), in_specs=[pl.BlockSpe...]
    ppermute x2, starting transfers between devices: 10.8 us -> 14 us  [other_core(): return lax.ppermute(array, 'replica', [(i, i ^ 1) for i in range(replicas)])]
    pallas_call x7 -> x5, Pallas kernels: 6.24 us -> 5.58 us  [_select(): pl.pallas_call(kernel, in_specs=[pl.BlockSpec(memory_space=pltpu.SMEM)] +...]
  transfers between devices with their start and end apart: 34 -> 30, of which waited for: 6 -> 7; matrix products, arithmetic and copies ran while one was open for 4% -> 5% of each run, Pallas kernels for 6% -> 6%
where the time goes in v6:
time: 192 us; the launch traced here: 190 us
  starting transfers between devices  114 us (59%)
  waiting for transfers between devices  40.6 us (21%)
  Pallas kernels  19.5 us (10%)
  local copies, waits for them, and re-layouts  4.8 us (2%)
  matrix products  4.8 us (2%)
  other arithmetic  4.41 us (2%)
    ppermute x26, starting transfers between devices, shift(): lax.ppermute(array, 'expert', [(i, (i + places) % groups) for i in range(...  85.9 us
    all_to_all x2, waiting for transfers between devices, over_chips(): lax.all_to_all(array, 'replica', split_axis=0, concat_axis=0, tiled=True,...  21 us
    ppermute x26, waiting for transfers between devices, shift(): lax.ppermute(array, 'expert', [(i, (i + places) % groups) for i in range(...  19.7 us
    all_to_all x2, starting transfers between devices, over_chips(): lax.all_to_all(array, 'replica', split_axis=0, concat_axis=0, tiled=True,...  14.2 us
    ppermute x2, starting transfers between devices, other_core(): return lax.ppermute(array, 'replica', [(i, i ^ 1) for i in range(replicas)])  14 us
    pallas_call x2, Pallas kernels, _term(): pl.pallas_call(_term_kernel, grid=(width // block,), in_specs=[pl.BlockSp...  6.61 us
    pallas_call x5, Pallas kernels, _select(): pl.pallas_call(kernel, in_specs=[pl.BlockSpec(memory_space=pltpu.SMEM)] +...  5.58 us
    dot_general x1, matrix products, body(): lax.dot_general(rows, both, (((1,), (1,)), ((), ())), preferred_element_t...  4.8 us
  transfers between devices with their start and end apart: 30, of which 7 were waited for; matrix products, arithmetic and copies ran while one was open for 5% of the time, Pallas kernels for 6%

profile of v6, /device:TPU:1, one launch (start us, length us, event | category | flops | bytes accessed | tf_op | source)
XLA Modules:
  0.0 189.6 jit_solution(14479307322640266519)
XLA Ops:
  3.1 7.6 %all-to-all-start = ((bf16[16,24,2560]{2,1,0:T(8,128)(2,1)}), bf16[16,24,2560]{2,1,0:T(8,128)(2,1)S(1)}, u32[]{:S(2)}, u32[]{:S(2)}) async-start(bf16[16,24,2560]{2,1,0:T(8,128)(2,1)} %copy-done.1), calls=%async_computation | async-start | bytes 3932160 | tf_op jit(solution)/shard_map/all_to_all | solution.py:304
  11.6 11.1 %collective-permute-start.4 = (bf16[136,1280]{1,0:T(8,128)(2,1)}, bf16[136,1280]{1,0:T(8,128)(2,1)}, u32[]{:S(2)}, u32[]{:S(2)}) collective-permute-start(bf16[136,1280]{1,0:T(8,128)(2,1)} %get-tuple-element.28.refs_3_), channel_id=1, source_target_pairs={{0,480},{32,0},{64,32},{96,64},{128,96},{160,128},{192,160},{224,1... | collective-permute-start | bytes 1044488 | tf_op jit(solution)/shard_map/ppermute | solution.py:319
  22.7 1.9 %collective-permute-start = (bf16[136,1280]{1,0:T(8,128)(2,1)}, bf16[136,1280]{1,0:T(8,128)(2,1)}, u32[]{:S(2)}, u32[]{:S(2)}) collective-permute-start(bf16[136,1280]{1,0:T(8,128)(2,1)} %get-tuple-element.28.refs_3_), channel_id=1, source_target_pairs={{0,32},{32,64},{64,96},{96,128},{128,160},{160,192},{192,224},{224... | collective-permute-start | bytes 1044488 | tf_op jit(solution)/shard_map/ppermute | solution.py:319
  24.6 1.9 %collective-permute-start.1 = (bf16[128,1280]{1,0:T(8,128)(2,1)}, bf16[128,1280]{1,0:T(8,128)(2,1)}, u32[]{:S(2)}, u32[]{:S(2)}) collective-permute-start(bf16[128,1280]{1,0:T(8,128)(2,1)} %get-tuple-element.29.refs_2_.refs_0_), channel_id=1, source_target_pairs={{0,32},{32,64},{64,96},{96,128},{128,160},{160,192},{192,224},{224... | collective-permute-start | bytes 983048 | tf_op jit(solution)/shard_map/ppermute | solution.py:319
  26.5 4.6 %collective-permute-start.3 = (bf16[128,1280]{1,0:T(8,128)(2,1)}, bf16[128,1280]{1,0:T(8,128)(2,1)}, u32[]{:S(2)}, u32[]{:S(2)}) collective-permute-start(bf16[128,1280]{1,0:T(8,128)(2,1)} %get-tuple-element.29.refs_2_.refs_0_), channel_id=1, source_target_pairs={{0,480},{32,0},{64,32},{96,64},{128,96},{160,128},{192,160},{224,1... | collective-permute-start | bytes 983048 | tf_op jit(solution)/shard_map/ppermute | solution.py:319
  31.1 3.6 %collective-permute-start.8 = (bf16[136,1280]{1,0:T(8,128)(2,1)}, bf16[136,1280]{1,0:T(8,128)(2,1)}, u32[]{:S(2)}, u32[]{:S(2)}) collective-permute-start(bf16[136,1280]{1,0:T(8,128)(2,1)} %collective-permute-done.4.refs_5_), channel_id=1, source_target_pairs={{0,480},{32,0},{64,32},{96,64},{128,96},{160,128},{192,160},{224,1... | collective-permute-start | bytes 1044488 | tf_op jit(solution)/shard_map/ppermute | solution.py:319
  37.6 1.9 %collective-permute-start.7 = (bf16[136,1280]{1,0:T(8,128)(2,1)}, bf16[136,1280]{1,0:T(8,128)(2,1)}, u32[]{:S(2)}, u32[]{:S(2)}) collective-permute-start(bf16[136,1280]{1,0:T(8,128)(2,1)} %collective-permute-done.refs_4_), channel_id=1, source_target_pairs={{0,32},{32,64},{64,96},{96,128},{128,160},{160,192},{192,224},{224... | collective-permute-start | bytes 1044488 | tf_op jit(solution)/shard_map/ppermute | solution.py:319
  39.5 2.0 %collective-permute-done.1.refs_1_ = bf16[128,1280]{1,0:T(8,128)(2,1)} collective-permute-done((bf16[128,1280]{1,0:T(8,128)(2,1)}, bf16[128,1280]{1,0:T(8,128)(2,1)}, u32[]{:S(2)}, u32[]{:S(2)}) %collective-permute-start.1) | collective-permute-done | bytes 327712 | tf_op jit(solution)/shard_map/ppermute | solution.py:319
  43.5 4.6 %collective-permute-start.6 = (bf16[128,1280]{1,0:T(8,128)(2,1)}, bf16[128,1280]{1,0:T(8,128)(2,1)}, u32[]{:S(2)}, u32[]{:S(2)}) collective-permute-start(bf16[128,1280]{1,0:T(8,128)(2,1)} %collective-permute-done.3.refs_2_), channel_id=1, source_target_pairs={{0,480},{32,0},{64,32},{96,64},{128,96},{160,128},{192,160},{224,1... | collective-permute-start | bytes 983048 | tf_op jit(solution)/shard_map/ppermute | solution.py:319
  48.1 1.9 %collective-permute-start.12 = (bf16[136,1280]{1,0:T(8,128)(2,1)}, bf16[136,1280]{1,0:T(8,128)(2,1)}, u32[]{:S(2)}, u32[]{:S(2)}) collective-permute-start(bf16[136,1280]{1,0:T(8,128)(2,1)} %collective-permute-done.8.refs_3_), channel_id=1, source_target_pairs={{0,480},{32,0},{64,32},{96,64},{128,96},{160,128},{192,160},{224,1... | collective-permute-start | bytes 1044488 | tf_op jit(solution)/shard_map/ppermute | solution.py:319
  50.0 3.4 %collective-permute-start.11 = (bf16[136,1280]{1,0:T(8,128)(2,1)}, bf16[136,1280]{1,0:T(8,128)(2,1)}, u32[]{:S(2)}, u32[]{:S(2)}) collective-permute-start(bf16[136,1280]{1,0:T(8,128)(2,1)} %collective-permute-done.7.refs_2_), channel_id=1, source_target_pairs={{0,32},{32,64},{64,96},{96,128},{128,160},{160,192},{192,224},{224... | collective-permute-start | bytes 1044488 | tf_op jit(solution)/shard_map/ppermute | solution.py:319
  57.4 4.6 %collective-permute-start.10 = (bf16[128,1280]{1,0:T(8,128)(2,1)}, bf16[128,1280]{1,0:T(8,128)(2,1)S(1)}, u32[]{:S(2)}, u32[]{:S(2)}) collective-permute-start(bf16[128,1280]{1,0:T(8,128)(2,1)} %collective-permute-done.6.refs_1_), channel_id=1, source_target_pairs={{0,480},{32,0},{64,32},{96,64},{128,96},{160,128},{192,160},{224,1... | collective-permute-start | bytes 983048 | tf_op jit(solution)/shard_map/ppermute | solution.py:319
  62.0 3.6 %collective-permute-start.16 = (bf16[136,1280]{1,0:T(8,128)(2,1)}, bf16[136,1280]{1,0:T(8,128)(2,1)S(1)}, u32[]{:S(2)}, u32[]{:S(2)}) collective-permute-start(bf16[136,1280]{1,0:T(8,128)(2,1)} %collective-permute-done.12.refs_3_), channel_id=1, source_target_pairs={{0,480},{32,0},{64,32},{96,64},{128,96},{160,128},{192,160},{224,1... | collective-permute-start | bytes 1044488 | tf_op jit(solution)/shard_map/ppermute | solution.py:319
  71.8 4.6 %collective-permute-start.18 = (bf16[128,1280]{1,0:T(8,128)(2,1)S(1)}, bf16[128,1280]{1,0:T(8,128)(2,1)S(1)}, u32[]{:S(2)}, u32[]{:S(2)}) collective-permute-start(bf16[128,1280]{1,0:T(8,128)(2,1)S(1)} %collective-permute-done.10.refs_1_), channel_id=1, source_target_pairs={{0,480},{32,0},{64,32},{96,64},{128,96},{160,128},{192,160},{224,1... | collective-permute-start | bytes 983048 | tf_op jit(solution)/shard_map/ppermute | solution.py:319
  76.4 2.7 %collective-permute-start.17 = (bf16[136,1280]{1,0:T(8,128)(2,1)S(1)}, bf16[136,1280]{1,0:T(8,128)(2,1)S(1)}, u32[]{:S(2)}, u32[]{:S(2)}) collective-permute-start(bf16[136,1280]{1,0:T(8,128)(2,1)S(1)} %collective-permute-done.16.refs_3_), channel_id=1, source_target_pairs={{0,480},{32,0},{64,32},{96,64},{128,96},{160,128},{192,160},{224,1... | collective-permute-start | bytes 1044488 | tf_op jit(solution)/shard_map/ppermute | solution.py:319
  79.2 2.5 %collective-permute-start.15 = (bf16[136,1280]{1,0:T(8,128)(2,1)S(1)}, bf16[136,1280]{1,0:T(8,128)(2,1)S(1)}, u32[]{:S(2)}, u32[]{:S(2)}) collective-permute-start(bf16[136,1280]{1,0:T(8,128)(2,1)S(1)} %collective-permute-done.14.refs_2_), channel_id=1, source_target_pairs={{0,32},{32,64},{64,96},{96,128},{128,160},{160,192},{192,224},{224... | collective-permute-start | bytes 1044488 | tf_op jit(solution)/shard_map/ppermute | solution.py:319
  85.2 4.6 %collective-permute-start.20 = (bf16[128,1280]{1,0:T(8,128)(2,1)S(1)}, bf16[128,1280]{1,0:T(8,128)(2,1)S(1)}, u32[]{:S(2)}, u32[]{:S(2)}) collective-permute-start(bf16[128,1280]{1,0:T(8,128)(2,1)S(1)} %collective-permute-done.18.refs_1_), channel_id=1, source_target_pairs={{0,480},{32,0},{64,32},{96,64},{128,96},{160,128},{192,160},{224,1... | collective-permute-start | bytes 983048 | tf_op jit(solution)/shard_map/ppermute | solution.py:319
  90.3 2.8 %collective-permute-start.25 = (bf16[56,1280]{1,0:T(8,128)(2,1)S(1)}, bf16[56,1280]{1,0:T(8,128)(2,1)S(1)}, u32[]{:S(2)}, u32[]{:S(2)}) collective-permute-start(bf16[56,1280]{1,0:T(8,128)(2,1)S(1)} %get-tuple-element.47), channel_id=1, source_target_pairs={{0,416},{32,448},{64,480},{96,0},{128,32},{160,64},{192,96},{224,1... | collective-permute-start | bytes 430088 | tf_op jit(solution)/shard_map/ppermute | solution.py:319
  93.1 4.6 %collective-permute-done.13.first_ref.refs_0_ = bf16[128,1280]{1,0:T(8,128)(2,1)S(1)} collective-permute-done((bf16[128,1280]{1,0:T(8,128)(2,1)S(1)}, bf16[128,1280]{1,0:T(8,128)(2,1)S(1)}, u32[]{:S(2)}, u32[]{:S(2)}) %collective-permute-start.13) | collective-permute-done | bytes 327712 | tf_op jit(solution)/shard_map/ppermute | solution.py:319
  98.5 1.9 %collective-permute-start.23 = (bf16[56,2560]{1,0:T(8,128)(2,1)S(1)}, bf16[56,2560]{1,0:T(8,128)(2,1)S(1)}, u32[]{:S(2)}, u32[]{:S(2)}) collective-permute-start(bf16[56,2560]{1,0:T(8,128)(2,1)S(1)} %get-tuple-element.45), channel_id=1, source_target_pairs={{0,448},{32,480},{64,0},{96,32},{128,64},{160,96},{192,128},{224,1... | collective-permute-start | bytes 860168 | tf_op jit(solution)/shard_map/ppermute | solution.py:319
  100.4 4.3 %collective-permute-start.22 = (bf16[56,2560]{1,0:T(8,128)(2,1)S(1)}, bf16[56,2560]{1,0:T(8,128)(2,1)S(1)}, u32[]{:S(2)}, u32[]{:S(2)}) collective-permute-start(bf16[56,2560]{1,0:T(8,128)(2,1)S(1)} %get-tuple-element.44), channel_id=1, source_target_pairs={{0,64},{32,96},{64,128},{96,160},{128,192},{160,224},{192,256},{22... | collective-permute-start | bytes 860168 | tf_op jit(solution)/shard_map/ppermute | solution.py:319
  104.7 6.0 %collective-permute-start.21 = (bf16[56,2560]{1,0:T(8,128)(2,1)S(1)}, bf16[56,2560]{1,0:T(8,128)(2,1)S(1)}, u32[]{:S(2)}, u32[]{:S(2)}) collective-permute-start(bf16[56,2560]{1,0:T(8,128)(2,1)S(1)} %get-tuple-element.43), channel_id=1, source_target_pairs={{0,480},{32,0},{64,32},{96,64},{128,96},{160,128},{192,160},{224,1... | collective-permute-start | bytes 860168 | tf_op jit(solution)/shard_map/ppermute | solution.py:319
  114.9 11.9 %collective-permute-done.24.refs_2_ = bf16[56,1280]{1,0:T(8,128)(2,1)S(1)} collective-permute-done((bf16[56,1280]{1,0:T(8,128)(2,1)S(1)}, bf16[56,1280]{1,0:T(8,128)(2,1)S(1)}, u32[]{:S(2)}, u32[]{:S(2)}) %collective-permute-start.24) | collective-permute-done | bytes 143392 | tf_op jit(solution)/shard_map/ppermute | solution.py:319
  127.0 3.3 %term_other.1 = bf16[384,2560]{1,0:T(8,128)(2,1)S(1)} custom-call(bf16[384,896]{1,0:T(8,128)(2,1)S(1)} %get-tuple-element.49.saved_ref, bf16[896,2560]{1,0:T(8,128)(2,1)S(1)} %bitcast.18), custom_call_target="tpu_custom_call" | custom-call | flops 1761607680 | bytes 7241728 | tf_op jit(solution)/shard_map/term_other/pallas_call | solution.py:269
  130.3 12.1 %collective-permute-start.26 = (bf16[384,2560]{1,0:T(8,128)(2,1)S(1)}, bf16[384,2560]{1,0:T(8,128)(2,1)S(1)}, u32[]{:S(2)}, u32[]{:S(2)}) collective-permute-start(bf16[384,2560]{1,0:T(8,128)(2,1)S(1)} %term_other.1), channel_id=1, source_target_pairs={{0,1},{1,0},{2,3},{3,2},{4,5},{5,4},{6,7},{7,6},{8,9},{9,8},{10,11... | collective-permute-start | bytes 5898248 | tf_op jit(solution)/shard_map/ppermute | solution.py:309
  142.4 1.9 %collective-permute-start.27 = (bf16[16,24,2560]{2,1,0:T(8,128)(2,1)S(1)}, bf16[16,24,2560]{2,1,0:T(8,128)(2,1)}, u32[]{:S(2)}, u32[]{:S(2)}) collective-permute-start(bf16[16,24,2560]{2,1,0:T(8,128)(2,1)S(1)} %all-to-all-done.refs_6_), channel_id=1, source_target_pairs={{0,1},{1,0},{2,3},{3,2},{4,5},{5,4},{6,7},{7,6},{8,9},{9,8},{10,11... | collective-permute-start | bytes 5898248 | tf_op jit(solution)/shard_map/ppermute | solution.py:309
  144.3 3.3 %term_mine.1 = bf16[384,2560]{1,0:T(8,128)(2,1)S(1)} custom-call(bf16[384,896]{1,0:T(8,128)(2,1)S(1)} %get-tuple-element.32.saved_ref, bf16[896,2560]{1,0:T(8,128)(2,1)S(1)} %bitcast.19), custom_call_target="tpu_custom_call" | custom-call | flops 1761607680 | bytes 7241728 | tf_op jit(solution)/shard_map/term_mine/pallas_call | solution.py:269
  149.5 6.6 %all-to-all-start.1 = ((bf16[16,24,2560]{2,1,0:T(8,128)(2,1)}), bf16[16,24,2560]{2,1,0:T(8,128)(2,1)}, u32[]{:S(2)}, u32[]{:S(2)}) async-start(bf16[16,24,2560]{2,1,0:T(8,128)(2,1)} %bitcast.29), calls=%async_computation.1 | async-start | bytes 3932160 | tf_op jit(solution)/shard_map/all_to_all | solution.py:304
  156.2 2.6 %maximum_select_fusion = bf16[16,2,24,2560]{3,2,0,1:T(8,128)(2,1)S(1)} fusion(bf16[16,1,24,2560]{3,2,0,1:T(8,128)(2,1)} %bitcast.11, bf16[16,1,24,2560]{3,2,0,1:T(8,128)(2,1)S(1)} %bitcast.23, pred[]{:T(512)S(6)} %eq.3), kind=kLoop, calls=%fused_computation | loop fusion | flops 5898240 | bytes 7864321 | tf_op jit(solution)/shard_map/jit(_where)/select_n | solution.py:373
  159.9 4.8 %fusion = bf16[1,896,768]{2,1,0:T(8,128)(2,1)} fusion(bf16[896,2560]{1,0:T(8,128)(2,1)S(1)} %bitcast.22, bf16[768,2560]{1,0:T(8,128)(2,1)S(1)} %bitcast.30), kind=kOutput, calls=%fused_computation.3 | convolution fusion | flops 3523903488 | bytes 9895936 | tf_op jit(solution)/shard_map/dot_general | solution.py:378
  164.7 21.0 %all-to-all-done.1.parts_ref = bf16[16,24,2560]{2,1,0:T(8,128)(2,1)} async-done(((bf16[16,24,2560]{2,1,0:T(8,128)(2,1)}), bf16[16,24,2560]{2,1,0:T(8,128)(2,1)}, u32[]{:S(2)}, u32[]{:S(2)}) %all-to-all-start.1) | async-done | bytes 1966112 | tf_op jit(solution)/shard_map/all_to_all | solution.py:304
  185.7 3.9 %sum_parts.1 = f32[24,1,2560]{2,1,0:T(1,128)} custom-call(bf16[16,24,2560]{2,1,0:T(8,128)(2,1)} %all-to-all-done.1.parts_ref), custom_call_target="tpu_custom_call" | custom-call | flops 983040 | bytes 1966080 | tf_op jit(solution)/shard_map/sum_parts/pallas_call | solution.py:247
  (67 shorter events, 30.1 us)
Async XLA Ops:
  0.6 10.0 %copy-start.2 = (bf16[1,128,2560]{2,1,0:T(8,128)(2,1)S(1)}, bf16[1,128,2560]{2,1,0:T(8,128)(2,1)}, u32[]{:S(2)}) copy-start(bf16[1,128,2560]{2,1,0:T(8,128)(2,1)} %param.5) | copy-start | bytes 1966084
  3.1 50.3 %all-to-all-start = ((bf16[16,24,2560]{2,1,0:T(8,128)(2,1)}), bf16[16,24,2560]{2,1,0:T(8,128)(2,1)S(1)}, u32[]{:S(2)}, u32[]{:S(2)}) async-start(bf16[16,24,2560]{2,1,0:T(8,128)(2,1)} %copy-done.1), calls=%async_computation | async-start | bytes 3932160 | tf_op jit(solution)/shard_map/all_to_all | solution.py:304
  11.6 19.6 %collective-permute-start.4 = (bf16[136,1280]{1,0:T(8,128)(2,1)}, bf16[136,1280]{1,0:T(8,128)(2,1)}, u32[]{:S(2)}, u32[]{:S(2)}) collective-permute-start(bf16[136,1280]{1,0:T(8,128)(2,1)} %get-tuple-element.28.refs_3_), channel_id=1, source_target_pairs={{0,480},{32,0},{64,32},{96,64},{128,96},{160,128},{192,160},{224,1... | collective-permute-start | bytes 1044488 | tf_op jit(solution)/shard_map/ppermute | solution.py:319
  22.7 14.9 %collective-permute-start = (bf16[136,1280]{1,0:T(8,128)(2,1)}, bf16[136,1280]{1,0:T(8,128)(2,1)}, u32[]{:S(2)}, u32[]{:S(2)}) collective-permute-start(bf16[136,1280]{1,0:T(8,128)(2,1)} %get-tuple-element.28.refs_3_), channel_id=1, source_target_pairs={{0,32},{32,64},{64,96},{96,128},{128,160},{160,192},{192,224},{224... | collective-permute-start | bytes 1044488 | tf_op jit(solution)/shard_map/ppermute | solution.py:319
  24.6 16.9 %collective-permute-start.1 = (bf16[128,1280]{1,0:T(8,128)(2,1)}, bf16[128,1280]{1,0:T(8,128)(2,1)}, u32[]{:S(2)}, u32[]{:S(2)}) collective-permute-start(bf16[128,1280]{1,0:T(8,128)(2,1)} %get-tuple-element.29.refs_2_.refs_0_), channel_id=1, source_target_pairs={{0,32},{32,64},{64,96},{96,128},{128,160},{160,192},{192,224},{224... | collective-permute-start | bytes 983048 | tf_op jit(solution)/shard_map/ppermute | solution.py:319
  26.5 16.9 %collective-permute-start.3 = (bf16[128,1280]{1,0:T(8,128)(2,1)}, bf16[128,1280]{1,0:T(8,128)(2,1)}, u32[]{:S(2)}, u32[]{:S(2)}) collective-permute-start(bf16[128,1280]{1,0:T(8,128)(2,1)} %get-tuple-element.29.refs_2_.refs_0_), channel_id=1, source_target_pairs={{0,480},{32,0},{64,32},{96,64},{128,96},{160,128},{192,160},{224,1... | collective-permute-start | bytes 983048 | tf_op jit(solution)/shard_map/ppermute | solution.py:319
  31.1 16.9 %collective-permute-start.8 = (bf16[136,1280]{1,0:T(8,128)(2,1)}, bf16[136,1280]{1,0:T(8,128)(2,1)}, u32[]{:S(2)}, u32[]{:S(2)}) collective-permute-start(bf16[136,1280]{1,0:T(8,128)(2,1)} %collective-permute-done.4.refs_5_), channel_id=1, source_target_pairs={{0,480},{32,0},{64,32},{96,64},{128,96},{160,128},{192,160},{224,1... | collective-permute-start | bytes 1044488 | tf_op jit(solution)/shard_map/ppermute | solution.py:319
  37.6 12.4 %collective-permute-start.7 = (bf16[136,1280]{1,0:T(8,128)(2,1)}, bf16[136,1280]{1,0:T(8,128)(2,1)}, u32[]{:S(2)}, u32[]{:S(2)}) collective-permute-start(bf16[136,1280]{1,0:T(8,128)(2,1)} %collective-permute-done.refs_4_), channel_id=1, source_target_pairs={{0,32},{32,64},{64,96},{96,128},{128,160},{160,192},{192,224},{224... | collective-permute-start | bytes 1044488 | tf_op jit(solution)/shard_map/ppermute | solution.py:319
  41.5 14.0 %collective-permute-start.2 = (bf16[128,1280]{1,0:T(8,128)(2,1)}, bf16[128,1280]{1,0:T(8,128)(2,1)}, u32[]{:S(2)}, u32[]{:S(2)}) collective-permute-start(bf16[128,1280]{1,0:T(8,128)(2,1)} %collective-permute-done.1.refs_1_), channel_id=1, source_target_pairs={{0,32},{32,64},{64,96},{96,128},{128,160},{160,192},{192,224},{224... | collective-permute-start | bytes 983048 | tf_op jit(solution)/shard_map/ppermute | solution.py:319
  43.5 14.0 %collective-permute-start.6 = (bf16[128,1280]{1,0:T(8,128)(2,1)}, bf16[128,1280]{1,0:T(8,128)(2,1)}, u32[]{:S(2)}, u32[]{:S(2)}) collective-permute-start(bf16[128,1280]{1,0:T(8,128)(2,1)} %collective-permute-done.3.refs_2_), channel_id=1, source_target_pairs={{0,480},{32,0},{64,32},{96,64},{128,96},{160,128},{192,160},{224,1... | collective-permute-start | bytes 983048 | tf_op jit(solution)/shard_map/ppermute | solution.py:319
  48.1 14.0 %collective-permute-start.12 = (bf16[136,1280]{1,0:T(8,128)(2,1)}, bf16[136,1280]{1,0:T(8,128)(2,1)}, u32[]{:S(2)}, u32[]{:S(2)}) collective-permute-start(bf16[136,1280]{1,0:T(8,128)(2,1)} %collective-permute-done.8.refs_3_), channel_id=1, source_target_pairs={{0,480},{32,0},{64,32},{96,64},{128,96},{160,128},{192,160},{224,1... | collective-permute-start | bytes 1044488 | tf_op jit(solution)/shard_map/ppermute | solution.py:319
  50.0 15.7 %collective-permute-start.11 = (bf16[136,1280]{1,0:T(8,128)(2,1)}, bf16[136,1280]{1,0:T(8,128)(2,1)}, u32[]{:S(2)}, u32[]{:S(2)}) collective-permute-start(bf16[136,1280]{1,0:T(8,128)(2,1)} %collective-permute-done.7.refs_2_), channel_id=1, source_target_pairs={{0,32},{32,64},{64,96},{96,128},{128,160},{160,192},{192,224},{224... | collective-permute-start | bytes 1044488 | tf_op jit(solution)/shard_map/ppermute | solution.py:319
  55.5 14.4 %collective-permute-start.5 = (bf16[128,1280]{1,0:T(8,128)(2,1)}, bf16[128,1280]{1,0:T(8,128)(2,1)S(1)}, u32[]{:S(2)}, u32[]{:S(2)}) collective-permute-start(bf16[128,1280]{1,0:T(8,128)(2,1)} %collective-permute-done.2.refs_0_), channel_id=1, source_target_pairs={{0,32},{32,64},{64,96},{96,128},{128,160},{160,192},{192,224},{224... | collective-permute-start | bytes 983048 | tf_op jit(solution)/shard_map/ppermute | solution.py:319
  57.4 14.4 %collective-permute-start.10 = (bf16[128,1280]{1,0:T(8,128)(2,1)}, bf16[128,1280]{1,0:T(8,128)(2,1)S(1)}, u32[]{:S(2)}, u32[]{:S(2)}) collective-permute-start(bf16[128,1280]{1,0:T(8,128)(2,1)} %collective-permute-done.6.refs_1_), channel_id=1, source_target_pairs={{0,480},{32,0},{64,32},{96,64},{128,96},{160,128},{192,160},{224,1... | collective-permute-start | bytes 983048 | tf_op jit(solution)/shard_map/ppermute | solution.py:319
  62.0 14.4 %collective-permute-start.16 = (bf16[136,1280]{1,0:T(8,128)(2,1)}, bf16[136,1280]{1,0:T(8,128)(2,1)S(1)}, u32[]{:S(2)}, u32[]{:S(2)}) collective-permute-start(bf16[136,1280]{1,0:T(8,128)(2,1)} %collective-permute-done.12.refs_3_), channel_id=1, source_target_pairs={{0,480},{32,0},{64,32},{96,64},{128,96},{160,128},{192,160},{224,1... | collective-permute-start | bytes 1044488 | tf_op jit(solution)/shard_map/ppermute | solution.py:319
  65.7 13.5 %collective-permute-start.14 = (bf16[136,1280]{1,0:T(8,128)(2,1)}, bf16[136,1280]{1,0:T(8,128)(2,1)S(1)}, u32[]{:S(2)}, u32[]{:S(2)}) collective-permute-start(bf16[136,1280]{1,0:T(8,128)(2,1)} %collective-permute-done.11.refs_2_), channel_id=1, source_target_pairs={{0,32},{32,64},{64,96},{96,128},{128,160},{160,192},{192,224},{224... | collective-permute-start | bytes 1044488 | tf_op jit(solution)/shard_map/ppermute | solution.py:319
  69.9 13.4 %collective-permute-start.9 = (bf16[128,1280]{1,0:T(8,128)(2,1)S(1)}, bf16[128,1280]{1,0:T(8,128)(2,1)S(1)}, u32[]{:S(2)}, u32[]{:S(2)}) collective-permute-start(bf16[128,1280]{1,0:T(8,128)(2,1)S(1)} %collective-permute-done.5.refs_0_), channel_id=1, source_target_pairs={{0,32},{32,64},{64,96},{96,128},{128,160},{160,192},{192,224},{224... | collective-permute-start | bytes 983048 | tf_op jit(solution)/shard_map/ppermute | solution.py:319
  71.8 13.4 %collective-permute-start.18 = (bf16[128,1280]{1,0:T(8,128)(2,1)S(1)}, bf16[128,1280]{1,0:T(8,128)(2,1)S(1)}, u32[]{:S(2)}, u32[]{:S(2)}) collective-permute-start(bf16[128,1280]{1,0:T(8,128)(2,1)S(1)} %collective-permute-done.10.refs_1_), channel_id=1, source_target_pairs={{0,480},{32,0},{64,32},{96,64},{128,96},{160,128},{192,160},{224,1... | collective-permute-start | bytes 983048 | tf_op jit(solution)/shard_map/ppermute | solution.py:319
  76.4 13.8 %collective-permute-start.17 = (bf16[136,1280]{1,0:T(8,128)(2,1)S(1)}, bf16[136,1280]{1,0:T(8,128)(2,1)S(1)}, u32[]{:S(2)}, u32[]{:S(2)}) collective-permute-start(bf16[136,1280]{1,0:T(8,128)(2,1)S(1)} %collective-permute-done.16.refs_3_), channel_id=1, source_target_pairs={{0,480},{32,0},{64,32},{96,64},{128,96},{160,128},{192,160},{224,1... | collective-permute-start | bytes 1044488 | tf_op jit(solution)/shard_map/ppermute | solution.py:319
  79.2 14.0 %collective-permute-start.15 = (bf16[136,1280]{1,0:T(8,128)(2,1)S(1)}, bf16[136,1280]{1,0:T(8,128)(2,1)S(1)}, u32[]{:S(2)}, u32[]{:S(2)}) collective-permute-start(bf16[136,1280]{1,0:T(8,128)(2,1)S(1)} %collective-permute-done.14.refs_2_), channel_id=1, source_target_pairs={{0,32},{32,64},{64,96},{96,128},{128,160},{160,192},{192,224},{224... | collective-permute-start | bytes 1044488 | tf_op jit(solution)/shard_map/ppermute | solution.py:319
  83.3 14.5 %collective-permute-start.13 = (bf16[128,1280]{1,0:T(8,128)(2,1)S(1)}, bf16[128,1280]{1,0:T(8,128)(2,1)S(1)}, u32[]{:S(2)}, u32[]{:S(2)}) collective-permute-start(bf16[128,1280]{1,0:T(8,128)(2,1)S(1)} %collective-permute-done.9.refs_0_), channel_id=1, source_target_pairs={{0,32},{32,64},{64,96},{96,128},{128,160},{160,192},{192,224},{224... | collective-permute-start | bytes 983048 | tf_op jit(solution)/shard_map/ppermute | solution.py:319
  85.2 12.9 %collective-permute-start.20 = (bf16[128,1280]{1,0:T(8,128)(2,1)S(1)}, bf16[128,1280]{1,0:T(8,128)(2,1)S(1)}, u32[]{:S(2)}, u32[]{:S(2)}) collective-permute-start(bf16[128,1280]{1,0:T(8,128)(2,1)S(1)} %collective-permute-done.18.refs_1_), channel_id=1, source_target_pairs={{0,480},{32,0},{64,32},{96,64},{128,96},{160,128},{192,160},{224,1... | collective-permute-start | bytes 983048 | tf_op jit(solution)/shard_map/ppermute | solution.py:319
  90.3 22.3 %collective-permute-start.25 = (bf16[56,1280]{1,0:T(8,128)(2,1)S(1)}, bf16[56,1280]{1,0:T(8,128)(2,1)S(1)}, u32[]{:S(2)}, u32[]{:S(2)}) collective-permute-start(bf16[56,1280]{1,0:T(8,128)(2,1)S(1)} %get-tuple-element.47), channel_id=1, source_target_pairs={{0,416},{32,448},{64,480},{96,0},{128,32},{160,64},{192,96},{224,1... | collective-permute-start | bytes 430088 | tf_op jit(solution)/shard_map/ppermute | solution.py:319
  98.5 28.3 %collective-permute-start.23 = (bf16[56,2560]{1,0:T(8,128)(2,1)S(1)}, bf16[56,2560]{1,0:T(8,128)(2,1)S(1)}, u32[]{:S(2)}, u32[]{:S(2)}) collective-permute-start(bf16[56,2560]{1,0:T(8,128)(2,1)S(1)} %get-tuple-element.45), channel_id=1, source_target_pairs={{0,448},{32,480},{64,0},{96,32},{128,64},{160,96},{192,128},{224,1... | collective-permute-start | bytes 860168 | tf_op jit(solution)/shard_map/ppermute | solution.py:319
  100.4 26.4 %collective-permute-start.22 = (bf16[56,2560]{1,0:T(8,128)(2,1)S(1)}, bf16[56,2560]{1,0:T(8,128)(2,1)S(1)}, u32[]{:S(2)}, u32[]{:S(2)}) collective-permute-start(bf16[56,2560]{1,0:T(8,128)(2,1)S(1)} %get-tuple-element.44), channel_id=1, source_target_pairs={{0,64},{32,96},{64,128},{96,160},{128,192},{160,224},{192,256},{22... | collective-permute-start | bytes 860168 | tf_op jit(solution)/shard_map/ppermute | solution.py:319
  104.7 22.2 %collective-permute-start.21 = (bf16[56,2560]{1,0:T(8,128)(2,1)S(1)}, bf16[56,2560]{1,0:T(8,128)(2,1)S(1)}, u32[]{:S(2)}, u32[]{:S(2)}) collective-permute-start(bf16[56,2560]{1,0:T(8,128)(2,1)S(1)} %get-tuple-element.43), channel_id=1, source_target_pairs={{0,480},{32,0},{64,32},{96,64},{128,96},{160,128},{192,160},{224,1... | collective-permute-start | bytes 860168 | tf_op jit(solution)/shard_map/ppermute | solution.py:319
  110.7 16.2 %collective-permute-start.19 = (bf16[56,2560]{1,0:T(8,128)(2,1)S(1)}, bf16[56,2560]{1,0:T(8,128)(2,1)S(1)}, u32[]{:S(2)}, u32[]{:S(2)}) collective-permute-start(bf16[56,2560]{1,0:T(8,128)(2,1)S(1)} %get-tuple-element.41), channel_id=1, source_target_pairs={{0,32},{32,64},{64,96},{96,128},{128,160},{160,192},{192,224},{224... | collective-permute-start | bytes 860168 | tf_op jit(solution)/shard_map/ppermute | solution.py:319
  112.6 14.2 %collective-permute-start.24 = (bf16[56,1280]{1,0:T(8,128)(2,1)S(1)}, bf16[56,1280]{1,0:T(8,128)(2,1)S(1)}, u32[]{:S(2)}, u32[]{:S(2)}) collective-permute-start(bf16[56,1280]{1,0:T(8,128)(2,1)S(1)} %get-tuple-element.46), channel_id=1, source_target_pairs={{0,96},{32,128},{64,160},{96,192},{128,224},{160,256},{192,288},{2... | collective-permute-start | bytes 430088 | tf_op jit(solution)/shard_map/ppermute | solution.py:319
  127.0 20.6 %copy-start = (bf16[16,56,2560]{2,1,0:T(8,128)(2,1)}, bf16[16,56,2560]{2,1,0:T(8,128)(2,1)S(1)}, u32[]{:S(2)}) copy-start(bf16[16,56,2560]{2,1,0:T(8,128)(2,1)S(1)} %place_near.1) | copy-start | bytes 13762564
  130.3 17.3 %collective-permute-start.26 = (bf16[384,2560]{1,0:T(8,128)(2,1)S(1)}, bf16[384,2560]{1,0:T(8,128)(2,1)S(1)}, u32[]{:S(2)}, u32[]{:S(2)}) collective-permute-start(bf16[384,2560]{1,0:T(8,128)(2,1)S(1)} %term_other.1), channel_id=1, source_target_pairs={{0,1},{1,0},{2,3},{3,2},{4,5},{5,4},{6,7},{7,6},{8,9},{9,8},{10,11... | collective-permute-start | bytes 5898248 | tf_op jit(solution)/shard_map/ppermute | solution.py:309
  142.4 13.8 %collective-permute-start.27 = (bf16[16,24,2560]{2,1,0:T(8,128)(2,1)S(1)}, bf16[16,24,2560]{2,1,0:T(8,128)(2,1)}, u32[]{:S(2)}, u32[]{:S(2)}) collective-permute-start(bf16[16,24,2560]{2,1,0:T(8,128)(2,1)S(1)} %all-to-all-done.refs_6_), channel_id=1, source_target_pairs={{0,1},{1,0},{2,3},{3,2},{4,5},{5,4},{6,7},{7,6},{8,9},{9,8},{10,11... | collective-permute-start | bytes 5898248 | tf_op jit(solution)/shard_map/ppermute | solution.py:309
  149.5 36.2 %all-to-all-start.1 = ((bf16[16,24,2560]{2,1,0:T(8,128)(2,1)}), bf16[16,24,2560]{2,1,0:T(8,128)(2,1)}, u32[]{:S(2)}, u32[]{:S(2)}) async-start(bf16[16,24,2560]{2,1,0:T(8,128)(2,1)} %bitcast.29), calls=%async_computation.1 | async-start | bytes 3932160 | tf_op jit(solution)/shard_map/all_to_all | solution.py:304
  (7 other events, 26.3 us)

commit v7 on v6

--- a/solution.py
+++ b/solution.py
@@ -201,15 +201,20 @@
 
 
 def _copies(array, copies):
-    def kernel(array_ref, out_ref):
+    def kernel(array_ref, out_ref, sems):
+        started = []
         for i in range(copies):
-            out_ref[i] = array_ref[...]
+            started.append(pltpu.make_async_copy(array_ref, out_ref.at[i], sems.at[i]))
+            started[-1].start()
+        for copy in started:
+            copy.wait()
 
     return pl.pallas_call(
         kernel,
         in_specs=[pl.BlockSpec(memory_space=pltpu.VMEM)],
-        out_specs=pl.BlockSpec(memory_space=pltpu.VMEM),
-        out_shape=jax.ShapeDtypeStruct((copies,) + array.shape, BF),
+        out_specs=pl.BlockSpec(memory_space=pltpu.HBM),
+        out_shape=pltpu.HBM((copies,) + array.shape, BF),
+        scratch_shapes=[pltpu.SemaphoreType.DMA((copies,))],
         compiler_params=pltpu.CompilerParams(vmem_limit_bytes=VMEM),
         cost_estimate=pl.CostEstimate(
             flops=0, bytes_accessed=2 * (copies + 1) * array.size, transcendentals=0
@@ -218,63 +223,27 @@
     )(array)
 
 
-def _once(array, after):
-    def kernel(*_):
-        pass
-
-    return pl.pallas_call(
-        kernel,
-        in_specs=[pl.BlockSpec(memory_space=pltpu.HBM), pl.BlockSpec(memory_space=pl.ANY)],
-        out_specs=pl.BlockSpec(memory_space=pltpu.HBM),
-        out_shape=pltpu.HBM(array.shape, BF),
-        input_output_aliases={0: 0},
-        cost_estimate=pl.CostEstimate(flops=0, bytes_accessed=0, transcendentals=0),
-        name="once",
-    )(array, after)
-
-
-def _sum_kernel(parts_ref, out_ref):
-    total = parts_ref[0].astype(F32)
-    for i in range(1, parts_ref.shape[0]):
-        total += parts_ref[i].astype(F32)
-    for i in range(total.shape[0]):
-        out_ref[i, :, :] = total[i : i + 1, :]
-
-
-def _sum(parts):
-    chips, units, width = parts.shape
-    block = 512 if width % 512 == 0 else LANES
-    return pl.pallas_call(
-        _sum_kernel,
-        grid=(width // block,),
-        in_specs=[pl.BlockSpec((chips, units, block), lambda j: (0, 0, j))],
-        out_specs=pl.BlockSpec((units, 1, block), lambda j: (0, 0, j)),
-        out_shape=jax.ShapeDtypeStruct((units, 1, width), F32),
-        compiler_params=pltpu.CompilerParams(vmem_limit_bytes=VMEM),
-        cost_estimate=pl.CostEstimate(
-            flops=parts.size, bytes_accessed=2 * parts.size, transcendentals=0
-        ),
-        name="sum_parts",
-    )(parts)
-
-
-def _term_kernel(saved_ref, rows_ref, out_ref):
-    out_ref[...] = jnp.dot(saved_ref[...], rows_ref[...], preferred_element_type=F32).astype(BF)
-
-
-def _term(saved_t, rows, name):
+def _term(saved_t, rows, name, more=None):
     units, depth = saved_t.shape
     width = rows.shape[1]
     block = 512 if width % 512 == 0 else LANES
-    return pl.pallas_call(
-        _term_kernel,
+
+    def kernel(saved_ref, rows_ref, *refs):
+        columns = pl.ds(pl.multiple_of(pl.program_id(0) * block, block), block)
+        term = jnp.dot(saved_ref[...], rows_ref[:, columns], preferred_element_type=F32).astype(BF)
+        if more is not None:
+            term = (term.astype(F32) + refs[0][:, columns].astype(F32)).astype(BF)
+        refs[-1][...] = term
+
+    operands = [saved_t, rows] + ([] if more is None else [more])
+    return pl.pallas_call(
+        kernel,
         grid=(width // block,),
-        in_specs=[
-            pl.BlockSpec((units, depth), lambda j: (0, 0)),
-            pl.BlockSpec((depth, block), lambda j: (0, j)),
-        ],
+        in_specs=[pl.BlockSpec(memory_space=pltpu.VMEM)] * len(operands),
         out_specs=pl.BlockSpec((units, block), lambda j: (0, j)),
-        out_shape=jax.ShapeDtypeStruct((units, width), BF),
+        out_shape=jax.ShapeDtypeStruct((units, width), BF)
+        if more is None
+        else pltpu.HBM((units, width), BF),
         compiler_params=pltpu.CompilerParams(vmem_limit_bytes=VMEM),
         cost_estimate=pl.CostEstimate(
             flops=2 * units * depth * width,
@@ -282,7 +251,7 @@
             transcendentals=0,
         ),
         name=name,
-    )(saved_t, rows)
+    )(*operands)
 
 
 def body(grads, routes, gates, hidden, down_weight):
@@ -357,15 +326,15 @@
     rows = pick(rows, [-relay, relay], f"select_{relay}")
     up_2, down_2, far_up = shift(up_2, 2), shift(down_2, -2), shift(up_3, 3)
     up_1, down_1 = shift(up_1, 1), shift(down_1, -1)
-    parts = [(-relay - 2, 0, up_2), (relay + 2, 0, down_2), (far, 0, far_up), (far, half, far_down)]
-    rows = _place(me, parts, rows, "place_far")
-    rows = _place(me, [(-relay - 1, 0, up_1), (relay + 1, 0, down_1)], rows, "place_near")
+    parts = [(-relay - 2, 0, up_2), (relay + 2, 0, down_2), (far, half, far_down)]
+    rows = _place(me, parts, rows, "place_early")
+    parts = [(-relay - 1, 0, up_1), (relay + 1, 0, down_1), (far, 0, far_up)]
+    rows = _place(me, parts, rows, "place_late")
     rows = rows.reshape(rows_dev, width)
 
     other = _term(saved_other, rows, "term_other")
     arrived = other_core(other)
-    mine = _term(saved_mine, rows, "term_mine")
-    pair = (mine.astype(F32) + arrived.astype(F32)).astype(BF)
+    pair = _term(saved_mine, rows, "term_pair", arrived)
     pair, rows = lax.optimization_barrier((pair, rows))
     sums = over_chips(pair.reshape(chips, units_dev, width))
 
@@ -378,7 +347,7 @@
     d_rows = lax.dot_general(rows, both, (((1,), (1,)), ((), ())), preferred_element_type=F32)
     d_hidden = d_rows.astype(BF)[None]
     sums, d_hidden = lax.optimization_barrier((sums, d_hidden))
-    down_grad = _sum(sums)
+    down_grad = jnp.sum(sums.astype(F32), axis=0)[:, None, :]
     return (d_hidden, down_grad)
 
 

time: 192 us -> 191 us (level)
  Pallas kernels: 19.5 us -> 17.4 us
    pallas_call x3 -> x2, Pallas kernels: 10.5 us -> 7.03 us  [_term(): pl.pallas_call(kernel, grid=(width // block,), in_specs=[pl.BlockSpec(mem...]
    unnamed x18 -> x16, local copies, waits for them, and re-layouts: 4.33 us -> 3 us
  transfers between devices with their start and end apart: 30 -> 30, of which waited for: 7 -> 8; matrix products, arithmetic and copies ran while one was open for 5% -> 4% of each run, Pallas kernels for 6% -> 7%
where the time goes in v7:
time: 191 us; the launch traced here: 189 us
  starting transfers between devices  114 us (60%)
  waiting for transfers between devices  42.5 us (22%)
  Pallas kernels  17.4 us (9%)
  matrix products  4.79 us (3%)
  other arithmetic  4.48 us (2%)
  local copies, waits for them, and re-layouts  4.33 us (2%)
    ppermute x26, starting transfers between devices, shift(): lax.ppermute(array, 'expert', [(i, (i + places) % groups) for i in range(...  85.9 us
    all_to_all x2, waiting for transfers between devices, over_chips(): lax.all_to_all(array, 'replica', split_axis=0, concat_axis=0, tiled=True,...  21.3 us
    ppermute x26, waiting for transfers between devices, shift(): lax.ppermute(array, 'expert', [(i, (i + places) % groups) for i in range(...  19.6 us
    all_to_all x2, starting transfers between devices, over_chips(): lax.all_to_all(array, 'replica', split_axis=0, concat_axis=0, tiled=True,...  14.2 us
    ppermute x2, starting transfers between devices, other_core(): return lax.ppermute(array, 'replica', [(i, i ^ 1) for i in range(replicas)])  14.1 us
    pallas_call x2, Pallas kernels, _term(): pl.pallas_call(kernel, grid=(width // block,), in_specs=[pl.BlockSpec(mem...  7.03 us
    pallas_call x5, Pallas kernels, _select(): pl.pallas_call(kernel, in_specs=[pl.BlockSpec(memory_space=pltpu.SMEM)] +...  5.58 us
    dot_general x1, matrix products, body(): lax.dot_general(rows, both, (((1,), (1,)), ((), ())), preferred_element_t...  4.79 us
  transfers between devices with their start and end apart: 30, of which 8 were waited for; matrix products, arithmetic and copies ran while one was open for 4% of the time, Pallas kernels for 7%

profile of v7, /device:TPU:1, one launch (start us, length us, event | category | flops | bytes accessed | tf_op | source)
XLA Modules:
  0.0 189.0 jit_solution(4275966681116474650)
XLA Ops:
  3.1 7.6 %all-to-all-start = ((bf16[16,24,2560]{2,1,0:T(8,128)(2,1)}), bf16[16,24,2560]{2,1,0:T(8,128)(2,1)S(1)}, u32[]{:S(2)}, u32[]{:S(2)}) async-start(bf16[16,24,2560]{2,1,0:T(8,128)(2,1)} %unit_copies.1), calls=%async_computation | async-start | bytes 3932160 | tf_op jit(solution)/shard_map/all_to_all | solution.py:273
  11.6 11.1 %collective-permute-start.4 = (bf16[136,1280]{1,0:T(8,128)(2,1)}, bf16[136,1280]{1,0:T(8,128)(2,1)}, u32[]{:S(2)}, u32[]{:S(2)}) collective-permute-start(bf16[136,1280]{1,0:T(8,128)(2,1)} %get-tuple-element.28.refs_3_), channel_id=1, source_target_pairs={{0,480},{32,0},{64,32},{96,64},{128,96},{160,128},{192,160},{224,1... | collective-permute-start | bytes 1044488 | tf_op jit(solution)/shard_map/ppermute | solution.py:288
  22.7 1.9 %collective-permute-start = (bf16[136,1280]{1,0:T(8,128)(2,1)}, bf16[136,1280]{1,0:T(8,128)(2,1)}, u32[]{:S(2)}, u32[]{:S(2)}) collective-permute-start(bf16[136,1280]{1,0:T(8,128)(2,1)} %get-tuple-element.28.refs_3_), channel_id=1, source_target_pairs={{0,32},{32,64},{64,96},{96,128},{128,160},{160,192},{192,224},{224... | collective-permute-start | bytes 1044488 | tf_op jit(solution)/shard_map/ppermute | solution.py:288
  24.6 1.9 %collective-permute-start.1 = (bf16[128,1280]{1,0:T(8,128)(2,1)}, bf16[128,1280]{1,0:T(8,128)(2,1)}, u32[]{:S(2)}, u32[]{:S(2)}) collective-permute-start(bf16[128,1280]{1,0:T(8,128)(2,1)} %get-tuple-element.29.refs_2_.refs_0_), channel_id=1, source_target_pairs={{0,32},{32,64},{64,96},{96,128},{128,160},{160,192},{192,224},{224... | collective-permute-start | bytes 983048 | tf_op jit(solution)/shard_map/ppermute | solution.py:288
  26.6 4.6 %collective-permute-start.3 = (bf16[128,1280]{1,0:T(8,128)(2,1)}, bf16[128,1280]{1,0:T(8,128)(2,1)}, u32[]{:S(2)}, u32[]{:S(2)}) collective-permute-start(bf16[128,1280]{1,0:T(8,128)(2,1)} %get-tuple-element.29.refs_2_.refs_0_), channel_id=1, source_target_pairs={{0,480},{32,0},{64,32},{96,64},{128,96},{160,128},{192,160},{224,1... | collective-permute-start | bytes 983048 | tf_op jit(solution)/shard_map/ppermute | solution.py:288
  31.1 3.6 %collective-permute-start.8 = (bf16[136,1280]{1,0:T(8,128)(2,1)}, bf16[136,1280]{1,0:T(8,128)(2,1)}, u32[]{:S(2)}, u32[]{:S(2)}) collective-permute-start(bf16[136,1280]{1,0:T(8,128)(2,1)} %collective-permute-done.4.refs_5_), channel_id=1, source_target_pairs={{0,480},{32,0},{64,32},{96,64},{128,96},{160,128},{192,160},{224,1... | collective-permute-start | bytes 1044488 | tf_op jit(solution)/shard_map/ppermute | solution.py:288
  37.6 1.9 %collective-permute-start.7 = (bf16[136,1280]{1,0:T(8,128)(2,1)}, bf16[136,1280]{1,0:T(8,128)(2,1)}, u32[]{:S(2)}, u32[]{:S(2)}) collective-permute-start(bf16[136,1280]{1,0:T(8,128)(2,1)} %collective-permute-done.refs_4_), channel_id=1, source_target_pairs={{0,32},{32,64},{64,96},{96,128},{128,160},{160,192},{192,224},{224... | collective-permute-start | bytes 1044488 | tf_op jit(solution)/shard_map/ppermute | solution.py:288
  39.5 2.0 %collective-permute-done.1.refs_1_ = bf16[128,1280]{1,0:T(8,128)(2,1)} collective-permute-done((bf16[128,1280]{1,0:T(8,128)(2,1)}, bf16[128,1280]{1,0:T(8,128)(2,1)}, u32[]{:S(2)}, u32[]{:S(2)}) %collective-permute-start.1) | collective-permute-done | bytes 327712 | tf_op jit(solution)/shard_map/ppermute | solution.py:288
  43.5 4.6 %collective-permute-start.6 = (bf16[128,1280]{1,0:T(8,128)(2,1)}, bf16[128,1280]{1,0:T(8,128)(2,1)}, u32[]{:S(2)}, u32[]{:S(2)}) collective-permute-start(bf16[128,1280]{1,0:T(8,128)(2,1)} %collective-permute-done.3.refs_2_), channel_id=1, source_target_pairs={{0,480},{32,0},{64,32},{96,64},{128,96},{160,128},{192,160},{224,1... | collective-permute-start | bytes 983048 | tf_op jit(solution)/shard_map/ppermute | solution.py:288
  48.1 1.9 %collective-permute-start.12 = (bf16[136,1280]{1,0:T(8,128)(2,1)}, bf16[136,1280]{1,0:T(8,128)(2,1)}, u32[]{:S(2)}, u32[]{:S(2)}) collective-permute-start(bf16[136,1280]{1,0:T(8,128)(2,1)} %collective-permute-done.8.refs_3_), channel_id=1, source_target_pairs={{0,480},{32,0},{64,32},{96,64},{128,96},{160,128},{192,160},{224,1... | collective-permute-start | bytes 1044488 | tf_op jit(solution)/shard_map/ppermute | solution.py:288
  50.0 3.4 %collective-permute-start.11 = (bf16[136,1280]{1,0:T(8,128)(2,1)}, bf16[136,1280]{1,0:T(8,128)(2,1)}, u32[]{:S(2)}, u32[]{:S(2)}) collective-permute-start(bf16[136,1280]{1,0:T(8,128)(2,1)} %collective-permute-done.7.refs_2_), channel_id=1, source_target_pairs={{0,32},{32,64},{64,96},{96,128},{128,160},{160,192},{192,224},{224... | collective-permute-start | bytes 1044488 | tf_op jit(solution)/shard_map/ppermute | solution.py:288
  57.4 4.6 %collective-permute-start.10 = (bf16[128,1280]{1,0:T(8,128)(2,1)}, bf16[128,1280]{1,0:T(8,128)(2,1)S(1)}, u32[]{:S(2)}, u32[]{:S(2)}) collective-permute-start(bf16[128,1280]{1,0:T(8,128)(2,1)} %collective-permute-done.6.refs_1_), channel_id=1, source_target_pairs={{0,480},{32,0},{64,32},{96,64},{128,96},{160,128},{192,160},{224,1... | collective-permute-start | bytes 983048 | tf_op jit(solution)/shard_map/ppermute | solution.py:288
  62.0 3.6 %collective-permute-start.16 = (bf16[136,1280]{1,0:T(8,128)(2,1)}, bf16[136,1280]{1,0:T(8,128)(2,1)S(1)}, u32[]{:S(2)}, u32[]{:S(2)}) collective-permute-start(bf16[136,1280]{1,0:T(8,128)(2,1)} %collective-permute-done.12.refs_3_), channel_id=1, source_target_pairs={{0,480},{32,0},{64,32},{96,64},{128,96},{160,128},{192,160},{224,1... | collective-permute-start | bytes 1044488 | tf_op jit(solution)/shard_map/ppermute | solution.py:288
  71.8 4.6 %collective-permute-start.18 = (bf16[128,1280]{1,0:T(8,128)(2,1)S(1)}, bf16[128,1280]{1,0:T(8,128)(2,1)S(1)}, u32[]{:S(2)}, u32[]{:S(2)}) collective-permute-start(bf16[128,1280]{1,0:T(8,128)(2,1)S(1)} %collective-permute-done.10.refs_1_), channel_id=1, source_target_pairs={{0,480},{32,0},{64,32},{96,64},{128,96},{160,128},{192,160},{224,1... | collective-permute-start | bytes 983048 | tf_op jit(solution)/shard_map/ppermute | solution.py:288
  76.4 2.7 %collective-permute-start.17 = (bf16[136,1280]{1,0:T(8,128)(2,1)S(1)}, bf16[136,1280]{1,0:T(8,128)(2,1)S(1)}, u32[]{:S(2)}, u32[]{:S(2)}) collective-permute-start(bf16[136,1280]{1,0:T(8,128)(2,1)S(1)} %collective-permute-done.16.refs_3_), channel_id=1, source_target_pairs={{0,480},{32,0},{64,32},{96,64},{128,96},{160,128},{192,160},{224,1... | collective-permute-start | bytes 1044488 | tf_op jit(solution)/shard_map/ppermute | solution.py:288
  79.2 2.5 %collective-permute-start.15 = (bf16[136,1280]{1,0:T(8,128)(2,1)S(1)}, bf16[136,1280]{1,0:T(8,128)(2,1)S(1)}, u32[]{:S(2)}, u32[]{:S(2)}) collective-permute-start(bf16[136,1280]{1,0:T(8,128)(2,1)S(1)} %collective-permute-done.14.refs_2_), channel_id=1, source_target_pairs={{0,32},{32,64},{64,96},{96,128},{128,160},{160,192},{192,224},{224... | collective-permute-start | bytes 1044488 | tf_op jit(solution)/shard_map/ppermute | solution.py:288
  85.2 4.6 %collective-permute-start.20 = (bf16[128,1280]{1,0:T(8,128)(2,1)S(1)}, bf16[128,1280]{1,0:T(8,128)(2,1)S(1)}, u32[]{:S(2)}, u32[]{:S(2)}) collective-permute-start(bf16[128,1280]{1,0:T(8,128)(2,1)S(1)} %collective-permute-done.18.refs_1_), channel_id=1, source_target_pairs={{0,480},{32,0},{64,32},{96,64},{128,96},{160,128},{192,160},{224,1... | collective-permute-start | bytes 983048 | tf_op jit(solution)/shard_map/ppermute | solution.py:288
  90.4 2.8 %collective-permute-start.25 = (bf16[56,1280]{1,0:T(8,128)(2,1)S(1)}, bf16[56,1280]{1,0:T(8,128)(2,1)S(1)}, u32[]{:S(2)}, u32[]{:S(2)}) collective-permute-start(bf16[56,1280]{1,0:T(8,128)(2,1)S(1)} %get-tuple-element.47), channel_id=1, source_target_pairs={{0,416},{32,448},{64,480},{96,0},{128,32},{160,64},{192,96},{224,1... | collective-permute-start | bytes 430088 | tf_op jit(solution)/shard_map/ppermute | solution.py:288
  93.2 4.6 %collective-permute-done.13.first_ref.refs_0_ = bf16[128,1280]{1,0:T(8,128)(2,1)S(1)} collective-permute-done((bf16[128,1280]{1,0:T(8,128)(2,1)S(1)}, bf16[128,1280]{1,0:T(8,128)(2,1)S(1)}, u32[]{:S(2)}, u32[]{:S(2)}) %collective-permute-start.13) | collective-permute-done | bytes 327712 | tf_op jit(solution)/shard_map/ppermute | solution.py:288
  98.5 1.9 %collective-permute-start.24 = (bf16[56,2560]{1,0:T(8,128)(2,1)S(1)}, bf16[56,2560]{1,0:T(8,128)(2,1)S(1)}, u32[]{:S(2)}, u32[]{:S(2)}) collective-permute-start(bf16[56,2560]{1,0:T(8,128)(2,1)S(1)} %get-tuple-element.46), channel_id=1, source_target_pairs={{0,448},{32,480},{64,0},{96,32},{128,64},{160,96},{192,128},{224,1... | collective-permute-start | bytes 860168 | tf_op jit(solution)/shard_map/ppermute | solution.py:288
  100.4 4.3 %collective-permute-start.23 = (bf16[56,2560]{1,0:T(8,128)(2,1)S(1)}, bf16[56,2560]{1,0:T(8,128)(2,1)S(1)}, u32[]{:S(2)}, u32[]{:S(2)}) collective-permute-start(bf16[56,2560]{1,0:T(8,128)(2,1)S(1)} %get-tuple-element.45), channel_id=1, source_target_pairs={{0,64},{32,96},{64,128},{96,160},{128,192},{160,224},{192,256},{22... | collective-permute-start | bytes 860168 | tf_op jit(solution)/shard_map/ppermute | solution.py:288
  104.7 6.0 %collective-permute-start.21 = (bf16[56,2560]{1,0:T(8,128)(2,1)S(1)}, bf16[56,2560]{1,0:T(8,128)(2,1)S(1)}, u32[]{:S(2)}, u32[]{:S(2)}) collective-permute-start(bf16[56,2560]{1,0:T(8,128)(2,1)S(1)} %get-tuple-element.43), channel_id=1, source_target_pairs={{0,480},{32,0},{64,32},{96,64},{128,96},{160,128},{192,160},{224,1... | collective-permute-start | bytes 860168 | tf_op jit(solution)/shard_map/ppermute | solution.py:288
  110.7 1.9 %collective-permute-start.19 = (bf16[56,2560]{1,0:T(8,128)(2,1)S(1)}, bf16[56,2560]{1,0:T(8,128)(2,1)S(1)}, u32[]{:S(2)}, u32[]{:S(2)}) collective-permute-start(bf16[56,2560]{1,0:T(8,128)(2,1)S(1)} %get-tuple-element.41), channel_id=1, source_target_pairs={{0,32},{32,64},{64,96},{96,128},{128,160},{160,192},{192,224},{224... | collective-permute-start | bytes 860168 | tf_op jit(solution)/shard_map/ppermute | solution.py:288
  115.0 11.8 %collective-permute-done.22.refs_2_ = bf16[56,1280]{1,0:T(8,128)(2,1)S(1)} collective-permute-done((bf16[56,1280]{1,0:T(8,128)(2,1)S(1)}, bf16[56,1280]{1,0:T(8,128)(2,1)S(1)}, u32[]{:S(2)}, u32[]{:S(2)}) %collective-permute-start.22) | collective-permute-done | bytes 143392 | tf_op jit(solution)/shard_map/ppermute | solution.py:288
  126.9 3.0 %term_other.1 = bf16[384,2560]{1,0:T(8,128)(2,1)S(1)} custom-call(bf16[384,896]{1,0:T(8,128)(2,1)S(1)} %get-tuple-element.49.saved_ref, bf16[896,2560]{1,0:T(8,128)(2,1)S(1)} %bitcast.18), custom_call_target="tpu_custom_call" | custom-call | flops 1761607680 | bytes 7241728 | tf_op jit(solution)/shard_map/term_other/pallas_call | solution.py:239
  129.9 12.2 %collective-permute-start.26 = (bf16[384,2560]{1,0:T(8,128)(2,1)S(1)}, bf16[384,2560]{1,0:T(8,128)(2,1)S(1)}, u32[]{:S(2)}, u32[]{:S(2)}) collective-permute-start(bf16[384,2560]{1,0:T(8,128)(2,1)S(1)} %term_other.1), channel_id=1, source_target_pairs={{0,1},{1,0},{2,3},{3,2},{4,5},{5,4},{6,7},{7,6},{8,9},{9,8},{10,11... | collective-permute-start | bytes 5898248 | tf_op jit(solution)/shard_map/ppermute | solution.py:278
  142.1 1.9 %collective-permute-start.27 = (bf16[16,24,2560]{2,1,0:T(8,128)(2,1)S(1)}, bf16[16,24,2560]{2,1,0:T(8,128)(2,1)}, u32[]{:S(2)}, u32[]{:S(2)}) collective-permute-start(bf16[16,24,2560]{2,1,0:T(8,128)(2,1)S(1)} %all-to-all-done.refs_6_), channel_id=1, source_target_pairs={{0,1},{1,0},{2,3},{3,2},{4,5},{5,4},{6,7},{7,6},{8,9},{9,8},{10,11... | collective-permute-start | bytes 5898248 | tf_op jit(solution)/shard_map/ppermute | solution.py:278
  145.7 4.1 %term_pair.1 = bf16[384,2560]{1,0:T(8,128)(2,1)} custom-call(bf16[384,896]{1,0:T(8,128)(2,1)S(1)} %get-tuple-element.32.saved_ref, bf16[896,2560]{1,0:T(8,128)(2,1)S(1)} %bitcast.19, bf16[384,2560]{1,0:T(8,128)(2,1)S(1)} %collective-permute-done.26.refs_0_), custom_call_target="tpu_custom_call" | custom-call | flops 1761607680 | bytes 7241728 | tf_op jit(solution)/shard_map/term_pair/pallas_call | solution.py:239
  149.7 6.6 %all-to-all-start.1 = ((bf16[16,24,2560]{2,1,0:T(8,128)(2,1)}), bf16[16,24,2560]{2,1,0:T(8,128)(2,1)}, u32[]{:S(2)}, u32[]{:S(2)}) async-start(bf16[16,24,2560]{2,1,0:T(8,128)(2,1)} %bitcast.29), calls=%async_computation.1 | async-start | bytes 3932160 | tf_op jit(solution)/shard_map/all_to_all | solution.py:273
  156.3 2.6 %maximum_select_fusion = bf16[16,2,24,2560]{3,2,0,1:T(8,128)(2,1)S(1)} fusion(bf16[16,1,24,2560]{3,2,0,1:T(8,128)(2,1)} %bitcast.11, bf16[16,1,24,2560]{3,2,0,1:T(8,128)(2,1)S(1)} %bitcast.23, pred[]{:T(512)S(6)} %eq.3), kind=kLoop, calls=%fused_computation | loop fusion | flops 5898240 | bytes 7864321 | tf_op jit(solution)/shard_map/jit(_where)/select_n | solution.py:342
  160.2 4.8 %fusion = bf16[1,896,768]{2,1,0:T(8,128)(2,1)} fusion(bf16[896,2560]{1,0:T(8,128)(2,1)S(1)} %bitcast.22, bf16[768,2560]{1,0:T(8,128)(2,1)S(1)} %bitcast.30), kind=kOutput, calls=%fused_computation.3 | convolution fusion | flops 3523903488 | bytes 9895936 | tf_op jit(solution)/shard_map/dot_general | solution.py:347
  164.9 21.3 %all-to-all-done.1 = bf16[16,24,2560]{2,1,0:T(8,128)(2,1)} async-done(((bf16[16,24,2560]{2,1,0:T(8,128)(2,1)}), bf16[16,24,2560]{2,1,0:T(8,128)(2,1)}, u32[]{:S(2)}, u32[]{:S(2)}) %all-to-all-start.1) | async-done | bytes 1966112 | tf_op jit(solution)/shard_map/all_to_all | solution.py:273
  (65 shorter events, 30.7 us)
Async XLA Ops:
  0.6 10.0 %copy-start.1 = (bf16[1,128,2560]{2,1,0:T(8,128)(2,1)S(1)}, bf16[1,128,2560]{2,1,0:T(8,128)(2,1)}, u32[]{:S(2)}) copy-start(bf16[1,128,2560]{2,1,0:T(8,128)(2,1)} %param.5) | copy-start | bytes 1966084
  3.1 50.3 %all-to-all-start = ((bf16[16,24,2560]{2,1,0:T(8,128)(2,1)}), bf16[16,24,2560]{2,1,0:T(8,128)(2,1)S(1)}, u32[]{:S(2)}, u32[]{:S(2)}) async-start(bf16[16,24,2560]{2,1,0:T(8,128)(2,1)} %unit_copies.1), calls=%async_computation | async-start | bytes 3932160 | tf_op jit(solution)/shard_map/all_to_all | solution.py:273
  11.6 19.6 %collective-permute-start.4 = (bf16[136,1280]{1,0:T(8,128)(2,1)}, bf16[136,1280]{1,0:T(8,128)(2,1)}, u32[]{:S(2)}, u32[]{:S(2)}) collective-permute-start(bf16[136,1280]{1,0:T(8,128)(2,1)} %get-tuple-element.28.refs_3_), channel_id=1, source_target_pairs={{0,480},{32,0},{64,32},{96,64},{128,96},{160,128},{192,160},{224,1... | collective-permute-start | bytes 1044488 | tf_op jit(solution)/shard_map/ppermute | solution.py:288
  22.7 14.9 %collective-permute-start = (bf16[136,1280]{1,0:T(8,128)(2,1)}, bf16[136,1280]{1,0:T(8,128)(2,1)}, u32[]{:S(2)}, u32[]{:S(2)}) collective-permute-start(bf16[136,1280]{1,0:T(8,128)(2,1)} %get-tuple-element.28.refs_3_), channel_id=1, source_target_pairs={{0,32},{32,64},{64,96},{96,128},{128,160},{160,192},{192,224},{224... | collective-permute-start | bytes 1044488 | tf_op jit(solution)/shard_map/ppermute | solution.py:288
  24.6 16.9 %collective-permute-start.1 = (bf16[128,1280]{1,0:T(8,128)(2,1)}, bf16[128,1280]{1,0:T(8,128)(2,1)}, u32[]{:S(2)}, u32[]{:S(2)}) collective-permute-start(bf16[128,1280]{1,0:T(8,128)(2,1)} %get-tuple-element.29.refs_2_.refs_0_), channel_id=1, source_target_pairs={{0,32},{32,64},{64,96},{96,128},{128,160},{160,192},{192,224},{224... | collective-permute-start | bytes 983048 | tf_op jit(solution)/shard_map/ppermute | solution.py:288
  26.6 16.9 %collective-permute-start.3 = (bf16[128,1280]{1,0:T(8,128)(2,1)}, bf16[128,1280]{1,0:T(8,128)(2,1)}, u32[]{:S(2)}, u32[]{:S(2)}) collective-permute-start(bf16[128,1280]{1,0:T(8,128)(2,1)} %get-tuple-element.29.refs_2_.refs_0_), channel_id=1, source_target_pairs={{0,480},{32,0},{64,32},{96,64},{128,96},{160,128},{192,160},{224,1... | collective-permute-start | bytes 983048 | tf_op jit(solution)/shard_map/ppermute | solution.py:288
  31.1 16.9 %collective-permute-start.8 = (bf16[136,1280]{1,0:T(8,128)(2,1)}, bf16[136,1280]{1,0:T(8,128)(2,1)}, u32[]{:S(2)}, u32[]{:S(2)}) collective-permute-start(bf16[136,1280]{1,0:T(8,128)(2,1)} %collective-permute-done.4.refs_5_), channel_id=1, source_target_pairs={{0,480},{32,0},{64,32},{96,64},{128,96},{160,128},{192,160},{224,1... | collective-permute-start | bytes 1044488 | tf_op jit(solution)/shard_map/ppermute | solution.py:288
  37.6 12.4 %collective-permute-start.7 = (bf16[136,1280]{1,0:T(8,128)(2,1)}, bf16[136,1280]{1,0:T(8,128)(2,1)}, u32[]{:S(2)}, u32[]{:S(2)}) collective-permute-start(bf16[136,1280]{1,0:T(8,128)(2,1)} %collective-permute-done.refs_4_), channel_id=1, source_target_pairs={{0,32},{32,64},{64,96},{96,128},{128,160},{160,192},{192,224},{224... | collective-permute-start | bytes 1044488 | tf_op jit(solution)/shard_map/ppermute | solution.py:288
  41.5 14.0 %collective-permute-start.2 = (bf16[128,1280]{1,0:T(8,128)(2,1)}, bf16[128,1280]{1,0:T(8,128)(2,1)}, u32[]{:S(2)}, u32[]{:S(2)}) collective-permute-start(bf16[128,1280]{1,0:T(8,128)(2,1)} %collective-permute-done.1.refs_1_), channel_id=1, source_target_pairs={{0,32},{32,64},{64,96},{96,128},{128,160},{160,192},{192,224},{224... | collective-permute-start | bytes 983048 | tf_op jit(solution)/shard_map/ppermute | solution.py:288
  43.5 14.0 %collective-permute-start.6 = (bf16[128,1280]{1,0:T(8,128)(2,1)}, bf16[128,1280]{1,0:T(8,128)(2,1)}, u32[]{:S(2)}, u32[]{:S(2)}) collective-permute-start(bf16[128,1280]{1,0:T(8,128)(2,1)} %collective-permute-done.3.refs_2_), channel_id=1, source_target_pairs={{0,480},{32,0},{64,32},{96,64},{128,96},{160,128},{192,160},{224,1... | collective-permute-start | bytes 983048 | tf_op jit(solution)/shard_map/ppermute | solution.py:288
  48.1 14.0 %collective-permute-start.12 = (bf16[136,1280]{1,0:T(8,128)(2,1)}, bf16[136,1280]{1,0:T(8,128)(2,1)}, u32[]{:S(2)}, u32[]{:S(2)}) collective-permute-start(bf16[136,1280]{1,0:T(8,128)(2,1)} %collective-permute-done.8.refs_3_), channel_id=1, source_target_pairs={{0,480},{32,0},{64,32},{96,64},{128,96},{160,128},{192,160},{224,1... | collective-permute-start | bytes 1044488 | tf_op jit(solution)/shard_map/ppermute | solution.py:288
  50.0 15.7 %collective-permute-start.11 = (bf16[136,1280]{1,0:T(8,128)(2,1)}, bf16[136,1280]{1,0:T(8,128)(2,1)}, u32[]{:S(2)}, u32[]{:S(2)}) collective-permute-start(bf16[136,1280]{1,0:T(8,128)(2,1)} %collective-permute-done.7.refs_2_), channel_id=1, source_target_pairs={{0,32},{32,64},{64,96},{96,128},{128,160},{160,192},{192,224},{224... | collective-permute-start | bytes 1044488 | tf_op jit(solution)/shard_map/ppermute | solution.py:288
  55.5 14.4 %collective-permute-start.5 = (bf16[128,1280]{1,0:T(8,128)(2,1)}, bf16[128,1280]{1,0:T(8,128)(2,1)S(1)}, u32[]{:S(2)}, u32[]{:S(2)}) collective-permute-start(bf16[128,1280]{1,0:T(8,128)(2,1)} %collective-permute-done.2.refs_0_), channel_id=1, source_target_pairs={{0,32},{32,64},{64,96},{96,128},{128,160},{160,192},{192,224},{224... | collective-permute-start | bytes 983048 | tf_op jit(solution)/shard_map/ppermute | solution.py:288
  57.4 14.4 %collective-permute-start.10 = (bf16[128,1280]{1,0:T(8,128)(2,1)}, bf16[128,1280]{1,0:T(8,128)(2,1)S(1)}, u32[]{:S(2)}, u32[]{:S(2)}) collective-permute-start(bf16[128,1280]{1,0:T(8,128)(2,1)} %collective-permute-done.6.refs_1_), channel_id=1, source_target_pairs={{0,480},{32,0},{64,32},{96,64},{128,96},{160,128},{192,160},{224,1... | collective-permute-start | bytes 983048 | tf_op jit(solution)/shard_map/ppermute | solution.py:288
  62.0 14.4 %collective-permute-start.16 = (bf16[136,1280]{1,0:T(8,128)(2,1)}, bf16[136,1280]{1,0:T(8,128)(2,1)S(1)}, u32[]{:S(2)}, u32[]{:S(2)}) collective-permute-start(bf16[136,1280]{1,0:T(8,128)(2,1)} %collective-permute-done.12.refs_3_), channel_id=1, source_target_pairs={{0,480},{32,0},{64,32},{96,64},{128,96},{160,128},{192,160},{224,1... | collective-permute-start | bytes 1044488 | tf_op jit(solution)/shard_map/ppermute | solution.py:288
  65.7 13.5 %collective-permute-start.14 = (bf16[136,1280]{1,0:T(8,128)(2,1)}, bf16[136,1280]{1,0:T(8,128)(2,1)S(1)}, u32[]{:S(2)}, u32[]{:S(2)}) collective-permute-start(bf16[136,1280]{1,0:T(8,128)(2,1)} %collective-permute-done.11.refs_2_), channel_id=1, source_target_pairs={{0,32},{32,64},{64,96},{96,128},{128,160},{160,192},{192,224},{224... | collective-permute-start | bytes 1044488 | tf_op jit(solution)/shard_map/ppermute | solution.py:288
  69.9 13.4 %collective-permute-start.9 = (bf16[128,1280]{1,0:T(8,128)(2,1)S(1)}, bf16[128,1280]{1,0:T(8,128)(2,1)S(1)}, u32[]{:S(2)}, u32[]{:S(2)}) collective-permute-start(bf16[128,1280]{1,0:T(8,128)(2,1)S(1)} %collective-permute-done.5.refs_0_), channel_id=1, source_target_pairs={{0,32},{32,64},{64,96},{96,128},{128,160},{160,192},{192,224},{224... | collective-permute-start | bytes 983048 | tf_op jit(solution)/shard_map/ppermute | solution.py:288
  71.8 13.4 %collective-permute-start.18 = (bf16[128,1280]{1,0:T(8,128)(2,1)S(1)}, bf16[128,1280]{1,0:T(8,128)(2,1)S(1)}, u32[]{:S(2)}, u32[]{:S(2)}) collective-permute-start(bf16[128,1280]{1,0:T(8,128)(2,1)S(1)} %collective-permute-done.10.refs_1_), channel_id=1, source_target_pairs={{0,480},{32,0},{64,32},{96,64},{128,96},{160,128},{192,160},{224,1... | collective-permute-start | bytes 983048 | tf_op jit(solution)/shard_map/ppermute | solution.py:288
  76.4 13.8 %collective-permute-start.17 = (bf16[136,1280]{1,0:T(8,128)(2,1)S(1)}, bf16[136,1280]{1,0:T(8,128)(2,1)S(1)}, u32[]{:S(2)}, u32[]{:S(2)}) collective-permute-start(bf16[136,1280]{1,0:T(8,128)(2,1)S(1)} %collective-permute-done.16.refs_3_), channel_id=1, source_target_pairs={{0,480},{32,0},{64,32},{96,64},{128,96},{160,128},{192,160},{224,1... | collective-permute-start | bytes 1044488 | tf_op jit(solution)/shard_map/ppermute | solution.py:288
  79.2 14.0 %collective-permute-start.15 = (bf16[136,1280]{1,0:T(8,128)(2,1)S(1)}, bf16[136,1280]{1,0:T(8,128)(2,1)S(1)}, u32[]{:S(2)}, u32[]{:S(2)}) collective-permute-start(bf16[136,1280]{1,0:T(8,128)(2,1)S(1)} %collective-permute-done.14.refs_2_), channel_id=1, source_target_pairs={{0,32},{32,64},{64,96},{96,128},{128,160},{160,192},{192,224},{224... | collective-permute-start | bytes 1044488 | tf_op jit(solution)/shard_map/ppermute | solution.py:288
  83.3 14.5 %collective-permute-start.13 = (bf16[128,1280]{1,0:T(8,128)(2,1)S(1)}, bf16[128,1280]{1,0:T(8,128)(2,1)S(1)}, u32[]{:S(2)}, u32[]{:S(2)}) collective-permute-start(bf16[128,1280]{1,0:T(8,128)(2,1)S(1)} %collective-permute-done.9.refs_0_), channel_id=1, source_target_pairs={{0,32},{32,64},{64,96},{96,128},{128,160},{160,192},{192,224},{224... | collective-permute-start | bytes 983048 | tf_op jit(solution)/shard_map/ppermute | solution.py:288
  85.2 12.9 %collective-permute-start.20 = (bf16[128,1280]{1,0:T(8,128)(2,1)S(1)}, bf16[128,1280]{1,0:T(8,128)(2,1)S(1)}, u32[]{:S(2)}, u32[]{:S(2)}) collective-permute-start(bf16[128,1280]{1,0:T(8,128)(2,1)S(1)} %collective-permute-done.18.refs_1_), channel_id=1, source_target_pairs={{0,480},{32,0},{64,32},{96,64},{128,96},{160,128},{192,160},{224,1... | collective-permute-start | bytes 983048 | tf_op jit(solution)/shard_map/ppermute | solution.py:288
  90.4 22.3 %collective-permute-start.25 = (bf16[56,1280]{1,0:T(8,128)(2,1)S(1)}, bf16[56,1280]{1,0:T(8,128)(2,1)S(1)}, u32[]{:S(2)}, u32[]{:S(2)}) collective-permute-start(bf16[56,1280]{1,0:T(8,128)(2,1)S(1)} %get-tuple-element.47), channel_id=1, source_target_pairs={{0,416},{32,448},{64,480},{96,0},{128,32},{160,64},{192,96},{224,1... | collective-permute-start | bytes 430088 | tf_op jit(solution)/shard_map/ppermute | solution.py:288
  98.5 16.4 %collective-permute-start.24 = (bf16[56,2560]{1,0:T(8,128)(2,1)S(1)}, bf16[56,2560]{1,0:T(8,128)(2,1)S(1)}, u32[]{:S(2)}, u32[]{:S(2)}) collective-permute-start(bf16[56,2560]{1,0:T(8,128)(2,1)S(1)} %get-tuple-element.46), channel_id=1, source_target_pairs={{0,448},{32,480},{64,0},{96,32},{128,64},{160,96},{192,128},{224,1... | collective-permute-start | bytes 860168 | tf_op jit(solution)/shard_map/ppermute | solution.py:288
  100.4 14.5 %collective-permute-start.23 = (bf16[56,2560]{1,0:T(8,128)(2,1)S(1)}, bf16[56,2560]{1,0:T(8,128)(2,1)S(1)}, u32[]{:S(2)}, u32[]{:S(2)}) collective-permute-start(bf16[56,2560]{1,0:T(8,128)(2,1)S(1)} %get-tuple-element.45), channel_id=1, source_target_pairs={{0,64},{32,96},{64,128},{96,160},{128,192},{160,224},{192,256},{22... | collective-permute-start | bytes 860168 | tf_op jit(solution)/shard_map/ppermute | solution.py:288
  104.7 22.1 %collective-permute-start.21 = (bf16[56,2560]{1,0:T(8,128)(2,1)S(1)}, bf16[56,2560]{1,0:T(8,128)(2,1)S(1)}, u32[]{:S(2)}, u32[]{:S(2)}) collective-permute-start(bf16[56,2560]{1,0:T(8,128)(2,1)S(1)} %get-tuple-element.43), channel_id=1, source_target_pairs={{0,480},{32,0},{64,32},{96,64},{128,96},{160,128},{192,160},{224,1... | collective-permute-start | bytes 860168 | tf_op jit(solution)/shard_map/ppermute | solution.py:288
  110.7 16.1 %collective-permute-start.19 = (bf16[56,2560]{1,0:T(8,128)(2,1)S(1)}, bf16[56,2560]{1,0:T(8,128)(2,1)S(1)}, u32[]{:S(2)}, u32[]{:S(2)}) collective-permute-start(bf16[56,2560]{1,0:T(8,128)(2,1)S(1)} %get-tuple-element.41), channel_id=1, source_target_pairs={{0,32},{32,64},{64,96},{96,128},{128,160},{160,192},{192,224},{224... | collective-permute-start | bytes 860168 | tf_op jit(solution)/shard_map/ppermute | solution.py:288
  112.7 14.2 %collective-permute-start.22 = (bf16[56,1280]{1,0:T(8,128)(2,1)S(1)}, bf16[56,1280]{1,0:T(8,128)(2,1)S(1)}, u32[]{:S(2)}, u32[]{:S(2)}) collective-permute-start(bf16[56,1280]{1,0:T(8,128)(2,1)S(1)} %get-tuple-element.44), channel_id=1, source_target_pairs={{0,96},{32,128},{64,160},{96,192},{128,224},{160,256},{192,288},{2... | collective-permute-start | bytes 430088 | tf_op jit(solution)/shard_map/ppermute | solution.py:288
  126.9 22.8 %copy-start = (bf16[16,56,2560]{2,1,0:T(8,128)(2,1)}, bf16[16,56,2560]{2,1,0:T(8,128)(2,1)S(1)}, u32[]{:S(2)}) copy-start(bf16[16,56,2560]{2,1,0:T(8,128)(2,1)S(1)} %place_late.1) | copy-start | bytes 13762564
  129.9 15.8 %collective-permute-start.26 = (bf16[384,2560]{1,0:T(8,128)(2,1)S(1)}, bf16[384,2560]{1,0:T(8,128)(2,1)S(1)}, u32[]{:S(2)}, u32[]{:S(2)}) collective-permute-start(bf16[384,2560]{1,0:T(8,128)(2,1)S(1)} %term_other.1), channel_id=1, source_target_pairs={{0,1},{1,0},{2,3},{3,2},{4,5},{5,4},{6,7},{7,6},{8,9},{9,8},{10,11... | collective-permute-start | bytes 5898248 | tf_op jit(solution)/shard_map/ppermute | solution.py:278
  142.1 14.2 %collective-permute-start.27 = (bf16[16,24,2560]{2,1,0:T(8,128)(2,1)S(1)}, bf16[16,24,2560]{2,1,0:T(8,128)(2,1)}, u32[]{:S(2)}, u32[]{:S(2)}) collective-permute-start(bf16[16,24,2560]{2,1,0:T(8,128)(2,1)S(1)} %all-to-all-done.refs_6_), channel_id=1, source_target_pairs={{0,1},{1,0},{2,3},{3,2},{4,5},{5,4},{6,7},{7,6},{8,9},{9,8},{10,11... | collective-permute-start | bytes 5898248 | tf_op jit(solution)/shard_map/ppermute | solution.py:278
  149.7 36.5 %all-to-all-start.1 = ((bf16[16,24,2560]{2,1,0:T(8,128)(2,1)}), bf16[16,24,2560]{2,1,0:T(8,128)(2,1)}, u32[]{:S(2)}, u32[]{:S(2)}) async-start(bf16[16,24,2560]{2,1,0:T(8,128)(2,1)} %bitcast.29), calls=%async_computation.1 | async-start | bytes 3932160 | tf_op jit(solution)/shard_map/all_to_all | solution.py:273
  (6 other events, 25.0 us)

commit v8 on v7

--- a/solution.py
+++ b/solution.py
@@ -211,7 +211,7 @@
 
     return pl.pallas_call(
         kernel,
-        in_specs=[pl.BlockSpec(memory_space=pltpu.VMEM)],
+        in_specs=[pl.BlockSpec(memory_space=pltpu.HBM)],
         out_specs=pl.BlockSpec(memory_space=pltpu.HBM),
         out_shape=pltpu.HBM((copies,) + array.shape, BF),
         scratch_shapes=[pltpu.SemaphoreType.DMA((copies,))],
@@ -226,7 +226,7 @@
 def _term(saved_t, rows, name, more=None):
     units, depth = saved_t.shape
     width = rows.shape[1]
-    block = 512 if width % 512 == 0 else LANES
+    block = 1280 if width % 1280 == 0 else LANES
 
     def kernel(saved_ref, rows_ref, *refs):
         columns = pl.ds(pl.multiple_of(pl.program_id(0) * block, block), block)
@@ -252,6 +252,29 @@
         ),
         name=name,
     )(*operands)
+
+
+def _sum(parts):
+    chips, units, width = parts.shape
+
+    def kernel(parts_ref, out_ref):
+        total = parts_ref[0].astype(F32)
+        for i in range(1, chips):
+            total += parts_ref[i].astype(F32)
+        for i in range(units):
+            out_ref[i, :, :] = total[i : i + 1, :]
+
+    return pl.pallas_call(
+        kernel,
+        in_specs=[pl.BlockSpec(memory_space=pltpu.VMEM)],
+        out_specs=pl.BlockSpec(memory_space=pltpu.VMEM),
+        out_shape=jax.ShapeDtypeStruct((units, 1, width), F32),
+        compiler_params=pltpu.CompilerParams(vmem_limit_bytes=VMEM),
+        cost_estimate=pl.CostEstimate(
+            flops=parts.size, bytes_accessed=2 * parts.size, transcendentals=0
+        ),
+        name="sum_parts",
+    )(parts)
 
 
 def body(grads, routes, gates, hidden, down_weight):
@@ -347,7 +370,7 @@
     d_rows = lax.dot_general(rows, both, (((1,), (1,)), ((), ())), preferred_element_type=F32)
     d_hidden = d_rows.astype(BF)[None]
     sums, d_hidden = lax.optimization_barrier((sums, d_hidden))
-    down_grad = jnp.sum(sums.astype(F32), axis=0)[:, None, :]
+    down_grad = _sum(sums)
     return (d_hidden, down_grad)
 
 

time: 191 us -> 190 us (level)
    pallas_call x1 -> x2, Pallas kernels: 1.44 us -> 4 us  [the longest x1 2.53 us: _sum(): pl.pallas_call(kernel, in_specs=[pl.BlockSpec(memory_space=pltpu.VMEM)],...]
where the time goes in v8:
time: 190 us; the launch traced here: 188 us
  starting transfers between devices  114 us (60%)
  waiting for transfers between devices  42.5 us (22%)
  Pallas kernels  18.8 us (10%)
  matrix products  4.79 us (3%)
  local copies, waits for them, and re-layouts  3.48 us (2%)
  other arithmetic  2.58 us (1%)
    ppermute x26, starting transfers between devices, shift(): lax.ppermute(array, 'expert', [(i, (i + places) % groups) for i in range(...  86 us
    all_to_all x2, waiting for transfers between devices, over_chips(): lax.all_to_all(array, 'replica', split_axis=0, concat_axis=0, tiled=True,...  21.3 us
    ppermute x26, waiting for transfers between devices, shift(): lax.ppermute(array, 'expert', [(i, (i + places) % groups) for i in range(...  19.5 us
    all_to_all x2, starting transfers between devices, over_chips(): lax.all_to_all(array, 'replica', split_axis=0, concat_axis=0, tiled=True,...  14.3 us
    ppermute x2, starting transfers between devices, other_core(): return lax.ppermute(array, 'replica', [(i, i ^ 1) for i in range(replicas)])  14.1 us
    pallas_call x2, Pallas kernels, _term(): pl.pallas_call(kernel, grid=(width // block,), in_specs=[pl.BlockSpec(mem...  5.96 us
    pallas_call x5, Pallas kernels, _select(): pl.pallas_call(kernel, in_specs=[pl.BlockSpec(memory_space=pltpu.SMEM)] +...  5.58 us
    dot_general x1, matrix products, body(): lax.dot_general(rows, both, (((1,), (1,)), ((), ())), preferred_element_t...  4.79 us
  transfers between devices with their start and end apart: 30, of which 8 were waited for; matrix products, arithmetic and copies ran while one was open for 4% of the time, Pallas kernels for 7%

profile of v8, /device:TPU:1, one launch (start us, length us, event | category | flops | bytes accessed | tf_op | source)
XLA Modules:
  0.0 187.8 jit_solution(6872201558739523995)
XLA Ops:
  3.1 7.6 %all-to-all-start = ((bf16[16,24,2560]{2,1,0:T(8,128)(2,1)}), bf16[16,24,2560]{2,1,0:T(8,128)(2,1)S(1)}, u32[]{:S(2)}, u32[]{:S(2)}) async-start(bf16[16,24,2560]{2,1,0:T(8,128)(2,1)} %unit_copies.1), calls=%async_computation | async-start | bytes 3932160 | tf_op jit(solution)/shard_map/all_to_all | solution.py:296
  11.6 11.1 %collective-permute-start.4 = (bf16[136,1280]{1,0:T(8,128)(2,1)}, bf16[136,1280]{1,0:T(8,128)(2,1)}, u32[]{:S(2)}, u32[]{:S(2)}) collective-permute-start(bf16[136,1280]{1,0:T(8,128)(2,1)} %get-tuple-element.28.refs_3_), channel_id=1, source_target_pairs={{0,480},{32,0},{64,32},{96,64},{128,96},{160,128},{192,160},{224,1... | collective-permute-start | bytes 1044488 | tf_op jit(solution)/shard_map/ppermute | solution.py:311
  22.7 1.9 %collective-permute-start = (bf16[136,1280]{1,0:T(8,128)(2,1)}, bf16[136,1280]{1,0:T(8,128)(2,1)}, u32[]{:S(2)}, u32[]{:S(2)}) collective-permute-start(bf16[136,1280]{1,0:T(8,128)(2,1)} %get-tuple-element.28.refs_3_), channel_id=1, source_target_pairs={{0,32},{32,64},{64,96},{96,128},{128,160},{160,192},{192,224},{224... | collective-permute-start | bytes 1044488 | tf_op jit(solution)/shard_map/ppermute | solution.py:311
  24.6 1.9 %collective-permute-start.1 = (bf16[128,1280]{1,0:T(8,128)(2,1)}, bf16[128,1280]{1,0:T(8,128)(2,1)}, u32[]{:S(2)}, u32[]{:S(2)}) collective-permute-start(bf16[128,1280]{1,0:T(8,128)(2,1)} %get-tuple-element.29.refs_2_.refs_0_), channel_id=1, source_target_pairs={{0,32},{32,64},{64,96},{96,128},{128,160},{160,192},{192,224},{224... | collective-permute-start | bytes 983048 | tf_op jit(solution)/shard_map/ppermute | solution.py:311
  26.6 4.6 %collective-permute-start.3 = (bf16[128,1280]{1,0:T(8,128)(2,1)}, bf16[128,1280]{1,0:T(8,128)(2,1)}, u32[]{:S(2)}, u32[]{:S(2)}) collective-permute-start(bf16[128,1280]{1,0:T(8,128)(2,1)} %get-tuple-element.29.refs_2_.refs_0_), channel_id=1, source_target_pairs={{0,480},{32,0},{64,32},{96,64},{128,96},{160,128},{192,160},{224,1... | collective-permute-start | bytes 983048 | tf_op jit(solution)/shard_map/ppermute | solution.py:311
  31.2 3.6 %collective-permute-start.8 = (bf16[136,1280]{1,0:T(8,128)(2,1)}, bf16[136,1280]{1,0:T(8,128)(2,1)}, u32[]{:S(2)}, u32[]{:S(2)}) collective-permute-start(bf16[136,1280]{1,0:T(8,128)(2,1)} %collective-permute-done.4.refs_5_), channel_id=1, source_target_pairs={{0,480},{32,0},{64,32},{96,64},{128,96},{160,128},{192,160},{224,1... | collective-permute-start | bytes 1044488 | tf_op jit(solution)/shard_map/ppermute | solution.py:311
  37.6 1.9 %collective-permute-start.7 = (bf16[136,1280]{1,0:T(8,128)(2,1)}, bf16[136,1280]{1,0:T(8,128)(2,1)}, u32[]{:S(2)}, u32[]{:S(2)}) collective-permute-start(bf16[136,1280]{1,0:T(8,128)(2,1)} %collective-permute-done.refs_4_), channel_id=1, source_target_pairs={{0,32},{32,64},{64,96},{96,128},{128,160},{160,192},{192,224},{224... | collective-permute-start | bytes 1044488 | tf_op jit(solution)/shard_map/ppermute | solution.py:311
  39.5 2.0 %collective-permute-done.1.refs_1_ = bf16[128,1280]{1,0:T(8,128)(2,1)} collective-permute-done((bf16[128,1280]{1,0:T(8,128)(2,1)}, bf16[128,1280]{1,0:T(8,128)(2,1)}, u32[]{:S(2)}, u32[]{:S(2)}) %collective-permute-start.1) | collective-permute-done | bytes 327712 | tf_op jit(solution)/shard_map/ppermute | solution.py:311
  43.5 4.6 %collective-permute-start.6 = (bf16[128,1280]{1,0:T(8,128)(2,1)}, bf16[128,1280]{1,0:T(8,128)(2,1)}, u32[]{:S(2)}, u32[]{:S(2)}) collective-permute-start(bf16[128,1280]{1,0:T(8,128)(2,1)} %collective-permute-done.3.refs_2_), channel_id=1, source_target_pairs={{0,480},{32,0},{64,32},{96,64},{128,96},{160,128},{192,160},{224,1... | collective-permute-start | bytes 983048 | tf_op jit(solution)/shard_map/ppermute | solution.py:311
  48.1 1.9 %collective-permute-start.12 = (bf16[136,1280]{1,0:T(8,128)(2,1)}, bf16[136,1280]{1,0:T(8,128)(2,1)}, u32[]{:S(2)}, u32[]{:S(2)}) collective-permute-start(bf16[136,1280]{1,0:T(8,128)(2,1)} %collective-permute-done.8.refs_3_), channel_id=1, source_target_pairs={{0,480},{32,0},{64,32},{96,64},{128,96},{160,128},{192,160},{224,1... | collective-permute-start | bytes 1044488 | tf_op jit(solution)/shard_map/ppermute | solution.py:311
  50.0 3.4 %collective-permute-start.11 = (bf16[136,1280]{1,0:T(8,128)(2,1)}, bf16[136,1280]{1,0:T(8,128)(2,1)}, u32[]{:S(2)}, u32[]{:S(2)}) collective-permute-start(bf16[136,1280]{1,0:T(8,128)(2,1)} %collective-permute-done.7.refs_2_), channel_id=1, source_target_pairs={{0,32},{32,64},{64,96},{96,128},{128,160},{160,192},{192,224},{224... | collective-permute-start | bytes 1044488 | tf_op jit(solution)/shard_map/ppermute | solution.py:311
  57.5 4.6 %collective-permute-start.10 = (bf16[128,1280]{1,0:T(8,128)(2,1)}, bf16[128,1280]{1,0:T(8,128)(2,1)S(1)}, u32[]{:S(2)}, u32[]{:S(2)}) collective-permute-start(bf16[128,1280]{1,0:T(8,128)(2,1)} %collective-permute-done.6.refs_1_), channel_id=1, source_target_pairs={{0,480},{32,0},{64,32},{96,64},{128,96},{160,128},{192,160},{224,1... | collective-permute-start | bytes 983048 | tf_op jit(solution)/shard_map/ppermute | solution.py:311
  62.1 3.6 %collective-permute-start.16 = (bf16[136,1280]{1,0:T(8,128)(2,1)}, bf16[136,1280]{1,0:T(8,128)(2,1)S(1)}, u32[]{:S(2)}, u32[]{:S(2)}) collective-permute-start(bf16[136,1280]{1,0:T(8,128)(2,1)} %collective-permute-done.12.refs_3_), channel_id=1, source_target_pairs={{0,480},{32,0},{64,32},{96,64},{128,96},{160,128},{192,160},{224,1... | collective-permute-start | bytes 1044488 | tf_op jit(solution)/shard_map/ppermute | solution.py:311
  71.8 4.6 %collective-permute-start.18 = (bf16[128,1280]{1,0:T(8,128)(2,1)S(1)}, bf16[128,1280]{1,0:T(8,128)(2,1)S(1)}, u32[]{:S(2)}, u32[]{:S(2)}) collective-permute-start(bf16[128,1280]{1,0:T(8,128)(2,1)S(1)} %collective-permute-done.10.refs_1_), channel_id=1, source_target_pairs={{0,480},{32,0},{64,32},{96,64},{128,96},{160,128},{192,160},{224,1... | collective-permute-start | bytes 983048 | tf_op jit(solution)/shard_map/ppermute | solution.py:311
  76.4 2.7 %collective-permute-start.17 = (bf16[136,1280]{1,0:T(8,128)(2,1)S(1)}, bf16[136,1280]{1,0:T(8,128)(2,1)S(1)}, u32[]{:S(2)}, u32[]{:S(2)}) collective-permute-start(bf16[136,1280]{1,0:T(8,128)(2,1)S(1)} %collective-permute-done.16.refs_3_), channel_id=1, source_target_pairs={{0,480},{32,0},{64,32},{96,64},{128,96},{160,128},{192,160},{224,1... | collective-permute-start | bytes 1044488 | tf_op jit(solution)/shard_map/ppermute | solution.py:311
  79.2 2.5 %collective-permute-start.15 = (bf16[136,1280]{1,0:T(8,128)(2,1)S(1)}, bf16[136,1280]{1,0:T(8,128)(2,1)S(1)}, u32[]{:S(2)}, u32[]{:S(2)}) collective-permute-start(bf16[136,1280]{1,0:T(8,128)(2,1)S(1)} %collective-permute-done.14.refs_2_), channel_id=1, source_target_pairs={{0,32},{32,64},{64,96},{96,128},{128,160},{160,192},{192,224},{224... | collective-permute-start | bytes 1044488 | tf_op jit(solution)/shard_map/ppermute | solution.py:311
  85.3 4.6 %collective-permute-start.20 = (bf16[128,1280]{1,0:T(8,128)(2,1)S(1)}, bf16[128,1280]{1,0:T(8,128)(2,1)S(1)}, u32[]{:S(2)}, u32[]{:S(2)}) collective-permute-start(bf16[128,1280]{1,0:T(8,128)(2,1)S(1)} %collective-permute-done.18.refs_1_), channel_id=1, source_target_pairs={{0,480},{32,0},{64,32},{96,64},{128,96},{160,128},{192,160},{224,1... | collective-permute-start | bytes 983048 | tf_op jit(solution)/shard_map/ppermute | solution.py:311
  90.4 2.8 %collective-permute-start.25 = (bf16[56,1280]{1,0:T(8,128)(2,1)S(1)}, bf16[56,1280]{1,0:T(8,128)(2,1)S(1)}, u32[]{:S(2)}, u32[]{:S(2)}) collective-permute-start(bf16[56,1280]{1,0:T(8,128)(2,1)S(1)} %get-tuple-element.47), channel_id=1, source_target_pairs={{0,416},{32,448},{64,480},{96,0},{128,32},{160,64},{192,96},{224,1... | collective-permute-start | bytes 430088 | tf_op jit(solution)/shard_map/ppermute | solution.py:311
  93.2 4.6 %collective-permute-done.13.first_ref.refs_0_ = bf16[128,1280]{1,0:T(8,128)(2,1)S(1)} collective-permute-done((bf16[128,1280]{1,0:T(8,128)(2,1)S(1)}, bf16[128,1280]{1,0:T(8,128)(2,1)S(1)}, u32[]{:S(2)}, u32[]{:S(2)}) %collective-permute-start.13) | collective-permute-done | bytes 327712 | tf_op jit(solution)/shard_map/ppermute | solution.py:311
  100.5 4.3 %collective-permute-start.23 = (bf16[56,2560]{1,0:T(8,128)(2,1)S(1)}, bf16[56,2560]{1,0:T(8,128)(2,1)S(1)}, u32[]{:S(2)}, u32[]{:S(2)}) collective-permute-start(bf16[56,2560]{1,0:T(8,128)(2,1)S(1)} %get-tuple-element.45), channel_id=1, source_target_pairs={{0,64},{32,96},{64,128},{96,160},{128,192},{160,224},{192,256},{22... | collective-permute-start | bytes 860168 | tf_op jit(solution)/shard_map/ppermute | solution.py:311
  104.7 6.0 %collective-permute-start.21 = (bf16[56,2560]{1,0:T(8,128)(2,1)S(1)}, bf16[56,2560]{1,0:T(8,128)(2,1)S(1)}, u32[]{:S(2)}, u32[]{:S(2)}) collective-permute-start(bf16[56,2560]{1,0:T(8,128)(2,1)S(1)} %get-tuple-element.43), channel_id=1, source_target_pairs={{0,480},{32,0},{64,32},{96,64},{128,96},{160,128},{192,160},{224,1... | collective-permute-start | bytes 860168 | tf_op jit(solution)/shard_map/ppermute | solution.py:311
  110.7 1.9 %collective-permute-start.19 = (bf16[56,2560]{1,0:T(8,128)(2,1)S(1)}, bf16[56,2560]{1,0:T(8,128)(2,1)S(1)}, u32[]{:S(2)}, u32[]{:S(2)}) collective-permute-start(bf16[56,2560]{1,0:T(8,128)(2,1)S(1)} %get-tuple-element.41), channel_id=1, source_target_pairs={{0,32},{32,64},{64,96},{96,128},{128,160},{160,192},{192,224},{224... | collective-permute-start | bytes 860168 | tf_op jit(solution)/shard_map/ppermute | solution.py:311
  115.0 11.8 %collective-permute-done.22.refs_2_ = bf16[56,1280]{1,0:T(8,128)(2,1)S(1)} collective-permute-done((bf16[56,1280]{1,0:T(8,128)(2,1)S(1)}, bf16[56,1280]{1,0:T(8,128)(2,1)S(1)}, u32[]{:S(2)}, u32[]{:S(2)}) %collective-permute-start.22) | collective-permute-done | bytes 143392 | tf_op jit(solution)/shard_map/ppermute | solution.py:311
  126.9 2.5 %term_other.1 = bf16[384,2560]{1,0:T(8,128)(2,1)S(1)} custom-call(bf16[384,896]{1,0:T(8,128)(2,1)S(1)} %get-tuple-element.49.saved_ref, bf16[896,2560]{1,0:T(8,128)(2,1)S(1)} %bitcast.18), custom_call_target="tpu_custom_call" | custom-call | flops 1761607680 | bytes 7241728 | tf_op jit(solution)/shard_map/term_other/pallas_call | solution.py:239
  129.4 12.2 %collective-permute-start.26 = (bf16[384,2560]{1,0:T(8,128)(2,1)S(1)}, bf16[384,2560]{1,0:T(8,128)(2,1)S(1)}, u32[]{:S(2)}, u32[]{:S(2)}) collective-permute-start(bf16[384,2560]{1,0:T(8,128)(2,1)S(1)} %term_other.1), channel_id=1, source_target_pairs={{0,1},{1,0},{2,3},{3,2},{4,5},{5,4},{6,7},{7,6},{8,9},{9,8},{10,11... | collective-permute-start | bytes 5898248 | tf_op jit(solution)/shard_map/ppermute | solution.py:301
  141.6 1.9 %collective-permute-start.27 = (bf16[16,24,2560]{2,1,0:T(8,128)(2,1)S(1)}, bf16[16,24,2560]{2,1,0:T(8,128)(2,1)}, u32[]{:S(2)}, u32[]{:S(2)}) collective-permute-start(bf16[16,24,2560]{2,1,0:T(8,128)(2,1)S(1)} %all-to-all-done.refs_6_), channel_id=1, source_target_pairs={{0,1},{1,0},{2,3},{3,2},{4,5},{5,4},{6,7},{7,6},{8,9},{9,8},{10,11... | collective-permute-start | bytes 5898248 | tf_op jit(solution)/shard_map/ppermute | solution.py:301
  145.2 3.4 %term_pair.1 = bf16[384,2560]{1,0:T(8,128)(2,1)} custom-call(bf16[384,896]{1,0:T(8,128)(2,1)S(1)} %get-tuple-element.32.saved_ref, bf16[896,2560]{1,0:T(8,128)(2,1)S(1)} %bitcast.19, bf16[384,2560]{1,0:T(8,128)(2,1)S(1)} %collective-permute-done.26.refs_0_), custom_call_target="tpu_custom_call" | custom-call | flops 1761607680 | bytes 7241728 | tf_op jit(solution)/shard_map/term_pair/pallas_call | solution.py:239
  148.7 6.7 %all-to-all-start.1 = ((bf16[16,24,2560]{2,1,0:T(8,128)(2,1)}), bf16[16,24,2560]{2,1,0:T(8,128)(2,1)}, u32[]{:S(2)}, u32[]{:S(2)}) async-start(bf16[16,24,2560]{2,1,0:T(8,128)(2,1)} %bitcast.29), calls=%async_computation.1 | async-start | bytes 3932160 | tf_op jit(solution)/shard_map/all_to_all | solution.py:296
  155.4 2.6 %maximum_select_fusion = bf16[16,2,24,2560]{3,2,0,1:T(8,128)(2,1)S(1)} fusion(bf16[16,1,24,2560]{3,2,0,1:T(8,128)(2,1)} %bitcast.11, bf16[16,1,24,2560]{3,2,0,1:T(8,128)(2,1)S(1)} %bitcast.23, pred[]{:T(512)S(6)} %eq.3), kind=kLoop, calls=%fused_computation | loop fusion | flops 5898240 | bytes 7864321 | tf_op jit(solution)/shard_map/jit(_where)/select_n | solution.py:365
  159.1 4.8 %fusion = bf16[1,896,768]{2,1,0:T(8,128)(2,1)} fusion(bf16[896,2560]{1,0:T(8,128)(2,1)S(1)} %bitcast.22, bf16[768,2560]{1,0:T(8,128)(2,1)S(1)} %bitcast.30), kind=kOutput, calls=%fused_computation.2 | convolution fusion | flops 3523903488 | bytes 9895936 | tf_op jit(solution)/shard_map/dot_general | solution.py:370
  163.9 21.3 %all-to-all-done.1.parts_ref = bf16[16,24,2560]{2,1,0:T(8,128)(2,1)} async-done(((bf16[16,24,2560]{2,1,0:T(8,128)(2,1)}), bf16[16,24,2560]{2,1,0:T(8,128)(2,1)}, u32[]{:S(2)}, u32[]{:S(2)}) %all-to-all-start.1) | async-done | bytes 1966112 | tf_op jit(solution)/shard_map/all_to_all | solution.py:296
  185.3 2.5 %sum_parts.1 = f32[24,1,2560]{2,1,0:T(1,128)} custom-call(bf16[16,24,2560]{2,1,0:T(8,128)(2,1)} %all-to-all-done.1.parts_ref), custom_call_target="tpu_custom_call" | custom-call | flops 983040 | bytes 1966080 | tf_op jit(solution)/shard_map/sum_parts/pallas_call | solution.py:267
  (64 shorter events, 30.0 us)
Async XLA Ops:
  0.6 10.1 %copy-start.1 = (bf16[1,128,2560]{2,1,0:T(8,128)(2,1)S(1)}, bf16[1,128,2560]{2,1,0:T(8,128)(2,1)}, u32[]{:S(2)}) copy-start(bf16[1,128,2560]{2,1,0:T(8,128)(2,1)} %param.5) | copy-start | bytes 1966084
  3.1 50.3 %all-to-all-start = ((bf16[16,24,2560]{2,1,0:T(8,128)(2,1)}), bf16[16,24,2560]{2,1,0:T(8,128)(2,1)S(1)}, u32[]{:S(2)}, u32[]{:S(2)}) async-start(bf16[16,24,2560]{2,1,0:T(8,128)(2,1)} %unit_copies.1), calls=%async_computation | async-start | bytes 3932160 | tf_op jit(solution)/shard_map/all_to_all | solution.py:296
  11.6 19.6 %collective-permute-start.4 = (bf16[136,1280]{1,0:T(8,128)(2,1)}, bf16[136,1280]{1,0:T(8,128)(2,1)}, u32[]{:S(2)}, u32[]{:S(2)}) collective-permute-start(bf16[136,1280]{1,0:T(8,128)(2,1)} %get-tuple-element.28.refs_3_), channel_id=1, source_target_pairs={{0,480},{32,0},{64,32},{96,64},{128,96},{160,128},{192,160},{224,1... | collective-permute-start | bytes 1044488 | tf_op jit(solution)/shard_map/ppermute | solution.py:311
  22.7 14.9 %collective-permute-start = (bf16[136,1280]{1,0:T(8,128)(2,1)}, bf16[136,1280]{1,0:T(8,128)(2,1)}, u32[]{:S(2)}, u32[]{:S(2)}) collective-permute-start(bf16[136,1280]{1,0:T(8,128)(2,1)} %get-tuple-element.28.refs_3_), channel_id=1, source_target_pairs={{0,32},{32,64},{64,96},{96,128},{128,160},{160,192},{192,224},{224... | collective-permute-start | bytes 1044488 | tf_op jit(solution)/shard_map/ppermute | solution.py:311
  24.6 16.9 %collective-permute-start.1 = (bf16[128,1280]{1,0:T(8,128)(2,1)}, bf16[128,1280]{1,0:T(8,128)(2,1)}, u32[]{:S(2)}, u32[]{:S(2)}) collective-permute-start(bf16[128,1280]{1,0:T(8,128)(2,1)} %get-tuple-element.29.refs_2_.refs_0_), channel_id=1, source_target_pairs={{0,32},{32,64},{64,96},{96,128},{128,160},{160,192},{192,224},{224... | collective-permute-start | bytes 983048 | tf_op jit(solution)/shard_map/ppermute | solution.py:311
  26.6 16.9 %collective-permute-start.3 = (bf16[128,1280]{1,0:T(8,128)(2,1)}, bf16[128,1280]{1,0:T(8,128)(2,1)}, u32[]{:S(2)}, u32[]{:S(2)}) collective-permute-start(bf16[128,1280]{1,0:T(8,128)(2,1)} %get-tuple-element.29.refs_2_.refs_0_), channel_id=1, source_target_pairs={{0,480},{32,0},{64,32},{96,64},{128,96},{160,128},{192,160},{224,1... | collective-permute-start | bytes 983048 | tf_op jit(solution)/shard_map/ppermute | solution.py:311
  31.2 16.9 %collective-permute-start.8 = (bf16[136,1280]{1,0:T(8,128)(2,1)}, bf16[136,1280]{1,0:T(8,128)(2,1)}, u32[]{:S(2)}, u32[]{:S(2)}) collective-permute-start(bf16[136,1280]{1,0:T(8,128)(2,1)} %collective-permute-done.4.refs_5_), channel_id=1, source_target_pairs={{0,480},{32,0},{64,32},{96,64},{128,96},{160,128},{192,160},{224,1... | collective-permute-start | bytes 1044488 | tf_op jit(solution)/shard_map/ppermute | solution.py:311
  37.6 12.4 %collective-permute-start.7 = (bf16[136,1280]{1,0:T(8,128)(2,1)}, bf16[136,1280]{1,0:T(8,128)(2,1)}, u32[]{:S(2)}, u32[]{:S(2)}) collective-permute-start(bf16[136,1280]{1,0:T(8,128)(2,1)} %collective-permute-done.refs_4_), channel_id=1, source_target_pairs={{0,32},{32,64},{64,96},{96,128},{128,160},{160,192},{192,224},{224... | collective-permute-start | bytes 1044488 | tf_op jit(solution)/shard_map/ppermute | solution.py:311
  41.6 14.0 %collective-permute-start.2 = (bf16[128,1280]{1,0:T(8,128)(2,1)}, bf16[128,1280]{1,0:T(8,128)(2,1)}, u32[]{:S(2)}, u32[]{:S(2)}) collective-permute-start(bf16[128,1280]{1,0:T(8,128)(2,1)} %collective-permute-done.1.refs_1_), channel_id=1, source_target_pairs={{0,32},{32,64},{64,96},{96,128},{128,160},{160,192},{192,224},{224... | collective-permute-start | bytes 983048 | tf_op jit(solution)/shard_map/ppermute | solution.py:311
  43.5 14.0 %collective-permute-start.6 = (bf16[128,1280]{1,0:T(8,128)(2,1)}, bf16[128,1280]{1,0:T(8,128)(2,1)}, u32[]{:S(2)}, u32[]{:S(2)}) collective-permute-start(bf16[128,1280]{1,0:T(8,128)(2,1)} %collective-permute-done.3.refs_2_), channel_id=1, source_target_pairs={{0,480},{32,0},{64,32},{96,64},{128,96},{160,128},{192,160},{224,1... | collective-permute-start | bytes 983048 | tf_op jit(solution)/shard_map/ppermute | solution.py:311
  48.1 14.0 %collective-permute-start.12 = (bf16[136,1280]{1,0:T(8,128)(2,1)}, bf16[136,1280]{1,0:T(8,128)(2,1)}, u32[]{:S(2)}, u32[]{:S(2)}) collective-permute-start(bf16[136,1280]{1,0:T(8,128)(2,1)} %collective-permute-done.8.refs_3_), channel_id=1, source_target_pairs={{0,480},{32,0},{64,32},{96,64},{128,96},{160,128},{192,160},{224,1... | collective-permute-start | bytes 1044488 | tf_op jit(solution)/shard_map/ppermute | solution.py:311
  50.0 15.7 %collective-permute-start.11 = (bf16[136,1280]{1,0:T(8,128)(2,1)}, bf16[136,1280]{1,0:T(8,128)(2,1)}, u32[]{:S(2)}, u32[]{:S(2)}) collective-permute-start(bf16[136,1280]{1,0:T(8,128)(2,1)} %collective-permute-done.7.refs_2_), channel_id=1, source_target_pairs={{0,32},{32,64},{64,96},{96,128},{128,160},{160,192},{192,224},{224... | collective-permute-start | bytes 1044488 | tf_op jit(solution)/shard_map/ppermute | solution.py:311
  55.5 14.4 %collective-permute-start.5 = (bf16[128,1280]{1,0:T(8,128)(2,1)}, bf16[128,1280]{1,0:T(8,128)(2,1)S(1)}, u32[]{:S(2)}, u32[]{:S(2)}) collective-permute-start(bf16[128,1280]{1,0:T(8,128)(2,1)} %collective-permute-done.2.refs_0_), channel_id=1, source_target_pairs={{0,32},{32,64},{64,96},{96,128},{128,160},{160,192},{192,224},{224... | collective-permute-start | bytes 983048 | tf_op jit(solution)/shard_map/ppermute | solution.py:311
  57.5 14.4 %collective-permute-start.10 = (bf16[128,1280]{1,0:T(8,128)(2,1)}, bf16[128,1280]{1,0:T(8,128)(2,1)S(1)}, u32[]{:S(2)}, u32[]{:S(2)}) collective-permute-start(bf16[128,1280]{1,0:T(8,128)(2,1)} %collective-permute-done.6.refs_1_), channel_id=1, source_target_pairs={{0,480},{32,0},{64,32},{96,64},{128,96},{160,128},{192,160},{224,1... | collective-permute-start | bytes 983048 | tf_op jit(solution)/shard_map/ppermute | solution.py:311
  62.1 14.4 %collective-permute-start.16 = (bf16[136,1280]{1,0:T(8,128)(2,1)}, bf16[136,1280]{1,0:T(8,128)(2,1)S(1)}, u32[]{:S(2)}, u32[]{:S(2)}) collective-permute-start(bf16[136,1280]{1,0:T(8,128)(2,1)} %collective-permute-done.12.refs_3_), channel_id=1, source_target_pairs={{0,480},{32,0},{64,32},{96,64},{128,96},{160,128},{192,160},{224,1... | collective-permute-start | bytes 1044488 | tf_op jit(solution)/shard_map/ppermute | solution.py:311
  65.7 13.5 %collective-permute-start.14 = (bf16[136,1280]{1,0:T(8,128)(2,1)}, bf16[136,1280]{1,0:T(8,128)(2,1)S(1)}, u32[]{:S(2)}, u32[]{:S(2)}) collective-permute-start(bf16[136,1280]{1,0:T(8,128)(2,1)} %collective-permute-done.11.refs_2_), channel_id=1, source_target_pairs={{0,32},{32,64},{64,96},{96,128},{128,160},{160,192},{192,224},{224... | collective-permute-start | bytes 1044488 | tf_op jit(solution)/shard_map/ppermute | solution.py:311
  69.9 13.4 %collective-permute-start.9 = (bf16[128,1280]{1,0:T(8,128)(2,1)S(1)}, bf16[128,1280]{1,0:T(8,128)(2,1)S(1)}, u32[]{:S(2)}, u32[]{:S(2)}) collective-permute-start(bf16[128,1280]{1,0:T(8,128)(2,1)S(1)} %collective-permute-done.5.refs_0_), channel_id=1, source_target_pairs={{0,32},{32,64},{64,96},{96,128},{128,160},{160,192},{192,224},{224... | collective-permute-start | bytes 983048 | tf_op jit(solution)/shard_map/ppermute | solution.py:311
  71.8 13.4 %collective-permute-start.18 = (bf16[128,1280]{1,0:T(8,128)(2,1)S(1)}, bf16[128,1280]{1,0:T(8,128)(2,1)S(1)}, u32[]{:S(2)}, u32[]{:S(2)}) collective-permute-start(bf16[128,1280]{1,0:T(8,128)(2,1)S(1)} %collective-permute-done.10.refs_1_), channel_id=1, source_target_pairs={{0,480},{32,0},{64,32},{96,64},{128,96},{160,128},{192,160},{224,1... | collective-permute-start | bytes 983048 | tf_op jit(solution)/shard_map/ppermute | solution.py:311
  76.4 13.8 %collective-permute-start.17 = (bf16[136,1280]{1,0:T(8,128)(2,1)S(1)}, bf16[136,1280]{1,0:T(8,128)(2,1)S(1)}, u32[]{:S(2)}, u32[]{:S(2)}) collective-permute-start(bf16[136,1280]{1,0:T(8,128)(2,1)S(1)} %collective-permute-done.16.refs_3_), channel_id=1, source_target_pairs={{0,480},{32,0},{64,32},{96,64},{128,96},{160,128},{192,160},{224,1... | collective-permute-start | bytes 1044488 | tf_op jit(solution)/shard_map/ppermute | solution.py:311
  79.2 14.0 %collective-permute-start.15 = (bf16[136,1280]{1,0:T(8,128)(2,1)S(1)}, bf16[136,1280]{1,0:T(8,128)(2,1)S(1)}, u32[]{:S(2)}, u32[]{:S(2)}) collective-permute-start(bf16[136,1280]{1,0:T(8,128)(2,1)S(1)} %collective-permute-done.14.refs_2_), channel_id=1, source_target_pairs={{0,32},{32,64},{64,96},{96,128},{128,160},{160,192},{192,224},{224... | collective-permute-start | bytes 1044488 | tf_op jit(solution)/shard_map/ppermute | solution.py:311
  83.3 14.5 %collective-permute-start.13 = (bf16[128,1280]{1,0:T(8,128)(2,1)S(1)}, bf16[128,1280]{1,0:T(8,128)(2,1)S(1)}, u32[]{:S(2)}, u32[]{:S(2)}) collective-permute-start(bf16[128,1280]{1,0:T(8,128)(2,1)S(1)} %collective-permute-done.9.refs_0_), channel_id=1, source_target_pairs={{0,32},{32,64},{64,96},{96,128},{128,160},{160,192},{192,224},{224... | collective-permute-start | bytes 983048 | tf_op jit(solution)/shard_map/ppermute | solution.py:311
  85.3 12.9 %collective-permute-start.20 = (bf16[128,1280]{1,0:T(8,128)(2,1)S(1)}, bf16[128,1280]{1,0:T(8,128)(2,1)S(1)}, u32[]{:S(2)}, u32[]{:S(2)}) collective-permute-start(bf16[128,1280]{1,0:T(8,128)(2,1)S(1)} %collective-permute-done.18.refs_1_), channel_id=1, source_target_pairs={{0,480},{32,0},{64,32},{96,64},{128,96},{160,128},{192,160},{224,1... | collective-permute-start | bytes 983048 | tf_op jit(solution)/shard_map/ppermute | solution.py:311
  90.4 22.3 %collective-permute-start.25 = (bf16[56,1280]{1,0:T(8,128)(2,1)S(1)}, bf16[56,1280]{1,0:T(8,128)(2,1)S(1)}, u32[]{:S(2)}, u32[]{:S(2)}) collective-permute-start(bf16[56,1280]{1,0:T(8,128)(2,1)S(1)} %get-tuple-element.47), channel_id=1, source_target_pairs={{0,416},{32,448},{64,480},{96,0},{128,32},{160,64},{192,96},{224,1... | collective-permute-start | bytes 430088 | tf_op jit(solution)/shard_map/ppermute | solution.py:311
  98.5 16.4 %collective-permute-start.24 = (bf16[56,2560]{1,0:T(8,128)(2,1)S(1)}, bf16[56,2560]{1,0:T(8,128)(2,1)S(1)}, u32[]{:S(2)}, u32[]{:S(2)}) collective-permute-start(bf16[56,2560]{1,0:T(8,128)(2,1)S(1)} %get-tuple-element.46), channel_id=1, source_target_pairs={{0,448},{32,480},{64,0},{96,32},{128,64},{160,96},{192,128},{224,1... | collective-permute-start | bytes 860168 | tf_op jit(solution)/shard_map/ppermute | solution.py:311
  100.5 14.5 %collective-permute-start.23 = (bf16[56,2560]{1,0:T(8,128)(2,1)S(1)}, bf16[56,2560]{1,0:T(8,128)(2,1)S(1)}, u32[]{:S(2)}, u32[]{:S(2)}) collective-permute-start(bf16[56,2560]{1,0:T(8,128)(2,1)S(1)} %get-tuple-element.45), channel_id=1, source_target_pairs={{0,64},{32,96},{64,128},{96,160},{128,192},{160,224},{192,256},{22... | collective-permute-start | bytes 860168 | tf_op jit(solution)/shard_map/ppermute | solution.py:311
  104.7 22.1 %collective-permute-start.21 = (bf16[56,2560]{1,0:T(8,128)(2,1)S(1)}, bf16[56,2560]{1,0:T(8,128)(2,1)S(1)}, u32[]{:S(2)}, u32[]{:S(2)}) collective-permute-start(bf16[56,2560]{1,0:T(8,128)(2,1)S(1)} %get-tuple-element.43), channel_id=1, source_target_pairs={{0,480},{32,0},{64,32},{96,64},{128,96},{160,128},{192,160},{224,1... | collective-permute-start | bytes 860168 | tf_op jit(solution)/shard_map/ppermute | solution.py:311
  110.7 16.1 %collective-permute-start.19 = (bf16[56,2560]{1,0:T(8,128)(2,1)S(1)}, bf16[56,2560]{1,0:T(8,128)(2,1)S(1)}, u32[]{:S(2)}, u32[]{:S(2)}) collective-permute-start(bf16[56,2560]{1,0:T(8,128)(2,1)S(1)} %get-tuple-element.41), channel_id=1, source_target_pairs={{0,32},{32,64},{64,96},{96,128},{128,160},{160,192},{192,224},{224... | collective-permute-start | bytes 860168 | tf_op jit(solution)/shard_map/ppermute | solution.py:311
  112.7 14.1 %collective-permute-start.22 = (bf16[56,1280]{1,0:T(8,128)(2,1)S(1)}, bf16[56,1280]{1,0:T(8,128)(2,1)S(1)}, u32[]{:S(2)}, u32[]{:S(2)}) collective-permute-start(bf16[56,1280]{1,0:T(8,128)(2,1)S(1)} %get-tuple-element.44), channel_id=1, source_target_pairs={{0,96},{32,128},{64,160},{96,192},{128,224},{160,256},{192,288},{2... | collective-permute-start | bytes 430088 | tf_op jit(solution)/shard_map/ppermute | solution.py:311
  126.9 21.8 %copy-start = (bf16[16,56,2560]{2,1,0:T(8,128)(2,1)}, bf16[16,56,2560]{2,1,0:T(8,128)(2,1)S(1)}, u32[]{:S(2)}) copy-start(bf16[16,56,2560]{2,1,0:T(8,128)(2,1)S(1)} %place_late.1) | copy-start | bytes 13762564
  129.4 15.8 %collective-permute-start.26 = (bf16[384,2560]{1,0:T(8,128)(2,1)S(1)}, bf16[384,2560]{1,0:T(8,128)(2,1)S(1)}, u32[]{:S(2)}, u32[]{:S(2)}) collective-permute-start(bf16[384,2560]{1,0:T(8,128)(2,1)S(1)} %term_other.1), channel_id=1, source_target_pairs={{0,1},{1,0},{2,3},{3,2},{4,5},{5,4},{6,7},{7,6},{8,9},{9,8},{10,11... | collective-permute-start | bytes 5898248 | tf_op jit(solution)/shard_map/ppermute | solution.py:301
  141.6 13.7 %collective-permute-start.27 = (bf16[16,24,2560]{2,1,0:T(8,128)(2,1)S(1)}, bf16[16,24,2560]{2,1,0:T(8,128)(2,1)}, u32[]{:S(2)}, u32[]{:S(2)}) collective-permute-start(bf16[16,24,2560]{2,1,0:T(8,128)(2,1)S(1)} %all-to-all-done.refs_6_), channel_id=1, source_target_pairs={{0,1},{1,0},{2,3},{3,2},{4,5},{5,4},{6,7},{7,6},{8,9},{9,8},{10,11... | collective-permute-start | bytes 5898248 | tf_op jit(solution)/shard_map/ppermute | solution.py:301
  148.7 36.6 %all-to-all-start.1 = ((bf16[16,24,2560]{2,1,0:T(8,128)(2,1)}), bf16[16,24,2560]{2,1,0:T(8,128)(2,1)}, u32[]{:S(2)}, u32[]{:S(2)}) async-start(bf16[16,24,2560]{2,1,0:T(8,128)(2,1)} %bitcast.29), calls=%async_computation.1 | async-start | bytes 3932160 | tf_op jit(solution)/shard_map/all_to_all | solution.py:296
  (6 other events, 25.1 us)

commit v9 on v8

--- a/solution.py
+++ b/solution.py
@@ -324,8 +324,8 @@
     saved_mine, saved_other = _split(hidden[0], core.reshape(1), units_dev, own_first)
     for hop in range(1, relay + 1):
         if hop == 2:
-            b_up, saved_mine, saved_other = lax.optimization_barrier(
-                (b_up, saved_mine, saved_other)
+            b_up, b_down, saved_mine, saved_other = lax.optimization_barrier(
+                (b_up, b_down, saved_mine, saved_other)
             )
         if hop >= 3:
             a_up, rows = lax.optimization_barrier((a_up, rows))

time: 190 us -> 187 us (0.984)
  waiting for transfers between devices: 42.5 us -> 36.9 us
  starting transfers between devices: 114 us -> 117 us
    ppermute x26, waiting for transfers between devices: 19.5 us -> 13.9 us  [shift(): lax.ppermute(array, 'expert', [(i, (i + places) % groups) for i in range(...]
    ppermute x2, starting transfers between devices: 14.1 us -> 16.7 us  [other_core(): return lax.ppermute(array, 'replica', [(i, i ^ 1) for i in range(replicas)])]
    ppermute x26, starting transfers between devices: 86 us -> 88.1 us  [shift(): lax.ppermute(array, 'expert', [(i, (i + places) % groups) for i in range(...]
where the time goes in v9:
time: 187 us; the launch traced here: 185 us
  starting transfers between devices  117 us (63%)
  waiting for transfers between devices  36.9 us (20%)
  Pallas kernels  18.8 us (10%)
  matrix products  4.81 us (3%)
  local copies, waits for them, and re-layouts  3.48 us (2%)
  other arithmetic  2.58 us (1%)
    ppermute x26, starting transfers between devices, shift(): lax.ppermute(array, 'expert', [(i, (i + places) % groups) for i in range(...  88.1 us
    all_to_all x2, waiting for transfers between devices, over_chips(): lax.all_to_all(array, 'replica', split_axis=0, concat_axis=0, tiled=True,...  21.3 us
    ppermute x2, starting transfers between devices, other_core(): return lax.ppermute(array, 'replica', [(i, i ^ 1) for i in range(replicas)])  16.7 us
    ppermute x26, waiting for transfers between devices, shift(): lax.ppermute(array, 'expert', [(i, (i + places) % groups) for i in range(...  13.9 us
    all_to_all x2, starting transfers between devices, over_chips(): lax.all_to_all(array, 'replica', split_axis=0, concat_axis=0, tiled=True,...  12.5 us
    pallas_call x2, Pallas kernels, _term(): pl.pallas_call(kernel, grid=(width // block,), in_specs=[pl.BlockSpec(mem...  5.96 us
    pallas_call x5, Pallas kernels, _select(): pl.pallas_call(kernel, in_specs=[pl.BlockSpec(memory_space=pltpu.SMEM)] +...  5.59 us
    dot_general x1, matrix products, body(): lax.dot_general(rows, both, (((1,), (1,)), ((), ())), preferred_element_t...  4.81 us
  transfers between devices with their start and end apart: 30, of which 8 were waited for; matrix products, arithmetic and copies ran while one was open for 4% of the time, Pallas kernels for 7%

profile of v9, /device:TPU:1, one launch (start us, length us, event | category | flops | bytes accessed | tf_op | source)
XLA Modules:
  0.0 185.0 jit_solution(6244924683521619811)
XLA Ops:
  3.1 7.6 %all-to-all-start = ((bf16[16,24,2560]{2,1,0:T(8,128)(2,1)}), bf16[16,24,2560]{2,1,0:T(8,128)(2,1)S(1)}, u32[]{:S(2)}, u32[]{:S(2)}) async-start(bf16[16,24,2560]{2,1,0:T(8,128)(2,1)} %unit_copies.1), calls=%async_computation | async-start | bytes 3932160 | tf_op jit(solution)/shard_map/all_to_all | solution.py:296
  11.6 3.5 %collective-permute-start = (bf16[136,1280]{1,0:T(8,128)(2,1)}, bf16[136,1280]{1,0:T(8,128)(2,1)}, u32[]{:S(2)}, u32[]{:S(2)}) collective-permute-start(bf16[136,1280]{1,0:T(8,128)(2,1)} %get-tuple-element.29.refs_3_), channel_id=1, source_target_pairs={{0,32},{32,64},{64,96},{96,128},{128,160},{160,192},{192,224},{224... | collective-permute-start | bytes 1044488 | tf_op jit(solution)/shard_map/ppermute | solution.py:311
  15.1 9.5 %collective-permute-start.1 = (bf16[136,1280]{1,0:T(8,128)(2,1)}, bf16[136,1280]{1,0:T(8,128)(2,1)}, u32[]{:S(2)}, u32[]{:S(2)}) collective-permute-start(bf16[136,1280]{1,0:T(8,128)(2,1)} %get-tuple-element.29.refs_3_), channel_id=1, source_target_pairs={{0,480},{32,0},{64,32},{96,64},{128,96},{160,128},{192,160},{224,1... | collective-permute-start | bytes 1044488 | tf_op jit(solution)/shard_map/ppermute | solution.py:311
  24.6 1.9 %collective-permute-start.2 = (bf16[128,1280]{1,0:T(8,128)(2,1)}, bf16[128,1280]{1,0:T(8,128)(2,1)}, u32[]{:S(2)}, u32[]{:S(2)}) collective-permute-start(bf16[128,1280]{1,0:T(8,128)(2,1)} %get-tuple-element.30.refs_2_.refs_0_), channel_id=1, source_target_pairs={{0,32},{32,64},{64,96},{96,128},{128,160},{160,192},{192,224},{224... | collective-permute-start | bytes 983048 | tf_op jit(solution)/shard_map/ppermute | solution.py:311
  26.6 4.6 %collective-permute-start.4 = (bf16[128,1280]{1,0:T(8,128)(2,1)}, bf16[128,1280]{1,0:T(8,128)(2,1)}, u32[]{:S(2)}, u32[]{:S(2)}) collective-permute-start(bf16[128,1280]{1,0:T(8,128)(2,1)} %get-tuple-element.30.refs_2_.refs_0_), channel_id=1, source_target_pairs={{0,480},{32,0},{64,32},{96,64},{128,96},{160,128},{192,160},{224,1... | collective-permute-start | bytes 983048 | tf_op jit(solution)/shard_map/ppermute | solution.py:311
  34.0 2.8 %collective-permute-start.8 = (bf16[136,1280]{1,0:T(8,128)(2,1)}, bf16[136,1280]{1,0:T(8,128)(2,1)}, u32[]{:S(2)}, u32[]{:S(2)}) collective-permute-start(bf16[136,1280]{1,0:T(8,128)(2,1)} %collective-permute-done.1.refs_5_), channel_id=1, source_target_pairs={{0,480},{32,0},{64,32},{96,64},{128,96},{160,128},{192,160},{224,1... | collective-permute-start | bytes 1044488 | tf_op jit(solution)/shard_map/ppermute | solution.py:311
  36.8 2.5 %collective-permute-start.7 = (bf16[136,1280]{1,0:T(8,128)(2,1)}, bf16[136,1280]{1,0:T(8,128)(2,1)}, u32[]{:S(2)}, u32[]{:S(2)}) collective-permute-start(bf16[136,1280]{1,0:T(8,128)(2,1)} %collective-permute-done.refs_4_), channel_id=1, source_target_pairs={{0,32},{32,64},{64,96},{96,128},{128,160},{160,192},{192,224},{224... | collective-permute-start | bytes 1044488 | tf_op jit(solution)/shard_map/ppermute | solution.py:311
  39.3 1.9 %collective-permute-start.3 = (bf16[128,1280]{1,0:T(8,128)(2,1)}, bf16[128,1280]{1,0:T(8,128)(2,1)}, u32[]{:S(2)}, u32[]{:S(2)}) collective-permute-start(bf16[128,1280]{1,0:T(8,128)(2,1)} %collective-permute-done.2.refs_1_), channel_id=1, source_target_pairs={{0,32},{32,64},{64,96},{96,128},{128,160},{160,192},{192,224},{224... | collective-permute-start | bytes 983048 | tf_op jit(solution)/shard_map/ppermute | solution.py:311
  41.2 4.6 %collective-permute-start.6 = (bf16[128,1280]{1,0:T(8,128)(2,1)}, bf16[128,1280]{1,0:T(8,128)(2,1)}, u32[]{:S(2)}, u32[]{:S(2)}) collective-permute-start(bf16[128,1280]{1,0:T(8,128)(2,1)} %collective-permute-done.4.refs_2_), channel_id=1, source_target_pairs={{0,480},{32,0},{64,32},{96,64},{128,96},{160,128},{192,160},{224,1... | collective-permute-start | bytes 983048 | tf_op jit(solution)/shard_map/ppermute | solution.py:311
  46.3 5.3 %collective-permute-start.12 = (bf16[136,1280]{1,0:T(8,128)(2,1)}, bf16[136,1280]{1,0:T(8,128)(2,1)}, u32[]{:S(2)}, u32[]{:S(2)}) collective-permute-start(bf16[136,1280]{1,0:T(8,128)(2,1)} %collective-permute-done.8.refs_3_), channel_id=1, source_target_pairs={{0,480},{32,0},{64,32},{96,64},{128,96},{160,128},{192,160},{224,1... | collective-permute-start | bytes 1044488 | tf_op jit(solution)/shard_map/ppermute | solution.py:311
  51.6 1.9 %collective-permute-start.11 = (bf16[136,1280]{1,0:T(8,128)(2,1)}, bf16[136,1280]{1,0:T(8,128)(2,1)}, u32[]{:S(2)}, u32[]{:S(2)}) collective-permute-start(bf16[136,1280]{1,0:T(8,128)(2,1)} %collective-permute-done.7.refs_2_), channel_id=1, source_target_pairs={{0,32},{32,64},{64,96},{96,128},{128,160},{160,192},{192,224},{224... | collective-permute-start | bytes 1044488 | tf_op jit(solution)/shard_map/ppermute | solution.py:311
  57.4 4.6 %collective-permute-start.10 = (bf16[128,1280]{1,0:T(8,128)(2,1)}, bf16[128,1280]{1,0:T(8,128)(2,1)S(1)}, u32[]{:S(2)}, u32[]{:S(2)}) collective-permute-start(bf16[128,1280]{1,0:T(8,128)(2,1)} %collective-permute-done.6.refs_1_), channel_id=1, source_target_pairs={{0,480},{32,0},{64,32},{96,64},{128,96},{160,128},{192,160},{224,1... | collective-permute-start | bytes 983048 | tf_op jit(solution)/shard_map/ppermute | solution.py:311
  62.0 3.4 %collective-permute-start.16 = (bf16[136,1280]{1,0:T(8,128)(2,1)}, bf16[136,1280]{1,0:T(8,128)(2,1)S(1)}, u32[]{:S(2)}, u32[]{:S(2)}) collective-permute-start(bf16[136,1280]{1,0:T(8,128)(2,1)} %collective-permute-done.12.refs_3_), channel_id=1, source_target_pairs={{0,480},{32,0},{64,32},{96,64},{128,96},{160,128},{192,160},{224,1... | collective-permute-start | bytes 1044488 | tf_op jit(solution)/shard_map/ppermute | solution.py:311
  70.9 4.6 %collective-permute-start.18 = (bf16[128,1280]{1,0:T(8,128)(2,1)S(1)}, bf16[128,1280]{1,0:T(8,128)(2,1)S(1)}, u32[]{:S(2)}, u32[]{:S(2)}) collective-permute-start(bf16[128,1280]{1,0:T(8,128)(2,1)S(1)} %collective-permute-done.10.refs_1_), channel_id=1, source_target_pairs={{0,480},{32,0},{64,32},{96,64},{128,96},{160,128},{192,160},{224,1... | collective-permute-start | bytes 983048 | tf_op jit(solution)/shard_map/ppermute | solution.py:311
  75.5 3.6 %collective-permute-start.17 = (bf16[136,1280]{1,0:T(8,128)(2,1)S(1)}, bf16[136,1280]{1,0:T(8,128)(2,1)S(1)}, u32[]{:S(2)}, u32[]{:S(2)}) collective-permute-start(bf16[136,1280]{1,0:T(8,128)(2,1)S(1)} %collective-permute-done.16.refs_3_), channel_id=1, source_target_pairs={{0,480},{32,0},{64,32},{96,64},{128,96},{160,128},{192,160},{224,1... | collective-permute-start | bytes 1044488 | tf_op jit(solution)/shard_map/ppermute | solution.py:311
  85.0 4.6 %collective-permute-start.20 = (bf16[128,1280]{1,0:T(8,128)(2,1)S(1)}, bf16[128,1280]{1,0:T(8,128)(2,1)S(1)}, u32[]{:S(2)}, u32[]{:S(2)}) collective-permute-start(bf16[128,1280]{1,0:T(8,128)(2,1)S(1)} %collective-permute-done.18.refs_1_), channel_id=1, source_target_pairs={{0,480},{32,0},{64,32},{96,64},{128,96},{160,128},{192,160},{224,1... | collective-permute-start | bytes 983048 | tf_op jit(solution)/shard_map/ppermute | solution.py:311
  90.1 3.4 %collective-permute-start.25 = (bf16[56,1280]{1,0:T(8,128)(2,1)S(1)}, bf16[56,1280]{1,0:T(8,128)(2,1)S(1)}, u32[]{:S(2)}, u32[]{:S(2)}) collective-permute-start(bf16[56,1280]{1,0:T(8,128)(2,1)S(1)} %get-tuple-element.49), channel_id=1, source_target_pairs={{0,416},{32,448},{64,480},{96,0},{128,32},{160,64},{192,96},{224,1... | collective-permute-start | bytes 430088 | tf_op jit(solution)/shard_map/ppermute | solution.py:311
  93.6 3.5 %collective-permute-done.13.first_ref.refs_0_ = bf16[128,1280]{1,0:T(8,128)(2,1)S(1)} collective-permute-done((bf16[128,1280]{1,0:T(8,128)(2,1)S(1)}, bf16[128,1280]{1,0:T(8,128)(2,1)S(1)}, u32[]{:S(2)}, u32[]{:S(2)}) %collective-permute-start.13) | collective-permute-done | bytes 327712 | tf_op jit(solution)/shard_map/ppermute | solution.py:311
  97.8 3.7 %collective-permute-start.24 = (bf16[56,2560]{1,0:T(8,128)(2,1)S(1)}, bf16[56,2560]{1,0:T(8,128)(2,1)S(1)}, u32[]{:S(2)}, u32[]{:S(2)}) collective-permute-start(bf16[56,2560]{1,0:T(8,128)(2,1)S(1)} %get-tuple-element.48), channel_id=1, source_target_pairs={{0,448},{32,480},{64,0},{96,32},{128,64},{160,96},{192,128},{224,1... | collective-permute-start | bytes 860168 | tf_op jit(solution)/shard_map/ppermute | solution.py:311
  101.5 2.5 %collective-permute-start.23 = (bf16[56,2560]{1,0:T(8,128)(2,1)S(1)}, bf16[56,2560]{1,0:T(8,128)(2,1)S(1)}, u32[]{:S(2)}, u32[]{:S(2)}) collective-permute-start(bf16[56,2560]{1,0:T(8,128)(2,1)S(1)} %get-tuple-element.47), channel_id=1, source_target_pairs={{0,64},{32,96},{64,128},{96,160},{128,192},{160,224},{192,256},{22... | collective-permute-start | bytes 860168 | tf_op jit(solution)/shard_map/ppermute | solution.py:311
  104.0 4.2 %collective-permute-start.21 = (bf16[56,2560]{1,0:T(8,128)(2,1)S(1)}, bf16[56,2560]{1,0:T(8,128)(2,1)S(1)}, u32[]{:S(2)}, u32[]{:S(2)}) collective-permute-start(bf16[56,2560]{1,0:T(8,128)(2,1)S(1)} %get-tuple-element.45), channel_id=1, source_target_pairs={{0,480},{32,0},{64,32},{96,64},{128,96},{160,128},{192,160},{224,1... | collective-permute-start | bytes 860168 | tf_op jit(solution)/shard_map/ppermute | solution.py:311
  110.2 3.5 %collective-permute-start.22 = (bf16[56,1280]{1,0:T(8,128)(2,1)S(1)}, bf16[56,1280]{1,0:T(8,128)(2,1)S(1)}, u32[]{:S(2)}, u32[]{:S(2)}) collective-permute-start(bf16[56,1280]{1,0:T(8,128)(2,1)S(1)} %get-tuple-element.46), channel_id=1, source_target_pairs={{0,96},{32,128},{64,160},{96,192},{128,224},{160,256},{192,288},{2... | collective-permute-start | bytes 430088 | tf_op jit(solution)/shard_map/ppermute | solution.py:311
  114.2 5.0 %collective-permute-done.22.refs_2_ = bf16[56,1280]{1,0:T(8,128)(2,1)S(1)} collective-permute-done((bf16[56,1280]{1,0:T(8,128)(2,1)S(1)}, bf16[56,1280]{1,0:T(8,128)(2,1)S(1)}, u32[]{:S(2)}, u32[]{:S(2)}) %collective-permute-start.22) | collective-permute-done | bytes 143392 | tf_op jit(solution)/shard_map/ppermute | solution.py:311
  119.2 4.1 %collective-permute-done.21.refs_1_ = bf16[56,2560]{1,0:T(8,128)(2,1)S(1)} collective-permute-done((bf16[56,2560]{1,0:T(8,128)(2,1)S(1)}, bf16[56,2560]{1,0:T(8,128)(2,1)S(1)}, u32[]{:S(2)}, u32[]{:S(2)}) %collective-permute-start.21) | collective-permute-done | bytes 286752 | tf_op jit(solution)/shard_map/ppermute | solution.py:311
  123.3 2.5 %term_other.1 = bf16[384,2560]{1,0:T(8,128)(2,1)S(1)} custom-call(bf16[384,896]{1,0:T(8,128)(2,1)S(1)} %get-tuple-element.51.saved_ref, bf16[896,2560]{1,0:T(8,128)(2,1)S(1)} %bitcast.18), custom_call_target="tpu_custom_call" | custom-call | flops 1761607680 | bytes 7241728 | tf_op jit(solution)/shard_map/term_other/pallas_call | solution.py:239
  125.9 14.8 %collective-permute-start.26 = (bf16[384,2560]{1,0:T(8,128)(2,1)S(1)}, bf16[384,2560]{1,0:T(8,128)(2,1)S(1)}, u32[]{:S(2)}, u32[]{:S(2)}) collective-permute-start(bf16[384,2560]{1,0:T(8,128)(2,1)S(1)} %term_other.1), channel_id=1, source_target_pairs={{0,1},{1,0},{2,3},{3,2},{4,5},{5,4},{6,7},{7,6},{8,9},{9,8},{10,11... | collective-permute-start | bytes 5898248 | tf_op jit(solution)/shard_map/ppermute | solution.py:301
  144.3 3.4 %term_pair.1 = bf16[384,2560]{1,0:T(8,128)(2,1)} custom-call(bf16[384,896]{1,0:T(8,128)(2,1)S(1)} %get-tuple-element.33.saved_ref, bf16[896,2560]{1,0:T(8,128)(2,1)S(1)} %bitcast.19, bf16[384,2560]{1,0:T(8,128)(2,1)S(1)} %collective-permute-done.26.refs_0_), custom_call_target="tpu_custom_call" | custom-call | flops 1761607680 | bytes 7241728 | tf_op jit(solution)/shard_map/term_pair/pallas_call | solution.py:239
  147.7 4.9 %all-to-all-start.1 = ((bf16[16,24,2560]{2,1,0:T(8,128)(2,1)}), bf16[16,24,2560]{2,1,0:T(8,128)(2,1)}, u32[]{:S(2)}, u32[]{:S(2)}) async-start(bf16[16,24,2560]{2,1,0:T(8,128)(2,1)} %bitcast.29), calls=%async_computation.1 | async-start | bytes 3932160 | tf_op jit(solution)/shard_map/all_to_all | solution.py:296
  152.6 2.6 %maximum_select_fusion = bf16[16,2,24,2560]{3,2,0,1:T(8,128)(2,1)S(1)} fusion(bf16[16,1,24,2560]{3,2,0,1:T(8,128)(2,1)} %bitcast.11, bf16[16,1,24,2560]{3,2,0,1:T(8,128)(2,1)S(1)} %bitcast.23, pred[]{:T(512)S(6)} %eq.3), kind=kLoop, calls=%fused_computation | loop fusion | flops 5898240 | bytes 7864321 | tf_op jit(solution)/shard_map/jit(_where)/select_n | solution.py:365
  156.4 4.8 %fusion = bf16[1,896,768]{2,1,0:T(8,128)(2,1)} fusion(bf16[896,2560]{1,0:T(8,128)(2,1)S(1)} %bitcast.22, bf16[768,2560]{1,0:T(8,128)(2,1)S(1)} %bitcast.30), kind=kOutput, calls=%fused_computation.2 | convolution fusion | flops 3523903488 | bytes 9895936 | tf_op jit(solution)/shard_map/dot_general | solution.py:370
  161.2 21.3 %all-to-all-done.1.parts_ref = bf16[16,24,2560]{2,1,0:T(8,128)(2,1)} async-done(((bf16[16,24,2560]{2,1,0:T(8,128)(2,1)}), bf16[16,24,2560]{2,1,0:T(8,128)(2,1)}, u32[]{:S(2)}, u32[]{:S(2)}) %all-to-all-start.1) | async-done | bytes 1966112 | tf_op jit(solution)/shard_map/all_to_all | solution.py:296
  182.5 2.5 %sum_parts.1 = f32[24,1,2560]{2,1,0:T(1,128)} custom-call(bf16[16,24,2560]{2,1,0:T(8,128)(2,1)} %all-to-all-done.1.parts_ref), custom_call_target="tpu_custom_call" | custom-call | flops 983040 | bytes 1966080 | tf_op jit(solution)/shard_map/sum_parts/pallas_call | solution.py:267
  (64 shorter events, 30.3 us)
Async XLA Ops:
  0.6 10.1 %copy-start.1 = (bf16[1,128,2560]{2,1,0:T(8,128)(2,1)S(1)}, bf16[1,128,2560]{2,1,0:T(8,128)(2,1)}, u32[]{:S(2)}) copy-start(bf16[1,128,2560]{2,1,0:T(8,128)(2,1)} %param.5) | copy-start | bytes 1966084
  3.1 50.5 %all-to-all-start = ((bf16[16,24,2560]{2,1,0:T(8,128)(2,1)}), bf16[16,24,2560]{2,1,0:T(8,128)(2,1)S(1)}, u32[]{:S(2)}, u32[]{:S(2)}) async-start(bf16[16,24,2560]{2,1,0:T(8,128)(2,1)} %unit_copies.1), calls=%async_computation | async-start | bytes 3932160 | tf_op jit(solution)/shard_map/all_to_all | solution.py:296
  11.6 22.3 %collective-permute-start = (bf16[136,1280]{1,0:T(8,128)(2,1)}, bf16[136,1280]{1,0:T(8,128)(2,1)}, u32[]{:S(2)}, u32[]{:S(2)}) collective-permute-start(bf16[136,1280]{1,0:T(8,128)(2,1)} %get-tuple-element.29.refs_3_), channel_id=1, source_target_pairs={{0,32},{32,64},{64,96},{96,128},{128,160},{160,192},{192,224},{224... | collective-permute-start | bytes 1044488 | tf_op jit(solution)/shard_map/ppermute | solution.py:311
  15.1 18.8 %collective-permute-start.1 = (bf16[136,1280]{1,0:T(8,128)(2,1)}, bf16[136,1280]{1,0:T(8,128)(2,1)}, u32[]{:S(2)}, u32[]{:S(2)}) collective-permute-start(bf16[136,1280]{1,0:T(8,128)(2,1)} %get-tuple-element.29.refs_3_), channel_id=1, source_target_pairs={{0,480},{32,0},{64,32},{96,64},{128,96},{160,128},{192,160},{224,1... | collective-permute-start | bytes 1044488 | tf_op jit(solution)/shard_map/ppermute | solution.py:311
  24.6 14.6 %collective-permute-start.2 = (bf16[128,1280]{1,0:T(8,128)(2,1)}, bf16[128,1280]{1,0:T(8,128)(2,1)}, u32[]{:S(2)}, u32[]{:S(2)}) collective-permute-start(bf16[128,1280]{1,0:T(8,128)(2,1)} %get-tuple-element.30.refs_2_.refs_0_), channel_id=1, source_target_pairs={{0,32},{32,64},{64,96},{96,128},{128,160},{160,192},{192,224},{224... | collective-permute-start | bytes 983048 | tf_op jit(solution)/shard_map/ppermute | solution.py:311
  26.6 14.6 %collective-permute-start.4 = (bf16[128,1280]{1,0:T(8,128)(2,1)}, bf16[128,1280]{1,0:T(8,128)(2,1)}, u32[]{:S(2)}, u32[]{:S(2)}) collective-permute-start(bf16[128,1280]{1,0:T(8,128)(2,1)} %get-tuple-element.30.refs_2_.refs_0_), channel_id=1, source_target_pairs={{0,480},{32,0},{64,32},{96,64},{128,96},{160,128},{192,160},{224,1... | collective-permute-start | bytes 983048 | tf_op jit(solution)/shard_map/ppermute | solution.py:311
  34.0 12.3 %collective-permute-start.8 = (bf16[136,1280]{1,0:T(8,128)(2,1)}, bf16[136,1280]{1,0:T(8,128)(2,1)}, u32[]{:S(2)}, u32[]{:S(2)}) collective-permute-start(bf16[136,1280]{1,0:T(8,128)(2,1)} %collective-permute-done.1.refs_5_), channel_id=1, source_target_pairs={{0,480},{32,0},{64,32},{96,64},{128,96},{160,128},{192,160},{224,1... | collective-permute-start | bytes 1044488 | tf_op jit(solution)/shard_map/ppermute | solution.py:311
  36.8 14.9 %collective-permute-start.7 = (bf16[136,1280]{1,0:T(8,128)(2,1)}, bf16[136,1280]{1,0:T(8,128)(2,1)}, u32[]{:S(2)}, u32[]{:S(2)}) collective-permute-start(bf16[136,1280]{1,0:T(8,128)(2,1)} %collective-permute-done.refs_4_), channel_id=1, source_target_pairs={{0,32},{32,64},{64,96},{96,128},{128,160},{160,192},{192,224},{224... | collective-permute-start | bytes 1044488 | tf_op jit(solution)/shard_map/ppermute | solution.py:311
  39.3 16.2 %collective-permute-start.3 = (bf16[128,1280]{1,0:T(8,128)(2,1)}, bf16[128,1280]{1,0:T(8,128)(2,1)}, u32[]{:S(2)}, u32[]{:S(2)}) collective-permute-start(bf16[128,1280]{1,0:T(8,128)(2,1)} %collective-permute-done.2.refs_1_), channel_id=1, source_target_pairs={{0,32},{32,64},{64,96},{96,128},{128,160},{160,192},{192,224},{224... | collective-permute-start | bytes 983048 | tf_op jit(solution)/shard_map/ppermute | solution.py:311
  41.2 16.2 %collective-permute-start.6 = (bf16[128,1280]{1,0:T(8,128)(2,1)}, bf16[128,1280]{1,0:T(8,128)(2,1)}, u32[]{:S(2)}, u32[]{:S(2)}) collective-permute-start(bf16[128,1280]{1,0:T(8,128)(2,1)} %collective-permute-done.4.refs_2_), channel_id=1, source_target_pairs={{0,480},{32,0},{64,32},{96,64},{128,96},{160,128},{192,160},{224,1... | collective-permute-start | bytes 983048 | tf_op jit(solution)/shard_map/ppermute | solution.py:311
  46.3 15.7 %collective-permute-start.12 = (bf16[136,1280]{1,0:T(8,128)(2,1)}, bf16[136,1280]{1,0:T(8,128)(2,1)}, u32[]{:S(2)}, u32[]{:S(2)}) collective-permute-start(bf16[136,1280]{1,0:T(8,128)(2,1)} %collective-permute-done.8.refs_3_), channel_id=1, source_target_pairs={{0,480},{32,0},{64,32},{96,64},{128,96},{160,128},{192,160},{224,1... | collective-permute-start | bytes 1044488 | tf_op jit(solution)/shard_map/ppermute | solution.py:311
  51.6 13.8 %collective-permute-start.11 = (bf16[136,1280]{1,0:T(8,128)(2,1)}, bf16[136,1280]{1,0:T(8,128)(2,1)}, u32[]{:S(2)}, u32[]{:S(2)}) collective-permute-start(bf16[136,1280]{1,0:T(8,128)(2,1)} %collective-permute-done.7.refs_2_), channel_id=1, source_target_pairs={{0,32},{32,64},{64,96},{96,128},{128,160},{160,192},{192,224},{224... | collective-permute-start | bytes 1044488 | tf_op jit(solution)/shard_map/ppermute | solution.py:311
  55.5 13.5 %collective-permute-start.5 = (bf16[128,1280]{1,0:T(8,128)(2,1)}, bf16[128,1280]{1,0:T(8,128)(2,1)S(1)}, u32[]{:S(2)}, u32[]{:S(2)}) collective-permute-start(bf16[128,1280]{1,0:T(8,128)(2,1)} %collective-permute-done.3.refs_0_), channel_id=1, source_target_pairs={{0,32},{32,64},{64,96},{96,128},{128,160},{160,192},{192,224},{224... | collective-permute-start | bytes 983048 | tf_op jit(solution)/shard_map/ppermute | solution.py:311
  57.4 13.5 %collective-permute-start.10 = (bf16[128,1280]{1,0:T(8,128)(2,1)}, bf16[128,1280]{1,0:T(8,128)(2,1)S(1)}, u32[]{:S(2)}, u32[]{:S(2)}) collective-permute-start(bf16[128,1280]{1,0:T(8,128)(2,1)} %collective-permute-done.6.refs_1_), channel_id=1, source_target_pairs={{0,480},{32,0},{64,32},{96,64},{128,96},{160,128},{192,160},{224,1... | collective-permute-start | bytes 983048 | tf_op jit(solution)/shard_map/ppermute | solution.py:311
  62.0 13.5 %collective-permute-start.16 = (bf16[136,1280]{1,0:T(8,128)(2,1)}, bf16[136,1280]{1,0:T(8,128)(2,1)S(1)}, u32[]{:S(2)}, u32[]{:S(2)}) collective-permute-start(bf16[136,1280]{1,0:T(8,128)(2,1)} %collective-permute-done.12.refs_3_), channel_id=1, source_target_pairs={{0,480},{32,0},{64,32},{96,64},{128,96},{160,128},{192,160},{224,1... | collective-permute-start | bytes 1044488 | tf_op jit(solution)/shard_map/ppermute | solution.py:311
  65.4 13.7 %collective-permute-start.14 = (bf16[136,1280]{1,0:T(8,128)(2,1)}, bf16[136,1280]{1,0:T(8,128)(2,1)S(1)}, u32[]{:S(2)}, u32[]{:S(2)}) collective-permute-start(bf16[136,1280]{1,0:T(8,128)(2,1)} %collective-permute-done.11.refs_2_), channel_id=1, source_target_pairs={{0,32},{32,64},{64,96},{96,128},{128,160},{160,192},{192,224},{224... | collective-permute-start | bytes 1044488 | tf_op jit(solution)/shard_map/ppermute | solution.py:311
  69.0 14.1 %collective-permute-start.9 = (bf16[128,1280]{1,0:T(8,128)(2,1)S(1)}, bf16[128,1280]{1,0:T(8,128)(2,1)S(1)}, u32[]{:S(2)}, u32[]{:S(2)}) collective-permute-start(bf16[128,1280]{1,0:T(8,128)(2,1)S(1)} %collective-permute-done.5.refs_0_), channel_id=1, source_target_pairs={{0,32},{32,64},{64,96},{96,128},{128,160},{160,192},{192,224},{224... | collective-permute-start | bytes 983048 | tf_op jit(solution)/shard_map/ppermute | solution.py:311
  70.9 14.1 %collective-permute-start.18 = (bf16[128,1280]{1,0:T(8,128)(2,1)S(1)}, bf16[128,1280]{1,0:T(8,128)(2,1)S(1)}, u32[]{:S(2)}, u32[]{:S(2)}) collective-permute-start(bf16[128,1280]{1,0:T(8,128)(2,1)S(1)} %collective-permute-done.10.refs_1_), channel_id=1, source_target_pairs={{0,480},{32,0},{64,32},{96,64},{128,96},{160,128},{192,160},{224,1... | collective-permute-start | bytes 983048 | tf_op jit(solution)/shard_map/ppermute | solution.py:311
  75.5 14.4 %collective-permute-start.17 = (bf16[136,1280]{1,0:T(8,128)(2,1)S(1)}, bf16[136,1280]{1,0:T(8,128)(2,1)S(1)}, u32[]{:S(2)}, u32[]{:S(2)}) collective-permute-start(bf16[136,1280]{1,0:T(8,128)(2,1)S(1)} %collective-permute-done.16.refs_3_), channel_id=1, source_target_pairs={{0,480},{32,0},{64,32},{96,64},{128,96},{160,128},{192,160},{224,1... | collective-permute-start | bytes 1044488 | tf_op jit(solution)/shard_map/ppermute | solution.py:311
  79.1 14.4 %collective-permute-start.15 = (bf16[136,1280]{1,0:T(8,128)(2,1)S(1)}, bf16[136,1280]{1,0:T(8,128)(2,1)S(1)}, u32[]{:S(2)}, u32[]{:S(2)}) collective-permute-start(bf16[136,1280]{1,0:T(8,128)(2,1)S(1)} %collective-permute-done.14.refs_2_), channel_id=1, source_target_pairs={{0,32},{32,64},{64,96},{96,128},{128,160},{160,192},{192,224},{224... | collective-permute-start | bytes 1044488 | tf_op jit(solution)/shard_map/ppermute | solution.py:311
  83.1 14.0 %collective-permute-start.13 = (bf16[128,1280]{1,0:T(8,128)(2,1)S(1)}, bf16[128,1280]{1,0:T(8,128)(2,1)S(1)}, u32[]{:S(2)}, u32[]{:S(2)}) collective-permute-start(bf16[128,1280]{1,0:T(8,128)(2,1)S(1)} %collective-permute-done.9.refs_0_), channel_id=1, source_target_pairs={{0,32},{32,64},{64,96},{96,128},{128,160},{160,192},{192,224},{224... | collective-permute-start | bytes 983048 | tf_op jit(solution)/shard_map/ppermute | solution.py:311
  85.0 12.5 %collective-permute-start.20 = (bf16[128,1280]{1,0:T(8,128)(2,1)S(1)}, bf16[128,1280]{1,0:T(8,128)(2,1)S(1)}, u32[]{:S(2)}, u32[]{:S(2)}) collective-permute-start(bf16[128,1280]{1,0:T(8,128)(2,1)S(1)} %collective-permute-done.18.refs_1_), channel_id=1, source_target_pairs={{0,480},{32,0},{64,32},{96,64},{128,96},{160,128},{192,160},{224,1... | collective-permute-start | bytes 983048 | tf_op jit(solution)/shard_map/ppermute | solution.py:311
  90.1 20.1 %collective-permute-start.25 = (bf16[56,1280]{1,0:T(8,128)(2,1)S(1)}, bf16[56,1280]{1,0:T(8,128)(2,1)S(1)}, u32[]{:S(2)}, u32[]{:S(2)}) collective-permute-start(bf16[56,1280]{1,0:T(8,128)(2,1)S(1)} %get-tuple-element.49), channel_id=1, source_target_pairs={{0,416},{32,448},{64,480},{96,0},{128,32},{160,64},{192,96},{224,1... | collective-permute-start | bytes 430088 | tf_op jit(solution)/shard_map/ppermute | solution.py:311
  97.8 16.4 %collective-permute-start.24 = (bf16[56,2560]{1,0:T(8,128)(2,1)S(1)}, bf16[56,2560]{1,0:T(8,128)(2,1)S(1)}, u32[]{:S(2)}, u32[]{:S(2)}) collective-permute-start(bf16[56,2560]{1,0:T(8,128)(2,1)S(1)} %get-tuple-element.48), channel_id=1, source_target_pairs={{0,448},{32,480},{64,0},{96,32},{128,64},{160,96},{192,128},{224,1... | collective-permute-start | bytes 860168 | tf_op jit(solution)/shard_map/ppermute | solution.py:311
  101.5 12.7 %collective-permute-start.23 = (bf16[56,2560]{1,0:T(8,128)(2,1)S(1)}, bf16[56,2560]{1,0:T(8,128)(2,1)S(1)}, u32[]{:S(2)}, u32[]{:S(2)}) collective-permute-start(bf16[56,2560]{1,0:T(8,128)(2,1)S(1)} %get-tuple-element.47), channel_id=1, source_target_pairs={{0,64},{32,96},{64,128},{96,160},{128,192},{160,224},{192,256},{22... | collective-permute-start | bytes 860168 | tf_op jit(solution)/shard_map/ppermute | solution.py:311
  104.0 19.3 %collective-permute-start.21 = (bf16[56,2560]{1,0:T(8,128)(2,1)S(1)}, bf16[56,2560]{1,0:T(8,128)(2,1)S(1)}, u32[]{:S(2)}, u32[]{:S(2)}) collective-permute-start(bf16[56,2560]{1,0:T(8,128)(2,1)S(1)} %get-tuple-element.45), channel_id=1, source_target_pairs={{0,480},{32,0},{64,32},{96,64},{128,96},{160,128},{192,160},{224,1... | collective-permute-start | bytes 860168 | tf_op jit(solution)/shard_map/ppermute | solution.py:311
  108.2 15.0 %collective-permute-start.19 = (bf16[56,2560]{1,0:T(8,128)(2,1)S(1)}, bf16[56,2560]{1,0:T(8,128)(2,1)S(1)}, u32[]{:S(2)}, u32[]{:S(2)}) collective-permute-start(bf16[56,2560]{1,0:T(8,128)(2,1)S(1)} %get-tuple-element.43), channel_id=1, source_target_pairs={{0,32},{32,64},{64,96},{96,128},{128,160},{160,192},{192,224},{224... | collective-permute-start | bytes 860168 | tf_op jit(solution)/shard_map/ppermute | solution.py:311
  110.2 9.1 %collective-permute-start.22 = (bf16[56,1280]{1,0:T(8,128)(2,1)S(1)}, bf16[56,1280]{1,0:T(8,128)(2,1)S(1)}, u32[]{:S(2)}, u32[]{:S(2)}) collective-permute-start(bf16[56,1280]{1,0:T(8,128)(2,1)S(1)} %get-tuple-element.46), channel_id=1, source_target_pairs={{0,96},{32,128},{64,160},{96,192},{128,224},{160,256},{192,288},{2... | collective-permute-start | bytes 430088 | tf_op jit(solution)/shard_map/ppermute | solution.py:311
  123.3 24.3 %copy-start = (bf16[16,56,2560]{2,1,0:T(8,128)(2,1)}, bf16[16,56,2560]{2,1,0:T(8,128)(2,1)S(1)}, u32[]{:S(2)}) copy-start(bf16[16,56,2560]{2,1,0:T(8,128)(2,1)S(1)} %place_late.1) | copy-start | bytes 13762564
  125.9 18.4 %collective-permute-start.26 = (bf16[384,2560]{1,0:T(8,128)(2,1)S(1)}, bf16[384,2560]{1,0:T(8,128)(2,1)S(1)}, u32[]{:S(2)}, u32[]{:S(2)}) collective-permute-start(bf16[384,2560]{1,0:T(8,128)(2,1)S(1)} %term_other.1), channel_id=1, source_target_pairs={{0,1},{1,0},{2,3},{3,2},{4,5},{5,4},{6,7},{7,6},{8,9},{9,8},{10,11... | collective-permute-start | bytes 5898248 | tf_op jit(solution)/shard_map/ppermute | solution.py:301
  140.7 11.9 %collective-permute-start.27 = (bf16[16,24,2560]{2,1,0:T(8,128)(2,1)S(1)}, bf16[16,24,2560]{2,1,0:T(8,128)(2,1)}, u32[]{:S(2)}, u32[]{:S(2)}) collective-permute-start(bf16[16,24,2560]{2,1,0:T(8,128)(2,1)S(1)} %all-to-all-done.refs_6_), channel_id=1, source_target_pairs={{0,1},{1,0},{2,3},{3,2},{4,5},{5,4},{6,7},{7,6},{8,9},{9,8},{10,11... | collective-permute-start | bytes 5898248 | tf_op jit(solution)/shard_map/ppermute | solution.py:301
  147.7 34.8 %all-to-all-start.1 = ((bf16[16,24,2560]{2,1,0:T(8,128)(2,1)}), bf16[16,24,2560]{2,1,0:T(8,128)(2,1)}, u32[]{:S(2)}, u32[]{:S(2)}) async-start(bf16[16,24,2560]{2,1,0:T(8,128)(2,1)} %bitcast.29), calls=%async_computation.1 | async-start | bytes 3932160 | tf_op jit(solution)/shard_map/all_to_all | solution.py:296
  (6 other events, 25.1 us)

commit v10 on v9

--- a/solution.py
+++ b/solution.py
@@ -200,29 +200,6 @@
     )(me, *arrays, rows)
 
 
-def _copies(array, copies):
-    def kernel(array_ref, out_ref, sems):
-        started = []
-        for i in range(copies):
-            started.append(pltpu.make_async_copy(array_ref, out_ref.at[i], sems.at[i]))
-            started[-1].start()
-        for copy in started:
-            copy.wait()
-
-    return pl.pallas_call(
-        kernel,
-        in_specs=[pl.BlockSpec(memory_space=pltpu.HBM)],
-        out_specs=pl.BlockSpec(memory_space=pltpu.HBM),
-        out_shape=pltpu.HBM((copies,) + array.shape, BF),
-        scratch_shapes=[pltpu.SemaphoreType.DMA((copies,))],
-        compiler_params=pltpu.CompilerParams(vmem_limit_bytes=VMEM),
-        cost_estimate=pl.CostEstimate(
-            flops=0, bytes_accessed=2 * (copies + 1) * array.size, transcendentals=0
-        ),
-        name="unit_copies",
-    )(array)
-
-
 def _term(saved_t, rows, name, more=None):
     units, depth = saved_t.shape
     width = rows.shape[1]
@@ -300,7 +277,9 @@
     def other_core(array):
         return lax.ppermute(array, "replica", [(i, i ^ 1) for i in range(replicas)])
 
-    weights_mine = over_chips(_copies(down_weight[:, 0, :], chips))
+    weights_mine = over_chips(
+        jnp.broadcast_to(down_weight[:, 0, :][None], (chips, units_dev, width))
+    )
 
     own_first, own_second = _pack(grads[0], routes.transpose(2, 0, 1), gates[0].T)
 

time: 187 us -> 187 us (level)
    broadcast_in_dim x0 -> x1, local copies, waits for them, and re-layouts: none -> 2.4 us  [body(): jnp.broadcast_to(down_weight[:, 0, :][None], (chips, units_dev, width))]
where the time goes in v10:
time: 187 us; the launch traced here: 185 us
  starting transfers between devices  117 us (63%)
  waiting for transfers between devices  36.9 us (20%)
  Pallas kernels  17.3 us (9%)
  local copies, waits for them, and re-layouts  4.93 us (3%)
  matrix products  4.8 us (3%)
  other arithmetic  2.56 us (1%)
    ppermute x26, starting transfers between devices, shift(): lax.ppermute(array, 'expert', [(i, (i + places) % groups) for i in range(...  88.1 us
    all_to_all x2, waiting for transfers between devices, over_chips(): lax.all_to_all(array, 'replica', split_axis=0, concat_axis=0, tiled=True,...  21.4 us
    ppermute x2, starting transfers between devices, other_core(): return lax.ppermute(array, 'replica', [(i, i ^ 1) for i in range(replicas)])  16.7 us
    ppermute x26, waiting for transfers between devices, shift(): lax.ppermute(array, 'expert', [(i, (i + places) % groups) for i in range(...  13.9 us
    all_to_all x2, starting transfers between devices, over_chips(): lax.all_to_all(array, 'replica', split_axis=0, concat_axis=0, tiled=True,...  12.4 us
    pallas_call x2, Pallas kernels, _term(): pl.pallas_call(kernel, grid=(width // block,), in_specs=[pl.BlockSpec(mem...  5.94 us
    pallas_call x5, Pallas kernels, _select(): pl.pallas_call(kernel, in_specs=[pl.BlockSpec(memory_space=pltpu.SMEM)] +...  5.59 us
    dot_general x1, matrix products, body(): lax.dot_general(rows, both, (((1,), (1,)), ((), ())), preferred_element_t...  4.8 us
  transfers between devices with their start and end apart: 30, of which 8 were waited for; matrix products, arithmetic and copies ran while one was open for 4% of the time, Pallas kernels for 7%

profile of v10, /device:TPU:1, one launch (start us, length us, event | category | flops | bytes accessed | tf_op | source)
XLA Modules:
  0.0 185.0 jit_solution(14100140798714170414)
XLA Ops:
  0.7 2.4 %broadcast_in_dim.11 = bf16[16,24,2560]{2,1,0:T(8,128)(2,1)} broadcast(bf16[24,2560]{1,0:T(8,128)(2,1)} %bitcast.30), dimensions={1,2} | broadcast | bytes 2088960 | tf_op jit(solution)/shard_map/broadcast_in_dim | solution.py:281
  3.1 7.6 %all-to-all-start = ((bf16[16,24,2560]{2,1,0:T(8,128)(2,1)}), bf16[16,24,2560]{2,1,0:T(8,128)(2,1)S(1)}, u32[]{:S(2)}, u32[]{:S(2)}) async-start(bf16[16,24,2560]{2,1,0:T(8,128)(2,1)} %broadcast_in_dim.11), calls=%async_computation | async-start | bytes 3932160 | tf_op jit(solution)/shard_map/all_to_all | solution.py:273
  11.6 3.5 %collective-permute-start = (bf16[136,1280]{1,0:T(8,128)(2,1)}, bf16[136,1280]{1,0:T(8,128)(2,1)}, u32[]{:S(2)}, u32[]{:S(2)}) collective-permute-start(bf16[136,1280]{1,0:T(8,128)(2,1)} %get-tuple-element.29.refs_3_), channel_id=1, source_target_pairs={{0,32},{32,64},{64,96},{96,128},{128,160},{160,192},{192,224},{224... | collective-permute-start | bytes 1044488 | tf_op jit(solution)/shard_map/ppermute | solution.py:290
  15.1 9.5 %collective-permute-start.1 = (bf16[136,1280]{1,0:T(8,128)(2,1)}, bf16[136,1280]{1,0:T(8,128)(2,1)}, u32[]{:S(2)}, u32[]{:S(2)}) collective-permute-start(bf16[136,1280]{1,0:T(8,128)(2,1)} %get-tuple-element.29.refs_3_), channel_id=1, source_target_pairs={{0,480},{32,0},{64,32},{96,64},{128,96},{160,128},{192,160},{224,1... | collective-permute-start | bytes 1044488 | tf_op jit(solution)/shard_map/ppermute | solution.py:290
  24.6 1.9 %collective-permute-start.2 = (bf16[128,1280]{1,0:T(8,128)(2,1)}, bf16[128,1280]{1,0:T(8,128)(2,1)}, u32[]{:S(2)}, u32[]{:S(2)}) collective-permute-start(bf16[128,1280]{1,0:T(8,128)(2,1)} %get-tuple-element.30.refs_2_.refs_0_), channel_id=1, source_target_pairs={{0,32},{32,64},{64,96},{96,128},{128,160},{160,192},{192,224},{224... | collective-permute-start | bytes 983048 | tf_op jit(solution)/shard_map/ppermute | solution.py:290
  26.5 4.6 %collective-permute-start.4 = (bf16[128,1280]{1,0:T(8,128)(2,1)}, bf16[128,1280]{1,0:T(8,128)(2,1)}, u32[]{:S(2)}, u32[]{:S(2)}) collective-permute-start(bf16[128,1280]{1,0:T(8,128)(2,1)} %get-tuple-element.30.refs_2_.refs_0_), channel_id=1, source_target_pairs={{0,480},{32,0},{64,32},{96,64},{128,96},{160,128},{192,160},{224,1... | collective-permute-start | bytes 983048 | tf_op jit(solution)/shard_map/ppermute | solution.py:290
  33.9 2.8 %collective-permute-start.8 = (bf16[136,1280]{1,0:T(8,128)(2,1)}, bf16[136,1280]{1,0:T(8,128)(2,1)}, u32[]{:S(2)}, u32[]{:S(2)}) collective-permute-start(bf16[136,1280]{1,0:T(8,128)(2,1)} %collective-permute-done.1.refs_5_), channel_id=1, source_target_pairs={{0,480},{32,0},{64,32},{96,64},{128,96},{160,128},{192,160},{224,1... | collective-permute-start | bytes 1044488 | tf_op jit(solution)/shard_map/ppermute | solution.py:290
  36.7 2.5 %collective-permute-start.7 = (bf16[136,1280]{1,0:T(8,128)(2,1)}, bf16[136,1280]{1,0:T(8,128)(2,1)}, u32[]{:S(2)}, u32[]{:S(2)}) collective-permute-start(bf16[136,1280]{1,0:T(8,128)(2,1)} %collective-permute-done.refs_4_), channel_id=1, source_target_pairs={{0,32},{32,64},{64,96},{96,128},{128,160},{160,192},{192,224},{224... | collective-permute-start | bytes 1044488 | tf_op jit(solution)/shard_map/ppermute | solution.py:290
  39.2 1.9 %collective-permute-start.3 = (bf16[128,1280]{1,0:T(8,128)(2,1)}, bf16[128,1280]{1,0:T(8,128)(2,1)}, u32[]{:S(2)}, u32[]{:S(2)}) collective-permute-start(bf16[128,1280]{1,0:T(8,128)(2,1)} %collective-permute-done.2.refs_1_), channel_id=1, source_target_pairs={{0,32},{32,64},{64,96},{96,128},{128,160},{160,192},{192,224},{224... | collective-permute-start | bytes 983048 | tf_op jit(solution)/shard_map/ppermute | solution.py:290
  41.2 4.6 %collective-permute-start.6 = (bf16[128,1280]{1,0:T(8,128)(2,1)}, bf16[128,1280]{1,0:T(8,128)(2,1)}, u32[]{:S(2)}, u32[]{:S(2)}) collective-permute-start(bf16[128,1280]{1,0:T(8,128)(2,1)} %collective-permute-done.4.refs_2_), channel_id=1, source_target_pairs={{0,480},{32,0},{64,32},{96,64},{128,96},{160,128},{192,160},{224,1... | collective-permute-start | bytes 983048 | tf_op jit(solution)/shard_map/ppermute | solution.py:290
  46.3 5.3 %collective-permute-start.12 = (bf16[136,1280]{1,0:T(8,128)(2,1)}, bf16[136,1280]{1,0:T(8,128)(2,1)}, u32[]{:S(2)}, u32[]{:S(2)}) collective-permute-start(bf16[136,1280]{1,0:T(8,128)(2,1)} %collective-permute-done.8.refs_3_), channel_id=1, source_target_pairs={{0,480},{32,0},{64,32},{96,64},{128,96},{160,128},{192,160},{224,1... | collective-permute-start | bytes 1044488 | tf_op jit(solution)/shard_map/ppermute | solution.py:290
  57.4 4.6 %collective-permute-start.10 = (bf16[128,1280]{1,0:T(8,128)(2,1)}, bf16[128,1280]{1,0:T(8,128)(2,1)S(1)}, u32[]{:S(2)}, u32[]{:S(2)}) collective-permute-start(bf16[128,1280]{1,0:T(8,128)(2,1)} %collective-permute-done.6.refs_1_), channel_id=1, source_target_pairs={{0,480},{32,0},{64,32},{96,64},{128,96},{160,128},{192,160},{224,1... | collective-permute-start | bytes 983048 | tf_op jit(solution)/shard_map/ppermute | solution.py:290
  62.0 3.4 %collective-permute-start.16 = (bf16[136,1280]{1,0:T(8,128)(2,1)}, bf16[136,1280]{1,0:T(8,128)(2,1)S(1)}, u32[]{:S(2)}, u32[]{:S(2)}) collective-permute-start(bf16[136,1280]{1,0:T(8,128)(2,1)} %collective-permute-done.12.refs_3_), channel_id=1, source_target_pairs={{0,480},{32,0},{64,32},{96,64},{128,96},{160,128},{192,160},{224,1... | collective-permute-start | bytes 1044488 | tf_op jit(solution)/shard_map/ppermute | solution.py:290
  70.9 4.6 %collective-permute-start.18 = (bf16[128,1280]{1,0:T(8,128)(2,1)S(1)}, bf16[128,1280]{1,0:T(8,128)(2,1)S(1)}, u32[]{:S(2)}, u32[]{:S(2)}) collective-permute-start(bf16[128,1280]{1,0:T(8,128)(2,1)S(1)} %collective-permute-done.10.refs_1_), channel_id=1, source_target_pairs={{0,480},{32,0},{64,32},{96,64},{128,96},{160,128},{192,160},{224,1... | collective-permute-start | bytes 983048 | tf_op jit(solution)/shard_map/ppermute | solution.py:290
  75.5 3.6 %collective-permute-start.17 = (bf16[136,1280]{1,0:T(8,128)(2,1)S(1)}, bf16[136,1280]{1,0:T(8,128)(2,1)S(1)}, u32[]{:S(2)}, u32[]{:S(2)}) collective-permute-start(bf16[136,1280]{1,0:T(8,128)(2,1)S(1)} %collective-permute-done.16.refs_3_), channel_id=1, source_target_pairs={{0,480},{32,0},{64,32},{96,64},{128,96},{160,128},{192,160},{224,1... | collective-permute-start | bytes 1044488 | tf_op jit(solution)/shard_map/ppermute | solution.py:290
  85.0 4.6 %collective-permute-start.20 = (bf16[128,1280]{1,0:T(8,128)(2,1)S(1)}, bf16[128,1280]{1,0:T(8,128)(2,1)S(1)}, u32[]{:S(2)}, u32[]{:S(2)}) collective-permute-start(bf16[128,1280]{1,0:T(8,128)(2,1)S(1)} %collective-permute-done.18.refs_1_), channel_id=1, source_target_pairs={{0,480},{32,0},{64,32},{96,64},{128,96},{160,128},{192,160},{224,1... | collective-permute-start | bytes 983048 | tf_op jit(solution)/shard_map/ppermute | solution.py:290
  90.1 3.4 %collective-permute-start.25 = (bf16[56,1280]{1,0:T(8,128)(2,1)S(1)}, bf16[56,1280]{1,0:T(8,128)(2,1)S(1)}, u32[]{:S(2)}, u32[]{:S(2)}) collective-permute-start(bf16[56,1280]{1,0:T(8,128)(2,1)S(1)} %get-tuple-element.49), channel_id=1, source_target_pairs={{0,416},{32,448},{64,480},{96,0},{128,32},{160,64},{192,96},{224,1... | collective-permute-start | bytes 430088 | tf_op jit(solution)/shard_map/ppermute | solution.py:290
  93.5 3.5 %collective-permute-done.13.first_ref.refs_0_ = bf16[128,1280]{1,0:T(8,128)(2,1)S(1)} collective-permute-done((bf16[128,1280]{1,0:T(8,128)(2,1)S(1)}, bf16[128,1280]{1,0:T(8,128)(2,1)S(1)}, u32[]{:S(2)}, u32[]{:S(2)}) %collective-permute-start.13) | collective-permute-done | bytes 327712 | tf_op jit(solution)/shard_map/ppermute | solution.py:290
  97.8 3.7 %collective-permute-start.24 = (bf16[56,2560]{1,0:T(8,128)(2,1)S(1)}, bf16[56,2560]{1,0:T(8,128)(2,1)S(1)}, u32[]{:S(2)}, u32[]{:S(2)}) collective-permute-start(bf16[56,2560]{1,0:T(8,128)(2,1)S(1)} %get-tuple-element.48), channel_id=1, source_target_pairs={{0,448},{32,480},{64,0},{96,32},{128,64},{160,96},{192,128},{224,1... | collective-permute-start | bytes 860168 | tf_op jit(solution)/shard_map/ppermute | solution.py:290
  101.4 2.5 %collective-permute-start.23 = (bf16[56,2560]{1,0:T(8,128)(2,1)S(1)}, bf16[56,2560]{1,0:T(8,128)(2,1)S(1)}, u32[]{:S(2)}, u32[]{:S(2)}) collective-permute-start(bf16[56,2560]{1,0:T(8,128)(2,1)S(1)} %get-tuple-element.47), channel_id=1, source_target_pairs={{0,64},{32,96},{64,128},{96,160},{128,192},{160,224},{192,256},{22... | collective-permute-start | bytes 860168 | tf_op jit(solution)/shard_map/ppermute | solution.py:290
  103.9 4.2 %collective-permute-start.21 = (bf16[56,2560]{1,0:T(8,128)(2,1)S(1)}, bf16[56,2560]{1,0:T(8,128)(2,1)S(1)}, u32[]{:S(2)}, u32[]{:S(2)}) collective-permute-start(bf16[56,2560]{1,0:T(8,128)(2,1)S(1)} %get-tuple-element.45), channel_id=1, source_target_pairs={{0,480},{32,0},{64,32},{96,64},{128,96},{160,128},{192,160},{224,1... | collective-permute-start | bytes 860168 | tf_op jit(solution)/shard_map/ppermute | solution.py:290
  110.1 3.5 %collective-permute-start.22 = (bf16[56,1280]{1,0:T(8,128)(2,1)S(1)}, bf16[56,1280]{1,0:T(8,128)(2,1)S(1)}, u32[]{:S(2)}, u32[]{:S(2)}) collective-permute-start(bf16[56,1280]{1,0:T(8,128)(2,1)S(1)} %get-tuple-element.46), channel_id=1, source_target_pairs={{0,96},{32,128},{64,160},{96,192},{128,224},{160,256},{192,288},{2... | collective-permute-start | bytes 430088 | tf_op jit(solution)/shard_map/ppermute | solution.py:290
  114.2 5.0 %collective-permute-done.22.refs_2_ = bf16[56,1280]{1,0:T(8,128)(2,1)S(1)} collective-permute-done((bf16[56,1280]{1,0:T(8,128)(2,1)S(1)}, bf16[56,1280]{1,0:T(8,128)(2,1)S(1)}, u32[]{:S(2)}, u32[]{:S(2)}) %collective-permute-start.22) | collective-permute-done | bytes 143392 | tf_op jit(solution)/shard_map/ppermute | solution.py:290
  119.2 4.1 %collective-permute-done.21.refs_1_ = bf16[56,2560]{1,0:T(8,128)(2,1)S(1)} collective-permute-done((bf16[56,2560]{1,0:T(8,128)(2,1)S(1)}, bf16[56,2560]{1,0:T(8,128)(2,1)S(1)}, u32[]{:S(2)}, u32[]{:S(2)}) %collective-permute-start.21) | collective-permute-done | bytes 286752 | tf_op jit(solution)/shard_map/ppermute | solution.py:290
  123.3 2.5 %term_other.1 = bf16[384,2560]{1,0:T(8,128)(2,1)S(1)} custom-call(bf16[384,896]{1,0:T(8,128)(2,1)S(1)} %get-tuple-element.51.saved_ref, bf16[896,2560]{1,0:T(8,128)(2,1)S(1)} %bitcast.18), custom_call_target="tpu_custom_call" | custom-call | flops 1761607680 | bytes 7241728 | tf_op jit(solution)/shard_map/term_other/pallas_call | solution.py:216
  125.8 14.8 %collective-permute-start.26 = (bf16[384,2560]{1,0:T(8,128)(2,1)S(1)}, bf16[384,2560]{1,0:T(8,128)(2,1)S(1)}, u32[]{:S(2)}, u32[]{:S(2)}) collective-permute-start(bf16[384,2560]{1,0:T(8,128)(2,1)S(1)} %term_other.1), channel_id=1, source_target_pairs={{0,1},{1,0},{2,3},{3,2},{4,5},{5,4},{6,7},{7,6},{8,9},{9,8},{10,11... | collective-permute-start | bytes 5898248 | tf_op jit(solution)/shard_map/ppermute | solution.py:278
  144.2 3.4 %term_pair.1 = bf16[384,2560]{1,0:T(8,128)(2,1)} custom-call(bf16[384,896]{1,0:T(8,128)(2,1)S(1)} %get-tuple-element.33.saved_ref, bf16[896,2560]{1,0:T(8,128)(2,1)S(1)} %bitcast.19, bf16[384,2560]{1,0:T(8,128)(2,1)S(1)} %collective-permute-done.26.refs_0_), custom_call_target="tpu_custom_call" | custom-call | flops 1761607680 | bytes 7241728 | tf_op jit(solution)/shard_map/term_pair/pallas_call | solution.py:216
  147.7 4.9 %all-to-all-start.1 = ((bf16[16,24,2560]{2,1,0:T(8,128)(2,1)}), bf16[16,24,2560]{2,1,0:T(8,128)(2,1)}, u32[]{:S(2)}, u32[]{:S(2)}) async-start(bf16[16,24,2560]{2,1,0:T(8,128)(2,1)} %bitcast.28), calls=%async_computation.1 | async-start | bytes 3932160 | tf_op jit(solution)/shard_map/all_to_all | solution.py:273
  152.6 2.6 %maximum_select_fusion = bf16[16,2,24,2560]{3,2,0,1:T(8,128)(2,1)S(1)} fusion(bf16[16,1,24,2560]{3,2,0,1:T(8,128)(2,1)} %bitcast.11, bf16[16,1,24,2560]{3,2,0,1:T(8,128)(2,1)S(1)} %bitcast.23, pred[]{:T(512)S(6)} %eq.3), kind=kLoop, calls=%fused_computation | loop fusion | flops 5898240 | bytes 7864321 | tf_op jit(solution)/shard_map/jit(_where)/select_n | solution.py:344
  156.3 4.8 %fusion = bf16[1,896,768]{2,1,0:T(8,128)(2,1)} fusion(bf16[896,2560]{1,0:T(8,128)(2,1)S(1)} %bitcast.22, bf16[768,2560]{1,0:T(8,128)(2,1)S(1)} %bitcast.29), kind=kOutput, calls=%fused_computation.2 | convolution fusion | flops 3523903488 | bytes 9895936 | tf_op jit(solution)/shard_map/dot_general | solution.py:349
  161.1 21.4 %all-to-all-done.1.parts_ref = bf16[16,24,2560]{2,1,0:T(8,128)(2,1)} async-done(((bf16[16,24,2560]{2,1,0:T(8,128)(2,1)}), bf16[16,24,2560]{2,1,0:T(8,128)(2,1)}, u32[]{:S(2)}, u32[]{:S(2)}) %all-to-all-start.1) | async-done | bytes 1966112 | tf_op jit(solution)/shard_map/all_to_all | solution.py:273
  182.5 2.5 %sum_parts.1 = f32[24,1,2560]{2,1,0:T(1,128)} custom-call(bf16[16,24,2560]{2,1,0:T(8,128)(2,1)} %all-to-all-done.1.parts_ref), custom_call_target="tpu_custom_call" | custom-call | flops 983040 | bytes 1966080 | tf_op jit(solution)/shard_map/sum_parts/pallas_call | solution.py:244
  (62 shorter events, 29.8 us)
Async XLA Ops:
  0.6 10.0 %copy-start.1 = (bf16[1,128,2560]{2,1,0:T(8,128)(2,1)S(1)}, bf16[1,128,2560]{2,1,0:T(8,128)(2,1)}, u32[]{:S(2)}) copy-start(bf16[1,128,2560]{2,1,0:T(8,128)(2,1)} %param.5) | copy-start | bytes 1966084
  3.1 50.5 %all-to-all-start = ((bf16[16,24,2560]{2,1,0:T(8,128)(2,1)}), bf16[16,24,2560]{2,1,0:T(8,128)(2,1)S(1)}, u32[]{:S(2)}, u32[]{:S(2)}) async-start(bf16[16,24,2560]{2,1,0:T(8,128)(2,1)} %broadcast_in_dim.11), calls=%async_computation | async-start | bytes 3932160 | tf_op jit(solution)/shard_map/all_to_all | solution.py:273
  11.6 22.3 %collective-permute-start = (bf16[136,1280]{1,0:T(8,128)(2,1)}, bf16[136,1280]{1,0:T(8,128)(2,1)}, u32[]{:S(2)}, u32[]{:S(2)}) collective-permute-start(bf16[136,1280]{1,0:T(8,128)(2,1)} %get-tuple-element.29.refs_3_), channel_id=1, source_target_pairs={{0,32},{32,64},{64,96},{96,128},{128,160},{160,192},{192,224},{224... | collective-permute-start | bytes 1044488 | tf_op jit(solution)/shard_map/ppermute | solution.py:290
  15.1 18.8 %collective-permute-start.1 = (bf16[136,1280]{1,0:T(8,128)(2,1)}, bf16[136,1280]{1,0:T(8,128)(2,1)}, u32[]{:S(2)}, u32[]{:S(2)}) collective-permute-start(bf16[136,1280]{1,0:T(8,128)(2,1)} %get-tuple-element.29.refs_3_), channel_id=1, source_target_pairs={{0,480},{32,0},{64,32},{96,64},{128,96},{160,128},{192,160},{224,1... | collective-permute-start | bytes 1044488 | tf_op jit(solution)/shard_map/ppermute | solution.py:290
  24.6 14.6 %collective-permute-start.2 = (bf16[128,1280]{1,0:T(8,128)(2,1)}, bf16[128,1280]{1,0:T(8,128)(2,1)}, u32[]{:S(2)}, u32[]{:S(2)}) collective-permute-start(bf16[128,1280]{1,0:T(8,128)(2,1)} %get-tuple-element.30.refs_2_.refs_0_), channel_id=1, source_target_pairs={{0,32},{32,64},{64,96},{96,128},{128,160},{160,192},{192,224},{224... | collective-permute-start | bytes 983048 | tf_op jit(solution)/shard_map/ppermute | solution.py:290
  26.5 14.6 %collective-permute-start.4 = (bf16[128,1280]{1,0:T(8,128)(2,1)}, bf16[128,1280]{1,0:T(8,128)(2,1)}, u32[]{:S(2)}, u32[]{:S(2)}) collective-permute-start(bf16[128,1280]{1,0:T(8,128)(2,1)} %get-tuple-element.30.refs_2_.refs_0_), channel_id=1, source_target_pairs={{0,480},{32,0},{64,32},{96,64},{128,96},{160,128},{192,160},{224,1... | collective-permute-start | bytes 983048 | tf_op jit(solution)/shard_map/ppermute | solution.py:290
  33.9 12.3 %collective-permute-start.8 = (bf16[136,1280]{1,0:T(8,128)(2,1)}, bf16[136,1280]{1,0:T(8,128)(2,1)}, u32[]{:S(2)}, u32[]{:S(2)}) collective-permute-start(bf16[136,1280]{1,0:T(8,128)(2,1)} %collective-permute-done.1.refs_5_), channel_id=1, source_target_pairs={{0,480},{32,0},{64,32},{96,64},{128,96},{160,128},{192,160},{224,1... | collective-permute-start | bytes 1044488 | tf_op jit(solution)/shard_map/ppermute | solution.py:290
  36.7 14.9 %collective-permute-start.7 = (bf16[136,1280]{1,0:T(8,128)(2,1)}, bf16[136,1280]{1,0:T(8,128)(2,1)}, u32[]{:S(2)}, u32[]{:S(2)}) collective-permute-start(bf16[136,1280]{1,0:T(8,128)(2,1)} %collective-permute-done.refs_4_), channel_id=1, source_target_pairs={{0,32},{32,64},{64,96},{96,128},{128,160},{160,192},{192,224},{224... | collective-permute-start | bytes 1044488 | tf_op jit(solution)/shard_map/ppermute | solution.py:290
  39.2 16.2 %collective-permute-start.3 = (bf16[128,1280]{1,0:T(8,128)(2,1)}, bf16[128,1280]{1,0:T(8,128)(2,1)}, u32[]{:S(2)}, u32[]{:S(2)}) collective-permute-start(bf16[128,1280]{1,0:T(8,128)(2,1)} %collective-permute-done.2.refs_1_), channel_id=1, source_target_pairs={{0,32},{32,64},{64,96},{96,128},{128,160},{160,192},{192,224},{224... | collective-permute-start | bytes 983048 | tf_op jit(solution)/shard_map/ppermute | solution.py:290
  41.2 16.2 %collective-permute-start.6 = (bf16[128,1280]{1,0:T(8,128)(2,1)}, bf16[128,1280]{1,0:T(8,128)(2,1)}, u32[]{:S(2)}, u32[]{:S(2)}) collective-permute-start(bf16[128,1280]{1,0:T(8,128)(2,1)} %collective-permute-done.4.refs_2_), channel_id=1, source_target_pairs={{0,480},{32,0},{64,32},{96,64},{128,96},{160,128},{192,160},{224,1... | collective-permute-start | bytes 983048 | tf_op jit(solution)/shard_map/ppermute | solution.py:290
  46.3 15.7 %collective-permute-start.12 = (bf16[136,1280]{1,0:T(8,128)(2,1)}, bf16[136,1280]{1,0:T(8,128)(2,1)}, u32[]{:S(2)}, u32[]{:S(2)}) collective-permute-start(bf16[136,1280]{1,0:T(8,128)(2,1)} %collective-permute-done.8.refs_3_), channel_id=1, source_target_pairs={{0,480},{32,0},{64,32},{96,64},{128,96},{160,128},{192,160},{224,1... | collective-permute-start | bytes 1044488 | tf_op jit(solution)/shard_map/ppermute | solution.py:290
  51.6 13.8 %collective-permute-start.11 = (bf16[136,1280]{1,0:T(8,128)(2,1)}, bf16[136,1280]{1,0:T(8,128)(2,1)}, u32[]{:S(2)}, u32[]{:S(2)}) collective-permute-start(bf16[136,1280]{1,0:T(8,128)(2,1)} %collective-permute-done.7.refs_2_), channel_id=1, source_target_pairs={{0,32},{32,64},{64,96},{96,128},{128,160},{160,192},{192,224},{224... | collective-permute-start | bytes 1044488 | tf_op jit(solution)/shard_map/ppermute | solution.py:290
  55.5 13.5 %collective-permute-start.5 = (bf16[128,1280]{1,0:T(8,128)(2,1)}, bf16[128,1280]{1,0:T(8,128)(2,1)S(1)}, u32[]{:S(2)}, u32[]{:S(2)}) collective-permute-start(bf16[128,1280]{1,0:T(8,128)(2,1)} %collective-permute-done.3.refs_0_), channel_id=1, source_target_pairs={{0,32},{32,64},{64,96},{96,128},{128,160},{160,192},{192,224},{224... | collective-permute-start | bytes 983048 | tf_op jit(solution)/shard_map/ppermute | solution.py:290
  57.4 13.5 %collective-permute-start.10 = (bf16[128,1280]{1,0:T(8,128)(2,1)}, bf16[128,1280]{1,0:T(8,128)(2,1)S(1)}, u32[]{:S(2)}, u32[]{:S(2)}) collective-permute-start(bf16[128,1280]{1,0:T(8,128)(2,1)} %collective-permute-done.6.refs_1_), channel_id=1, source_target_pairs={{0,480},{32,0},{64,32},{96,64},{128,96},{160,128},{192,160},{224,1... | collective-permute-start | bytes 983048 | tf_op jit(solution)/shard_map/ppermute | solution.py:290
  62.0 13.5 %collective-permute-start.16 = (bf16[136,1280]{1,0:T(8,128)(2,1)}, bf16[136,1280]{1,0:T(8,128)(2,1)S(1)}, u32[]{:S(2)}, u32[]{:S(2)}) collective-permute-start(bf16[136,1280]{1,0:T(8,128)(2,1)} %collective-permute-done.12.refs_3_), channel_id=1, source_target_pairs={{0,480},{32,0},{64,32},{96,64},{128,96},{160,128},{192,160},{224,1... | collective-permute-start | bytes 1044488 | tf_op jit(solution)/shard_map/ppermute | solution.py:290
  65.4 13.7 %collective-permute-start.14 = (bf16[136,1280]{1,0:T(8,128)(2,1)}, bf16[136,1280]{1,0:T(8,128)(2,1)S(1)}, u32[]{:S(2)}, u32[]{:S(2)}) collective-permute-start(bf16[136,1280]{1,0:T(8,128)(2,1)} %collective-permute-done.11.refs_2_), channel_id=1, source_target_pairs={{0,32},{32,64},{64,96},{96,128},{128,160},{160,192},{192,224},{224... | collective-permute-start | bytes 1044488 | tf_op jit(solution)/shard_map/ppermute | solution.py:290
  69.0 14.1 %collective-permute-start.9 = (bf16[128,1280]{1,0:T(8,128)(2,1)S(1)}, bf16[128,1280]{1,0:T(8,128)(2,1)S(1)}, u32[]{:S(2)}, u32[]{:S(2)}) collective-permute-start(bf16[128,1280]{1,0:T(8,128)(2,1)S(1)} %collective-permute-done.5.refs_0_), channel_id=1, source_target_pairs={{0,32},{32,64},{64,96},{96,128},{128,160},{160,192},{192,224},{224... | collective-permute-start | bytes 983048 | tf_op jit(solution)/shard_map/ppermute | solution.py:290
  70.9 14.1 %collective-permute-start.18 = (bf16[128,1280]{1,0:T(8,128)(2,1)S(1)}, bf16[128,1280]{1,0:T(8,128)(2,1)S(1)}, u32[]{:S(2)}, u32[]{:S(2)}) collective-permute-start(bf16[128,1280]{1,0:T(8,128)(2,1)S(1)} %collective-permute-done.10.refs_1_), channel_id=1, source_target_pairs={{0,480},{32,0},{64,32},{96,64},{128,96},{160,128},{192,160},{224,1... | collective-permute-start | bytes 983048 | tf_op jit(solution)/shard_map/ppermute | solution.py:290
  75.5 14.4 %collective-permute-start.17 = (bf16[136,1280]{1,0:T(8,128)(2,1)S(1)}, bf16[136,1280]{1,0:T(8,128)(2,1)S(1)}, u32[]{:S(2)}, u32[]{:S(2)}) collective-permute-start(bf16[136,1280]{1,0:T(8,128)(2,1)S(1)} %collective-permute-done.16.refs_3_), channel_id=1, source_target_pairs={{0,480},{32,0},{64,32},{96,64},{128,96},{160,128},{192,160},{224,1... | collective-permute-start | bytes 1044488 | tf_op jit(solution)/shard_map/ppermute | solution.py:290
  79.1 14.5 %collective-permute-start.15 = (bf16[136,1280]{1,0:T(8,128)(2,1)S(1)}, bf16[136,1280]{1,0:T(8,128)(2,1)S(1)}, u32[]{:S(2)}, u32[]{:S(2)}) collective-permute-start(bf16[136,1280]{1,0:T(8,128)(2,1)S(1)} %collective-permute-done.14.refs_2_), channel_id=1, source_target_pairs={{0,32},{32,64},{64,96},{96,128},{128,160},{160,192},{192,224},{224... | collective-permute-start | bytes 1044488 | tf_op jit(solution)/shard_map/ppermute | solution.py:290
  83.0 14.0 %collective-permute-start.13 = (bf16[128,1280]{1,0:T(8,128)(2,1)S(1)}, bf16[128,1280]{1,0:T(8,128)(2,1)S(1)}, u32[]{:S(2)}, u32[]{:S(2)}) collective-permute-start(bf16[128,1280]{1,0:T(8,128)(2,1)S(1)} %collective-permute-done.9.refs_0_), channel_id=1, source_target_pairs={{0,32},{32,64},{64,96},{96,128},{128,160},{160,192},{192,224},{224... | collective-permute-start | bytes 983048 | tf_op jit(solution)/shard_map/ppermute | solution.py:290
  85.0 12.4 %collective-permute-start.20 = (bf16[128,1280]{1,0:T(8,128)(2,1)S(1)}, bf16[128,1280]{1,0:T(8,128)(2,1)S(1)}, u32[]{:S(2)}, u32[]{:S(2)}) collective-permute-start(bf16[128,1280]{1,0:T(8,128)(2,1)S(1)} %collective-permute-done.18.refs_1_), channel_id=1, source_target_pairs={{0,480},{32,0},{64,32},{96,64},{128,96},{160,128},{192,160},{224,1... | collective-permute-start | bytes 983048 | tf_op jit(solution)/shard_map/ppermute | solution.py:290
  90.1 20.0 %collective-permute-start.25 = (bf16[56,1280]{1,0:T(8,128)(2,1)S(1)}, bf16[56,1280]{1,0:T(8,128)(2,1)S(1)}, u32[]{:S(2)}, u32[]{:S(2)}) collective-permute-start(bf16[56,1280]{1,0:T(8,128)(2,1)S(1)} %get-tuple-element.49), channel_id=1, source_target_pairs={{0,416},{32,448},{64,480},{96,0},{128,32},{160,64},{192,96},{224,1... | collective-permute-start | bytes 430088 | tf_op jit(solution)/shard_map/ppermute | solution.py:290
  97.8 16.4 %collective-permute-start.24 = (bf16[56,2560]{1,0:T(8,128)(2,1)S(1)}, bf16[56,2560]{1,0:T(8,128)(2,1)S(1)}, u32[]{:S(2)}, u32[]{:S(2)}) collective-permute-start(bf16[56,2560]{1,0:T(8,128)(2,1)S(1)} %get-tuple-element.48), channel_id=1, source_target_pairs={{0,448},{32,480},{64,0},{96,32},{128,64},{160,96},{192,128},{224,1... | collective-permute-start | bytes 860168 | tf_op jit(solution)/shard_map/ppermute | solution.py:290
  101.4 12.7 %collective-permute-start.23 = (bf16[56,2560]{1,0:T(8,128)(2,1)S(1)}, bf16[56,2560]{1,0:T(8,128)(2,1)S(1)}, u32[]{:S(2)}, u32[]{:S(2)}) collective-permute-start(bf16[56,2560]{1,0:T(8,128)(2,1)S(1)} %get-tuple-element.47), channel_id=1, source_target_pairs={{0,64},{32,96},{64,128},{96,160},{128,192},{160,224},{192,256},{22... | collective-permute-start | bytes 860168 | tf_op jit(solution)/shard_map/ppermute | solution.py:290
  103.9 19.3 %collective-permute-start.21 = (bf16[56,2560]{1,0:T(8,128)(2,1)S(1)}, bf16[56,2560]{1,0:T(8,128)(2,1)S(1)}, u32[]{:S(2)}, u32[]{:S(2)}) collective-permute-start(bf16[56,2560]{1,0:T(8,128)(2,1)S(1)} %get-tuple-element.45), channel_id=1, source_target_pairs={{0,480},{32,0},{64,32},{96,64},{128,96},{160,128},{192,160},{224,1... | collective-permute-start | bytes 860168 | tf_op jit(solution)/shard_map/ppermute | solution.py:290
  108.2 15.1 %collective-permute-start.19 = (bf16[56,2560]{1,0:T(8,128)(2,1)S(1)}, bf16[56,2560]{1,0:T(8,128)(2,1)S(1)}, u32[]{:S(2)}, u32[]{:S(2)}) collective-permute-start(bf16[56,2560]{1,0:T(8,128)(2,1)S(1)} %get-tuple-element.43), channel_id=1, source_target_pairs={{0,32},{32,64},{64,96},{96,128},{128,160},{160,192},{192,224},{224... | collective-permute-start | bytes 860168 | tf_op jit(solution)/shard_map/ppermute | solution.py:290
  110.1 9.1 %collective-permute-start.22 = (bf16[56,1280]{1,0:T(8,128)(2,1)S(1)}, bf16[56,1280]{1,0:T(8,128)(2,1)S(1)}, u32[]{:S(2)}, u32[]{:S(2)}) collective-permute-start(bf16[56,1280]{1,0:T(8,128)(2,1)S(1)} %get-tuple-element.46), channel_id=1, source_target_pairs={{0,96},{32,128},{64,160},{96,192},{128,224},{160,256},{192,288},{2... | collective-permute-start | bytes 430088 | tf_op jit(solution)/shard_map/ppermute | solution.py:290
  123.3 24.4 %copy-start = (bf16[16,56,2560]{2,1,0:T(8,128)(2,1)}, bf16[16,56,2560]{2,1,0:T(8,128)(2,1)S(1)}, u32[]{:S(2)}) copy-start(bf16[16,56,2560]{2,1,0:T(8,128)(2,1)S(1)} %place_late.1) | copy-start | bytes 13762564
  125.8 18.4 %collective-permute-start.26 = (bf16[384,2560]{1,0:T(8,128)(2,1)S(1)}, bf16[384,2560]{1,0:T(8,128)(2,1)S(1)}, u32[]{:S(2)}, u32[]{:S(2)}) collective-permute-start(bf16[384,2560]{1,0:T(8,128)(2,1)S(1)} %term_other.1), channel_id=1, source_target_pairs={{0,1},{1,0},{2,3},{3,2},{4,5},{5,4},{6,7},{7,6},{8,9},{9,8},{10,11... | collective-permute-start | bytes 5898248 | tf_op jit(solution)/shard_map/ppermute | solution.py:278
  140.7 11.9 %collective-permute-start.27 = (bf16[16,24,2560]{2,1,0:T(8,128)(2,1)S(1)}, bf16[16,24,2560]{2,1,0:T(8,128)(2,1)}, u32[]{:S(2)}, u32[]{:S(2)}) collective-permute-start(bf16[16,24,2560]{2,1,0:T(8,128)(2,1)S(1)} %all-to-all-done.refs_6_), channel_id=1, source_target_pairs={{0,1},{1,0},{2,3},{3,2},{4,5},{5,4},{6,7},{7,6},{8,9},{9,8},{10,11... | collective-permute-start | bytes 5898248 | tf_op jit(solution)/shard_map/ppermute | solution.py:278
  147.7 34.8 %all-to-all-start.1 = ((bf16[16,24,2560]{2,1,0:T(8,128)(2,1)}), bf16[16,24,2560]{2,1,0:T(8,128)(2,1)}, u32[]{:S(2)}, u32[]{:S(2)}) async-start(bf16[16,24,2560]{2,1,0:T(8,128)(2,1)} %bitcast.28), calls=%async_computation.1 | async-start | bytes 3932160 | tf_op jit(solution)/shard_map/all_to_all | solution.py:273
  (5 other events, 26.0 us)
